TPU v7x, 32 devices: a whole 2x2x4 slice. The times are simulated.
32 devices in a mesh: grp: 2 (over x), tile: 16 (over z, y, core).
Axes of the slice: x: 2, y: 2, z: 4, core: 2. Of those that a mesh axis runs over, the one named last changes fastest.
Arguments:
- subgrids: bfloat16 [8192, 2, 1024], P(('grp', 'tile')), parts along dimension 0, may hold values from -10 to 10
- stations: int32 [8192, 2], P(('grp', 'tile')), parts along dimension 0, may hold values from 0 to 127, as said below
- time_slots: int32 [8192], P(('grp', 'tile')), parts along dimension 0, may hold values from 0 to 7
- assign: int32 [32, 16, 64], P(('grp', 'tile')), parts along dimension 0, may hold values from 0 to 255, as said below
- counts: int32 [32, 16], P(('grp', 'tile')), parts along dimension 0, may hold values from 0 to 64, as said below
- beam_coefs: bfloat16 [256, 8, 256], P(('grp', 'tile')), parts along dimension 0, may hold values from -0.5 to 0.5
- beam_basis: bfloat16 [2, 128, 1024], replicated, may hold values from -6 to 6
- frequencies: float32 [64], P('grp'), parts along dimension 0, may hold values from 0.5 to 2
- uv_tracks: float32 [32, 16, 64, 2, 4], P(('grp', 'tile')), parts along dimension 0, may hold values from -8 to 8
- observed: float32 [32, 16, 64, 2, 128], P(('grp', 'tile')), parts along dimension 0, may hold values from -6 to 6
Outputs:
- residual: float32 [32, 16, 64, 2, 128], P(('grp', 'tile')), parts along dimension 0
There are 2 independent parts, one for each index of `grp`. A program takes and returns all parts, laid end to end along the dimension named above; an argument that names none is the same for every part. Nothing has to cross between parts.
Inputs may be any that keep to these rules, and one draw needn't show every extreme that they name: `assign`: for every source s, the live slots (c < counts[s, d]) of all d together name each of the numbers 0 to 255 exactly once; slots that are not live hold 0. `counts`: each row sums to 256. In every draw one baseline block receives 64 subgrids from every source. The two stations of a row differ.
All inputs are finite; a program needn't handle non-finite values.
Results may differ from a plain program's by a relative error of at most 0.0021.
Values may be sent and summed in bfloat16 or wider, within the bound.
No kernel may reach another device: no remote copies, remote signals or barrier semaphores. Data moves between devices by JAX's collectives and lax.ppermute only.
A program may use at most 64 MiB of HBM per device.

v0:
```python
import math

import jax
import jax.numpy as jnp
from jax import lax
from jax.sharding import PartitionSpec as P

TWO_PI = 2.0 * math.pi


def beam_matrix(beam_basis):
    real_part = beam_basis[0]
    imag_part = beam_basis[1]
    upper = jnp.concatenate([real_part, imag_part], axis=1)
    lower = jnp.concatenate([-imag_part, real_part], axis=1)
    return jnp.concatenate([upper, lower], axis=0)


def inverse_transform(grids):
    number = grids.shape[0]
    sub_edge = math.isqrt(grids.shape[2])
    index_ints = jnp.arange(sub_edge, dtype=jnp.int32)
    products = index_ints[:, None] * index_ints[None, :] % sub_edge
    angles = TWO_PI / sub_edge * products.astype(jnp.float32)
    cosine = jnp.cos(angles) / sub_edge
    sine = jnp.sin(angles) / sub_edge
    grid_re = grids[:, 0].astype(jnp.float32).reshape(number, sub_edge, sub_edge)
    grid_im = grids[:, 1].astype(jnp.float32).reshape(number, sub_edge, sub_edge)
    highest = lax.Precision.HIGHEST
    half_re = jnp.einsum("nba,ax->nbx", grid_re, cosine, precision=highest) - jnp.einsum(
        "nba,ax->nbx", grid_im, sine, precision=highest
    )
    half_im = jnp.einsum("nba,ax->nbx", grid_re, sine, precision=highest) + jnp.einsum(
        "nba,ax->nbx", grid_im, cosine, precision=highest
    )
    image_re = jnp.einsum("yb,nbx->nyx", cosine, half_re, precision=highest) - jnp.einsum(
        "yb,nbx->nyx", sine, half_im, precision=highest
    )
    image_im = jnp.einsum("yb,nbx->nyx", cosine, half_im, precision=highest) + jnp.einsum(
        "yb,nbx->nyx", sine, half_re, precision=highest
    )
    stacked = jnp.stack([image_re, image_im], axis=1)
    return stacked.reshape(number, 2, sub_edge * sub_edge).astype(jnp.bfloat16)


def predict_block(images, first_rows, second_rows, weights, tracks, table, matrix, frequencies):
    number = images.shape[0]
    pixels = images.shape[2]
    sub_edge = math.isqrt(pixels)
    beam_first = jnp.dot(table[first_rows], matrix, preferred_element_type=jnp.float32)
    beam_second = jnp.dot(table[second_rows], matrix, preferred_element_type=jnp.float32)
    first_re = beam_first[:, :pixels]
    first_im = beam_first[:, pixels:]
    second_re = beam_second[:, :pixels]
    second_im = beam_second[:, pixels:]
    gain_re = first_re * second_re + first_im * second_im
    gain_im = first_im * second_re - first_re * second_im
    image_re = images[:, 0].astype(jnp.float32)
    image_im = images[:, 1].astype(jnp.float32)
    weighted_re = (
        (image_re * gain_re - image_im * gain_im)
        .astype(jnp.bfloat16)
        .reshape(number, sub_edge, sub_edge)
    )
    weighted_im = (
        (image_re * gain_im + image_im * gain_re)
        .astype(jnp.bfloat16)
        .reshape(number, sub_edge, sub_edge)
    )
    weighted = jnp.concatenate([weighted_re, weighted_im], axis=2)
    u_coord = (tracks[:, 0, :, None] * frequencies[None, None, :]).reshape(number, -1)
    v_coord = (tracks[:, 1, :, None] * frequencies[None, None, :]).reshape(number, -1)
    visible = u_coord.shape[1]
    offsets = jnp.arange(sub_edge, dtype=jnp.float32) - 0.5 * sub_edge
    angle_u = -TWO_PI / sub_edge * offsets[None, :, None] * u_coord[:, None, :]
    cos_u = jnp.cos(angle_u).astype(jnp.bfloat16)
    sin_u = jnp.sin(angle_u).astype(jnp.bfloat16)
    phase = jnp.concatenate(
        [jnp.concatenate([cos_u, sin_u], axis=2), jnp.concatenate([-sin_u, cos_u], axis=2)], axis=1
    )
    partial_sums = jnp.einsum("byx,bxj->byj", weighted, phase, preferred_element_type=jnp.float32)
    part_re = partial_sums[:, :, :visible]
    part_im = partial_sums[:, :, visible:]
    angle_v = -TWO_PI / sub_edge * offsets[None, :, None] * v_coord[:, None, :]
    cos_v = jnp.cos(angle_v)
    sin_v = jnp.sin(angle_v)
    model_re = jnp.sum(part_re * cos_v - part_im * sin_v, axis=1)
    model_im = jnp.sum(part_re * sin_v + part_im * cos_v, axis=1)
    return jnp.stack([model_re, model_im], axis=1) * weights[:, None, None]


def run_blocks(images, first_rows, second_rows, weights, tracks, table, matrix, frequencies):
    number = images.shape[0]
    block_len = math.gcd(number, 64)
    groups = number // block_len

    def one_block(members):
        return predict_block(
            members[0], members[1], members[2], members[3], members[4], table, matrix, frequencies
        )

    models = lax.map(
        one_block,
        (
            images.reshape(groups, block_len, 2, images.shape[2]),
            first_rows.reshape(groups, block_len),
            second_rows.reshape(groups, block_len),
            weights.reshape(groups, block_len),
            tracks.reshape(groups, block_len, 2, tracks.shape[2]),
        ),
    )
    return models.reshape(number, 2, models.shape[3])


def per_device(
    subgrids,
    stations,
    time_slots,
    assign,
    counts,
    beam_coefs,
    beam_basis,
    frequencies,
    uv_tracks,
    observed,
):
    tiles_count = lax.axis_size("tile")
    capacity = assign.shape[2]
    total = tiles_count * capacity
    routing = assign[0]
    live_slots = (jnp.arange(capacity, dtype=jnp.int32)[None, :] < counts[0][:, None]).astype(
        jnp.int32
    )
    table = lax.all_gather(beam_coefs, "tile", axis=0, tiled=True)
    slot_count = table.shape[1]
    table = table.reshape(table.shape[0] * slot_count, table.shape[2])
    first_rows = stations[:, 0] * slot_count + time_slots
    second_rows = stations[:, 1] * slot_count + time_slots
    matrix = beam_matrix(beam_basis)
    visible = observed.shape[4]
    steps_count = uv_tracks.shape[4]
    labels = jnp.stack([first_rows[routing], second_rows[routing], live_slots], axis=2)
    payload = inverse_transform(subgrids)[routing]
    arrived, labels_in = (
        lax.all_to_all(payload, "tile", split_axis=0, concat_axis=0, tiled=True),
        lax.all_to_all(labels, "tile", split_axis=0, concat_axis=0, tiled=True),
    )
    images = arrived.reshape(total, 2, arrived.shape[3])
    labels_in = labels_in.reshape(total, 3)
    models = run_blocks(
        images,
        labels_in[:, 0],
        labels_in[:, 1],
        labels_in[:, 2].astype(jnp.float32),
        uv_tracks[0].reshape(total, 2, steps_count),
        table,
        matrix,
        frequencies,
    )
    residual = observed[0] - models.reshape(tiles_count, capacity, 2, visible)
    return residual[None]


def solution(mesh):
    return jax.shard_map(
        per_device,
        mesh=mesh,
        in_specs=(
            P(("grp", "tile"), None, None),
            P(("grp", "tile"), None),
            P(("grp", "tile")),
            P(("grp", "tile"), None, None),
            P(("grp", "tile"), None),
            P(("grp", "tile"), None, None),
            P(),
            P("grp"),
            P(("grp", "tile"), None, None, None, None),
            P(("grp", "tile"), None, None, None, None),
        ),
        out_specs=P(("grp", "tile"), None, None, None, None),
        check_vma=False,
    )
```

profile of v0, /device:TPU:9, one launch (start us, length us, event | category | flops | bytes accessed | tf_op | source)
XLA Modules:
  0.0 498.9 jit_solution(10866833762531005221)
XLA Ops:
  2.2 6.8 %gather_fusion.4 = s32[1024]{0:T(1024)S(1)} fusion(s32[256]{0:T(256)S(1)} %get-tuple-element.193, s32[1024]{0:T(1024)S(1)} %broadcast_clamp_fusion), kind=kCustom, calls=%fused_computation.4 | custom fusion | bytes 12288 | tf_op jit(solution)/shard_map/gather | solution.py:142
  9.1 6.8 %gather_fusion.3 = s32[1024]{0:T(1024)S(1)} fusion(s32[256]{0:T(256)S(1)} %get-tuple-element.192, s32[1024]{0:T(1024)S(1)} %broadcast_clamp_fusion), kind=kCustom, calls=%fused_computation.3 | custom fusion | bytes 12288 | tf_op jit(solution)/shard_map/gather | solution.py:142
  16.9 6.6 %all-to-all-start.1 = ((s32[16,1,192]{2,1,0:T(1,128)}), s32[16,1,192]{2,1,0:T(1,128)S(1)}, u32[]{:S(2)}, u32[]{:S(2)}) async-start(s32[16,1,192]{2,1,0:T(1,128)} %reshape.345), calls=%async_computation.1 | async-start | bytes 32768 | tf_op jit(solution)/shard_map/all_to_all | solution.py:146
  23.5 2.3 fusion.120
  28.1 2.3 copy.94
  31.9 1.7 fusion.44
  33.6 1.7 fusion.40
  35.3 1.7 fusion.38
  37.1 1.8 fusion.37
  41.4 2.6 pad_maximum_fusion
  44.1 15.4 %gather_fusion.2 = bf16[1024,2,1024]{2,1,0:T(2,128)(2,1)} fusion(bf16[256,2,1024]{2,1,0:T(2,128)(2,1)S(1)} %pad_maximum_fusion, s32[1024]{0:T(1024)S(1)} %broadcast_clamp_fusion), kind=kCustom, calls=%fused_computation.2 | custom fusion | bytes 8392704 | tf_op jit(solution)/shard_map/gather | solution.py:143
  59.5 5.5 %copy.107 = bf16[16,64,2,1024]{3,1,2,0:T(8,128)(2,1)} copy(bf16[16,64,2,1024]{3,2,1,0:T(2,128)(2,1)} %bitcast.158) | data formatting | bytes 8388608 | tf_op jit(solution)/shard_map/gather | solution.py:143
  65.1 6.1 %all-to-all-start = ((bf16[16,64,2,1024]{3,1,2,0:T(8,128)(2,1)}), bf16[16,64,2,1024]{3,1,2,0:T(8,128)(2,1)}, u32[]{:S(2)}, u32[]{:S(2)}) async-start(bf16[16,64,2,1024]{3,1,2,0:T(8,128)(2,1)} %copy.107), calls=%async_computation | async-start | bytes 8388608 | tf_op jit(solution)/shard_map/all_to_all | solution.py:145
  71.3 104.5 %all_gather.3 = bf16[128,8,256]{2,1,0:T(8,128)(2,1)S(1)} all-gather(bf16[8,8,256]{2,1,0:T(8,128)(2,1)S(1)} %copy-done.2), channel_id=1, replica_groups=mesh['grp'=2,'tile'=16] {'tile'}, dimensions={0}, use_global_device_ids=true | all-gather | bytes 557056 | tf_op jit(solution)/shard_map/all_gather | solution.py:134
  177.6 318.1 %while.12 = (s32[]{:T(128)}, f32[16,64,2,128]{3,2,1,0:T(2,128)}, bf16[16,64,2,1024]{3,1,2,0:T(8,128)(2,1)}, s32[16,64]{1,0:T(8,128)S(1)}, bf16[1024,256]{1,0:T(8...) while((s32[]{:T(128)}, f32[16,64,2,128]{3,2,1,0:T(2,128)}, ...), condition=%wide.region_3.4_spmd, body=%wide.region_0.3_spmd.sunk | while | flops 215910848 | bytes 15916553 | solution.py:102
  183.8 3.6 fusion.157
  187.5 4.0 fusion.156
  192.3 4.5 fusion.164
  203.7 3.6 fusion.157
  207.3 4.0 fusion.156
  212.2 4.5 fusion.164
  223.6 3.6 fusion.157
  227.2 4.0 fusion.156
  232.0 4.5 fusion.164
  243.5 3.6 fusion.157
  247.1 4.0 fusion.156
  251.9 4.5 fusion.164
  263.4 3.6 fusion.157
  267.0 4.0 fusion.156
  271.8 4.5 fusion.164
  283.3 3.6 fusion.157
  286.9 4.0 fusion.156
  291.7 4.5 fusion.164
  303.1 3.6 fusion.157
  306.8 4.0 fusion.156
  311.6 4.5 fusion.164
  323.0 3.6 fusion.157
  326.6 4.0 fusion.156
  331.5 4.5 fusion.164
  342.9 3.6 fusion.157
  346.5 4.0 fusion.156
  351.3 4.5 fusion.164
  362.8 3.6 fusion.157
  366.4 4.0 fusion.156
  371.2 4.5 fusion.164
  382.7 3.6 fusion.157
  386.3 4.0 fusion.156
  391.1 4.5 fusion.164
  402.6 3.6 fusion.157
  406.2 4.0 fusion.156
  411.0 4.5 fusion.164
  422.4 3.6 fusion.157
  426.1 4.0 fusion.156
  430.9 4.5 fusion.164
  442.3 3.6 fusion.157
  445.9 4.0 fusion.156
  450.7 4.5 fusion.164
  462.2 3.6 fusion.157
  465.8 4.0 fusion.156
  470.6 4.5 fusion.164
  482.1 3.6 fusion.157
  485.7 4.0 fusion.156
  490.5 4.5 fusion.164
  495.8 3.1 fusion.39
  (445 shorter events, 133.4 us)
Async XLA Ops:
  9.1 7.0 %copy-start.4 = (s32[1,16]{1,0:T(1,128)S(1)}, s32[1,16]{1,0:T(1,128)}, u32[]{:S(2)}) copy-start(s32[1,16]{1,0:T(1,128)} %param.16) | copy-start | bytes 196
  9.1 14.4 %copy-start = (bf16[256,2,1024]{2,1,0:T(2,128)(2,1)S(1)}, bf16[256,2,1024]{2,1,0:T(2,128)(2,1)}, u32[]{:S(2)}) copy-start(bf16[256,2,1024]{2,1,0:T(2,128)(2,1)} %param.12) | copy-start | bytes 3145732
  16.9 48.2 %all-to-all-start.1 = ((s32[16,1,192]{2,1,0:T(1,128)}), s32[16,1,192]{2,1,0:T(1,128)S(1)}, u32[]{:S(2)}, u32[]{:S(2)}) async-start(s32[16,1,192]{2,1,0:T(1,128)} %reshape.345), calls=%async_computation.1 | async-start | bytes 32768 | tf_op jit(solution)/shard_map/all_to_all | solution.py:146
  65.1 6.2 %copy-start.1 = (bf16[2,128,1024]{2,1,0:T(8,128)(2,1)S(1)}, bf16[2,128,1024]{2,1,0:T(8,128)(2,1)}, u32[]{:S(2)}) copy-start(bf16[2,128,1024]{2,1,0:T(8,128)(2,1)} %param.18) | copy-start | bytes 1572868
  65.1 6.2 %copy-start.2 = (bf16[8,8,256]{2,1,0:T(8,128)(2,1)S(1)}, bf16[8,8,256]{2,1,0:T(8,128)(2,1)}, u32[]{:S(2)}) copy-start(bf16[8,8,256]{2,1,0:T(8,128)(2,1)} %param.17) | copy-start | bytes 98308
  65.1 112.6 %all-to-all-start = ((bf16[16,64,2,1024]{3,1,2,0:T(8,128)(2,1)}), bf16[16,64,2,1024]{3,1,2,0:T(8,128)(2,1)}, u32[]{:S(2)}, u32[]{:S(2)}) async-start(bf16[16,64,2,1024]{3,1,2,0:T(8,128)(2,1)} %copy.107), calls=%async_computation | async-start | bytes 8388608 | tf_op jit(solution)/shard_map/all_to_all | solution.py:145
  71.2 106.4 %copy-start.3 = (f32[32]{0:T(128)S(1)}, f32[32]{0:T(128)}, u32[]{:S(2)}) copy-start(f32[32]{0:T(128)} %param.19) | copy-start | bytes 388
where the time goes:
time: 500 us; the launch traced here: 499 us
  other arithmetic  220 us (44%)
  local copies, waits for them, and re-layouts  128 us (26%)
  blocking collectives  104 us (21%)
  matrix products  31.3 us (6%)
  starting transfers between devices  12.8 us (3%)
    all_gather x1, blocking collectives, per_device(): table = lax.all_gather(beam_coefs, 'tile', axis=0, tiled=True)  104 us
    reduce_sum x16, other arithmetic, predict_block(): model_re = jnp.sum(part_re * cos_v - part_im * sin_v, axis=1)  71.7 us
    convert_element_type x16, other arithmetic, predict_block(): sin_u = jnp.sin(angle_u).astype(jnp.bfloat16)  64.7 us
    neg x16, other arithmetic, predict_block(): -sin_u  57.7 us
    squeeze x32, local copies, waits for them, and re-layouts, run_blocks(): lax.map(one_block, (images.reshape(groups, block_len, 2, images.shape[2])...  27 us
    gather x2, local copies, waits for them, and re-layouts, per_device(): payload = inverse_transform(subgrids)[routing]  21 us
    reshape x16, local copies, waits for them, and re-layouts, predict_block(): weighted_im = (image_re * gain_im + image_im * gain_re).astype(jnp.bfloat...  12.5 us
    reshape x16, local copies, waits for them, and re-layouts, predict_block(): weighted_re = (image_re * gain_re - image_im * gain_im).astype(jnp.bfloat...  12.5 us
  transfers between devices with their start and end apart: 2, of which 0 were waited for; matrix products, arithmetic and copies ran while one was open for 9% of the time, Pallas kernels for 0%

commit v1 on v0

v1 whole, which is shorter than its diff:
```python
import functools
import math

import jax
import jax.numpy as jnp
import ml_dtypes
import numpy as np
from jax import lax
from jax.experimental import pallas as pl
from jax.experimental.pallas import tpu as pltpu
from jax.sharding import PartitionSpec as P

TWO_PI = 2.0 * math.pi
F32 = jnp.float32
BF16 = jnp.bfloat16
VMEM_LIMIT = 56 * 1024 * 1024
NT = (((1,), (1,)), ((), ()))
TN = (((0,), (0,)), ((), ()))


def dot(a, b, dims=(((1,), (0,)), ((), ()))):
    return lax.dot_general(a, b, dims, preferred_element_type=F32)


def transform_matrices(edge):
    low = edge // 8
    b = np.arange(low)[:, None, None, None]
    a = np.arange(edge)[None, :, None, None]
    inner = np.arange(low)[None, None, :, None]
    x = np.arange(edge)[None, None, None, :]
    kept = []
    for outer in range(8):
        turns = (b * (outer + 8 * inner) + a * x) % edge
        angle = (TWO_PI / edge * turns).reshape(low * edge, low * edge)
        c, s = np.cos(angle) / edge**2, np.sin(angle) / edge**2
        kept.append(np.block([[c, s], [-s, c]]))
    full = np.stack(kept)
    high = full.astype(ml_dtypes.bfloat16)
    rest = (full - high.astype(np.float64)).astype(ml_dtypes.bfloat16)
    return high, rest


def eight_point(re, im):
    half = math.sqrt(0.5)

    def four(r, i):
        s0r, s0i, d0r, d0i = r[0] + r[2], i[0] + i[2], r[0] - r[2], i[0] - i[2]
        s1r, s1i, d1r, d1i = r[1] + r[3], i[1] + i[3], r[1] - r[3], i[1] - i[3]
        return (
            [s0r + s1r, d0r - d1i, s0r - s1r, d0r + d1i],
            [s0i + s1i, d0i + d1r, s0i - s1i, d0i - d1r],
        )

    er, ei = four(re[0::2], im[0::2])
    orr, oi = four(re[1::2], im[1::2])
    tr = [orr[0], half * (orr[1] - oi[1]), -oi[2], -half * (orr[3] + oi[3])]
    ti = [oi[0], half * (orr[1] + oi[1]), orr[2], half * (orr[3] - oi[3])]
    out_re = [er[m] + tr[m] for m in range(4)] + [er[m] - tr[m] for m in range(4)]
    out_im = [ei[m] + ti[m] for m in range(4)] + [ei[m] - ti[m] for m in range(4)]
    return out_re, out_im


def transform_kernel(cells, high, rest, image, sum_high, sum_rest):
    number = cells.shape[2]
    lanes = cells.shape[3]
    step = 16

    @pl.loop(0, number // step)
    def _(n):
        rows = pl.ds(pl.multiple_of(n * step, step), step)
        re = [cells[0, k, rows, :].astype(F32) for k in range(8)]
        im = [cells[1, k, rows, :].astype(F32) for k in range(8)]
        out_re, out_im = eight_point(re, im)
        for m in range(8):
            for part, value in ((0, out_re[m]), (1, out_im[m])):
                top = value.astype(BF16)
                cols = slice(part * lanes, (part + 1) * lanes)
                sum_high[m, rows, cols] = top
                sum_rest[m, rows, cols] = (value - top.astype(F32)).astype(BF16)

    @pl.loop(0, 8)
    def _(m):
        a, b = sum_high[m], sum_rest[m]
        total = dot(a, high[m]) + (dot(b, high[m]) + dot(a, rest[m]))
        image[m] = total.astype(BF16)


def unit_powers(turns):
    turns = turns - jnp.round(turns)
    angle = (0.5 * math.pi) * turns
    sq = angle * angle
    s = angle * (
        1.0 + sq * (-1.0 / 6 + sq * (1.0 / 120 + sq * (-1.0 / 5040 + sq * (1.0 / 362880))))
    )
    c = 1.0 + sq * (
        -0.5 + sq * (1.0 / 24 + sq * (-1.0 / 720 + sq * (1.0 / 40320 - sq * (1.0 / 3628800))))
    )
    for _ in range(2):
        c, s = 1.0 - 2.0 * (s * s), 2.0 * (s * c)
    return c, s


def cmul(ar, ai, br, bi):
    return ar * br - ai * bi, ar * bi + ai * br


def predict_kernel(
    table,
    slot_row,
    stations,
    time_slots,
    tracks,
    freq,
    basis,
    image,
    payload,
    route,
    weights,
    coef_first,
    coef_second,
    wre,
    wim,
    pure,
    puim,
    zrow,
    hre,
    him,
    zv,
    interleaved,
    *,
    slot_count,
):
    number = image.shape[1]
    slots = slot_row.shape[1]
    rows_all = table.shape[0]
    chan = freq.shape[1]
    steps = tracks.shape[0] // 2
    terms = basis.shape[1]

    down = lax.broadcasted_iota(jnp.int32, (number, slots), 0)
    route[...] = (slot_row[...] == down).astype(F32).astype(BF16)

    tr = tracks[...]
    t_hi = tr.astype(BF16)
    left = tr - t_hi.astype(F32)
    t_mid = left.astype(BF16)
    t_lo = (left - t_mid.astype(F32)).astype(BF16)
    pieces = jnp.concatenate(
        [t_hi.astype(F32), t_mid.astype(F32), t_lo.astype(F32)], axis=0
    ).astype(BF16)
    per_sub = dot(route[...], pieces, NT).astype(BF16)
    wide = 2 * steps * chan
    from_row = lax.broadcasted_iota(jnp.int32, (6 * steps, wide), 0) % (2 * steps)
    to_lane = lax.broadcasted_iota(jnp.int32, (6 * steps, wide), 1) // chan
    spread = (from_row == to_lane).astype(F32).astype(BF16)
    uv = dot(per_sub, spread)
    vis = steps * chan
    fr = jnp.concatenate([freq[...]] * steps, axis=1)
    scale = -1.0 / 32.0
    ur, ui = unit_powers(uv[:, :vis] * fr * scale)
    vr, vi = unit_powers(uv[:, vis:] * fr * scale)

    pure[pl.ds(0, number, stride=8), :] = jnp.ones_like(ur)
    puim[pl.ds(0, number, stride=8), :] = jnp.zeros_like(ur)
    pure[pl.ds(1, number, stride=8), :] = ur
    puim[pl.ds(1, number, stride=8), :] = ui
    cr, ci = ur, ui
    for k in range(2, 8):
        cr, ci = cmul(cr, ci, ur, ui)
        pure[pl.ds(k, number, stride=8), :] = cr
        puim[pl.ds(k, number, stride=8), :] = ci
    cr, ci = cmul(cr, ci, ur, ui)
    zrow[0] = cr
    zrow[1] = ci
    cr, ci = cmul(cr, ci, cr, ci)
    zrow[2] = cr
    zrow[3] = ci
    zv[0] = vr
    zv[1] = vi
    cr, ci = vr, vi
    for _ in range(3):
        cr, ci = cmul(cr, ci, cr, ci)
    zrow[4] = cr
    zrow[5] = ci

    index = (stations[...] * slot_count + time_slots[...]).astype(F32)
    index = jnp.concatenate([index, jnp.zeros((6, number), F32)], axis=0).T
    index = index.astype(jnp.int32)
    across = lax.broadcasted_iota(jnp.int32, (number, rows_all), 1)
    for which, coef in ((0, coef_first), (1, coef_second)):
        pick = (index[:, which : which + 1] == across).astype(F32).astype(BF16)
        coef[...] = dot(pick, table[...]).astype(BF16)

    for m in range(8):
        cols = slice(m * 128, (m + 1) * 128)
        b_re, b_im = basis[0, :, cols], basis[1, :, cols]
        weights[m, :terms, :128] = b_re
        weights[m, :terms, 128:] = b_im
        weights[m, terms:, :128] = -b_im
        weights[m, terms:, 128:] = b_re

    block = 64
    for m in range(8):
        @pl.loop(0, number // block)
        def _(n, m=m):
            rows = pl.ds(pl.multiple_of(n * block, block), block)
            first = dot(coef_first[rows, :], weights[m])
            second = dot(coef_second[rows, :], weights[m])
            f_re, f_im, s_re, s_im = first[:, :128], first[:, 128:], second[:, :128], second[:, 128:]
            g_re = f_re * s_re + f_im * s_im
            g_im = f_im * s_re - f_re * s_im
            i_re = image[m, rows, :128].astype(F32)
            i_im = image[m, rows, 128:].astype(F32)
            to = pl.ds(n * (block * 8) + m, block, stride=8)
            wre[to, :] = i_re * g_re - i_im * g_im
            wim[to, :] = i_re * g_im + i_im * g_re

    lane = lax.broadcasted_iota(jnp.int32, (8, 256), 1)
    inner = (lane // 32) % 4
    masks = [inner == j for j in range(4)]
    unroll = 4

    def one(g):
        at = pl.ds(pl.multiple_of(g * 8, 8), 8)
        w = jnp.concatenate([wre[at, :], wim[at, :]], axis=1)
        lhs = jnp.concatenate([jnp.where(k, w, 0.0) for k in masks], axis=0).astype(BF16)
        p_re, p_im = pure[at, :], puim[at, :]
        z = [jnp.broadcast_to(zrow[k, pl.ds(g, 1), :], (8, 128)) for k in range(6)]
        rr, ii, ri, ir = p_re * z[0], p_im * z[1], p_re * z[1], p_im * z[0]
        up_re, up_im = rr - ii, ri + ir
        dn_re, dn_im = rr + ii, ir - ri
        rr, ii, ri, ir = p_re * z[2], p_im * z[3], p_re * z[3], p_im * z[2]
        lo_re, lo_im = rr + ii, ir - ri
        c = jnp.concatenate([lo_re, dn_re, p_re, up_re], axis=0).astype(BF16)
        s = jnp.concatenate([lo_im, dn_im, p_im, up_im], axis=0).astype(BF16)
        top = jnp.concatenate([c, s], axis=1)
        low = jnp.concatenate([-s, c], axis=1)
        rhs = jnp.concatenate([top] * 4 + [low] * 4, axis=0)
        out = dot(lhs, rhs)
        h_re, h_im = out[24:32, :128], out[24:32, 128:]
        for j in (2, 1, 0):
            n_re = h_re * z[4] - h_im * z[5] + out[8 * j : 8 * j + 8, :128]
            h_im = h_re * z[5] + h_im * z[4] + out[8 * j : 8 * j + 8, 128:]
            h_re = n_re
        hre[at, :] = h_re
        him[at, :] = h_im

    @pl.loop(0, number // unroll)
    def _(n):
        for k in range(unroll):
            one(n * unroll + k)

    vr, vi = zv[0], zv[1]
    a_re = hre[pl.ds(7, number, stride=8), :]
    a_im = him[pl.ds(7, number, stride=8), :]
    for k in range(6, -1, -1):
        n_re = a_re * vr - a_im * vi + hre[pl.ds(k, number, stride=8), :]
        a_im = a_re * vi + a_im * vr + him[pl.ds(k, number, stride=8), :]
        a_re = n_re
    cr, ci = cmul(zrow[4], zrow[5], zrow[4], zrow[5])
    m_re, m_im = a_re * cr + a_im * ci, a_im * cr - a_re * ci
    models = jnp.concatenate([m_re, m_im], axis=1).astype(BF16)
    sent = dot(route[...], models, TN)
    interleaved[pl.ds(0, slots, stride=2), :] = sent[:, :128]
    interleaved[pl.ds(1, slots, stride=2), :] = sent[:, 128:]
    payload[...] = interleaved[...].astype(BF16)


def per_device(
    subgrids,
    stations,
    time_slots,
    assign,
    counts,
    beam_coefs,
    beam_basis,
    frequencies,
    uv_tracks,
    observed,
):
    tiles = lax.axis_size("tile")
    capacity = assign.shape[2]
    slots = tiles * capacity
    number = subgrids.shape[0]
    pixels = subgrids.shape[2]
    edge = math.isqrt(pixels)
    slot_count = beam_coefs.shape[1]
    terms2 = beam_coefs.shape[2]
    steps = uv_tracks.shape[4]
    chan = frequencies.shape[0]
    vis = steps * chan
    vmem = pl.BlockSpec(memory_space=pltpu.VMEM)
    params = pltpu.CompilerParams(vmem_limit_bytes=VMEM_LIMIT)

    own_tracks = jnp.transpose(uv_tracks[0], (0, 2, 3, 1)).reshape(tiles, 2 * steps, capacity)
    tracks = lax.all_to_all(own_tracks, "tile", split_axis=0, concat_axis=0, tiled=True)
    tracks = jnp.transpose(tracks, (1, 0, 2)).reshape(2 * steps, slots)
    table = lax.all_gather(beam_coefs, "tile", axis=0, tiled=True)
    table = table.reshape(table.shape[0] * slot_count, terms2)

    cells = jnp.transpose(subgrids.reshape(number, 2, 8, 128), (1, 2, 0, 3))
    high, rest = transform_matrices(edge)
    image = pl.pallas_call(
        transform_kernel,
        out_shape=jax.ShapeDtypeStruct((8, number, 256), BF16),
        in_specs=[vmem] * 3,
        out_specs=vmem,
        scratch_shapes=[
            pltpu.VMEM((8, number, 256), BF16),
            pltpu.VMEM((8, number, 256), BF16),
        ],
        compiler_params=params,
        name="transform",
    )(cells, jnp.asarray(high), jnp.asarray(rest))

    basis = jnp.transpose(
        beam_basis.reshape(2, terms2 // 2, 4, 8, edge), (0, 1, 3, 2, 4)
    ).reshape(2, terms2 // 2, pixels)
    live = jnp.arange(capacity, dtype=jnp.int32)[None, :] < counts[0][:, None]
    slot_row = jnp.where(live, assign[0], -1).reshape(1, slots)
    payload = pl.pallas_call(
        functools.partial(predict_kernel, slot_count=slot_count),
        out_shape=jax.ShapeDtypeStruct((2 * slots, vis), BF16),
        in_specs=[vmem] * 8,
        out_specs=vmem,
        scratch_shapes=[
            pltpu.VMEM((number, slots), BF16),
            pltpu.VMEM((8, 256, 256), BF16),
            pltpu.VMEM((number, terms2), BF16),
            pltpu.VMEM((number, terms2), BF16),
            pltpu.VMEM((number * 8, 128), F32),
            pltpu.VMEM((number * 8, 128), F32),
            pltpu.VMEM((number * 8, vis), F32),
            pltpu.VMEM((number * 8, vis), F32),
            pltpu.VMEM((6, number, vis), F32),
            pltpu.VMEM((number * 8, vis), F32),
            pltpu.VMEM((number * 8, vis), F32),
            pltpu.VMEM((2, number, vis), F32),
            pltpu.VMEM((2 * slots, vis), F32),
        ],
        compiler_params=params,
        name="predict",
    )(
        table,
        slot_row,
        stations.T,
        time_slots.reshape(1, number),
        tracks,
        frequencies.reshape(1, chan),
        basis,
        image,
    )
    arrived = lax.all_to_all(
        payload.reshape(tiles, 2 * capacity, vis), "tile", split_axis=0, concat_axis=0, tiled=True
    )
    residual = observed - arrived.reshape(observed.shape).astype(F32)
    return residual


def solution(mesh):
    return jax.shard_map(
        per_device,
        mesh=mesh,
        in_specs=(
            P(("grp", "tile"), None, None),
            P(("grp", "tile"), None),
            P(("grp", "tile")),
            P(("grp", "tile"), None, None),
            P(("grp", "tile"), None),
            P(("grp", "tile"), None, None),
            P(),
            P("grp"),
            P(("grp", "tile"), None, None, None, None),
            P(("grp", "tile"), None, None, None, None),
        ),
        out_specs=P(("grp", "tile"), None, None, None, None),
        check_vma=False,
    )
```

time: 500 us -> 91.8 us (0.18)
  the two profiles are of different devices: /device:TPU:9 before, /device:TPU:0 now
where the time goes in v1:
time: 91.8 us; the launch traced here: 91.3 us
  blocking collectives  42.7 us (47%)
  Pallas kernels  29.9 us (33%)
  local copies, waits for them, and re-layouts  8.61 us (9%)
  starting transfers between devices  7.52 us (8%)
  other arithmetic  2.46 us (3%)
    all_gather x1, blocking collectives, per_device(): table = lax.all_gather(beam_coefs, 'tile', axis=0, tiled=True)  24.6 us
    pallas_call x1, Pallas kernels, per_device(): pl.pallas_call(functools.partial(predict_kernel, slot_count=slot_count),...  24.1 us
    all_to_all x1, blocking collectives, per_device(): lax.all_to_all(payload.reshape(tiles, 2 * capacity, vis), 'tile', split_a...  18.1 us
    all_to_all x1, starting transfers between devices, per_device(): lax.all_to_all(own_tracks, 'tile', split_axis=0, concat_axis=0, tiled=True)  7.52 us
    pallas_call x1, Pallas kernels, per_device(): pl.pallas_call(transform_kernel, out_shape=jax.ShapeDtypeStruct((8, numbe...  5.77 us
    unnamed x14, local copies, waits for them, and re-layouts  4.86 us
  transfers between devices with their start and end apart: 1, of which 0 were waited for; matrix products, arithmetic and copies ran while one was open for 6% of the time, Pallas kernels for 6%

profile of v1, /device:TPU:0, one launch (start us, length us, event | category | flops | bytes accessed | tf_op | source)
XLA Modules:
  0.0 91.3 jit_solution(14161180160824975737)
XLA Ops:
  0.0 1.5 %reshape.86 = f32[16,1,512]{2,1,0:T(1,128)} reshape(f32[16,8,64]{2,1,0:T(8,128)} %bitcast.32) | data formatting | bytes 65536
  1.5 0.0 copy-start.2
  1.6 7.5 %all-to-all-start = ((f32[16,1,512]{2,1,0:T(1,128)}), f32[16,1,512]{2,1,0:T(1,128)S(1)}, u32[]{:S(2)}, u32[]{:S(2)}) async-start(f32[16,1,512]{2,1,0:T(1,128)} %reshape.86), calls=%async_computation | async-start | bytes 65536 | tf_op jit(solution)/shard_map/all_to_all | solution.py:296
  9.1 0.0 copy-done.2
  9.1 0.0 copy-start.4
  9.1 24.6 %all_gather.3 = bf16[128,8,256]{2,1,0:T(8,128)(2,1)} all-gather(bf16[8,8,256]{2,1,0:T(8,128)(2,1)S(1)} %copy-done.2), channel_id=1, replica_groups=mesh['grp'=2,'tile'=16] {'tile'}, dimensions={0}, use_global_device_ids=true | all-gather | bytes 557056 | tf_op jit(solution)/shard_map/all_gather | solution.py:298
  33.7 0.0 copy-start.3
  33.7 0.0 copy-done.4
  33.7 0.1 iota_compare_fusion
  33.8 0.1 lt.29
  33.9 0.5 copy-done.3
  34.4 0.1 squeeze.6
  34.5 0.6 broadcast_select_fusion.slot_row
  35.1 2.4 %copy.24 = bf16[256,2,1024]{0,2,1:T(8,128)(2,1)S(1)} copy(bf16[256,2,1024]{2,1,0:T(2,128)(2,1)} %param.12) | data formatting | bytes 2097152 | tf_op args[0]
  37.5 0.0 copy-start.1
  37.5 1.3 %copy.25 = bf16[256,2,8,128]{3,0,2,1:T(8,128)(2,1)} copy(bf16[256,2,8,128]{0,3,2,1:T(8,128)(2,1)S(1)} %bitcast.23) | data formatting | bytes 2097152 | tf_op jit(solution)/shard_map/reshape | solution.py:301
  38.8 0.0 copy-done.1
  38.8 0.3 copy.22
  39.1 0.1 copy.23
  39.1 1.0 %copy.26.basis = bf16[2,128,1024]{2,1,0:T(8,128)(2,1)} copy(bf16[2,128,1024]{1,2,0:T(8,128)(2,1)S(1)} %bitcast.26) | data formatting | bytes 1048576 | tf_op jit(solution)/shard_map/reshape | solution.py:318
  40.1 5.8 %transform.1.image = bf16[8,256,256]{2,1,0:T(8,128)(2,1)} custom-call(bf16[2,8,256,128]{3,2,1,0:T(8,128)(2,1)} %bitcast.24, bf16[8,256,256]{2,1,0:T(8,128)(2,1)} %constant.6.clone.high, bf16[8,256,256]{2,1,0:T(8,128)(2,1)} %constant.7.clone.rest), custom_call_target="tpu_custom_call" | custom-call | tf_op jit(solution)/shard_map/transform/pallas_call | solution.py:303
  45.9 0.0 all-to-all-done
  45.9 0.5 broadcast.11
  46.4 0.7 reduce
  47.2 0.1 reshape.87
  47.3 0.7 reshape.79.tracks
  48.0 24.1 %predict.1 = bf16[2048,128]{1,0:T(8,128)(2,1)} custom-call(bf16[1024,256]{1,0:T(8,128)(2,1)} %bitcast.28, s32[1,1024]{1,0:T(1,128)} %broadcast_select_fusion.slot_row, s32[2,256]{1,0:T(2,128)} %bitcast.33, s32[1,256]{1,0:T(1,128)} %bitcast.34, f32[8,1024]{1,0:T(8,128)} %reshape.79.tracks, f32[1,32]{1,0:T(1,128)} %bitcast.35, ...), custom_call_target="tpu_custom_call" | custom-call | tf_op jit(solution)/shard_map/predict/pallas_call | solution.py:321
  72.1 0.0 copy-start
  72.1 18.1 %all_to_all.10 = bf16[16,128,128]{2,1,0:T(8,128)(2,1)S(1)} all-to-all(bf16[16,128,128]{2,1,0:T(8,128)(2,1)} %bitcast.29), channel_id=1, replica_groups=mesh['grp'=2,'tile'=16] {'tile'}, dimensions={0} | all-to-all | bytes 1048576 | tf_op jit(solution)/shard_map/all_to_all | solution.py:353
  90.2 0.0 copy-done
  90.2 1.1 %convert_subtract_fusion = f32[1,16,16,8,128]{4,3,2,1,0:T(8,128)} fusion(f32[1,16,16,8,128]{4,3,2,1,0:T(8,128)S(1)} %bitcast.30, bf16[1,16,16,8,128]{4,3,2,1,0:T(8,128)(2,1)S(1)} %bitcast.25), kind=kLoop, calls=%fused_computation | loop fusion | flops 524288 | bytes 2621440 | tf_op jit(solution)/shard_map/sub | solution.py:356
  (1 shorter events, 0.0 us)
Async XLA Ops:
  1.5 7.5 %copy-start.2 = (bf16[8,8,256]{2,1,0:T(8,128)(2,1)S(1)}, bf16[8,8,256]{2,1,0:T(8,128)(2,1)}, u32[]{:S(2)}) copy-start(bf16[8,8,256]{2,1,0:T(8,128)(2,1)} %param.17) | copy-start | bytes 98308
  1.6 44.4 %all-to-all-start = ((f32[16,1,512]{2,1,0:T(1,128)}), f32[16,1,512]{2,1,0:T(1,128)S(1)}, u32[]{:S(2)}, u32[]{:S(2)}) async-start(f32[16,1,512]{2,1,0:T(1,128)} %reshape.86), calls=%async_computation | async-start | bytes 65536 | tf_op jit(solution)/shard_map/all_to_all | solution.py:296
  9.1 24.6 %copy-start.4 = (s32[1,16]{1,0:T(1,128)S(1)}, s32[1,16]{1,0:T(1,128)}, u32[]{:S(2)}) copy-start(s32[1,16]{1,0:T(1,128)} %param.16) | copy-start | bytes 196
  33.7 0.7 copy-start.3
  37.5 1.3 %copy-start.1 = (bf16[2,128,1024]{2,1,0:T(8,128)(2,1)S(1)}, bf16[2,128,1024]{2,1,0:T(8,128)(2,1)}, u32[]{:S(2)}) copy-start(bf16[2,128,1024]{2,1,0:T(8,128)(2,1)} %param.18) | copy-start | bytes 1572868
  72.1 18.1 %copy-start = (f32[1,16,64,2,128]{4,3,2,1,0:T(2,128)S(1)}, f32[1,16,64,2,128]{4,3,2,1,0:T(2,128)}, u32[]{:S(2)}) copy-start(f32[1,16,64,2,128]{4,3,2,1,0:T(2,128)} %param.21) | copy-start | bytes 3145732

commit v2 on v1

--- a/solution.py
+++ b/solution.py
@@ -104,54 +104,86 @@
     return ar * br - ai * bi, ar * bi + ai * br
 
 
-def predict_kernel(
-    table,
-    slot_row,
-    stations,
-    time_slots,
-    tracks,
-    freq,
-    basis,
-    image,
-    payload,
-    route,
-    weights,
-    coef_first,
-    coef_second,
-    wre,
-    wim,
-    pure,
-    puim,
-    zrow,
-    hre,
-    him,
-    zv,
-    interleaved,
-    *,
-    slot_count,
-):
+def pack_kernel(me, coefs, tracks, *out):
+    capacity = tracks.shape[2]
+    rows = coefs.shape[0]
+    width = coefs.shape[1]
+    for r in range(len(out)):
+        plane = (me[0] // 4) ^ r
+        tr = [tracks[plane * 4 + k] for k in range(4)]
+        if 4 * capacity < width:
+            tr.append(jnp.zeros((tr[0].shape[0], width - 4 * capacity), F32))
+        tr = jnp.concatenate(tr, axis=1)
+        t_hi = tr.astype(BF16).astype(F32)
+        t_mid = (tr - t_hi).astype(BF16).astype(F32)
+        t_lo = tr - t_hi - t_mid
+        pieces = jnp.concatenate([t_hi, t_mid, t_lo, jnp.zeros_like(tr)], axis=0)
+        out[r][:rows, :] = coefs[...]
+        out[r][rows:, :] = pieces.astype(BF16)
+
+
+def predict_kernel(me, counts, *refs, tiles, slot_count):
+    blocks = refs[:tiles]
+    (assign, stations, time_slots, freq, basis, image) = refs[tiles : tiles + 6]
+    payload = refs[tiles + 6 : 2 * tiles + 6]
+    (
+        table,
+        route,
+        weights,
+        coef_first,
+        coef_second,
+        wre,
+        wim,
+        pure,
+        puim,
+        zrow,
+        hre,
+        him,
+        zv,
+        interleaved,
+    ) = refs[2 * tiles + 6 :]
     number = image.shape[1]
-    slots = slot_row.shape[1]
+    capacity = assign.shape[1]
+    slots = tiles * capacity
     rows_all = table.shape[0]
+    rows_own = rows_all // tiles
     chan = freq.shape[1]
-    steps = tracks.shape[0] // 2
+    pieces_rows = blocks[0].shape[0] - rows_own
+    kinds = pieces_rows // 4
+    steps = kinds // 2
     terms = basis.shape[1]
-
-    down = lax.broadcasted_iota(jnp.int32, (number, slots), 0)
-    route[...] = (slot_row[...] == down).astype(F32).astype(BF16)
-
-    tr = tracks[...]
-    t_hi = tr.astype(BF16)
-    left = tr - t_hi.astype(F32)
-    t_mid = left.astype(BF16)
-    t_lo = (left - t_mid.astype(F32)).astype(BF16)
-    pieces = jnp.concatenate(
-        [t_hi.astype(F32), t_mid.astype(F32), t_lo.astype(F32)], axis=0
-    ).astype(BF16)
+    mine = me[0]
+
+    per = 128 // capacity
+    down = lax.broadcasted_iota(jnp.int32, (number, 128), 0)
+    slot = lax.broadcasted_iota(jnp.int32, (1, capacity), 1)
+    held = []
+    for n in range(tiles // per):
+        chosen, tracks = [], []
+        for r in range(n * per, (n + 1) * per):
+            other = mine ^ r
+            chosen.append(
+                jnp.where(slot < counts[0, other], assign[pl.ds(other, 1), :], -1)
+            )
+            whole = blocks[r][rows_own:, :].astype(F32)
+            piece = whole
+            for k in range(1, 4):
+                piece = jnp.where(
+                    mine % 4 == k,
+                    pltpu.roll(whole, whole.shape[1] - k * capacity, 1),
+                    piece,
+                )
+            tracks.append(piece[:, :capacity])
+            table[r * rows_own : (r + 1) * rows_own, :] = blocks[r][:rows_own, :]
+        chosen = jnp.concatenate(chosen, axis=1)
+        route[:, n * 128 : (n + 1) * 128] = (chosen == down).astype(F32).astype(BF16)
+        held.append(jnp.concatenate(tracks, axis=1).astype(BF16))
+    pieces = jnp.concatenate(held, axis=1)
+
     per_sub = dot(route[...], pieces, NT).astype(BF16)
     wide = 2 * steps * chan
-    from_row = lax.broadcasted_iota(jnp.int32, (6 * steps, wide), 0) % (2 * steps)
-    to_lane = lax.broadcasted_iota(jnp.int32, (6 * steps, wide), 1) // chan
+    from_row = lax.broadcasted_iota(jnp.int32, (pieces_rows, wide), 0) % kinds
+    to_lane = lax.broadcasted_iota(jnp.int32, (pieces_rows, wide), 1) // chan
     spread = (from_row == to_lane).astype(F32).astype(BF16)
     uv = dot(per_sub, spread)
     vis = steps * chan
@@ -183,7 +215,12 @@
     zrow[4] = cr
     zrow[5] = ci
 
-    index = (stations[...] * slot_count + time_slots[...]).astype(F32)
+    each = rows_own // slot_count
+    index = (
+        ((stations[...] // each) ^ mine) * rows_own
+        + stations[...] % each * slot_count
+        + time_slots[...]
+    ).astype(F32)
     index = jnp.concatenate([index, jnp.zeros((6, number), F32)], axis=0).T
     index = index.astype(jnp.int32)
     across = lax.broadcasted_iota(jnp.int32, (number, rows_all), 1)
@@ -263,7 +300,20 @@
     sent = dot(route[...], models, TN)
     interleaved[pl.ds(0, slots, stride=2), :] = sent[:, :128]
     interleaved[pl.ds(1, slots, stride=2), :] = sent[:, 128:]
-    payload[...] = interleaved[...].astype(BF16)
+    for r in range(tiles):
+        rows = slice(2 * capacity * r, 2 * capacity * (r + 1))
+        payload[r][...] = interleaved[rows, :].astype(BF16)
+
+
+def residual_kernel(me, observed, *refs):
+    arrived, residual = refs[:-1], refs[-1]
+    for r in range(len(arrived)):
+        source = me[0] ^ r
+        residual[source] = observed[source] - arrived[r][...].astype(F32)
+
+
+def exchange(value, step, tiles):
+    return lax.ppermute(value, "tile", [(i, i ^ step) for i in range(tiles)])
 
 
 def per_device(
@@ -292,11 +342,27 @@
     vmem = pl.BlockSpec(memory_space=pltpu.VMEM)
     params = pltpu.CompilerParams(vmem_limit_bytes=VMEM_LIMIT)
 
+    smem = pl.BlockSpec(memory_space=pltpu.SMEM)
+    me = lax.axis_index("tile").astype(jnp.int32).reshape(1)
     own_tracks = jnp.transpose(uv_tracks[0], (0, 2, 3, 1)).reshape(tiles, 2 * steps, capacity)
-    tracks = lax.all_to_all(own_tracks, "tile", split_axis=0, concat_axis=0, tiled=True)
-    tracks = jnp.transpose(tracks, (1, 0, 2)).reshape(2 * steps, slots)
-    table = lax.all_gather(beam_coefs, "tile", axis=0, tiled=True)
-    table = table.reshape(table.shape[0] * slot_count, terms2)
+    own_rows = beam_coefs.shape[0] * slot_count
+    outer = tiles // 4
+    block = jax.ShapeDtypeStruct((own_rows + 8 * steps, terms2), BF16)
+    packed = pl.pallas_call(
+        pack_kernel,
+        out_shape=[block] * outer,
+        in_specs=[smem, vmem, vmem],
+        out_specs=[vmem] * outer,
+        compiler_params=params,
+        name="pack",
+    )(me, beam_coefs.reshape(own_rows, terms2), own_tracks)
+    blocks = {0: packed[0]}
+    for r in range(1, outer):
+        blocks[4 * r] = exchange(packed[r], 4 * r, tiles)
+    for r in range(outer):
+        blocks[4 * r + 2] = exchange(blocks[4 * r], 2, tiles)
+    for r in range(0, tiles, 2):
+        blocks[r + 1] = exchange(blocks[r], 1, tiles)
 
     cells = jnp.transpose(subgrids.reshape(number, 2, 8, 128), (1, 2, 0, 3))
     high, rest = transform_matrices(edge)
@@ -316,14 +382,13 @@
     basis = jnp.transpose(
         beam_basis.reshape(2, terms2 // 2, 4, 8, edge), (0, 1, 3, 2, 4)
     ).reshape(2, terms2 // 2, pixels)
-    live = jnp.arange(capacity, dtype=jnp.int32)[None, :] < counts[0][:, None]
-    slot_row = jnp.where(live, assign[0], -1).reshape(1, slots)
     payload = pl.pallas_call(
-        functools.partial(predict_kernel, slot_count=slot_count),
-        out_shape=jax.ShapeDtypeStruct((2 * slots, vis), BF16),
-        in_specs=[vmem] * 8,
-        out_specs=vmem,
+        functools.partial(predict_kernel, tiles=tiles, slot_count=slot_count),
+        out_shape=[jax.ShapeDtypeStruct((2 * capacity, vis), BF16)] * tiles,
+        in_specs=[smem] * 2 + [vmem] * (tiles + 6),
+        out_specs=[vmem] * tiles,
         scratch_shapes=[
+            pltpu.VMEM((tiles * own_rows, terms2), BF16),
             pltpu.VMEM((number, slots), BF16),
             pltpu.VMEM((8, 256, 256), BF16),
             pltpu.VMEM((number, terms2), BF16),
@@ -341,20 +406,26 @@
         compiler_params=params,
         name="predict",
     )(
-        table,
-        slot_row,
+        me,
+        counts,
+        *[blocks[r] for r in range(tiles)],
+        assign[0],
         stations.T,
         time_slots.reshape(1, number),
-        tracks,
         frequencies.reshape(1, chan),
         basis,
         image,
     )
-    arrived = lax.all_to_all(
-        payload.reshape(tiles, 2 * capacity, vis), "tile", split_axis=0, concat_axis=0, tiled=True
-    )
-    residual = observed - arrived.reshape(observed.shape).astype(F32)
-    return residual
+    arrived = [payload[0]] + [exchange(payload[r], r, tiles) for r in range(1, tiles)]
+    residual = pl.pallas_call(
+        residual_kernel,
+        out_shape=jax.ShapeDtypeStruct((tiles, 2 * capacity, vis), F32),
+        in_specs=[smem] + [vmem] * (tiles + 1),
+        out_specs=vmem,
+        compiler_params=params,
+        name="residual",
+    )(me, observed.reshape(tiles, 2 * capacity, vis), *arrived)
+    return residual.reshape(observed.shape)
 
 
 def solution(mesh):

time: 91.8 us -> 84 us (0.915)
  blocking collectives: 42.7 us -> 0 us
  starting transfers between devices: 7.52 us -> 32.1 us
  waiting for transfers between devices: 0.01 us -> 10.7 us
  Pallas kernels: 29.9 us -> 34.3 us
  other arithmetic: 2.46 us -> 0 us
  local copies, waits for them, and re-layouts: 8.61 us -> 6.26 us
    ppermute x0 -> x30, starting transfers between devices: none -> 32.1 us  [exchange(): return lax.ppermute(value, 'tile', [(i, i ^ step) for i in range(tiles)])]
    all_gather x1 -> x0, blocking collectives: 24.6 us -> none  [per_device(): table = lax.all_gather(beam_coefs, 'tile', axis=0, tiled=True)]
    all_to_all x1 -> x0, blocking collectives: 18.1 us -> none  [per_device(): lax.all_to_all(payload.reshape(tiles, 2 * capacity, vis), 'tile', split_a...]
    ppermute x0 -> x30, waiting for transfers between devices: none -> 10.7 us  [exchange(): return lax.ppermute(value, 'tile', [(i, i ^ step) for i in range(tiles)])]
    all_to_all x1 -> x0, starting transfers between devices: 7.52 us -> none  [per_device(): lax.all_to_all(own_tracks, 'tile', split_axis=0, concat_axis=0, tiled=True)]
    pallas_call x1 -> x3, Pallas kernels: 24.1 us -> 28.4 us  [the longest x1 24.3 us: per_device(): pl.pallas_call(functools.partial(predict_kernel, tiles=tiles, slot_count=...]
    sub x1 -> x0, other arithmetic: 1.08 us -> none  [per_device(): residual = observed - arrived.reshape(observed.shape).astype(F32)]
    unnamed x14 -> x64, local copies, waits for them, and re-layouts: 4.86 us -> 3.88 us
  transfers between devices with their start and end apart: 1 -> 30, of which waited for: 0 -> 6; matrix products, arithmetic and copies ran while one was open for 6% -> 6% of each run, Pallas kernels for 6% -> 7%
where the time goes in v2:
time: 84 us; the launch traced here: 83.7 us
  Pallas kernels  34.3 us (41%)
  starting transfers between devices  32.1 us (38%)
  waiting for transfers between devices  10.7 us (13%)
  local copies, waits for them, and re-layouts  6.26 us (7%)
    ppermute x30, starting transfers between devices, exchange(): return lax.ppermute(value, 'tile', [(i, i ^ step) for i in range(tiles)])  32.1 us
    pallas_call x1, Pallas kernels, per_device(): pl.pallas_call(functools.partial(predict_kernel, tiles=tiles, slot_count=...  24.3 us
    ppermute x30, waiting for transfers between devices, exchange(): return lax.ppermute(value, 'tile', [(i, i ^ step) for i in range(tiles)])  10.7 us
    pallas_call x1, Pallas kernels, per_device(): pl.pallas_call(transform_kernel, out_shape=jax.ShapeDtypeStruct((8, numbe...  5.84 us
    unnamed x64, local copies, waits for them, and re-layouts  3.88 us
    pallas_call x1, Pallas kernels, per_device(): pl.pallas_call(residual_kernel, out_shape=jax.ShapeDtypeStruct((tiles, 2...  2.5 us
  transfers between devices with their start and end apart: 30, of which 6 were waited for; matrix products, arithmetic and copies ran while one was open for 6% of the time, Pallas kernels for 7%

profile of v2, /device:TPU:0, one launch (start us, length us, event | category | flops | bytes accessed | tf_op | source)
XLA Modules:
  0.0 83.7 jit_solution(6177784312970839907)
XLA Ops:
  0.0 1.6 %pack.1 = (bf16[96,256]{1,0:T(8,128)(2,1)}, bf16[96,256]{1,0:T(8,128)(2,1)}, bf16[96,256]{1,0:T(8,128)(2,1)}, bf16[96,256]{1,0:T(8,128)(2,1)}) custom-call(s32[1]{0:T(128)} %bitcast.me, bf16[64,256]{1,0:T(8,128)(2,1)} %bitcast.25, f32[16,8,64]{2,1,0:T(8,128)} %bitcast.24), custom_call_target="tpu_custom_call" | custom-call | tf_op jit(solution)/shard_map/pack/pallas_call | solution.py:351
  1.6 4.0 %collective-permute-start.7 = (bf16[96,256]{1,0:T(8,128)(2,1)}, bf16[96,256]{1,0:T(8,128)(2,1)S(1)}, u32[]{:S(2)}, u32[]{:S(2)}) collective-permute-start(bf16[96,256]{1,0:T(8,128)(2,1)} %get-tuple-element.27), channel_id=1, source_target_pairs={{0,8},{1,9},{2,10},{3,11},{4,12},{5,13},{6,14},{7,15},{8,0},{9,1},... | collective-permute-start | bytes 147464 | tf_op jit(solution)/shard_map/ppermute | solution.py:316
  5.6 1.3 %collective-permute-start.11 = (bf16[96,256]{1,0:T(8,128)(2,1)}, bf16[96,256]{1,0:T(8,128)(2,1)S(1)}, u32[]{:S(2)}, u32[]{:S(2)}) collective-permute-start(bf16[96,256]{1,0:T(8,128)(2,1)} %get-tuple-element.28), channel_id=1, source_target_pairs={{0,12},{1,13},{2,14},{3,15},{4,8},{5,9},{6,10},{7,11},{8,4},{9,5},... | collective-permute-start | bytes 147464 | tf_op jit(solution)/shard_map/ppermute | solution.py:316
  7.0 0.2 collective-permute-start.3
  7.2 1.5 %collective-permute-start.1 = (bf16[96,256]{1,0:T(8,128)(2,1)}, bf16[96,256]{1,0:T(8,128)(2,1)S(1)}, u32[]{:S(2)}, u32[]{:S(2)}) collective-permute-start(bf16[96,256]{1,0:T(8,128)(2,1)} %get-tuple-element.25.refs_0_), channel_id=1, source_target_pairs={{0,2},{1,3},{2,0},{3,1},{4,6},{5,7},{6,4},{7,5},{8,10},{9,11},{10,... | collective-permute-start | bytes 147464 | tf_op jit(solution)/shard_map/ppermute | solution.py:316
  8.7 0.0 collective-permute-start
  8.8 1.4 %collective-permute-start.9 = (bf16[96,256]{1,0:T(8,128)(2,1)S(1)}, bf16[96,256]{1,0:T(8,128)(2,1)S(1)}, u32[]{:S(2)}, u32[]{:S(2)}) collective-permute-start(bf16[96,256]{1,0:T(8,128)(2,1)S(1)} %collective-permute-done.7.refs_8_), channel_id=1, source_target_pairs={{0,2},{1,3},{2,0},{3,1},{4,6},{5,7},{6,4},{7,5},{8,10},{9,11},{10,... | collective-permute-start | bytes 147464 | tf_op jit(solution)/shard_map/ppermute | solution.py:316
  10.2 1.6 %collective-permute-done.11.refs_12_ = bf16[96,256]{1,0:T(8,128)(2,1)S(1)} collective-permute-done((bf16[96,256]{1,0:T(8,128)(2,1)}, bf16[96,256]{1,0:T(8,128)(2,1)S(1)}, u32[]{:S(2)}, u32[]{:S(2)}) %collective-permute-start.11) | collective-permute-done | bytes 49184 | tf_op jit(solution)/shard_map/ppermute | solution.py:316
  11.8 1.5 %collective-permute-start.13 = (bf16[96,256]{1,0:T(8,128)(2,1)S(1)}, bf16[96,256]{1,0:T(8,128)(2,1)S(1)}, u32[]{:S(2)}, u32[]{:S(2)}) collective-permute-start(bf16[96,256]{1,0:T(8,128)(2,1)S(1)} %collective-permute-done.11.refs_12_), channel_id=1, source_target_pairs={{0,2},{1,3},{2,0},{3,1},{4,6},{5,7},{6,4},{7,5},{8,10},{9,11},{10,... | collective-permute-start | bytes 147464 | tf_op jit(solution)/shard_map/ppermute | solution.py:316
  13.3 0.0 collective-permute-done.3.refs_4_
  13.3 0.5 collective-permute-start.5
  13.9 0.0 collective-permute-start.2
  13.9 0.0 collective-permute-done.refs_1_
  13.9 0.5 collective-permute-start.12
  14.4 0.0 collective-permute-done.9.refs_10_
  14.4 0.1 collective-permute-start.4
  14.5 1.4 %collective-permute-done.13.refs_14_ = bf16[96,256]{1,0:T(8,128)(2,1)S(1)} collective-permute-done((bf16[96,256]{1,0:T(8,128)(2,1)S(1)}, bf16[96,256]{1,0:T(8,128)(2,1)S(1)}, u32[]{:S(2)}, u32[]{:S(2)}) %collective-permute-start.13) | collective-permute-done | bytes 49184 | tf_op jit(solution)/shard_map/ppermute | solution.py:316
  15.9 1.5 %collective-permute-done.5.refs_6_ = bf16[96,256]{1,0:T(8,128)(2,1)S(1)} collective-permute-done((bf16[96,256]{1,0:T(8,128)(2,1)S(1)}, bf16[96,256]{1,0:T(8,128)(2,1)S(1)}, u32[]{:S(2)}, u32[]{:S(2)}) %collective-permute-start.5) | collective-permute-done | bytes 49184 | tf_op jit(solution)/shard_map/ppermute | solution.py:316
  17.4 0.0 collective-permute-start.10
  17.4 0.0 collective-permute-done.2.refs_3_
  17.5 0.5 collective-permute-start.14
  18.0 0.0 collective-permute-done.12.refs_13_
  18.0 0.1 collective-permute-start.6
  18.1 2.4 %copy.16 = bf16[256,2,1024]{0,2,1:T(8,128)(2,1)S(1)} copy(bf16[256,2,1024]{2,1,0:T(2,128)(2,1)} %param.12) | data formatting | bytes 2097152 | tf_op args[0]
  20.6 0.0 copy-start
  20.6 1.3 %copy.17 = bf16[256,2,8,128]{3,0,2,1:T(8,128)(2,1)} copy(bf16[256,2,8,128]{0,3,2,1:T(8,128)(2,1)S(1)} %bitcast.19) | data formatting | bytes 2097152 | tf_op jit(solution)/shard_map/reshape | solution.py:367
  21.9 0.3 copy.14
  22.2 0.1 copy.15
  22.2 1.0 %copy.18.refs_20_ = bf16[2,128,1024]{2,1,0:T(8,128)(2,1)} copy(bf16[2,128,1024]{1,2,0:T(8,128)(2,1)S(1)} %bitcast.21) | data formatting | bytes 1048576 | tf_op jit(solution)/shard_map/reshape | solution.py:384
  23.2 5.8 %transform.1.refs_21_ = bf16[8,256,256]{2,1,0:T(8,128)(2,1)} custom-call(bf16[2,8,256,128]{3,2,1,0:T(8,128)(2,1)} %bitcast.20, bf16[8,256,256]{2,1,0:T(8,128)(2,1)} %constant.8.clone.high, bf16[8,256,256]{2,1,0:T(8,128)(2,1)} %constant.9.clone.rest), custom_call_target="tpu_custom_call" | custom-call | tf_op jit(solution)/shard_map/transform/pallas_call | solution.py:369
  29.1 0.0 collective-permute-done.10.refs_11_
  29.2 0.5 copy-done.11
  29.7 0.0 copy-done.12
  29.7 0.0 copy-done.13
  29.7 0.0 copy-done.14
  29.8 0.0 copy-done.15
  29.8 24.3 %predict.1 = (bf16[128,128]{1,0:T(8,128)(2,1)}, bf16[128,128]{1,0:T(8,128)(2,1)}, bf16[128,128]{1,0:T(8,128)(2,1)}, bf16[128,128]{1,0:T(8,128)(2,1)}, bf16[128,1...) custom-call(s32[1]{0:T(128)} %bitcast.me, ...), custom_call_target="tpu_custom_call" | custom-call | tf_op jit(solution)/shard_map/predict/pallas_call | solution.py:385
  54.1 0.5 collective-permute-start.15
  54.6 0.5 collective-permute-start.16
  55.1 0.9 %collective-permute-start.17 = (bf16[128,128]{1,0:T(8,128)(2,1)}, bf16[128,128]{1,0:T(8,128)(2,1)S(1)}, u32[]{:S(2)}, u32[]{:S(2)}) collective-permute-start(bf16[128,128]{1,0:T(8,128)(2,1)} %get-tuple-element.32), channel_id=1, source_target_pairs={{0,3},{1,2},{2,1},{3,0},{4,7},{5,6},{6,5},{7,4},{8,11},{9,10},{10,... | collective-permute-start | bytes 98312 | tf_op jit(solution)/shard_map/ppermute | solution.py:316
  56.1 2.1 %collective-permute-start.19 = (bf16[128,128]{1,0:T(8,128)(2,1)}, bf16[128,128]{1,0:T(8,128)(2,1)S(1)}, u32[]{:S(2)}, u32[]{:S(2)}) collective-permute-start(bf16[128,128]{1,0:T(8,128)(2,1)} %get-tuple-element.34), channel_id=1, source_target_pairs={{0,5},{1,4},{2,7},{3,6},{4,1},{5,0},{6,3},{7,2},{8,13},{9,12},{10,... | collective-permute-start | bytes 98312 | tf_op jit(solution)/shard_map/ppermute | solution.py:316
  58.1 0.7 collective-permute-start.20
  58.9 0.2 collective-permute-done.16.refs_2_
  59.0 1.4 %collective-permute-start.21 = (bf16[128,128]{1,0:T(8,128)(2,1)}, bf16[128,128]{1,0:T(8,128)(2,1)S(1)}, u32[]{:S(2)}, u32[]{:S(2)}) collective-permute-start(bf16[128,128]{1,0:T(8,128)(2,1)} %get-tuple-element.36), channel_id=1, source_target_pairs={{0,7},{1,6},{2,5},{3,4},{4,3},{5,2},{6,1},{7,0},{8,15},{9,14},{10,... | collective-permute-start | bytes 98312 | tf_op jit(solution)/shard_map/ppermute | solution.py:316
  60.5 0.0 collective-permute-done.17.refs_3_
  60.5 1.8 %collective-permute-start.22 = (bf16[128,128]{1,0:T(8,128)(2,1)}, bf16[128,128]{1,0:T(8,128)(2,1)S(1)}, u32[]{:S(2)}, u32[]{:S(2)}) collective-permute-start(bf16[128,128]{1,0:T(8,128)(2,1)} %get-tuple-element.37), channel_id=1, source_target_pairs={{0,8},{1,9},{2,10},{3,11},{4,12},{5,13},{6,14},{7,15},{8,0},{9,1},... | collective-permute-start | bytes 98312 | tf_op jit(solution)/shard_map/ppermute | solution.py:316
  62.2 0.0 collective-permute-done.18.refs_4_
  62.2 1.2 %collective-permute-start.23 = (bf16[128,128]{1,0:T(8,128)(2,1)}, bf16[128,128]{1,0:T(8,128)(2,1)S(1)}, u32[]{:S(2)}, u32[]{:S(2)}) collective-permute-start(bf16[128,128]{1,0:T(8,128)(2,1)} %get-tuple-element.38), channel_id=1, source_target_pairs={{0,9},{1,8},{2,11},{3,10},{4,13},{5,12},{6,15},{7,14},{8,1},{9,0},... | collective-permute-start | bytes 98312 | tf_op jit(solution)/shard_map/ppermute | solution.py:316
  63.4 2.3 %collective-permute-start.24 = (bf16[128,128]{1,0:T(8,128)(2,1)}, bf16[128,128]{1,0:T(8,128)(2,1)S(1)}, u32[]{:S(2)}, u32[]{:S(2)}) collective-permute-start(bf16[128,128]{1,0:T(8,128)(2,1)} %get-tuple-element.39), channel_id=1, source_target_pairs={{0,10},{1,11},{2,8},{3,9},{4,14},{5,15},{6,12},{7,13},{8,2},{9,3},... | collective-permute-start | bytes 98312 | tf_op jit(solution)/shard_map/ppermute | solution.py:316
  65.7 0.0 collective-permute-done.20.refs_6_
  65.7 1.0 %collective-permute-start.25 = (bf16[128,128]{1,0:T(8,128)(2,1)}, bf16[128,128]{1,0:T(8,128)(2,1)S(1)}, u32[]{:S(2)}, u32[]{:S(2)}) collective-permute-start(bf16[128,128]{1,0:T(8,128)(2,1)} %get-tuple-element.40), channel_id=1, source_target_pairs={{0,11},{1,10},{2,9},{3,8},{4,15},{5,14},{6,13},{7,12},{8,3},{9,2},... | collective-permute-start | bytes 98312 | tf_op jit(solution)/shard_map/ppermute | solution.py:316
  66.7 0.0 collective-permute-done.21.refs_7_
  66.7 2.6 %collective-permute-start.26 = (bf16[128,128]{1,0:T(8,128)(2,1)}, bf16[128,128]{1,0:T(8,128)(2,1)S(1)}, u32[]{:S(2)}, u32[]{:S(2)}) collective-permute-start(bf16[128,128]{1,0:T(8,128)(2,1)} %get-tuple-element.41), channel_id=1, source_target_pairs={{0,12},{1,13},{2,14},{3,15},{4,8},{5,9},{6,10},{7,11},{8,4},{9,5},... | collective-permute-start | bytes 98312 | tf_op jit(solution)/shard_map/ppermute | solution.py:316
  69.2 1.3 %collective-permute-start.27 = (bf16[128,128]{1,0:T(8,128)(2,1)}, bf16[128,128]{1,0:T(8,128)(2,1)S(1)}, u32[]{:S(2)}, u32[]{:S(2)}) collective-permute-start(bf16[128,128]{1,0:T(8,128)(2,1)} %get-tuple-element.42), channel_id=1, source_target_pairs={{0,13},{1,12},{2,15},{3,14},{4,9},{5,8},{6,11},{7,10},{8,5},{9,4},... | collective-permute-start | bytes 98312 | tf_op jit(solution)/shard_map/ppermute | solution.py:316
  70.6 0.0 collective-permute-done.23.refs_9_
  70.6 3.4 %collective-permute-start.28 = (bf16[128,128]{1,0:T(8,128)(2,1)}, bf16[128,128]{1,0:T(8,128)(2,1)S(1)}, u32[]{:S(2)}, u32[]{:S(2)}) collective-permute-start(bf16[128,128]{1,0:T(8,128)(2,1)} %get-tuple-element.43), channel_id=1, source_target_pairs={{0,14},{1,15},{2,12},{3,13},{4,10},{5,11},{6,8},{7,9},{8,6},{9,7},... | collective-permute-start | bytes 98312 | tf_op jit(solution)/shard_map/ppermute | solution.py:316
  74.0 0.7 collective-permute-start.29
  74.7 0.0 collective-permute-done.25.refs_11_
  74.7 0.0 collective-permute-done.26.refs_12_
  74.7 0.0 collective-permute-done.27.refs_13_
  74.7 2.7 %collective-permute-done.28.refs_14_ = bf16[128,128]{1,0:T(8,128)(2,1)S(1)} collective-permute-done((bf16[128,128]{1,0:T(8,128)(2,1)}, bf16[128,128]{1,0:T(8,128)(2,1)S(1)}, u32[]{:S(2)}, u32[]{:S(2)}) %collective-permute-start.28) | collective-permute-done | bytes 32800 | tf_op jit(solution)/shard_map/ppermute | solution.py:316
  77.4 3.2 %collective-permute-done.29.refs_15_ = bf16[128,128]{1,0:T(8,128)(2,1)S(1)} collective-permute-done((bf16[128,128]{1,0:T(8,128)(2,1)}, bf16[128,128]{1,0:T(8,128)(2,1)S(1)}, u32[]{:S(2)}, u32[]{:S(2)}) %collective-permute-start.29) | collective-permute-done | bytes 32800 | tf_op jit(solution)/shard_map/ppermute | solution.py:316
  80.7 0.5 copy-done.30
  81.2 2.5 %residual.1 = f32[16,128,128]{2,1,0:T(8,128)} custom-call(s32[1]{0:T(128)} %bitcast.me, f32[16,128,128]{2,1,0:T(8,128)} %bitcast.23, bf16[128,128]{1,0:T(8,128)(2,1)} %get-tuple-element.29.refs_0_, bf16[128,128]{1,0:T(8,128)(2,1)} %copy-done.16, bf16[128,128]{1,0:T(8,128)(2,1)} %copy-done.17, bf16[128,128]{1,0:T(8,128)(2,1)} %copy-done.18, ...), custom_call_target="tpu_custom_call" | custom-call | tf_op jit(solution)/shard_map/residual/pallas_call | solution.py:420
  (67 shorter events, 0.1 us)
Async XLA Ops:
  1.6 7.1 %collective-permute-start.7 = (bf16[96,256]{1,0:T(8,128)(2,1)}, bf16[96,256]{1,0:T(8,128)(2,1)S(1)}, u32[]{:S(2)}, u32[]{:S(2)}) collective-permute-start(bf16[96,256]{1,0:T(8,128)(2,1)} %get-tuple-element.27), channel_id=1, source_target_pairs={{0,8},{1,9},{2,10},{3,11},{4,12},{5,13},{6,14},{7,15},{8,0},{9,1},... | collective-permute-start | bytes 147464 | tf_op jit(solution)/shard_map/ppermute | solution.py:316
  5.6 6.2 %collective-permute-start.11 = (bf16[96,256]{1,0:T(8,128)(2,1)}, bf16[96,256]{1,0:T(8,128)(2,1)S(1)}, u32[]{:S(2)}, u32[]{:S(2)}) collective-permute-start(bf16[96,256]{1,0:T(8,128)(2,1)} %get-tuple-element.28), channel_id=1, source_target_pairs={{0,12},{1,13},{2,14},{3,15},{4,8},{5,9},{6,10},{7,11},{8,4},{9,5},... | collective-permute-start | bytes 147464 | tf_op jit(solution)/shard_map/ppermute | solution.py:316
  7.0 6.4 %collective-permute-start.3 = (bf16[96,256]{1,0:T(8,128)(2,1)}, bf16[96,256]{1,0:T(8,128)(2,1)S(1)}, u32[]{:S(2)}, u32[]{:S(2)}) collective-permute-start(bf16[96,256]{1,0:T(8,128)(2,1)} %get-tuple-element.26), channel_id=1, source_target_pairs={{0,4},{1,5},{2,6},{3,7},{4,0},{5,1},{6,2},{7,3},{8,12},{9,13},{10,... | collective-permute-start | bytes 147464 | tf_op jit(solution)/shard_map/ppermute | solution.py:316
  7.2 6.6 %collective-permute-start.1 = (bf16[96,256]{1,0:T(8,128)(2,1)}, bf16[96,256]{1,0:T(8,128)(2,1)S(1)}, u32[]{:S(2)}, u32[]{:S(2)}) collective-permute-start(bf16[96,256]{1,0:T(8,128)(2,1)} %get-tuple-element.25.refs_0_), channel_id=1, source_target_pairs={{0,2},{1,3},{2,0},{3,1},{4,6},{5,7},{6,4},{7,5},{8,10},{9,11},{10,... | collective-permute-start | bytes 147464 | tf_op jit(solution)/shard_map/ppermute | solution.py:316
  8.7 5.1 %collective-permute-start = (bf16[96,256]{1,0:T(8,128)(2,1)}, bf16[96,256]{1,0:T(8,128)(2,1)S(1)}, u32[]{:S(2)}, u32[]{:S(2)}) collective-permute-start(bf16[96,256]{1,0:T(8,128)(2,1)} %get-tuple-element.25.refs_0_), channel_id=1, source_target_pairs={{0,1},{1,0},{2,3},{3,2},{4,5},{5,4},{6,7},{7,6},{8,9},{9,8},{10,11... | collective-permute-start | bytes 147464 | tf_op jit(solution)/shard_map/ppermute | solution.py:316
  8.8 11.7 %copy-start.1 = (bf16[96,256]{1,0:T(8,128)(2,1)}, bf16[96,256]{1,0:T(8,128)(2,1)S(1)}, u32[]{:S(2)}) copy-start(bf16[96,256]{1,0:T(8,128)(2,1)S(1)} %collective-permute-done.7.refs_8_) | copy-start | bytes 147460
  8.8 5.6 %collective-permute-start.9 = (bf16[96,256]{1,0:T(8,128)(2,1)S(1)}, bf16[96,256]{1,0:T(8,128)(2,1)S(1)}, u32[]{:S(2)}, u32[]{:S(2)}) collective-permute-start(bf16[96,256]{1,0:T(8,128)(2,1)S(1)} %collective-permute-done.7.refs_8_), channel_id=1, source_target_pairs={{0,2},{1,3},{2,0},{3,1},{4,6},{5,7},{6,4},{7,5},{8,10},{9,11},{10,... | collective-permute-start | bytes 147464 | tf_op jit(solution)/shard_map/ppermute | solution.py:316
  11.8 8.7 %copy-start.2 = (bf16[96,256]{1,0:T(8,128)(2,1)}, bf16[96,256]{1,0:T(8,128)(2,1)S(1)}, u32[]{:S(2)}) copy-start(bf16[96,256]{1,0:T(8,128)(2,1)S(1)} %collective-permute-done.11.refs_12_) | copy-start | bytes 147460
  11.8 4.1 %collective-permute-start.13 = (bf16[96,256]{1,0:T(8,128)(2,1)S(1)}, bf16[96,256]{1,0:T(8,128)(2,1)S(1)}, u32[]{:S(2)}, u32[]{:S(2)}) collective-permute-start(bf16[96,256]{1,0:T(8,128)(2,1)S(1)} %collective-permute-done.11.refs_12_), channel_id=1, source_target_pairs={{0,2},{1,3},{2,0},{3,1},{4,6},{5,7},{6,4},{7,5},{8,10},{9,11},{10,... | collective-permute-start | bytes 147464 | tf_op jit(solution)/shard_map/ppermute | solution.py:316
  13.3 7.1 %copy-start.3 = (bf16[96,256]{1,0:T(8,128)(2,1)}, bf16[96,256]{1,0:T(8,128)(2,1)S(1)}, u32[]{:S(2)}) copy-start(bf16[96,256]{1,0:T(8,128)(2,1)S(1)} %collective-permute-done.3.refs_4_) | copy-start | bytes 147460
  13.3 4.1 %collective-permute-start.5 = (bf16[96,256]{1,0:T(8,128)(2,1)S(1)}, bf16[96,256]{1,0:T(8,128)(2,1)S(1)}, u32[]{:S(2)}, u32[]{:S(2)}) collective-permute-start(bf16[96,256]{1,0:T(8,128)(2,1)S(1)} %collective-permute-done.3.refs_4_), channel_id=1, source_target_pairs={{0,2},{1,3},{2,0},{3,1},{4,6},{5,7},{6,4},{7,5},{8,10},{9,11},{10,... | collective-permute-start | bytes 147464 | tf_op jit(solution)/shard_map/ppermute | solution.py:316
  13.9 6.6 %copy-start.4 = (bf16[96,256]{1,0:T(8,128)(2,1)}, bf16[96,256]{1,0:T(8,128)(2,1)S(1)}, u32[]{:S(2)}) copy-start(bf16[96,256]{1,0:T(8,128)(2,1)S(1)} %collective-permute-done.1.refs_2_) | copy-start | bytes 147460
  13.9 3.6 %collective-permute-start.2 = (bf16[96,256]{1,0:T(8,128)(2,1)S(1)}, bf16[96,256]{1,0:T(8,128)(2,1)S(1)}, u32[]{:S(2)}, u32[]{:S(2)}) collective-permute-start(bf16[96,256]{1,0:T(8,128)(2,1)S(1)} %collective-permute-done.1.refs_2_), channel_id=1, source_target_pairs={{0,1},{1,0},{2,3},{3,2},{4,5},{5,4},{6,7},{7,6},{8,9},{9,8},{10,11... | collective-permute-start | bytes 147464 | tf_op jit(solution)/shard_map/ppermute | solution.py:316
  13.9 6.6 %copy-start.5 = (bf16[96,256]{1,0:T(8,128)(2,1)}, bf16[96,256]{1,0:T(8,128)(2,1)S(1)}, u32[]{:S(2)}) copy-start(bf16[96,256]{1,0:T(8,128)(2,1)S(1)} %collective-permute-done.refs_1_) | copy-start | bytes 147460
  13.9 4.1 %collective-permute-start.12 = (bf16[96,256]{1,0:T(8,128)(2,1)S(1)}, bf16[96,256]{1,0:T(8,128)(2,1)S(1)}, u32[]{:S(2)}, u32[]{:S(2)}) collective-permute-start(bf16[96,256]{1,0:T(8,128)(2,1)S(1)} %collective-permute-done.11.refs_12_), channel_id=1, source_target_pairs={{0,1},{1,0},{2,3},{3,2},{4,5},{5,4},{6,7},{7,6},{8,9},{9,8},{10,11... | collective-permute-start | bytes 147464 | tf_op jit(solution)/shard_map/ppermute | solution.py:316
  14.4 6.1 %copy-start.6 = (bf16[96,256]{1,0:T(8,128)(2,1)}, bf16[96,256]{1,0:T(8,128)(2,1)S(1)}, u32[]{:S(2)}) copy-start(bf16[96,256]{1,0:T(8,128)(2,1)S(1)} %collective-permute-done.9.refs_10_) | copy-start | bytes 147460
  14.4 14.7 %collective-permute-start.4 = (bf16[96,256]{1,0:T(8,128)(2,1)S(1)}, bf16[96,256]{1,0:T(8,128)(2,1)S(1)}, u32[]{:S(2)}, u32[]{:S(2)}) collective-permute-start(bf16[96,256]{1,0:T(8,128)(2,1)S(1)} %collective-permute-done.3.refs_4_), channel_id=1, source_target_pairs={{0,1},{1,0},{2,3},{3,2},{4,5},{5,4},{6,7},{7,6},{8,9},{9,8},{10,11... | collective-permute-start | bytes 147464 | tf_op jit(solution)/shard_map/ppermute | solution.py:316
  15.9 4.6 %copy-start.7 = (bf16[96,256]{1,0:T(8,128)(2,1)}, bf16[96,256]{1,0:T(8,128)(2,1)S(1)}, u32[]{:S(2)}) copy-start(bf16[96,256]{1,0:T(8,128)(2,1)S(1)} %collective-permute-done.13.refs_14_) | copy-start | bytes 147460
  15.9 13.2 %collective-permute-start.8 = (bf16[96,256]{1,0:T(8,128)(2,1)S(1)}, bf16[96,256]{1,0:T(8,128)(2,1)S(1)}, u32[]{:S(2)}, u32[]{:S(2)}) collective-permute-start(bf16[96,256]{1,0:T(8,128)(2,1)S(1)} %collective-permute-done.7.refs_8_), channel_id=1, source_target_pairs={{0,1},{1,0},{2,3},{3,2},{4,5},{5,4},{6,7},{7,6},{8,9},{9,8},{10,11... | collective-permute-start | bytes 147464 | tf_op jit(solution)/shard_map/ppermute | solution.py:316
  17.4 3.1 %copy-start.8 = (bf16[96,256]{1,0:T(8,128)(2,1)}, bf16[96,256]{1,0:T(8,128)(2,1)S(1)}, u32[]{:S(2)}) copy-start(bf16[96,256]{1,0:T(8,128)(2,1)S(1)} %collective-permute-done.5.refs_6_) | copy-start | bytes 147460
  17.4 11.7 %collective-permute-start.10 = (bf16[96,256]{1,0:T(8,128)(2,1)S(1)}, bf16[96,256]{1,0:T(8,128)(2,1)S(1)}, u32[]{:S(2)}, u32[]{:S(2)}) collective-permute-start(bf16[96,256]{1,0:T(8,128)(2,1)S(1)} %collective-permute-done.9.refs_10_), channel_id=1, source_target_pairs={{0,1},{1,0},{2,3},{3,2},{4,5},{5,4},{6,7},{7,6},{8,9},{9,8},{10,11... | collective-permute-start | bytes 147464 | tf_op jit(solution)/shard_map/ppermute | solution.py:316
  17.5 3.1 %copy-start.9 = (bf16[96,256]{1,0:T(8,128)(2,1)}, bf16[96,256]{1,0:T(8,128)(2,1)S(1)}, u32[]{:S(2)}) copy-start(bf16[96,256]{1,0:T(8,128)(2,1)S(1)} %collective-permute-done.2.refs_3_) | copy-start | bytes 147460
  17.5 11.7 %collective-permute-start.14 = (bf16[96,256]{1,0:T(8,128)(2,1)S(1)}, bf16[96,256]{1,0:T(8,128)(2,1)S(1)}, u32[]{:S(2)}, u32[]{:S(2)}) collective-permute-start(bf16[96,256]{1,0:T(8,128)(2,1)S(1)} %collective-permute-done.13.refs_14_), channel_id=1, source_target_pairs={{0,1},{1,0},{2,3},{3,2},{4,5},{5,4},{6,7},{7,6},{8,9},{9,8},{10,11... | collective-permute-start | bytes 147464 | tf_op jit(solution)/shard_map/ppermute | solution.py:316
  18.0 2.6 %copy-start.10 = (bf16[96,256]{1,0:T(8,128)(2,1)}, bf16[96,256]{1,0:T(8,128)(2,1)S(1)}, u32[]{:S(2)}) copy-start(bf16[96,256]{1,0:T(8,128)(2,1)S(1)} %collective-permute-done.12.refs_13_) | copy-start | bytes 147460
  18.0 11.2 %collective-permute-start.6 = (bf16[96,256]{1,0:T(8,128)(2,1)S(1)}, bf16[96,256]{1,0:T(8,128)(2,1)S(1)}, u32[]{:S(2)}, u32[]{:S(2)}) collective-permute-start(bf16[96,256]{1,0:T(8,128)(2,1)S(1)} %collective-permute-done.5.refs_6_), channel_id=1, source_target_pairs={{0,1},{1,0},{2,3},{3,2},{4,5},{5,4},{6,7},{7,6},{8,9},{9,8},{10,11... | collective-permute-start | bytes 147464 | tf_op jit(solution)/shard_map/ppermute | solution.py:316
  20.6 1.3 %copy-start = (bf16[2,128,1024]{2,1,0:T(8,128)(2,1)S(1)}, bf16[2,128,1024]{2,1,0:T(8,128)(2,1)}, u32[]{:S(2)}) copy-start(bf16[2,128,1024]{2,1,0:T(8,128)(2,1)} %param.18) | copy-start | bytes 1572868
  29.1 0.6 copy-start.11
  29.1 0.6 copy-start.12
  29.1 0.6 copy-start.13
  29.1 0.6 copy-start.14
  29.2 0.6 copy-start.15
  54.1 4.0 %collective-permute-start.15 = (bf16[128,128]{1,0:T(8,128)(2,1)}, bf16[128,128]{1,0:T(8,128)(2,1)S(1)}, u32[]{:S(2)}, u32[]{:S(2)}) collective-permute-start(bf16[128,128]{1,0:T(8,128)(2,1)} %get-tuple-element.30), channel_id=1, source_target_pairs={{0,1},{1,0},{2,3},{3,2},{4,5},{5,4},{6,7},{7,6},{8,9},{9,8},{10,11... | collective-permute-start | bytes 98312 | tf_op jit(solution)/shard_map/ppermute | solution.py:316
  54.6 4.4 %collective-permute-start.16 = (bf16[128,128]{1,0:T(8,128)(2,1)}, bf16[128,128]{1,0:T(8,128)(2,1)S(1)}, u32[]{:S(2)}, u32[]{:S(2)}) collective-permute-start(bf16[128,128]{1,0:T(8,128)(2,1)} %get-tuple-element.31), channel_id=1, source_target_pairs={{0,2},{1,3},{2,0},{3,1},{4,6},{5,7},{6,4},{7,5},{8,10},{9,11},{10,... | collective-permute-start | bytes 98312 | tf_op jit(solution)/shard_map/ppermute | solution.py:316
  55.1 5.3 %collective-permute-start.17 = (bf16[128,128]{1,0:T(8,128)(2,1)}, bf16[128,128]{1,0:T(8,128)(2,1)S(1)}, u32[]{:S(2)}, u32[]{:S(2)}) collective-permute-start(bf16[128,128]{1,0:T(8,128)(2,1)} %get-tuple-element.32), channel_id=1, source_target_pairs={{0,3},{1,2},{2,1},{3,0},{4,7},{5,6},{6,5},{7,4},{8,11},{9,10},{10,... | collective-permute-start | bytes 98312 | tf_op jit(solution)/shard_map/ppermute | solution.py:316
  56.1 6.2 %collective-permute-start.18 = (bf16[128,128]{1,0:T(8,128)(2,1)}, bf16[128,128]{1,0:T(8,128)(2,1)S(1)}, u32[]{:S(2)}, u32[]{:S(2)}) collective-permute-start(bf16[128,128]{1,0:T(8,128)(2,1)} %get-tuple-element.33), channel_id=1, source_target_pairs={{0,4},{1,5},{2,6},{3,7},{4,0},{5,1},{6,2},{7,3},{8,12},{9,13},{10,... | collective-permute-start | bytes 98312 | tf_op jit(solution)/shard_map/ppermute | solution.py:316
  56.1 7.4 %collective-permute-start.19 = (bf16[128,128]{1,0:T(8,128)(2,1)}, bf16[128,128]{1,0:T(8,128)(2,1)S(1)}, u32[]{:S(2)}, u32[]{:S(2)}) collective-permute-start(bf16[128,128]{1,0:T(8,128)(2,1)} %get-tuple-element.34), channel_id=1, source_target_pairs={{0,5},{1,4},{2,7},{3,6},{4,1},{5,0},{6,3},{7,2},{8,13},{9,12},{10,... | collective-permute-start | bytes 98312 | tf_op jit(solution)/shard_map/ppermute | solution.py:316
  58.1 22.4 %copy-start.16 = (bf16[128,128]{1,0:T(8,128)(2,1)}, bf16[128,128]{1,0:T(8,128)(2,1)S(1)}, u32[]{:S(2)}) copy-start(bf16[128,128]{1,0:T(8,128)(2,1)S(1)} %collective-permute-done.15.refs_1_) | copy-start | bytes 98308
  58.1 7.6 %collective-permute-start.20 = (bf16[128,128]{1,0:T(8,128)(2,1)}, bf16[128,128]{1,0:T(8,128)(2,1)S(1)}, u32[]{:S(2)}, u32[]{:S(2)}) collective-permute-start(bf16[128,128]{1,0:T(8,128)(2,1)} %get-tuple-element.35), channel_id=1, source_target_pairs={{0,6},{1,7},{2,4},{3,5},{4,2},{5,3},{6,0},{7,1},{8,14},{9,15},{10,... | collective-permute-start | bytes 98312 | tf_op jit(solution)/shard_map/ppermute | solution.py:316
  59.0 21.5 %copy-start.17 = (bf16[128,128]{1,0:T(8,128)(2,1)}, bf16[128,128]{1,0:T(8,128)(2,1)S(1)}, u32[]{:S(2)}) copy-start(bf16[128,128]{1,0:T(8,128)(2,1)S(1)} %collective-permute-done.16.refs_2_) | copy-start | bytes 98308
  59.0 7.6 %collective-permute-start.21 = (bf16[128,128]{1,0:T(8,128)(2,1)}, bf16[128,128]{1,0:T(8,128)(2,1)S(1)}, u32[]{:S(2)}, u32[]{:S(2)}) collective-permute-start(bf16[128,128]{1,0:T(8,128)(2,1)} %get-tuple-element.36), channel_id=1, source_target_pairs={{0,7},{1,6},{2,5},{3,4},{4,3},{5,2},{6,1},{7,0},{8,15},{9,14},{10,... | collective-permute-start | bytes 98312 | tf_op jit(solution)/shard_map/ppermute | solution.py:316
  60.5 20.1 %copy-start.18 = (bf16[128,128]{1,0:T(8,128)(2,1)}, bf16[128,128]{1,0:T(8,128)(2,1)S(1)}, u32[]{:S(2)}) copy-start(bf16[128,128]{1,0:T(8,128)(2,1)S(1)} %collective-permute-done.17.refs_3_) | copy-start | bytes 98308
  60.5 8.8 %collective-permute-start.22 = (bf16[128,128]{1,0:T(8,128)(2,1)}, bf16[128,128]{1,0:T(8,128)(2,1)S(1)}, u32[]{:S(2)}, u32[]{:S(2)}) collective-permute-start(bf16[128,128]{1,0:T(8,128)(2,1)} %get-tuple-element.37), channel_id=1, source_target_pairs={{0,8},{1,9},{2,10},{3,11},{4,12},{5,13},{6,14},{7,15},{8,0},{9,1},... | collective-permute-start | bytes 98312 | tf_op jit(solution)/shard_map/ppermute | solution.py:316
  62.2 18.4 %copy-start.19 = (bf16[128,128]{1,0:T(8,128)(2,1)}, bf16[128,128]{1,0:T(8,128)(2,1)S(1)}, u32[]{:S(2)}) copy-start(bf16[128,128]{1,0:T(8,128)(2,1)S(1)} %collective-permute-done.18.refs_4_) | copy-start | bytes 98308
  62.2 8.3 %collective-permute-start.23 = (bf16[128,128]{1,0:T(8,128)(2,1)}, bf16[128,128]{1,0:T(8,128)(2,1)S(1)}, u32[]{:S(2)}, u32[]{:S(2)}) collective-permute-start(bf16[128,128]{1,0:T(8,128)(2,1)} %get-tuple-element.38), channel_id=1, source_target_pairs={{0,9},{1,8},{2,11},{3,10},{4,13},{5,12},{6,15},{7,14},{8,1},{9,0},... | collective-permute-start | bytes 98312 | tf_op jit(solution)/shard_map/ppermute | solution.py:316
  63.4 17.1 %copy-start.20 = (bf16[128,128]{1,0:T(8,128)(2,1)}, bf16[128,128]{1,0:T(8,128)(2,1)S(1)}, u32[]{:S(2)}) copy-start(bf16[128,128]{1,0:T(8,128)(2,1)S(1)} %collective-permute-done.19.refs_5_) | copy-start | bytes 98308
  63.4 10.5 %collective-permute-start.24 = (bf16[128,128]{1,0:T(8,128)(2,1)}, bf16[128,128]{1,0:T(8,128)(2,1)S(1)}, u32[]{:S(2)}, u32[]{:S(2)}) collective-permute-start(bf16[128,128]{1,0:T(8,128)(2,1)} %get-tuple-element.39), channel_id=1, source_target_pairs={{0,10},{1,11},{2,8},{3,9},{4,14},{5,15},{6,12},{7,13},{8,2},{9,3},... | collective-permute-start | bytes 98312 | tf_op jit(solution)/shard_map/ppermute | solution.py:316
  65.7 14.9 %copy-start.21 = (bf16[128,128]{1,0:T(8,128)(2,1)}, bf16[128,128]{1,0:T(8,128)(2,1)S(1)}, u32[]{:S(2)}) copy-start(bf16[128,128]{1,0:T(8,128)(2,1)S(1)} %collective-permute-done.20.refs_6_) | copy-start | bytes 98308
  65.7 9.0 %collective-permute-start.25 = (bf16[128,128]{1,0:T(8,128)(2,1)}, bf16[128,128]{1,0:T(8,128)(2,1)S(1)}, u32[]{:S(2)}, u32[]{:S(2)}) collective-permute-start(bf16[128,128]{1,0:T(8,128)(2,1)} %get-tuple-element.40), channel_id=1, source_target_pairs={{0,11},{1,10},{2,9},{3,8},{4,15},{5,14},{6,13},{7,12},{8,3},{9,2},... | collective-permute-start | bytes 98312 | tf_op jit(solution)/shard_map/ppermute | solution.py:316
  66.7 13.9 %copy-start.22 = (bf16[128,128]{1,0:T(8,128)(2,1)}, bf16[128,128]{1,0:T(8,128)(2,1)S(1)}, u32[]{:S(2)}) copy-start(bf16[128,128]{1,0:T(8,128)(2,1)S(1)} %collective-permute-done.21.refs_7_) | copy-start | bytes 98308
  66.7 8.0 %collective-permute-start.26 = (bf16[128,128]{1,0:T(8,128)(2,1)}, bf16[128,128]{1,0:T(8,128)(2,1)S(1)}, u32[]{:S(2)}, u32[]{:S(2)}) collective-permute-start(bf16[128,128]{1,0:T(8,128)(2,1)} %get-tuple-element.41), channel_id=1, source_target_pairs={{0,12},{1,13},{2,14},{3,15},{4,8},{5,9},{6,10},{7,11},{8,4},{9,5},... | collective-permute-start | bytes 98312 | tf_op jit(solution)/shard_map/ppermute | solution.py:316
  69.2 11.4 %copy-start.23 = (bf16[128,128]{1,0:T(8,128)(2,1)}, bf16[128,128]{1,0:T(8,128)(2,1)S(1)}, u32[]{:S(2)}) copy-start(bf16[128,128]{1,0:T(8,128)(2,1)S(1)} %collective-permute-done.22.refs_8_) | copy-start | bytes 98308
  69.2 5.5 %collective-permute-start.27 = (bf16[128,128]{1,0:T(8,128)(2,1)}, bf16[128,128]{1,0:T(8,128)(2,1)S(1)}, u32[]{:S(2)}, u32[]{:S(2)}) collective-permute-start(bf16[128,128]{1,0:T(8,128)(2,1)} %get-tuple-element.42), channel_id=1, source_target_pairs={{0,13},{1,12},{2,15},{3,14},{4,9},{5,8},{6,11},{7,10},{8,5},{9,4},... | collective-permute-start | bytes 98312 | tf_op jit(solution)/shard_map/ppermute | solution.py:316
  70.6 10.1 %copy-start.24 = (bf16[128,128]{1,0:T(8,128)(2,1)}, bf16[128,128]{1,0:T(8,128)(2,1)S(1)}, u32[]{:S(2)}) copy-start(bf16[128,128]{1,0:T(8,128)(2,1)S(1)} %collective-permute-done.23.refs_9_) | copy-start | bytes 98308
  70.6 6.8 %collective-permute-start.28 = (bf16[128,128]{1,0:T(8,128)(2,1)}, bf16[128,128]{1,0:T(8,128)(2,1)S(1)}, u32[]{:S(2)}, u32[]{:S(2)}) collective-permute-start(bf16[128,128]{1,0:T(8,128)(2,1)} %get-tuple-element.43), channel_id=1, source_target_pairs={{0,14},{1,15},{2,12},{3,13},{4,10},{5,11},{6,8},{7,9},{8,6},{9,7},... | collective-permute-start | bytes 98312 | tf_op jit(solution)/shard_map/ppermute | solution.py:316
  74.0 6.6 %copy-start.25 = (bf16[128,128]{1,0:T(8,128)(2,1)}, bf16[128,128]{1,0:T(8,128)(2,1)S(1)}, u32[]{:S(2)}) copy-start(bf16[128,128]{1,0:T(8,128)(2,1)S(1)} %collective-permute-done.24.refs_10_) | copy-start | bytes 98308
  74.0 6.6 %collective-permute-start.29 = (bf16[128,128]{1,0:T(8,128)(2,1)}, bf16[128,128]{1,0:T(8,128)(2,1)S(1)}, u32[]{:S(2)}, u32[]{:S(2)}) collective-permute-start(bf16[128,128]{1,0:T(8,128)(2,1)} %get-tuple-element.44), channel_id=1, source_target_pairs={{0,15},{1,14},{2,13},{3,12},{4,11},{5,10},{6,9},{7,8},{8,7},{9,6},... | collective-permute-start | bytes 98312 | tf_op jit(solution)/shard_map/ppermute | solution.py:316
  74.7 6.0 %copy-start.26 = (bf16[128,128]{1,0:T(8,128)(2,1)}, bf16[128,128]{1,0:T(8,128)(2,1)S(1)}, u32[]{:S(2)}) copy-start(bf16[128,128]{1,0:T(8,128)(2,1)S(1)} %collective-permute-done.25.refs_11_) | copy-start | bytes 98308
  74.7 6.0 %copy-start.27 = (bf16[128,128]{1,0:T(8,128)(2,1)}, bf16[128,128]{1,0:T(8,128)(2,1)S(1)}, u32[]{:S(2)}) copy-start(bf16[128,128]{1,0:T(8,128)(2,1)S(1)} %collective-permute-done.26.refs_12_) | copy-start | bytes 98308
  74.7 6.0 %copy-start.28 = (bf16[128,128]{1,0:T(8,128)(2,1)}, bf16[128,128]{1,0:T(8,128)(2,1)S(1)}, u32[]{:S(2)}) copy-start(bf16[128,128]{1,0:T(8,128)(2,1)S(1)} %collective-permute-done.27.refs_13_) | copy-start | bytes 98308
  77.4 3.3 %copy-start.29 = (bf16[128,128]{1,0:T(8,128)(2,1)}, bf16[128,128]{1,0:T(8,128)(2,1)S(1)}, u32[]{:S(2)}) copy-start(bf16[128,128]{1,0:T(8,128)(2,1)S(1)} %collective-permute-done.28.refs_14_) | copy-start | bytes 98308
  80.6 0.6 copy-start.30

commit v3 on v1

--- a/solution.py
+++ b/solution.py
@@ -13,7 +13,7 @@
 TWO_PI = 2.0 * math.pi
 F32 = jnp.float32
 BF16 = jnp.bfloat16
-VMEM_LIMIT = 56 * 1024 * 1024
+VMEM_LIMIT = 36 * 1024 * 1024
 NT = (((1,), (1,)), ((), ()))
 TN = (((0,), (0,)), ((), ()))
 
@@ -60,29 +60,29 @@
     return out_re, out_im
 
 
-def transform_kernel(cells, high, rest, image, sum_high, sum_rest):
-    number = cells.shape[2]
-    lanes = cells.shape[3]
+def transform_kernel(cells, high, rest, image, wide, sums):
+    number = image.shape[1]
     step = 16
 
-    @pl.loop(0, number // step)
+    @pl.loop(0, number // step, unroll=2)
     def _(n):
         rows = pl.ds(pl.multiple_of(n * step, step), step)
-        re = [cells[0, k, rows, :].astype(F32) for k in range(8)]
-        im = [cells[1, k, rows, :].astype(F32) for k in range(8)]
+        span = pl.ds(pl.multiple_of(n * step * 16, step * 16), step * 16)
+        wide[span, :] = cells[span, :].astype(F32)
+        re = [wide[pl.ds(n * step * 16 + 2 * k, step, stride=16), :] for k in range(8)]
+        im = [wide[pl.ds(n * step * 16 + 2 * k + 1, step, stride=16), :] for k in range(8)]
         out_re, out_im = eight_point(re, im)
         for m in range(8):
-            for part, value in ((0, out_re[m]), (1, out_im[m])):
-                top = value.astype(BF16)
-                cols = slice(part * lanes, (part + 1) * lanes)
-                sum_high[m, rows, cols] = top
-                sum_rest[m, rows, cols] = (value - top.astype(F32)).astype(BF16)
-
-    @pl.loop(0, 8)
-    def _(m):
-        a, b = sum_high[m], sum_rest[m]
-        total = dot(a, high[m]) + (dot(b, high[m]) + dot(a, rest[m]))
-        image[m] = total.astype(BF16)
+            value = jnp.concatenate([out_re[m], out_im[m]], axis=1)
+            top = value.astype(BF16)
+            sums[m, rows, :256] = top
+            sums[m, rows, 256:] = (value - top.astype(F32)).astype(BF16)
+
+    for m in range(8):
+        both = sums[m]
+        left = jnp.concatenate([both, both[:, :256]], axis=1)
+        right = jnp.concatenate([high[m], high[m], rest[m]], axis=0)
+        image[m] = dot(left, right).astype(BF16)
 
 
 def unit_powers(turns):
@@ -104,20 +104,43 @@
     return ar * br - ai * bi, ar * bi + ai * br
 
 
+def pack_kernel(coefs, tracks, out):
+    capacity = tracks.shape[2]
+    rows = coefs.shape[0]
+    for d in range(tracks.shape[0]):
+        tr = tracks[d]
+        t_hi = tr.astype(BF16).astype(F32)
+        t_mid = (tr - t_hi).astype(BF16).astype(F32)
+        t_lo = tr - t_hi - t_mid
+        pieces = jnp.concatenate(
+            [
+                jnp.concatenate([t_hi, t_mid], axis=1),
+                jnp.concatenate([t_lo, jnp.zeros_like(tr)], axis=1),
+            ],
+            axis=0,
+        )
+        if 2 * capacity < 128:
+            blank = jnp.zeros((pieces.shape[0], 128 - 2 * capacity), F32)
+            pieces = jnp.concatenate([pieces, blank], axis=1)
+        out[d, :rows, :] = coefs[:, :128]
+        out[d, rows : 2 * rows, :] = coefs[:, 128:]
+        out[d, 2 * rows :, :] = pieces.astype(BF16)
+
+
 def predict_kernel(
-    table,
-    slot_row,
+    counts,
+    packed,
+    assign,
     stations,
     time_slots,
-    tracks,
     freq,
     basis,
     image,
     payload,
+    table,
     route,
     weights,
-    coef_first,
-    coef_second,
+    coef,
     wre,
     wim,
     pure,
@@ -131,27 +154,47 @@
     slot_count,
 ):
     number = image.shape[1]
-    slots = slot_row.shape[1]
+    tiles, capacity = assign.shape
+    slots = tiles * capacity
     rows_all = table.shape[0]
+    rows_own = rows_all // tiles
     chan = freq.shape[1]
-    steps = tracks.shape[0] // 2
+    kinds = (packed.shape[1] - 2 * rows_own) // 2
+    steps = kinds // 2
     terms = basis.shape[1]
 
-    down = lax.broadcasted_iota(jnp.int32, (number, slots), 0)
-    route[...] = (slot_row[...] == down).astype(F32).astype(BF16)
-
-    tr = tracks[...]
-    t_hi = tr.astype(BF16)
-    left = tr - t_hi.astype(F32)
-    t_mid = left.astype(BF16)
-    t_lo = (left - t_mid.astype(F32)).astype(BF16)
-    pieces = jnp.concatenate(
-        [t_hi.astype(F32), t_mid.astype(F32), t_lo.astype(F32)], axis=0
-    ).astype(BF16)
+    per = 128 // capacity
+    down = lax.broadcasted_iota(jnp.int32, (number, 128), 0)
+    slot = lax.broadcasted_iota(jnp.int32, (1, capacity), 1)
+    held = []
+    for n in range(tiles // per):
+        chosen, tracks = [], []
+        for d in range(n * per, (n + 1) * per):
+            chosen.append(jnp.where(slot < counts[0, d], assign[d : d + 1, :], -1))
+            piece = packed[d, 2 * rows_own :, :].astype(F32)
+            tracks.append(
+                jnp.concatenate(
+                    [
+                        piece[:kinds, :capacity],
+                        piece[:kinds, capacity : 2 * capacity],
+                        piece[kinds:, :capacity],
+                        jnp.zeros((kinds, capacity), F32),
+                    ],
+                    axis=0,
+                )
+            )
+            at = slice(d * rows_own, (d + 1) * rows_own)
+            table[at, :128] = packed[d, :rows_own, :]
+            table[at, 128:] = packed[d, rows_own : 2 * rows_own, :]
+        chosen = jnp.concatenate(chosen, axis=1)
+        route[:, n * 128 : (n + 1) * 128] = (chosen == down).astype(F32).astype(BF16)
+        held.append(jnp.concatenate(tracks, axis=1).astype(BF16))
+    pieces = jnp.concatenate(held, axis=1)
+
     per_sub = dot(route[...], pieces, NT).astype(BF16)
     wide = 2 * steps * chan
-    from_row = lax.broadcasted_iota(jnp.int32, (6 * steps, wide), 0) % (2 * steps)
-    to_lane = lax.broadcasted_iota(jnp.int32, (6 * steps, wide), 1) // chan
+    from_row = lax.broadcasted_iota(jnp.int32, (4 * kinds, wide), 0) % kinds
+    to_lane = lax.broadcasted_iota(jnp.int32, (4 * kinds, wide), 1) // chan
     spread = (from_row == to_lane).astype(F32).astype(BF16)
     uv = dot(per_sub, spread)
     vis = steps * chan
@@ -187,9 +230,9 @@
     index = jnp.concatenate([index, jnp.zeros((6, number), F32)], axis=0).T
     index = index.astype(jnp.int32)
     across = lax.broadcasted_iota(jnp.int32, (number, rows_all), 1)
-    for which, coef in ((0, coef_first), (1, coef_second)):
+    for which in range(2):
         pick = (index[:, which : which + 1] == across).astype(F32).astype(BF16)
-        coef[...] = dot(pick, table[...]).astype(BF16)
+        coef[which * number : (which + 1) * number, :] = dot(pick, table[...]).astype(BF16)
 
     for m in range(8):
         cols = slice(m * 128, (m + 1) * 128)
@@ -199,26 +242,25 @@
         weights[m, terms:, :128] = -b_im
         weights[m, terms:, 128:] = b_re
 
-    block = 64
+    block = 32
     for m in range(8):
-        @pl.loop(0, number // block)
-        def _(n, m=m):
-            rows = pl.ds(pl.multiple_of(n * block, block), block)
-            first = dot(coef_first[rows, :], weights[m])
-            second = dot(coef_second[rows, :], weights[m])
+        beams = dot(coef[...], weights[m])
+        for n in range(0, number, block):
+            first = beams[n : n + block, :]
+            second = beams[number + n : number + n + block, :]
             f_re, f_im, s_re, s_im = first[:, :128], first[:, 128:], second[:, :128], second[:, 128:]
             g_re = f_re * s_re + f_im * s_im
             g_im = f_im * s_re - f_re * s_im
-            i_re = image[m, rows, :128].astype(F32)
-            i_im = image[m, rows, 128:].astype(F32)
-            to = pl.ds(n * (block * 8) + m, block, stride=8)
+            i_re = image[m, n : n + block, :128].astype(F32)
+            i_im = image[m, n : n + block, 128:].astype(F32)
+            to = pl.ds(n * 8 + m, block, stride=8)
             wre[to, :] = i_re * g_re - i_im * g_im
             wim[to, :] = i_re * g_im + i_im * g_re
 
     lane = lax.broadcasted_iota(jnp.int32, (8, 256), 1)
     inner = (lane // 32) % 4
     masks = [inner == j for j in range(4)]
-    unroll = 4
+    unroll = 16
 
     def one(g):
         at = pl.ds(pl.multiple_of(g * 8, 8), 8)
@@ -290,15 +332,19 @@
     chan = frequencies.shape[0]
     vis = steps * chan
     vmem = pl.BlockSpec(memory_space=pltpu.VMEM)
-    params = pltpu.CompilerParams(vmem_limit_bytes=VMEM_LIMIT)
-
     own_tracks = jnp.transpose(uv_tracks[0], (0, 2, 3, 1)).reshape(tiles, 2 * steps, capacity)
-    tracks = lax.all_to_all(own_tracks, "tile", split_axis=0, concat_axis=0, tiled=True)
-    tracks = jnp.transpose(tracks, (1, 0, 2)).reshape(2 * steps, slots)
-    table = lax.all_gather(beam_coefs, "tile", axis=0, tiled=True)
-    table = table.reshape(table.shape[0] * slot_count, terms2)
-
-    cells = jnp.transpose(subgrids.reshape(number, 2, 8, 128), (1, 2, 0, 3))
+    own_rows = beam_coefs.shape[0] * slot_count
+    packed = pl.pallas_call(
+        pack_kernel,
+        out_shape=jax.ShapeDtypeStruct((tiles, 2 * own_rows + 4 * steps, 128), BF16),
+        in_specs=[vmem, vmem],
+        out_specs=vmem,
+        name="pack",
+    )(beam_coefs.reshape(own_rows, terms2), own_tracks)
+    packed = lax.all_to_all(packed, "tile", split_axis=0, concat_axis=0, tiled=True)
+
+    cells = jnp.transpose(subgrids.reshape(number, 2, 8, 128), (0, 2, 1, 3))
+    cells = cells.reshape(number * 16, 128)
     high, rest = transform_matrices(edge)
     image = pl.pallas_call(
         transform_kernel,
@@ -306,28 +352,27 @@
         in_specs=[vmem] * 3,
         out_specs=vmem,
         scratch_shapes=[
-            pltpu.VMEM((8, number, 256), BF16),
-            pltpu.VMEM((8, number, 256), BF16),
+            pltpu.VMEM((number * 16, 128), F32),
+            pltpu.VMEM((8, number, 512), BF16),
         ],
-        compiler_params=params,
+        compiler_params=pltpu.CompilerParams(vmem_limit_bytes=20 * 1024 * 1024),
         name="transform",
     )(cells, jnp.asarray(high), jnp.asarray(rest))
 
     basis = jnp.transpose(
         beam_basis.reshape(2, terms2 // 2, 4, 8, edge), (0, 1, 3, 2, 4)
     ).reshape(2, terms2 // 2, pixels)
-    live = jnp.arange(capacity, dtype=jnp.int32)[None, :] < counts[0][:, None]
-    slot_row = jnp.where(live, assign[0], -1).reshape(1, slots)
+    smem = pl.BlockSpec(memory_space=pltpu.SMEM)
     payload = pl.pallas_call(
         functools.partial(predict_kernel, slot_count=slot_count),
         out_shape=jax.ShapeDtypeStruct((2 * slots, vis), BF16),
-        in_specs=[vmem] * 8,
+        in_specs=[smem] + [vmem] * 7,
         out_specs=vmem,
         scratch_shapes=[
+            pltpu.VMEM((tiles * own_rows, terms2), BF16),
             pltpu.VMEM((number, slots), BF16),
             pltpu.VMEM((8, 256, 256), BF16),
-            pltpu.VMEM((number, terms2), BF16),
-            pltpu.VMEM((number, terms2), BF16),
+            pltpu.VMEM((2 * number, terms2), BF16),
             pltpu.VMEM((number * 8, 128), F32),
             pltpu.VMEM((number * 8, 128), F32),
             pltpu.VMEM((number * 8, vis), F32),
@@ -338,14 +383,14 @@
             pltpu.VMEM((2, number, vis), F32),
             pltpu.VMEM((2 * slots, vis), F32),
         ],
-        compiler_params=params,
+        compiler_params=pltpu.CompilerParams(vmem_limit_bytes=VMEM_LIMIT),
         name="predict",
     )(
-        table,
-        slot_row,
+        counts,
+        packed,
+        assign[0],
         stations.T,
         time_slots.reshape(1, number),
-        tracks,
         frequencies.reshape(1, chan),
         basis,
         image,
@@ -353,8 +398,7 @@
     arrived = lax.all_to_all(
         payload.reshape(tiles, 2 * capacity, vis), "tile", split_axis=0, concat_axis=0, tiled=True
     )
-    residual = observed - arrived.reshape(observed.shape).astype(F32)
-    return residual
+    return observed - arrived.reshape(observed.shape).astype(F32)
 
 
 def solution(mesh):

time: 91.8 us -> 57.8 us (0.63)
  blocking collectives: 42.7 us -> 18.8 us
  Pallas kernels: 29.9 us -> 15.7 us
  waiting for transfers between devices: 0.01 us -> 9.53 us
  local copies, waits for them, and re-layouts: 8.61 us -> 4.62 us
  other arithmetic: 2.46 us -> 1.08 us
    all_gather x1 -> x0, blocking collectives: 24.6 us -> none  [per_device(): table = lax.all_gather(beam_coefs, 'tile', axis=0, tiled=True)]
    pallas_call x1, Pallas kernels: 24.1 us -> 11.9 us  [per_device(): pl.pallas_call(functools.partial(predict_kernel, slot_count=slot_count),...]
    all_to_all x1, waiting for transfers between devices: 0.01 us -> 9.53 us  [per_device(): lax.all_to_all(packed, 'tile', split_axis=0, concat_axis=0, tiled=True)]
    pallas_call x1, Pallas kernels: 5.77 us -> 2.04 us  [per_device(): pl.pallas_call(transform_kernel, out_shape=jax.ShapeDtypeStruct((8, numbe...]
    reshape x2 -> x0, local copies, waits for them, and re-layouts: 2 us -> none  [the longest x1 1.31 us: per_device(): cells = jnp.transpose(subgrids.reshape(number, 2, 8, 128), (1, 2, 0, 3))]
    pallas_call x0 -> x1, Pallas kernels: none -> 1.76 us  [per_device(): pl.pallas_call(pack_kernel, out_shape=jax.ShapeDtypeStruct((tiles, 2 * ow...]
    unnamed x14 -> x21, local copies, waits for them, and re-layouts: 4.86 us -> 4.36 us
  transfers between devices with their start and end apart: 1 -> 1, of which waited for: 0 -> 1; matrix products, arithmetic and copies ran while one was open for 6% -> 1% of each run, Pallas kernels for 6% -> 4%
where the time goes in v3:
time: 57.8 us; the launch traced here: 57.3 us
  blocking collectives  18.8 us (33%)
  Pallas kernels  15.7 us (27%)
  waiting for transfers between devices  9.53 us (16%)
  starting transfers between devices  7.52 us (13%)
  local copies, waits for them, and re-layouts  4.62 us (8%)
  other arithmetic  1.08 us (2%)
    all_to_all x1, blocking collectives, per_device(): lax.all_to_all(payload.reshape(tiles, 2 * capacity, vis), 'tile', split_a...  18.8 us
    pallas_call x1, Pallas kernels, per_device(): pl.pallas_call(functools.partial(predict_kernel, slot_count=slot_count),...  11.9 us
    all_to_all x1, waiting for transfers between devices, per_device(): lax.all_to_all(packed, 'tile', split_axis=0, concat_axis=0, tiled=True)  9.53 us
    all_to_all x1, starting transfers between devices, per_device(): lax.all_to_all(packed, 'tile', split_axis=0, concat_axis=0, tiled=True)  7.52 us
    unnamed x21, local copies, waits for them, and re-layouts  4.36 us
    pallas_call x1, Pallas kernels, per_device(): pl.pallas_call(transform_kernel, out_shape=jax.ShapeDtypeStruct((8, numbe...  2.04 us
    pallas_call x1, Pallas kernels, per_device(): pl.pallas_call(pack_kernel, out_shape=jax.ShapeDtypeStruct((tiles, 2 * ow...  1.76 us
  transfers between devices with their start and end apart: 1, of which 1 were waited for; matrix products, arithmetic and copies ran while one was open for 1% of the time, Pallas kernels for 4%

profile of v3, /device:TPU:0, one launch (start us, length us, event | category | flops | bytes accessed | tf_op | source)
XLA Modules:
  0.0 57.3 jit_solution(8102002371601746874)
XLA Ops:
  0.0 1.8 %pack.1 = bf16[16,144,128]{2,1,0:T(8,128)(2,1)} custom-call(bf16[64,256]{1,0:T(8,128)(2,1)} %bitcast.36, f32[16,8,64]{2,1,0:T(8,128)} %bitcast.35), custom_call_target="tpu_custom_call" | custom-call | tf_op jit(solution)/shard_map/pack/pallas_call | solution.py:337
  1.8 0.0 copy-start.9
  1.8 7.5 %all-to-all-start = ((bf16[16,144,128]{2,1,0:T(8,128)(2,1)}), bf16[16,144,128]{2,1,0:T(8,128)(2,1)S(1)}, u32[]{:S(2)}, u32[]{:S(2)}) async-start(bf16[16,144,128]{2,1,0:T(8,128)(2,1)} %pack.1), calls=%async_computation | async-start | bytes 1179648 | tf_op jit(solution)/shard_map/all_to_all | solution.py:344
  9.3 0.0 copy-done.9
  9.3 0.3 copy.15
  9.6 0.0 copy-start
  9.6 0.2 copy.18.basis
  9.9 0.9 %copy-done = bf16[256,2,1024]{2,1,0:T(2,128)(2,1)S(1)} copy-done((bf16[256,2,1024]{2,1,0:T(2,128)(2,1)S(1)}, bf16[256,2,1024]{2,1,0:T(2,128)(2,1)}, u32[]{:S(2)}) %copy-start) | copy-done | bytes 1048600
  10.8 0.0 copy-start.1
  10.8 1.2 %copy-done.1 = bf16[8,256,256]{2,1,0:T(8,128)(2,1)S(1)} copy-done((bf16[8,256,256]{2,1,0:T(8,128)(2,1)S(1)}, bf16[8,256,256]{2,1,0:T(8,128)(2,1)}, u32[]{:S(2)}) %copy-start.1) | copy-done | bytes 1048600
  12.0 0.0 copy-start.2
  12.0 1.2 %copy-done.2 = bf16[8,256,256]{2,1,0:T(8,128)(2,1)S(1)} copy-done((bf16[8,256,256]{2,1,0:T(8,128)(2,1)S(1)}, bf16[8,256,256]{2,1,0:T(8,128)(2,1)}, u32[]{:S(2)}) %copy-start.2) | copy-done | bytes 1048600
  13.3 0.0 copy-start.3
  13.3 0.0 copy-start.7
  13.3 2.0 %transform.1.image = bf16[8,256,256]{2,1,0:T(8,128)(2,1)S(1)} custom-call(bf16[4096,128]{1,0:T(8,128)(2,1)S(1)} %bitcast.26, bf16[8,256,256]{2,1,0:T(8,128)(2,1)S(1)} %copy-done.2, bf16[8,256,256]{2,1,0:T(8,128)(2,1)S(1)} %copy-done.1), custom_call_target="tpu_custom_call" | custom-call | tf_op jit(solution)/shard_map/transform/pallas_call | solution.py:349
  15.3 9.5 %all-to-all-done.packed = bf16[16,144,128]{2,1,0:T(8,128)(2,1)S(1)} async-done(((bf16[16,144,128]{2,1,0:T(8,128)(2,1)}), bf16[16,144,128]{2,1,0:T(8,128)(2,1)S(1)}, u32[]{:S(2)}, u32[]{:S(2)}) %all-to-all-start) | async-done | bytes 589856 | tf_op jit(solution)/shard_map/all_to_all | solution.py:344
  24.8 0.0 copy-start.4
  24.8 0.0 copy-start.5
  24.8 0.0 copy-start.6
  24.8 0.0 copy-done.3
  24.8 0.0 copy-done.7
  24.9 0.7 %copy-done.4 = s32[256,2]{0,1:T(2,128)S(1)} copy-done((s32[256,2]{0,1:T(2,128)S(1)}, s32[256,2]{0,1:T(2,128)}, u32[]{:S(2)}) %copy-start.4) | copy-done | bytes 2072
  25.5 0.0 copy-done.5
  25.5 0.0 copy-done.6
  25.5 11.9 %predict.1 = bf16[2048,128]{1,0:T(8,128)(2,1)S(1)} custom-call(s32[1,16]{1,0:T(1,128)S(1)} %copy-done.6, bf16[16,144,128]{2,1,0:T(8,128)(2,1)S(1)} %all-to-all-done.packed, s32[16,64]{1,0:T(8,128)S(1)} %bitcast.27, s32[2,256]{1,0:T(2,128)S(1)} %bitcast.28, s32[1,256]{1,0:T(1,128)S(1)} %bitcast.29, f32[1,32]{1,0:T(1,128)S(1)} %bitcast.30, ...), custom_call_target="tpu_custom_call" | custom-call | tf_op jit(solution)/shard_map/predict/pallas_call | solution.py:366
  37.4 0.0 copy-start.8
  37.4 18.8 %all_to_all.10 = bf16[16,128,128]{2,1,0:T(8,128)(2,1)S(1)} all-to-all(bf16[16,128,128]{2,1,0:T(8,128)(2,1)S(1)} %bitcast.25), channel_id=1, replica_groups=mesh['grp'=2,'tile'=16] {'tile'}, dimensions={0} | all-to-all | bytes 1048576 | tf_op jit(solution)/shard_map/all_to_all | solution.py:398
  56.3 0.0 copy-done.8
  56.3 1.1 %convert_subtract_fusion = f32[1,16,16,8,128]{4,3,2,1,0:T(8,128)} fusion(f32[1,16,16,8,128]{4,3,2,1,0:T(8,128)S(1)} %bitcast.34, bf16[1,16,16,8,128]{4,3,2,1,0:T(8,128)(2,1)S(1)} %bitcast.31), kind=kLoop, calls=%fused_computation | loop fusion | flops 524288 | bytes 2621440 | tf_op jit(solution)/shard_map/sub | solution.py:401
  (1 shorter events, 0.0 us)
Async XLA Ops:
  1.8 7.5 %copy-start.9 = (bf16[2,128,1024]{2,1,0:T(8,128)(2,1)S(1)}, bf16[2,128,1024]{2,1,0:T(8,128)(2,1)}, u32[]{:S(2)}) copy-start(bf16[2,128,1024]{2,1,0:T(8,128)(2,1)} %param.18) | copy-start | bytes 1572868
  1.8 23.1 %all-to-all-start = ((bf16[16,144,128]{2,1,0:T(8,128)(2,1)}), bf16[16,144,128]{2,1,0:T(8,128)(2,1)S(1)}, u32[]{:S(2)}, u32[]{:S(2)}) async-start(bf16[16,144,128]{2,1,0:T(8,128)(2,1)} %pack.1), calls=%async_computation | async-start | bytes 1179648 | tf_op jit(solution)/shard_map/all_to_all | solution.py:344
  9.6 1.2 %copy-start = (bf16[256,2,1024]{2,1,0:T(2,128)(2,1)S(1)}, bf16[256,2,1024]{2,1,0:T(2,128)(2,1)}, u32[]{:S(2)}) copy-start(bf16[256,2,1024]{2,1,0:T(2,128)(2,1)} %param.12) | copy-start | bytes 3145732
  10.8 1.2 %copy-start.1 = (bf16[8,256,256]{2,1,0:T(8,128)(2,1)S(1)}, bf16[8,256,256]{2,1,0:T(8,128)(2,1)}, u32[]{:S(2)}) copy-start(bf16[8,256,256]{2,1,0:T(8,128)(2,1)} %constant.5.clone.rest) | copy-start | bytes 3145732
  12.0 1.2 %copy-start.2 = (bf16[8,256,256]{2,1,0:T(8,128)(2,1)S(1)}, bf16[8,256,256]{2,1,0:T(8,128)(2,1)}, u32[]{:S(2)}) copy-start(bf16[8,256,256]{2,1,0:T(8,128)(2,1)} %constant.4.clone.high) | copy-start | bytes 3145732
  13.3 11.6 %copy-start.3 = (s32[1,16,64]{2,1,0:T(8,128)S(1)}, s32[1,16,64]{2,1,0:T(8,128)}, u32[]{:S(2)}) copy-start(s32[1,16,64]{2,1,0:T(8,128)} %param.15) | copy-start | bytes 12292
  13.3 11.6 %copy-start.7 = (f32[32]{0:T(128)S(1)}, f32[32]{0:T(128)}, u32[]{:S(2)}) copy-start(f32[32]{0:T(128)} %param.19) | copy-start | bytes 388
  24.8 0.7 %copy-start.4 = (s32[256,2]{0,1:T(2,128)S(1)}, s32[256,2]{0,1:T(2,128)}, u32[]{:S(2)}) copy-start(s32[256,2]{0,1:T(2,128)} %param.13) | copy-start | bytes 6148
  24.8 0.7 %copy-start.5 = (s32[256]{0:T(256)S(1)}, s32[256]{0:T(256)}, u32[]{:S(2)}) copy-start(s32[256]{0:T(256)} %param.14) | copy-start | bytes 3076
  24.8 0.7 %copy-start.6 = (s32[1,16]{1,0:T(1,128)S(1)}, s32[1,16]{1,0:T(1,128)}, u32[]{:S(2)}) copy-start(s32[1,16]{1,0:T(1,128)} %counts.1) | copy-start | bytes 196
  37.4 18.8 %copy-start.8 = (f32[1,16,64,2,128]{4,3,2,1,0:T(2,128)S(1)}, f32[1,16,64,2,128]{4,3,2,1,0:T(2,128)}, u32[]{:S(2)}) copy-start(f32[1,16,64,2,128]{4,3,2,1,0:T(2,128)} %param.21) | copy-start | bytes 3145732

commit v4 on v3

--- a/solution.py
+++ b/solution.py
@@ -15,7 +15,6 @@
 BF16 = jnp.bfloat16
 VMEM_LIMIT = 36 * 1024 * 1024
 NT = (((1,), (1,)), ((), ()))
-TN = (((0,), (0,)), ((), ()))
 
 
 def dot(a, b, dims=(((1,), (0,)), ((), ()))):
@@ -60,8 +59,11 @@
     return out_re, out_im
 
 
-def transform_kernel(cells, high, rest, image, wide, sums):
+def prepare_kernel(
+    counts, cells, high, rest, assign, stations, time_slots, basis, image, route, back, pick, weights, wide, sums, *, slot_count
+):
     number = image.shape[1]
+    tiles, capacity = assign.shape
     step = 16
 
     @pl.loop(0, number // step, unroll=2)
@@ -84,6 +86,35 @@
         right = jnp.concatenate([high[m], high[m], rest[m]], axis=0)
         image[m] = dot(left, right).astype(BF16)
 
+    per = 128 // capacity
+    down = lax.broadcasted_iota(jnp.int32, (number, 128), 0)
+    slot = lax.broadcasted_iota(jnp.int32, (1, capacity), 1)
+    for n in range(tiles // per):
+        chosen = [
+            jnp.where(slot < counts[0, d], assign[d : d + 1, :], -1)
+            for d in range(n * per, (n + 1) * per)
+        ]
+        hot = (jnp.concatenate(chosen, axis=1) == down).astype(F32)
+        route[:, n * 128 : (n + 1) * 128] = hot.astype(BF16)
+        back[n * 128 : (n + 1) * 128, :] = hot.T.astype(BF16)
+
+    index = (stations[...] * slot_count + time_slots[...]).astype(F32)
+    index = jnp.concatenate([index, jnp.zeros((6, number), F32)], axis=0).T
+    index = index.astype(jnp.int32)
+    across = lax.broadcasted_iota(jnp.int32, (number, pick.shape[1]), 1)
+    for which in range(2):
+        hot = (index[:, which : which + 1] == across).astype(F32)
+        pick[which * number : (which + 1) * number, :] = hot.astype(BF16)
+
+    terms = basis.shape[1]
+    for m in range(8):
+        cols = slice(m * 128, (m + 1) * 128)
+        b_re, b_im = basis[0, :, cols], basis[1, :, cols]
+        weights[m, :terms, :128] = b_re
+        weights[m, :terms, 128:] = b_im
+        weights[m, terms:, :128] = -b_im
+        weights[m, terms:, 128:] = b_re
+
 
 def unit_powers(turns):
     turns = turns - jnp.round(turns)
@@ -104,42 +135,47 @@
     return ar * br - ai * bi, ar * bi + ai * br
 
 
-def pack_kernel(coefs, tracks, out):
+def pack_kernel(me, coefs, tracks, *out):
     capacity = tracks.shape[2]
     rows = coefs.shape[0]
-    for d in range(tracks.shape[0]):
-        tr = tracks[d]
-        t_hi = tr.astype(BF16).astype(F32)
-        t_mid = (tr - t_hi).astype(BF16).astype(F32)
-        t_lo = tr - t_hi - t_mid
-        pieces = jnp.concatenate(
-            [
-                jnp.concatenate([t_hi, t_mid], axis=1),
-                jnp.concatenate([t_lo, jnp.zeros_like(tr)], axis=1),
-            ],
-            axis=0,
-        )
+    for r in range(len(out)):
+        plane = (me[0] // 4) ^ r
+        kept = []
+        for k in (0, 2):
+            tr = jnp.concatenate([tracks[plane * 4 + k], tracks[plane * 4 + k + 1]], axis=1)
+            t_hi = tr.astype(BF16).astype(F32)
+            t_mid = (tr - t_hi).astype(BF16).astype(F32)
+            kept += [t_hi, t_mid, tr - t_hi - t_mid]
+        pieces = jnp.concatenate(kept, axis=0)
         if 2 * capacity < 128:
             blank = jnp.zeros((pieces.shape[0], 128 - 2 * capacity), F32)
             pieces = jnp.concatenate([pieces, blank], axis=1)
-        out[d, :rows, :] = coefs[:, :128]
-        out[d, rows : 2 * rows, :] = coefs[:, 128:]
-        out[d, 2 * rows :, :] = pieces.astype(BF16)
+        out[r][:rows, :] = coefs[:, :128]
+        out[r][rows : 2 * rows, :] = coefs[:, 128:]
+        out[r][2 * rows :, :] = pieces.astype(BF16)
+
+
+def stack_kernel(*refs):
+    blocks, out = refs[:-2], refs[-1]
+    for r, block in enumerate(blocks):
+        out[r] = block[...]
 
 
 def predict_kernel(
-    counts,
-    packed,
-    assign,
-    stations,
-    time_slots,
+    me,
+    near,
+    over_y,
+    over_core,
+    over_both,
+    route,
+    back,
+    pick,
+    weights,
     freq,
-    basis,
     image,
     payload,
     table,
-    route,
-    weights,
+    lanes,
     coef,
     wre,
     wim,
@@ -150,46 +186,35 @@
     him,
     zv,
     interleaved,
-    *,
-    slot_count,
 ):
     number = image.shape[1]
-    tiles, capacity = assign.shape
+    tiles, kinds3, capacity = lanes.shape
     slots = tiles * capacity
-    rows_all = table.shape[0]
-    rows_own = rows_all // tiles
+    rows_own = table.shape[0] // tiles
     chan = freq.shape[1]
-    kinds = (packed.shape[1] - 2 * rows_own) // 2
+    kinds = kinds3 // 3
     steps = kinds // 2
-    terms = basis.shape[1]
-
+    mine = me[0]
+
+    for arrived, flip in ((near, 0), (over_y, 2), (over_core, 1), (over_both, 3)):
+        for r in range(arrived.shape[0]):
+            owner = mine ^ (4 * r + flip)
+            at = pl.ds(pl.multiple_of(owner * rows_own, rows_own), rows_own)
+            table[at, :128] = arrived[r, :rows_own, :]
+            table[at, 128:] = arrived[r, rows_own : 2 * rows_own, :]
+            piece = arrived[r, 2 * rows_own :, :].astype(F32)
+            piece = jnp.where(mine & 2 == 0, piece[:kinds3, :], piece[kinds3:, :])
+            moved = jnp.where(mine & 1 == 0, piece, pltpu.roll(piece, 128 - capacity, 1))
+            lanes[owner] = moved[:, :capacity]
     per = 128 // capacity
-    down = lax.broadcasted_iota(jnp.int32, (number, 128), 0)
-    slot = lax.broadcasted_iota(jnp.int32, (1, capacity), 1)
-    held = []
-    for n in range(tiles // per):
-        chosen, tracks = [], []
-        for d in range(n * per, (n + 1) * per):
-            chosen.append(jnp.where(slot < counts[0, d], assign[d : d + 1, :], -1))
-            piece = packed[d, 2 * rows_own :, :].astype(F32)
-            tracks.append(
-                jnp.concatenate(
-                    [
-                        piece[:kinds, :capacity],
-                        piece[:kinds, capacity : 2 * capacity],
-                        piece[kinds:, :capacity],
-                        jnp.zeros((kinds, capacity), F32),
-                    ],
-                    axis=0,
-                )
-            )
-            at = slice(d * rows_own, (d + 1) * rows_own)
-            table[at, :128] = packed[d, :rows_own, :]
-            table[at, 128:] = packed[d, rows_own : 2 * rows_own, :]
-        chosen = jnp.concatenate(chosen, axis=1)
-        route[:, n * 128 : (n + 1) * 128] = (chosen == down).astype(F32).astype(BF16)
-        held.append(jnp.concatenate(tracks, axis=1).astype(BF16))
-    pieces = jnp.concatenate(held, axis=1)
+    pieces = jnp.concatenate(
+        [
+            jnp.concatenate([lanes[d] for d in range(n * per, (n + 1) * per)], axis=1)
+            for n in range(tiles // per)
+        ],
+        axis=1,
+    )
+    pieces = jnp.concatenate([pieces, jnp.zeros((kinds, slots), F32)], axis=0).astype(BF16)
 
     per_sub = dot(route[...], pieces, NT).astype(BF16)
     wide = 2 * steps * chan
@@ -226,21 +251,7 @@
     zrow[4] = cr
     zrow[5] = ci
 
-    index = (stations[...] * slot_count + time_slots[...]).astype(F32)
-    index = jnp.concatenate([index, jnp.zeros((6, number), F32)], axis=0).T
-    index = index.astype(jnp.int32)
-    across = lax.broadcasted_iota(jnp.int32, (number, rows_all), 1)
-    for which in range(2):
-        pick = (index[:, which : which + 1] == across).astype(F32).astype(BF16)
-        coef[which * number : (which + 1) * number, :] = dot(pick, table[...]).astype(BF16)
-
-    for m in range(8):
-        cols = slice(m * 128, (m + 1) * 128)
-        b_re, b_im = basis[0, :, cols], basis[1, :, cols]
-        weights[m, :terms, :128] = b_re
-        weights[m, :terms, 128:] = b_im
-        weights[m, terms:, :128] = -b_im
-        weights[m, terms:, 128:] = b_re
+    coef[...] = dot(pick[...], table[...]).astype(BF16)
 
     block = 32
     for m in range(8):
@@ -302,10 +313,14 @@
     cr, ci = cmul(zrow[4], zrow[5], zrow[4], zrow[5])
     m_re, m_im = a_re * cr + a_im * ci, a_im * cr - a_re * ci
     models = jnp.concatenate([m_re, m_im], axis=1).astype(BF16)
-    sent = dot(route[...], models, TN)
+    sent = dot(back[...], models)
     interleaved[pl.ds(0, slots, stride=2), :] = sent[:, :128]
     interleaved[pl.ds(1, slots, stride=2), :] = sent[:, 128:]
     payload[...] = interleaved[...].astype(BF16)
+
+
+def exchange(value, step, tiles):
+    return lax.ppermute(value, "tile", [(i, i ^ step) for i in range(tiles)])
 
 
 def per_device(
@@ -334,44 +349,73 @@
     vmem = pl.BlockSpec(memory_space=pltpu.VMEM)
     own_tracks = jnp.transpose(uv_tracks[0], (0, 2, 3, 1)).reshape(tiles, 2 * steps, capacity)
     own_rows = beam_coefs.shape[0] * slot_count
+    smem = pl.BlockSpec(memory_space=pltpu.SMEM)
+    anywhere = pl.BlockSpec(memory_space=pl.ANY)
+    outer = tiles // 4
+    me = lax.axis_index("tile").astype(jnp.int32).reshape(1)
+    block = jax.ShapeDtypeStruct((2 * own_rows + 12 * steps, 128), BF16)
     packed = pl.pallas_call(
         pack_kernel,
-        out_shape=jax.ShapeDtypeStruct((tiles, 2 * own_rows + 4 * steps, 128), BF16),
-        in_specs=[vmem, vmem],
-        out_specs=vmem,
+        out_shape=[block] * outer,
+        in_specs=[smem, vmem, vmem],
+        out_specs=[vmem] * outer,
         name="pack",
-    )(beam_coefs.reshape(own_rows, terms2), own_tracks)
-    packed = lax.all_to_all(packed, "tile", split_axis=0, concat_axis=0, tiled=True)
+    )(me, beam_coefs.reshape(own_rows, terms2), own_tracks)
+    along = [packed[0]] + [exchange(packed[r], 4 * r, tiles) for r in range(1, outer)]
 
     cells = jnp.transpose(subgrids.reshape(number, 2, 8, 128), (0, 2, 1, 3))
     cells = cells.reshape(number * 16, 128)
+    basis = jnp.transpose(
+        beam_basis.reshape(2, terms2 // 2, 4, 8, edge), (0, 1, 3, 2, 4)
+    ).reshape(2, terms2 // 2, pixels)
     high, rest = transform_matrices(edge)
-    image = pl.pallas_call(
-        transform_kernel,
-        out_shape=jax.ShapeDtypeStruct((8, number, 256), BF16),
-        in_specs=[vmem] * 3,
-        out_specs=vmem,
+    image, route, back, pick, weights = pl.pallas_call(
+        functools.partial(prepare_kernel, slot_count=slot_count),
+        out_shape=[
+            jax.ShapeDtypeStruct((8, number, 256), BF16),
+            jax.ShapeDtypeStruct((number, slots), BF16),
+            jax.ShapeDtypeStruct((slots, number), BF16),
+            jax.ShapeDtypeStruct((2 * number, tiles * own_rows), BF16),
+            jax.ShapeDtypeStruct((8, terms2, 256), BF16),
+        ],
+        in_specs=[smem] + [vmem] * 7,
+        out_specs=[vmem] * 5,
         scratch_shapes=[
             pltpu.VMEM((number * 16, 128), F32),
             pltpu.VMEM((8, number, 512), BF16),
         ],
-        compiler_params=pltpu.CompilerParams(vmem_limit_bytes=20 * 1024 * 1024),
-        name="transform",
-    )(cells, jnp.asarray(high), jnp.asarray(rest))
-
-    basis = jnp.transpose(
-        beam_basis.reshape(2, terms2 // 2, 4, 8, edge), (0, 1, 3, 2, 4)
-    ).reshape(2, terms2 // 2, pixels)
-    smem = pl.BlockSpec(memory_space=pltpu.SMEM)
+        compiler_params=pltpu.CompilerParams(vmem_limit_bytes=24 * 1024 * 1024),
+        name="prepare",
+    )(
+        counts,
+        cells,
+        jnp.asarray(high),
+        jnp.asarray(rest),
+        assign[0],
+        stations.T,
+        time_slots.reshape(1, number),
+        basis,
+    )
+
+    near = pl.pallas_call(
+        stack_kernel,
+        out_shape=jax.ShapeDtypeStruct((outer,) + block.shape, BF16),
+        in_specs=[vmem] * outer + [anywhere],
+        out_specs=vmem,
+        name="stack",
+    )(*along, image)
+    over_y = exchange(near, 2, tiles)
+    over_core = exchange(near, 1, tiles)
+    over_both = exchange(over_y, 1, tiles)
+
     payload = pl.pallas_call(
-        functools.partial(predict_kernel, slot_count=slot_count),
+        predict_kernel,
         out_shape=jax.ShapeDtypeStruct((2 * slots, vis), BF16),
-        in_specs=[smem] + [vmem] * 7,
+        in_specs=[smem] + [vmem] * 10,
         out_specs=vmem,
         scratch_shapes=[
             pltpu.VMEM((tiles * own_rows, terms2), BF16),
-            pltpu.VMEM((number, slots), BF16),
-            pltpu.VMEM((8, 256, 256), BF16),
+            pltpu.VMEM((tiles, 6 * steps, capacity), F32),
             pltpu.VMEM((2 * number, terms2), BF16),
             pltpu.VMEM((number * 8, 128), F32),
             pltpu.VMEM((number * 8, 128), F32),
@@ -386,13 +430,16 @@
         compiler_params=pltpu.CompilerParams(vmem_limit_bytes=VMEM_LIMIT),
         name="predict",
     )(
-        counts,
-        packed,
-        assign[0],
-        stations.T,
-        time_slots.reshape(1, number),
+        me,
+        near,
+        over_y,
+        over_core,
+        over_both,
+        route,
+        back,
+        pick,
+        weights,
         frequencies.reshape(1, chan),
-        basis,
         image,
     )
     arrived = lax.all_to_all(

time: 57.8 us -> 64.3 us (1.11)
  local copies, waits for them, and re-layouts: 4.62 us -> 12.2 us
  waiting for transfers between devices: 9.53 us -> 5.62 us
  blocking collectives: 18.8 us -> 20.3 us
  Pallas kernels: 15.7 us -> 17.1 us
    all_to_all x1 -> x0, waiting for transfers between devices: 9.53 us -> none  [per_device(): lax.all_to_all(packed, 'tile', split_axis=0, concat_axis=0, tiled=True)]
    unnamed x21 -> x39, local copies, waits for them, and re-layouts: 4.36 us -> 11.9 us
    all_to_all x1 -> x0, starting transfers between devices: 7.52 us -> none  [per_device(): lax.all_to_all(packed, 'tile', split_axis=0, concat_axis=0, tiled=True)]
    ppermute x0 -> x6, starting transfers between devices: none -> 7.36 us  [exchange(): return lax.ppermute(value, 'tile', [(i, i ^ step) for i in range(tiles)])]
    ppermute x0 -> x6, waiting for transfers between devices: none -> 5.62 us  [exchange(): return lax.ppermute(value, 'tile', [(i, i ^ step) for i in range(tiles)])]
    all_to_all x1, blocking collectives: 18.8 us -> 20.3 us  [per_device(): lax.all_to_all(payload.reshape(tiles, 2 * capacity, vis), 'tile', split_a...]
    pallas_call x3 -> x4, Pallas kernels: 15.7 us -> 17.1 us  [the longest x1 11.1 us: per_device(): pl.pallas_call(predict_kernel, out_shape=jax.ShapeDtypeStruct((2 * slots,...]
  transfers between devices with their start and end apart: 1 -> 6, of which waited for: 1 -> 2; matrix products, arithmetic and copies ran while one was open for 1% -> 2% of each run, Pallas kernels for 4% -> 4%
where the time goes in v4:
time: 64.3 us; the launch traced here: 63.8 us
  blocking collectives  20.3 us (32%)
  Pallas kernels  17.1 us (27%)
  local copies, waits for them, and re-layouts  12.2 us (19%)
  starting transfers between devices  7.36 us (11%)
  waiting for transfers between devices  5.62 us (9%)
  other arithmetic  1.08 us (2%)
    all_to_all x1, blocking collectives, per_device(): lax.all_to_all(payload.reshape(tiles, 2 * capacity, vis), 'tile', split_a...  20.3 us
    unnamed x39, local copies, waits for them, and re-layouts  11.9 us
    pallas_call x1, Pallas kernels, per_device(): pl.pallas_call(predict_kernel, out_shape=jax.ShapeDtypeStruct((2 * slots,...  11.1 us
    ppermute x6, starting transfers between devices, exchange(): return lax.ppermute(value, 'tile', [(i, i ^ step) for i in range(tiles)])  7.36 us
    ppermute x6, waiting for transfers between devices, exchange(): return lax.ppermute(value, 'tile', [(i, i ^ step) for i in range(tiles)])  5.62 us
    pallas_call x1, Pallas kernels, per_device(): pl.pallas_call(functools.partial(prepare_kernel, slot_count=slot_count),...  2.8 us
    pallas_call x1, Pallas kernels, per_device(): pl.pallas_call(pack_kernel, out_shape=[block] * outer, in_specs=[smem, vm...  1.61 us
    pallas_call x1, Pallas kernels, per_device(): pl.pallas_call(stack_kernel, out_shape=jax.ShapeDtypeStruct((outer,) + bl...  1.53 us
  transfers between devices with their start and end apart: 6, of which 2 were waited for; matrix products, arithmetic and copies ran while one was open for 2% of the time, Pallas kernels for 4%

profile of v4, /device:TPU:0, one launch (start us, length us, event | category | flops | bytes accessed | tf_op | source)
XLA Modules:
  0.0 63.8 jit_solution(5567099685323542701)
XLA Ops:
  0.0 1.6 %pack.1 = (bf16[176,128]{1,0:T(8,128)(2,1)}, bf16[176,128]{1,0:T(8,128)(2,1)}, bf16[176,128]{1,0:T(8,128)(2,1)}, bf16[176,128]{1,0:T(8,128)(2,1)}) custom-call(s32[1]{0:T(128)} %bitcast.me, bf16[64,256]{1,0:T(8,128)(2,1)} %bitcast.37, f32[16,8,64]{2,1,0:T(8,128)} %bitcast.36), custom_call_target="tpu_custom_call" | custom-call | tf_op jit(solution)/shard_map/pack/pallas_call | solution.py:357
  1.6 3.0 %collective-permute-start = (bf16[176,128]{1,0:T(8,128)(2,1)}, bf16[176,128]{1,0:T(8,128)(2,1)S(1)}, u32[]{:S(2)}, u32[]{:S(2)}) collective-permute-start(bf16[176,128]{1,0:T(8,128)(2,1)} %get-tuple-element.15), channel_id=1, source_target_pairs={{0,4},{1,5},{2,6},{3,7},{4,0},{5,1},{6,2},{7,3},{8,12},{9,13},{10,... | collective-permute-start | bytes 135176 | tf_op jit(solution)/shard_map/ppermute | solution.py:323
  4.6 2.6 %collective-permute-start.1 = (bf16[176,128]{1,0:T(8,128)(2,1)}, bf16[176,128]{1,0:T(8,128)(2,1)S(1)}, u32[]{:S(2)}, u32[]{:S(2)}) collective-permute-start(bf16[176,128]{1,0:T(8,128)(2,1)} %get-tuple-element.16), channel_id=1, source_target_pairs={{0,8},{1,9},{2,10},{3,11},{4,12},{5,13},{6,14},{7,15},{8,0},{9,1},... | collective-permute-start | bytes 135176 | tf_op jit(solution)/shard_map/ppermute | solution.py:323
  7.2 0.0 collective-permute-start.2
  7.2 1.3 %copy.16 = bf16[2,128,1024]{1,2,0:T(8,128)(2,1)S(1)} copy(bf16[2,128,1024]{2,1,0:T(8,128)(2,1)} %param.18) | data formatting | bytes 1048576 | tf_op args[6]
  8.5 0.0 copy-start.2
  8.6 0.0 copy-start.10
  8.6 0.2 copy.18.basis
  8.8 0.0 copy-start.11
  8.9 0.0 copy-start.12
  8.9 0.0 copy-start.13
  8.9 0.9 %copy-done.2 = bf16[256,2,1024]{2,1,0:T(2,128)(2,1)S(1)} copy-done((bf16[256,2,1024]{2,1,0:T(2,128)(2,1)S(1)}, bf16[256,2,1024]{2,1,0:T(2,128)(2,1)}, u32[]{:S(2)}) %copy-start.2) | copy-done | bytes 1048600
  9.8 0.0 copy-done.10
  9.8 0.0 copy-done.11
  9.8 0.0 copy-done.12
  9.8 0.0 copy-done.13
  9.8 0.0 copy-start.5
  9.8 1.2 %copy-done.5 = bf16[8,256,256]{2,1,0:T(8,128)(2,1)S(1)} copy-done((bf16[8,256,256]{2,1,0:T(8,128)(2,1)S(1)}, bf16[8,256,256]{2,1,0:T(8,128)(2,1)}, u32[]{:S(2)}) %copy-start.5) | copy-done | bytes 1048600
  11.0 0.0 copy-start.6
  11.0 1.2 %copy-done.6 = bf16[8,256,256]{2,1,0:T(8,128)(2,1)S(1)} copy-done((bf16[8,256,256]{2,1,0:T(8,128)(2,1)S(1)}, bf16[8,256,256]{2,1,0:T(8,128)(2,1)}, u32[]{:S(2)}) %copy-start.6) | copy-done | bytes 1048600
  12.2 2.8 %prepare.1 = (bf16[8,256,256]{2,1,0:T(8,128)(2,1)S(1)}, bf16[256,1024]{1,0:T(8,128)(2,1)S(1)}, bf16[1024,256]{1,0:T(8,128)(2,1)S(1)}, bf16[512,1024]{1,0:T(8,128)(2,1)S(1)}, bf16[8,256,256]{2,1,0:T(8,128)(2,1)S(1)}) custom-call(s32[1,16]{1,0:T(1,128)S(1)} %copy-done.13, bf16[4096,128]{1,0:T(8,128)(2,1)S(1)} %bitcast.27, bf16[8,256,256]{2,1,0:T(8,128)(2,1)S(1)} %copy-done.6, ...), custom_call_target="tpu_custom_call" | custom-call | tf_op jit(solution)/shard_map/prepare/pallas_call | solution.py:372
  15.1 0.0 copy-start
  15.1 1.0 %copy-done = bf16[8,256,256]{2,1,0:T(8,128)(2,1)} copy-done((bf16[8,256,256]{2,1,0:T(8,128)(2,1)}, bf16[8,256,256]{2,1,0:T(8,128)(2,1)S(1)}, u32[]{:S(2)}) %copy-start) | copy-done | bytes 1048600
  16.0 0.0 copy-start.3
  16.0 1.0 %copy-done.3 = bf16[8,256,256]{2,1,0:T(8,128)(2,1)} copy-done((bf16[8,256,256]{2,1,0:T(8,128)(2,1)}, bf16[8,256,256]{2,1,0:T(8,128)(2,1)S(1)}, u32[]{:S(2)}) %copy-start.3) | copy-done | bytes 1048600
  17.0 0.0 copy-start.8
  17.0 0.8 %copy-done.8 = bf16[1024,256]{1,0:T(8,128)(2,1)} copy-done((bf16[1024,256]{1,0:T(8,128)(2,1)}, bf16[1024,256]{1,0:T(8,128)(2,1)S(1)}, u32[]{:S(2)}) %copy-start.8) | copy-done | bytes 524312
  17.9 0.0 collective-permute-done.refs_1_
  17.9 0.0 copy-start.16
  17.9 0.0 copy-start.1
  17.9 0.0 collective-permute-done.1.refs_2_
  17.9 0.0 copy-start.17
  17.9 0.0 collective-permute-done.2.refs_3_
  17.9 0.0 copy-start.18
  17.9 0.6 copy-done.16
  18.5 0.0 copy-done.17
  18.5 0.0 copy-done.18
  18.5 1.5 %stack.1.near = bf16[4,176,128]{2,1,0:T(8,128)(2,1)} custom-call(bf16[176,128]{1,0:T(8,128)(2,1)} %get-tuple-element.14.refs_0_, bf16[176,128]{1,0:T(8,128)(2,1)} %copy-done.16, bf16[176,128]{1,0:T(8,128)(2,1)} %copy-done.17, bf16[176,128]{1,0:T(8,128)(2,1)} %copy-done.18, bf16[8,256,256]{2,1,0:T(8,128)(2,1)} %copy-done), custom_call_target="tpu_custom_call" | custom-call | tf_op jit(solution)/shard_map/stack/pallas_call | solution.py:400
  20.1 1.7 %collective-permute-start.3 = (bf16[4,176,128]{2,1,0:T(8,128)(2,1)}, bf16[4,176,128]{2,1,0:T(8,128)(2,1)S(1)}, u32[]{:S(2)}, u32[]{:S(2)}) collective-permute-start(bf16[4,176,128]{2,1,0:T(8,128)(2,1)} %stack.1.near), channel_id=1, source_target_pairs={{0,2},{1,3},{2,0},{3,1},{4,6},{5,7},{6,4},{7,5},{8,10},{9,11},{10,... | collective-permute-start | bytes 540680 | tf_op jit(solution)/shard_map/ppermute | solution.py:323
  21.8 0.0 collective-permute-start.4
  21.8 4.2 %collective-permute-done.3.over_y = bf16[4,176,128]{2,1,0:T(8,128)(2,1)S(1)} collective-permute-done((bf16[4,176,128]{2,1,0:T(8,128)(2,1)}, bf16[4,176,128]{2,1,0:T(8,128)(2,1)S(1)}, u32[]{:S(2)}, u32[]{:S(2)}) %collective-permute-start.3) | collective-permute-done | bytes 180256 | tf_op jit(solution)/shard_map/ppermute | solution.py:323
  26.0 0.0 collective-permute-start.5
  26.0 0.0 collective-permute-done.4.over_core
  26.0 1.4 %collective-permute-done.5.over_both = bf16[4,176,128]{2,1,0:T(8,128)(2,1)S(1)} collective-permute-done((bf16[4,176,128]{2,1,0:T(8,128)(2,1)S(1)}, bf16[4,176,128]{2,1,0:T(8,128)(2,1)S(1)}, u32[]{:S(2)}, u32[]{:S(2)}) %collective-permute-start.5) | collective-permute-done | bytes 180256 | tf_op jit(solution)/shard_map/ppermute | solution.py:323
  27.4 0.0 copy-start.14
  27.4 0.0 copy-done.1
  27.4 0.7 %copy-done.14 = f32[32]{0:T(128)S(1)} copy-done((f32[32]{0:T(128)S(1)}, f32[32]{0:T(128)}, u32[]{:S(2)}) %copy-start.14) | copy-done | bytes 152
  28.1 0.0 copy-start.4
  28.1 1.2 %copy-done.4 = bf16[8,256,256]{2,1,0:T(8,128)(2,1)S(1)} copy-done((bf16[8,256,256]{2,1,0:T(8,128)(2,1)S(1)}, bf16[8,256,256]{2,1,0:T(8,128)(2,1)}, u32[]{:S(2)}) %copy-start.4) | copy-done | bytes 1048600
  29.3 0.0 copy-start.7
  29.3 0.9 %copy-done.7 = bf16[4,176,128]{2,1,0:T(8,128)(2,1)S(1)} copy-done((bf16[4,176,128]{2,1,0:T(8,128)(2,1)S(1)}, bf16[4,176,128]{2,1,0:T(8,128)(2,1)}, u32[]{:S(2)}) %copy-start.7) | copy-done | bytes 180248
  30.2 0.0 copy-start.9
  30.2 1.0 %copy-done.9 = bf16[1024,256]{1,0:T(8,128)(2,1)S(1)} copy-done((bf16[1024,256]{1,0:T(8,128)(2,1)S(1)}, bf16[1024,256]{1,0:T(8,128)(2,1)}, u32[]{:S(2)}) %copy-start.9) | copy-done | bytes 524312
  31.3 11.1 %predict.1 = bf16[2048,128]{1,0:T(8,128)(2,1)S(1)} custom-call(s32[1]{0:T(128)} %bitcast.me, bf16[4,176,128]{2,1,0:T(8,128)(2,1)S(1)} %copy-done.7, bf16[4,176,128]{2,1,0:T(8,128)(2,1)S(1)} %collective-permute-done.3.over_y, bf16[4,176,128]{2,1,0:T(8,128)(2,1)S(1)} %collective-permute-done.4.over_core, ...), custom_call_target="tpu_custom_call" | custom-call | tf_op jit(solution)/shard_map/predict/pallas_call | solution.py:411
  42.4 0.0 copy-start.15
  42.4 20.3 %all_to_all.5 = bf16[16,128,128]{2,1,0:T(8,128)(2,1)S(1)} all-to-all(bf16[16,128,128]{2,1,0:T(8,128)(2,1)S(1)} %bitcast.26), channel_id=1, replica_groups=mesh['grp'=2,'tile'=16] {'tile'}, dimensions={0} | all-to-all | bytes 1048576 | tf_op jit(solution)/shard_map/all_to_all | solution.py:445
  62.7 0.0 copy-done.15
  62.7 1.1 %convert_subtract_fusion = f32[1,16,16,8,128]{4,3,2,1,0:T(8,128)} fusion(f32[1,16,16,8,128]{4,3,2,1,0:T(8,128)S(1)} %bitcast.35, bf16[1,16,16,8,128]{4,3,2,1,0:T(8,128)(2,1)S(1)} %bitcast.32), kind=kLoop, calls=%fused_computation | loop fusion | flops 524288 | bytes 2621440 | tf_op jit(solution)/shard_map/sub | solution.py:448
  (1 shorter events, 0.0 us)
Async XLA Ops:
  1.6 16.3 %collective-permute-start = (bf16[176,128]{1,0:T(8,128)(2,1)}, bf16[176,128]{1,0:T(8,128)(2,1)S(1)}, u32[]{:S(2)}, u32[]{:S(2)}) collective-permute-start(bf16[176,128]{1,0:T(8,128)(2,1)} %get-tuple-element.15), channel_id=1, source_target_pairs={{0,4},{1,5},{2,6},{3,7},{4,0},{5,1},{6,2},{7,3},{8,12},{9,13},{10,... | collective-permute-start | bytes 135176 | tf_op jit(solution)/shard_map/ppermute | solution.py:323
  4.6 13.2 %collective-permute-start.1 = (bf16[176,128]{1,0:T(8,128)(2,1)}, bf16[176,128]{1,0:T(8,128)(2,1)S(1)}, u32[]{:S(2)}, u32[]{:S(2)}) collective-permute-start(bf16[176,128]{1,0:T(8,128)(2,1)} %get-tuple-element.16), channel_id=1, source_target_pairs={{0,8},{1,9},{2,10},{3,11},{4,12},{5,13},{6,14},{7,15},{8,0},{9,1},... | collective-permute-start | bytes 135176 | tf_op jit(solution)/shard_map/ppermute | solution.py:323
  7.2 10.7 %collective-permute-start.2 = (bf16[176,128]{1,0:T(8,128)(2,1)}, bf16[176,128]{1,0:T(8,128)(2,1)S(1)}, u32[]{:S(2)}, u32[]{:S(2)}) collective-permute-start(bf16[176,128]{1,0:T(8,128)(2,1)} %get-tuple-element.17), channel_id=1, source_target_pairs={{0,12},{1,13},{2,14},{3,15},{4,8},{5,9},{6,10},{7,11},{8,4},{9,5},... | collective-permute-start | bytes 135176 | tf_op jit(solution)/shard_map/ppermute | solution.py:323
  8.5 1.2 %copy-start.2 = (bf16[256,2,1024]{2,1,0:T(2,128)(2,1)S(1)}, bf16[256,2,1024]{2,1,0:T(2,128)(2,1)}, u32[]{:S(2)}) copy-start(bf16[256,2,1024]{2,1,0:T(2,128)(2,1)} %param.12) | copy-start | bytes 3145732
  8.6 1.2 %copy-start.10 = (s32[1,16,64]{2,1,0:T(8,128)S(1)}, s32[1,16,64]{2,1,0:T(8,128)}, u32[]{:S(2)}) copy-start(s32[1,16,64]{2,1,0:T(8,128)} %param.15) | copy-start | bytes 12292
  8.8 0.9 %copy-start.11 = (s32[256,2]{0,1:T(2,128)S(1)}, s32[256,2]{0,1:T(2,128)}, u32[]{:S(2)}) copy-start(s32[256,2]{0,1:T(2,128)} %param.13) | copy-start | bytes 6148
  8.9 0.9 %copy-start.12 = (s32[256]{0:T(256)S(1)}, s32[256]{0:T(256)}, u32[]{:S(2)}) copy-start(s32[256]{0:T(256)} %param.14) | copy-start | bytes 3076
  8.9 0.9 %copy-start.13 = (s32[1,16]{1,0:T(1,128)S(1)}, s32[1,16]{1,0:T(1,128)}, u32[]{:S(2)}) copy-start(s32[1,16]{1,0:T(1,128)} %counts.1) | copy-start | bytes 196
  9.8 1.2 %copy-start.5 = (bf16[8,256,256]{2,1,0:T(8,128)(2,1)S(1)}, bf16[8,256,256]{2,1,0:T(8,128)(2,1)}, u32[]{:S(2)}) copy-start(bf16[8,256,256]{2,1,0:T(8,128)(2,1)} %constant.9.clone.rest) | copy-start | bytes 3145732
  11.0 1.2 %copy-start.6 = (bf16[8,256,256]{2,1,0:T(8,128)(2,1)S(1)}, bf16[8,256,256]{2,1,0:T(8,128)(2,1)}, u32[]{:S(2)}) copy-start(bf16[8,256,256]{2,1,0:T(8,128)(2,1)} %constant.8.clone.high) | copy-start | bytes 3145732
  15.1 1.0 %copy-start = (bf16[8,256,256]{2,1,0:T(8,128)(2,1)}, bf16[8,256,256]{2,1,0:T(8,128)(2,1)S(1)}, u32[]{:S(2)}) copy-start(bf16[8,256,256]{2,1,0:T(8,128)(2,1)S(1)} %get-tuple-element.18.refs_4_.image) | copy-start | bytes 3145732
  16.0 1.0 %copy-start.3 = (bf16[8,256,256]{2,1,0:T(8,128)(2,1)}, bf16[8,256,256]{2,1,0:T(8,128)(2,1)S(1)}, u32[]{:S(2)}) copy-start(bf16[8,256,256]{2,1,0:T(8,128)(2,1)S(1)} %get-tuple-element.22.weights) | copy-start | bytes 3145732
  17.0 0.8 %copy-start.8 = (bf16[1024,256]{1,0:T(8,128)(2,1)}, bf16[1024,256]{1,0:T(8,128)(2,1)S(1)}, u32[]{:S(2)}) copy-start(bf16[1024,256]{1,0:T(8,128)(2,1)S(1)} %get-tuple-element.20.back) | copy-start | bytes 1572868
  17.9 0.6 copy-start.16
  17.9 9.5 %copy-start.1 = (bf16[8,256,256]{2,1,0:T(8,128)(2,1)S(1)}, bf16[8,256,256]{2,1,0:T(8,128)(2,1)}, u32[]{:S(2)}) copy-start(bf16[8,256,256]{2,1,0:T(8,128)(2,1)} %copy-done) | copy-start | bytes 3145732
  17.9 0.6 copy-start.17
  17.9 0.6 copy-start.18
  20.1 5.9 %collective-permute-start.3 = (bf16[4,176,128]{2,1,0:T(8,128)(2,1)}, bf16[4,176,128]{2,1,0:T(8,128)(2,1)S(1)}, u32[]{:S(2)}, u32[]{:S(2)}) collective-permute-start(bf16[4,176,128]{2,1,0:T(8,128)(2,1)} %stack.1.near), channel_id=1, source_target_pairs={{0,2},{1,3},{2,0},{3,1},{4,6},{5,7},{6,4},{7,5},{8,10},{9,11},{10,... | collective-permute-start | bytes 540680 | tf_op jit(solution)/shard_map/ppermute | solution.py:323
  21.8 4.2 %collective-permute-start.4 = (bf16[4,176,128]{2,1,0:T(8,128)(2,1)}, bf16[4,176,128]{2,1,0:T(8,128)(2,1)S(1)}, u32[]{:S(2)}, u32[]{:S(2)}) collective-permute-start(bf16[4,176,128]{2,1,0:T(8,128)(2,1)} %stack.1.near), channel_id=1, source_target_pairs={{0,1},{1,0},{2,3},{3,2},{4,5},{5,4},{6,7},{7,6},{8,9},{9,8},{10,11... | collective-permute-start | bytes 540680 | tf_op jit(solution)/shard_map/ppermute | solution.py:323
  26.0 1.4 %collective-permute-start.5 = (bf16[4,176,128]{2,1,0:T(8,128)(2,1)S(1)}, bf16[4,176,128]{2,1,0:T(8,128)(2,1)S(1)}, u32[]{:S(2)}, u32[]{:S(2)}) collective-permute-start(bf16[4,176,128]{2,1,0:T(8,128)(2,1)S(1)} %collective-permute-done.3.over_y), channel_id=1, source_target_pairs={{0,1},{1,0},{2,3},{3,2},{4,5},{5,4},{6,7},{7,6},{8,9},{9,8},{10,11... | collective-permute-start | bytes 540680 | tf_op jit(solution)/shard_map/ppermute | solution.py:323
  27.4 0.7 %copy-start.14 = (f32[32]{0:T(128)S(1)}, f32[32]{0:T(128)}, u32[]{:S(2)}) copy-start(f32[32]{0:T(128)} %param.19) | copy-start | bytes 388
  28.1 1.2 %copy-start.4 = (bf16[8,256,256]{2,1,0:T(8,128)(2,1)S(1)}, bf16[8,256,256]{2,1,0:T(8,128)(2,1)}, u32[]{:S(2)}) copy-start(bf16[8,256,256]{2,1,0:T(8,128)(2,1)} %copy-done.3) | copy-start | bytes 3145732
  29.3 0.9 %copy-start.7 = (bf16[4,176,128]{2,1,0:T(8,128)(2,1)S(1)}, bf16[4,176,128]{2,1,0:T(8,128)(2,1)}, u32[]{:S(2)}) copy-start(bf16[4,176,128]{2,1,0:T(8,128)(2,1)} %stack.1.near) | copy-start | bytes 540676
  30.2 1.0 %copy-start.9 = (bf16[1024,256]{1,0:T(8,128)(2,1)S(1)}, bf16[1024,256]{1,0:T(8,128)(2,1)}, u32[]{:S(2)}) copy-start(bf16[1024,256]{1,0:T(8,128)(2,1)} %copy-done.8) | copy-start | bytes 1572868
  42.4 20.3 %copy-start.15 = (f32[1,16,64,2,128]{4,3,2,1,0:T(2,128)S(1)}, f32[1,16,64,2,128]{4,3,2,1,0:T(2,128)}, u32[]{:S(2)}) copy-start(f32[1,16,64,2,128]{4,3,2,1,0:T(2,128)} %param.21) | copy-start | bytes 3145732

commit v5 on v4

--- a/solution.py
+++ b/solution.py
@@ -13,7 +13,7 @@
 TWO_PI = 2.0 * math.pi
 F32 = jnp.float32
 BF16 = jnp.bfloat16
-VMEM_LIMIT = 36 * 1024 * 1024
+MIB = 1024 * 1024
 NT = (((1,), (1,)), ((), ()))
 
 
@@ -173,7 +173,8 @@
     weights,
     freq,
     image,
-    payload,
+    sent_a,
+    sent_b,
     table,
     lanes,
     coef,
@@ -316,7 +317,17 @@
     sent = dot(back[...], models)
     interleaved[pl.ds(0, slots, stride=2), :] = sent[:, :128]
     interleaved[pl.ds(1, slots, stride=2), :] = sent[:, 128:]
-    payload[...] = interleaved[...].astype(BF16)
+    half = capacity
+    for d in range(tiles):
+        for part, out in enumerate((sent_a, sent_b)):
+            rows = slice((2 * d + part) * half, (2 * d + part + 1) * half)
+            out[d // 4, d % 4] = interleaved[rows, :].astype(BF16)
+
+
+def residual_kernel(observed, first, second, residual):
+    rows = first.shape[2]
+    residual[:, :rows, :] = observed[:, :rows, :] - first[0].astype(F32)
+    residual[:, rows:, :] = observed[:, rows:, :] - second[0].astype(F32)
 
 
 def exchange(value, step, tiles):
@@ -359,6 +370,7 @@
         out_shape=[block] * outer,
         in_specs=[smem, vmem, vmem],
         out_specs=[vmem] * outer,
+        compiler_params=pltpu.CompilerParams(vmem_limit_bytes=2 * MIB * (1 + tiles // 16)),
         name="pack",
     )(me, beam_coefs.reshape(own_rows, terms2), own_tracks)
     along = [packed[0]] + [exchange(packed[r], 4 * r, tiles) for r in range(1, outer)]
@@ -384,7 +396,7 @@
             pltpu.VMEM((number * 16, 128), F32),
             pltpu.VMEM((8, number, 512), BF16),
         ],
-        compiler_params=pltpu.CompilerParams(vmem_limit_bytes=24 * 1024 * 1024),
+        compiler_params=pltpu.CompilerParams(vmem_limit_bytes=16 * MIB * (1 + tiles // 64)),
         name="prepare",
     )(
         counts,
@@ -402,17 +414,18 @@
         out_shape=jax.ShapeDtypeStruct((outer,) + block.shape, BF16),
         in_specs=[vmem] * outer + [anywhere],
         out_specs=vmem,
+        compiler_params=pltpu.CompilerParams(vmem_limit_bytes=2 * MIB * (tiles // 16)),
         name="stack",
     )(*along, image)
     over_y = exchange(near, 2, tiles)
     over_core = exchange(near, 1, tiles)
     over_both = exchange(over_y, 1, tiles)
 
-    payload = pl.pallas_call(
+    first, second = pl.pallas_call(
         predict_kernel,
-        out_shape=jax.ShapeDtypeStruct((2 * slots, vis), BF16),
+        out_shape=[jax.ShapeDtypeStruct((outer, 4, capacity, vis), BF16)] * 2,
         in_specs=[smem] + [vmem] * 10,
-        out_specs=vmem,
+        out_specs=[vmem] * 2,
         scratch_shapes=[
             pltpu.VMEM((tiles * own_rows, terms2), BF16),
             pltpu.VMEM((tiles, 6 * steps, capacity), F32),
@@ -427,7 +440,7 @@
             pltpu.VMEM((2, number, vis), F32),
             pltpu.VMEM((2 * slots, vis), F32),
         ],
-        compiler_params=pltpu.CompilerParams(vmem_limit_bytes=VMEM_LIMIT),
+        compiler_params=pltpu.CompilerParams(vmem_limit_bytes=20 * MIB * (1 + tiles // 64)),
         name="predict",
     )(
         me,
@@ -442,10 +455,30 @@
         frequencies.reshape(1, chan),
         image,
     )
-    arrived = lax.all_to_all(
-        payload.reshape(tiles, 2 * capacity, vis), "tile", split_axis=0, concat_axis=0, tiled=True
-    )
-    return observed - arrived.reshape(observed.shape).astype(F32)
+    columns = [[4 * r + k for r in range(outer)] for k in range(4)]
+    planes = [[4 * r + k for k in range(4)] for r in range(outer)]
+
+    def swap(value, axis, groups):
+        return lax.all_to_all(value, "tile", axis, axis, axis_index_groups=groups, tiled=True)
+
+    first = swap(first, 0, columns)
+    second = swap(second, 1, planes)
+    first = swap(first, 1, planes)
+    second = swap(second, 0, columns)
+    residual = pl.pallas_call(
+        residual_kernel,
+        grid=(outer,),
+        out_shape=jax.ShapeDtypeStruct((tiles, 2 * capacity, vis), F32),
+        in_specs=[
+            pl.BlockSpec((4, 2 * capacity, vis), lambda i: (i, 0, 0)),
+            pl.BlockSpec((1, 4, capacity, vis), lambda i: (i, 0, 0, 0)),
+            pl.BlockSpec((1, 4, capacity, vis), lambda i: (i, 0, 0, 0)),
+        ],
+        out_specs=pl.BlockSpec((4, 2 * capacity, vis), lambda i: (i, 0, 0)),
+        compiler_params=pltpu.CompilerParams(vmem_limit_bytes=4 * MIB),
+        name="residual",
+    )(observed.reshape(tiles, 2 * capacity, vis), first, second)
+    return residual.reshape(observed.shape)
 
 
 def solution(mesh):

time: 64.3 us -> 81.6 us (1.27)
  waiting for transfers between devices: 5.62 us -> 33.4 us
  blocking collectives: 20.3 us -> 0 us
  starting transfers between devices: 7.36 us -> 22.6 us
  local copies, waits for them, and re-layouts: 12.2 us -> 8.48 us
  other arithmetic: 1.08 us -> 0 us
    all_to_all x0 -> x4, waiting for transfers between devices: none -> 28 us  [swap(): lax.all_to_all(value, 'tile', axis, axis, axis_index_groups=groups, tiled...]
    all_to_all x1 -> x0, blocking collectives: 20.3 us -> none  [per_device(): lax.all_to_all(payload.reshape(tiles, 2 * capacity, vis), 'tile', split_a...]
    all_to_all x0 -> x4, starting transfers between devices: none -> 15.1 us  [swap(): lax.all_to_all(value, 'tile', axis, axis, axis_index_groups=groups, tiled...]
    unnamed x39 -> x23, local copies, waits for them, and re-layouts: 11.9 us -> 6.05 us
    pallas_call x1 -> x2, Pallas kernels: 11.1 us -> 13.4 us  [the longest x1 11.8 us: per_device(): pl.pallas_call(predict_kernel, out_shape=[jax.ShapeDtypeStruct((outer, 4,...]
    pallas_call x1, Pallas kernels: 1.61 us -> 0.09 us  [per_device(): pl.pallas_call(pack_kernel, out_shape=[block] * outer, in_specs=[smem, vm...]
    pallas_call x1, Pallas kernels: 1.53 us -> 0.01 us  [per_device(): pl.pallas_call(stack_kernel, out_shape=jax.ShapeDtypeStruct((outer,) + bl...]
    all_to_all x0 -> x3, local copies, waits for them, and re-layouts: none -> 1.45 us  [swap(): lax.all_to_all(value, 'tile', axis, axis, axis_index_groups=groups, tiled...]
  transfers between devices with their start and end apart: 6 -> 10, of which waited for: 2 -> 6; matrix products, arithmetic and copies ran while one was open for 2% -> 5% of each run, Pallas kernels for 4% -> 3%
where the time goes in v5:
time: 81.6 us; the launch traced here: 80.9 us
  waiting for transfers between devices  33.4 us (41%)
  starting transfers between devices  22.6 us (28%)
  Pallas kernels  16.3 us (20%)
  local copies, waits for them, and re-layouts  8.48 us (10%)
    all_to_all x4, waiting for transfers between devices, swap(): lax.all_to_all(value, 'tile', axis, axis, axis_index_groups=groups, tiled...  28 us
    all_to_all x4, starting transfers between devices, swap(): lax.all_to_all(value, 'tile', axis, axis, axis_index_groups=groups, tiled...  15.1 us
    pallas_call x1, Pallas kernels, per_device(): pl.pallas_call(predict_kernel, out_shape=[jax.ShapeDtypeStruct((outer, 4,...  11.8 us
    ppermute x6, starting transfers between devices, exchange(): return lax.ppermute(value, 'tile', [(i, i ^ step) for i in range(tiles)])  7.49 us
    unnamed x23, local copies, waits for them, and re-layouts  6.05 us
    ppermute x6, waiting for transfers between devices, exchange(): return lax.ppermute(value, 'tile', [(i, i ^ step) for i in range(tiles)])  5.41 us
    pallas_call x1, Pallas kernels, per_device(): pl.pallas_call(functools.partial(prepare_kernel, slot_count=slot_count),...  2.8 us
  transfers between devices with their start and end apart: 10, of which 6 were waited for; matrix products, arithmetic and copies ran while one was open for 5% of the time, Pallas kernels for 3%

profile of v5, /device:TPU:0, one launch (start us, length us, event | category | flops | bytes accessed | tf_op | source)
XLA Modules:
  0.0 80.9 jit_solution(5981451048972205637)
XLA Ops:
  0.0 0.0 copy-start.4
  0.0 0.8 %copy-done.4 = f32[1,16,64,2,4]{2,4,3,1,0:T(4,128)S(1)} copy-done((f32[1,16,64,2,4]{2,4,3,1,0:T(4,128)S(1)}, f32[1,16,64,2,4]{2,4,3,1,0:T(4,128)}, u32[]{:S(2)}) %copy-start.4) | copy-done | bytes 32792
  0.8 0.0 copy-start.5
  0.8 0.8 copy-done.5
  1.6 0.1 pack.1
  1.7 3.1 %collective-permute-start = (bf16[176,128]{1,0:T(8,128)(2,1)S(1)}, bf16[176,128]{1,0:T(8,128)(2,1)S(1)}, u32[]{:S(2)}, u32[]{:S(2)}) collective-permute-start(bf16[176,128]{1,0:T(8,128)(2,1)S(1)} %get-tuple-element.17), channel_id=1, source_target_pairs={{0,4},{1,5},{2,6},{3,7},{4,0},{5,1},{6,2},{7,3},{8,12},{9,13},{10,... | collective-permute-start | bytes 135176 | tf_op jit(solution)/shard_map/ppermute | solution.py:334
  4.8 2.6 %collective-permute-start.1 = (bf16[176,128]{1,0:T(8,128)(2,1)S(1)}, bf16[176,128]{1,0:T(8,128)(2,1)S(1)}, u32[]{:S(2)}, u32[]{:S(2)}) collective-permute-start(bf16[176,128]{1,0:T(8,128)(2,1)S(1)} %get-tuple-element.18), channel_id=1, source_target_pairs={{0,8},{1,9},{2,10},{3,11},{4,12},{5,13},{6,14},{7,15},{8,0},{9,1},... | collective-permute-start | bytes 135176 | tf_op jit(solution)/shard_map/ppermute | solution.py:334
  7.4 0.0 collective-permute-start.2
  7.4 0.0 copy-start.7
  7.4 0.0 copy-start.9
  7.4 1.3 %copy.20 = bf16[2,128,1024]{1,2,0:T(8,128)(2,1)S(1)} copy(bf16[2,128,1024]{2,1,0:T(8,128)(2,1)} %param.18) | data formatting | bytes 1048576 | tf_op args[6]
  8.7 0.0 copy-start.1
  8.7 0.0 copy-start.2
  8.8 0.0 copy-start.6
  8.8 0.2 copy.22.basis
  9.0 0.0 copy-start.8
  9.1 0.0 copy-done.7
  9.1 0.0 copy-done.9
  9.1 0.9 %copy-done.1 = bf16[256,2,1024]{2,1,0:T(2,128)(2,1)S(1)} copy-done((bf16[256,2,1024]{2,1,0:T(2,128)(2,1)S(1)}, bf16[256,2,1024]{2,1,0:T(2,128)(2,1)}, u32[]{:S(2)}) %copy-start.1) | copy-done | bytes 1048600
  10.0 0.3 copy-done.2
  10.3 0.0 copy-done.6
  10.3 0.0 copy-done.8
  10.3 0.0 copy-start.3
  10.3 1.2 %copy-done.3 = bf16[8,256,256]{2,1,0:T(8,128)(2,1)S(1)} copy-done((bf16[8,256,256]{2,1,0:T(8,128)(2,1)S(1)}, bf16[8,256,256]{2,1,0:T(8,128)(2,1)}, u32[]{:S(2)}) %copy-start.3) | copy-done | bytes 1048600
  11.5 2.8 %prepare.1 = (bf16[8,256,256]{2,1,0:T(8,128)(2,1)S(1)}, bf16[256,1024]{1,0:T(8,128)(2,1)S(1)}, bf16[1024,256]{1,0:T(8,128)(2,1)S(1)}, bf16[512,1024]{1,0:T(8,128)(2,1)S(1)}, bf16[8,256,256]{2,1,0:T(8,128)(2,1)S(1)}) custom-call(s32[1,16]{1,0:T(1,128)S(1)} %copy-done.9, bf16[4096,128]{1,0:T(8,128)(2,1)S(1)} %bitcast.23, bf16[8,256,256]{2,1,0:T(8,128)(2,1)S(1)} %copy-done.3, ...), custom_call_target="tpu_custom_call" | custom-call | tf_op jit(solution)/shard_map/prepare/pallas_call | solution.py:384
  14.3 0.0 collective-permute-done.refs_1_
  14.3 0.0 collective-permute-done.1.refs_2_
  14.3 0.0 collective-permute-done.2.refs_3_
  14.4 1.8 %collective-permute-start.3 = (bf16[4,176,128]{2,1,0:T(8,128)(2,1)S(1)}, bf16[4,176,128]{2,1,0:T(8,128)(2,1)S(1)}, u32[]{:S(2)}, u32[]{:S(2)}) collective-permute-start(bf16[4,176,128]{2,1,0:T(8,128)(2,1)S(1)} %stack.1.near), channel_id=1, source_target_pairs={{0,2},{1,3},{2,0},{3,1},{4,6},{5,7},{6,4},{7,5},{8,10},{9,11},{10,... | collective-permute-start | bytes 540680 | tf_op jit(solution)/shard_map/ppermute | solution.py:334
  16.2 0.0 collective-permute-start.4
  16.2 4.0 %collective-permute-done.3.over_y = bf16[4,176,128]{2,1,0:T(8,128)(2,1)S(1)} collective-permute-done((bf16[4,176,128]{2,1,0:T(8,128)(2,1)S(1)}, bf16[4,176,128]{2,1,0:T(8,128)(2,1)S(1)}, u32[]{:S(2)}, u32[]{:S(2)}) %collective-permute-start.3) | collective-permute-done | bytes 180256 | tf_op jit(solution)/shard_map/ppermute | solution.py:334
  20.2 0.0 collective-permute-start.5
  20.2 0.0 collective-permute-done.4.over_core
  20.2 1.4 %collective-permute-done.5.over_both = bf16[4,176,128]{2,1,0:T(8,128)(2,1)S(1)} collective-permute-done((bf16[4,176,128]{2,1,0:T(8,128)(2,1)S(1)}, bf16[4,176,128]{2,1,0:T(8,128)(2,1)S(1)}, u32[]{:S(2)}, u32[]{:S(2)}) %collective-permute-start.5) | collective-permute-done | bytes 180256 | tf_op jit(solution)/shard_map/ppermute | solution.py:334
  21.6 0.0 copy-start.10
  21.6 0.7 copy-done.10
  22.2 11.8 %predict.1 = (bf16[4,4,64,128]{3,2,1,0:T(8,128)(2,1)}, bf16[4,4,64,128]{3,2,1,0:T(8,128)(2,1)S(1)}) custom-call(s32[1]{0:T(128)} %bitcast.1.me, bf16[4,176,128]{2,1,0:T(8,128)(2,1)S(1)} %stack.1.near, bf16[4,176,128]{2,1,0:T(8,128)(2,1)S(1)} %collective-permute-done.3.over_y, bf16[4,176,128]{2,1,0:T(8,128)(2,1)S(1)} %collective-permute-done.4.over_core, ...), custom_call_target="tpu_custom_call" | custom-call | tf_op jit(solution)/shard_map/predict/pallas_call | solution.py:424
  34.1 4.9 %all-to-all-start = ((bf16[4,4,64,128]{3,2,1,0:T(8,128)(2,1)}), bf16[4,4,64,128]{3,2,1,0:T(8,128)(2,1)S(1)}, u32[]{:S(2)}, u32[]{:S(2)}) async-start(bf16[4,4,64,128]{3,2,1,0:T(8,128)(2,1)} %get-tuple-element.25), calls=%async_computation | async-start | bytes 524288 | tf_op jit(solution)/shard_map/all_to_all | solution.py:462
  38.9 0.7 copy.24
  39.6 8.5 %all-to-all-done = bf16[4,4,64,128]{3,2,1,0:T(8,128)(2,1)S(1)} async-done(((bf16[4,4,64,128]{3,2,1,0:T(8,128)(2,1)}), bf16[4,4,64,128]{3,2,1,0:T(8,128)(2,1)S(1)}, u32[]{:S(2)}, u32[]{:S(2)}) %all-to-all-start) | async-done | bytes 262176 | tf_op jit(solution)/shard_map/all_to_all | solution.py:462
  48.2 3.4 %all-to-all-start.2 = ((bf16[4,4,64,128]{3,2,0,1:T(8,128)(2,1)}), bf16[4,4,64,128]{3,2,0,1:T(8,128)(2,1)S(1)}, u32[]{:S(2)}, u32[]{:S(2)}) async-start(bf16[4,4,64,128]{3,2,0,1:T(8,128)(2,1)} %copy.24), calls=%async_computation.2 | async-start | bytes 524288 | tf_op jit(solution)/shard_map/all_to_all | solution.py:462
  51.6 0.7 copy.23
  52.3 0.0 copy-start
  52.3 5.3 %all-to-all-done.2 = bf16[4,4,64,128]{3,2,0,1:T(8,128)(2,1)S(1)} async-done(((bf16[4,4,64,128]{3,2,0,1:T(8,128)(2,1)}), bf16[4,4,64,128]{3,2,0,1:T(8,128)(2,1)S(1)}, u32[]{:S(2)}, u32[]{:S(2)}) %all-to-all-start.2) | async-done | bytes 262176 | tf_op jit(solution)/shard_map/all_to_all | solution.py:462
  57.6 3.4 %all-to-all-start.1 = ((bf16[4,4,64,128]{3,2,0,1:T(8,128)(2,1)}), bf16[4,4,64,128]{3,2,0,1:T(8,128)(2,1)S(1)}, u32[]{:S(2)}, u32[]{:S(2)}) async-start(bf16[4,4,64,128]{3,2,0,1:T(8,128)(2,1)} %copy.23), calls=%async_computation.1 | async-start | bytes 524288 | tf_op jit(solution)/shard_map/all_to_all | solution.py:462
  61.0 0.7 copy.25
  61.7 5.3 %all-to-all-done.1 = bf16[4,4,64,128]{3,2,0,1:T(8,128)(2,1)S(1)} async-done(((bf16[4,4,64,128]{3,2,0,1:T(8,128)(2,1)}), bf16[4,4,64,128]{3,2,0,1:T(8,128)(2,1)S(1)}, u32[]{:S(2)}, u32[]{:S(2)}) %all-to-all-start.1) | async-done | bytes 262176 | tf_op jit(solution)/shard_map/all_to_all | solution.py:462
  67.0 3.4 %all-to-all-start.3 = ((bf16[4,4,64,128]{3,2,1,0:T(8,128)(2,1)}), bf16[4,4,64,128]{3,2,1,0:T(8,128)(2,1)S(1)}, u32[]{:S(2)}, u32[]{:S(2)}) async-start(bf16[4,4,64,128]{3,2,1,0:T(8,128)(2,1)} %copy.25), calls=%async_computation.3 | async-start | bytes 524288 | tf_op jit(solution)/shard_map/all_to_all | solution.py:462
  70.4 8.9 %all-to-all-done.3.second = bf16[4,4,64,128]{3,2,1,0:T(8,128)(2,1)S(1)} async-done(((bf16[4,4,64,128]{3,2,1,0:T(8,128)(2,1)}), bf16[4,4,64,128]{3,2,1,0:T(8,128)(2,1)S(1)}, u32[]{:S(2)}, u32[]{:S(2)}) %all-to-all-start.3) | async-done | bytes 262176 | tf_op jit(solution)/shard_map/all_to_all | solution.py:462
  79.4 0.0 copy-done
  79.4 1.5 %residual.1 = f32[16,128,128]{2,1,0:T(8,128)} custom-call(f32[16,128,128]{2,1,0:T(8,128)S(1)} %bitcast.22, bf16[4,4,64,128]{3,2,1,0:T(8,128)(2,1)S(1)} %copy.26.first, bf16[4,4,64,128]{3,2,1,0:T(8,128)(2,1)S(1)} %all-to-all-done.3.second), custom_call_target="tpu_custom_call" | custom-call | tf_op jit(solution)/shard_map/residual/pallas_call | solution.py:468
  (3 shorter events, 0.1 us)
Async XLA Ops:
  0.0 0.8 %copy-start.4 = (f32[1,16,64,2,4]{2,4,3,1,0:T(4,128)S(1)}, f32[1,16,64,2,4]{2,4,3,1,0:T(4,128)}, u32[]{:S(2)}) copy-start(f32[1,16,64,2,4]{2,4,3,1,0:T(4,128)} %param.20) | copy-start | bytes 98308
  0.8 0.8 copy-start.5
  1.7 12.6 %collective-permute-start = (bf16[176,128]{1,0:T(8,128)(2,1)S(1)}, bf16[176,128]{1,0:T(8,128)(2,1)S(1)}, u32[]{:S(2)}, u32[]{:S(2)}) collective-permute-start(bf16[176,128]{1,0:T(8,128)(2,1)S(1)} %get-tuple-element.17), channel_id=1, source_target_pairs={{0,4},{1,5},{2,6},{3,7},{4,0},{5,1},{6,2},{7,3},{8,12},{9,13},{10,... | collective-permute-start | bytes 135176 | tf_op jit(solution)/shard_map/ppermute | solution.py:334
  4.8 9.5 %collective-permute-start.1 = (bf16[176,128]{1,0:T(8,128)(2,1)S(1)}, bf16[176,128]{1,0:T(8,128)(2,1)S(1)}, u32[]{:S(2)}, u32[]{:S(2)}) collective-permute-start(bf16[176,128]{1,0:T(8,128)(2,1)S(1)} %get-tuple-element.18), channel_id=1, source_target_pairs={{0,8},{1,9},{2,10},{3,11},{4,12},{5,13},{6,14},{7,15},{8,0},{9,1},... | collective-permute-start | bytes 135176 | tf_op jit(solution)/shard_map/ppermute | solution.py:334
  7.4 7.0 %collective-permute-start.2 = (bf16[176,128]{1,0:T(8,128)(2,1)S(1)}, bf16[176,128]{1,0:T(8,128)(2,1)S(1)}, u32[]{:S(2)}, u32[]{:S(2)}) collective-permute-start(bf16[176,128]{1,0:T(8,128)(2,1)S(1)} %get-tuple-element.19), channel_id=1, source_target_pairs={{0,12},{1,13},{2,14},{3,15},{4,8},{5,9},{6,10},{7,11},{8,4},{9,5},... | collective-permute-start | bytes 135176 | tf_op jit(solution)/shard_map/ppermute | solution.py:334
  7.4 1.7 %copy-start.7 = (s32[256,2]{0,1:T(2,128)S(1)}, s32[256,2]{0,1:T(2,128)}, u32[]{:S(2)}) copy-start(s32[256,2]{0,1:T(2,128)} %param.13) | copy-start | bytes 6148
  7.4 1.7 %copy-start.9 = (s32[1,16]{1,0:T(1,128)S(1)}, s32[1,16]{1,0:T(1,128)}, u32[]{:S(2)}) copy-start(s32[1,16]{1,0:T(1,128)} %counts.1) | copy-start | bytes 196
  8.7 1.2 %copy-start.1 = (bf16[256,2,1024]{2,1,0:T(2,128)(2,1)S(1)}, bf16[256,2,1024]{2,1,0:T(2,128)(2,1)}, u32[]{:S(2)}) copy-start(bf16[256,2,1024]{2,1,0:T(2,128)(2,1)} %param.12) | copy-start | bytes 3145732
  8.7 1.5 %copy-start.2 = (bf16[8,256,256]{2,1,0:T(8,128)(2,1)S(1)}, bf16[8,256,256]{2,1,0:T(8,128)(2,1)}, u32[]{:S(2)}) copy-start(bf16[8,256,256]{2,1,0:T(8,128)(2,1)} %constant.9.clone.rest) | copy-start | bytes 3145732
  8.8 1.5 %copy-start.6 = (s32[1,16,64]{2,1,0:T(8,128)S(1)}, s32[1,16,64]{2,1,0:T(8,128)}, u32[]{:S(2)}) copy-start(s32[1,16,64]{2,1,0:T(8,128)} %param.15) | copy-start | bytes 12292
  9.0 1.2 %copy-start.8 = (s32[256]{0:T(256)S(1)}, s32[256]{0:T(256)}, u32[]{:S(2)}) copy-start(s32[256]{0:T(256)} %param.14) | copy-start | bytes 3076
  10.3 1.2 %copy-start.3 = (bf16[8,256,256]{2,1,0:T(8,128)(2,1)S(1)}, bf16[8,256,256]{2,1,0:T(8,128)(2,1)}, u32[]{:S(2)}) copy-start(bf16[8,256,256]{2,1,0:T(8,128)(2,1)} %constant.8.clone.high) | copy-start | bytes 3145732
  14.4 5.8 %collective-permute-start.3 = (bf16[4,176,128]{2,1,0:T(8,128)(2,1)S(1)}, bf16[4,176,128]{2,1,0:T(8,128)(2,1)S(1)}, u32[]{:S(2)}, u32[]{:S(2)}) collective-permute-start(bf16[4,176,128]{2,1,0:T(8,128)(2,1)S(1)} %stack.1.near), channel_id=1, source_target_pairs={{0,2},{1,3},{2,0},{3,1},{4,6},{5,7},{6,4},{7,5},{8,10},{9,11},{10,... | collective-permute-start | bytes 540680 | tf_op jit(solution)/shard_map/ppermute | solution.py:334
  16.2 4.0 %collective-permute-start.4 = (bf16[4,176,128]{2,1,0:T(8,128)(2,1)S(1)}, bf16[4,176,128]{2,1,0:T(8,128)(2,1)S(1)}, u32[]{:S(2)}, u32[]{:S(2)}) collective-permute-start(bf16[4,176,128]{2,1,0:T(8,128)(2,1)S(1)} %stack.1.near), channel_id=1, source_target_pairs={{0,1},{1,0},{2,3},{3,2},{4,5},{5,4},{6,7},{7,6},{8,9},{9,8},{10,11... | collective-permute-start | bytes 540680 | tf_op jit(solution)/shard_map/ppermute | solution.py:334
  20.2 1.4 %collective-permute-start.5 = (bf16[4,176,128]{2,1,0:T(8,128)(2,1)S(1)}, bf16[4,176,128]{2,1,0:T(8,128)(2,1)S(1)}, u32[]{:S(2)}, u32[]{:S(2)}) collective-permute-start(bf16[4,176,128]{2,1,0:T(8,128)(2,1)S(1)} %collective-permute-done.3.over_y), channel_id=1, source_target_pairs={{0,1},{1,0},{2,3},{3,2},{4,5},{5,4},{6,7},{7,6},{8,9},{9,8},{10,11... | collective-permute-start | bytes 540680 | tf_op jit(solution)/shard_map/ppermute | solution.py:334
  21.6 0.7 copy-start.10
  34.1 14.1 %all-to-all-start = ((bf16[4,4,64,128]{3,2,1,0:T(8,128)(2,1)}), bf16[4,4,64,128]{3,2,1,0:T(8,128)(2,1)S(1)}, u32[]{:S(2)}, u32[]{:S(2)}) async-start(bf16[4,4,64,128]{3,2,1,0:T(8,128)(2,1)} %get-tuple-element.25), calls=%async_computation | async-start | bytes 524288 | tf_op jit(solution)/shard_map/all_to_all | solution.py:462
  48.2 9.4 %all-to-all-start.2 = ((bf16[4,4,64,128]{3,2,0,1:T(8,128)(2,1)}), bf16[4,4,64,128]{3,2,0,1:T(8,128)(2,1)S(1)}, u32[]{:S(2)}, u32[]{:S(2)}) async-start(bf16[4,4,64,128]{3,2,0,1:T(8,128)(2,1)} %copy.24), calls=%async_computation.2 | async-start | bytes 524288 | tf_op jit(solution)/shard_map/all_to_all | solution.py:462
  52.3 27.1 %copy-start = (f32[1,16,64,2,128]{4,3,2,1,0:T(2,128)S(1)}, f32[1,16,64,2,128]{4,3,2,1,0:T(2,128)}, u32[]{:S(2)}) copy-start(f32[1,16,64,2,128]{4,3,2,1,0:T(2,128)} %param.21) | copy-start | bytes 3145732
  57.6 9.4 %all-to-all-start.1 = ((bf16[4,4,64,128]{3,2,0,1:T(8,128)(2,1)}), bf16[4,4,64,128]{3,2,0,1:T(8,128)(2,1)S(1)}, u32[]{:S(2)}, u32[]{:S(2)}) async-start(bf16[4,4,64,128]{3,2,0,1:T(8,128)(2,1)} %copy.23), calls=%async_computation.1 | async-start | bytes 524288 | tf_op jit(solution)/shard_map/all_to_all | solution.py:462
  67.0 12.4 %all-to-all-start.3 = ((bf16[4,4,64,128]{3,2,1,0:T(8,128)(2,1)}), bf16[4,4,64,128]{3,2,1,0:T(8,128)(2,1)S(1)}, u32[]{:S(2)}, u32[]{:S(2)}) async-start(bf16[4,4,64,128]{3,2,1,0:T(8,128)(2,1)} %copy.25), calls=%async_computation.3 | async-start | bytes 524288 | tf_op jit(solution)/shard_map/all_to_all | solution.py:462

commit v6 on v4

--- a/solution.py
+++ b/solution.py
@@ -3,7 +3,6 @@
 
 import jax
 import jax.numpy as jnp
-import ml_dtypes
 import numpy as np
 from jax import lax
 from jax.experimental import pallas as pl
@@ -13,7 +12,7 @@
 TWO_PI = 2.0 * math.pi
 F32 = jnp.float32
 BF16 = jnp.bfloat16
-VMEM_LIMIT = 36 * 1024 * 1024
+MIB = 1024 * 1024
 NT = (((1,), (1,)), ((), ()))
 
 
@@ -21,22 +20,18 @@
     return lax.dot_general(a, b, dims, preferred_element_type=F32)
 
 
-def transform_matrices(edge):
+def transform_tables(edge):
     low = edge // 8
-    b = np.arange(low)[:, None, None, None]
-    a = np.arange(edge)[None, :, None, None]
+    outer = np.arange(8)[:, None, None, None]
+    b = np.arange(low)[None, :, None, None]
     inner = np.arange(low)[None, None, :, None]
-    x = np.arange(edge)[None, None, None, :]
-    kept = []
-    for outer in range(8):
-        turns = (b * (outer + 8 * inner) + a * x) % edge
-        angle = (TWO_PI / edge * turns).reshape(low * edge, low * edge)
-        c, s = np.cos(angle) / edge**2, np.sin(angle) / edge**2
-        kept.append(np.block([[c, s], [-s, c]]))
-    full = np.stack(kept)
-    high = full.astype(ml_dtypes.bfloat16)
-    rest = (full - high.astype(np.float64)).astype(ml_dtypes.bfloat16)
-    return high, rest
+    x = np.arange(edge)
+    turns = np.broadcast_to(b * (outer + 8 * inner) % edge, (8, low, low, edge))
+    rows = TWO_PI / edge * turns.reshape(8, low, low * edge)
+    cells = TWO_PI / edge * np.tile(x[:, None] * x[None, :] % edge, (1, low))
+    rows = np.stack([np.cos(rows), np.sin(rows)]).astype(np.float32)
+    cells = (np.stack([np.cos(cells), np.sin(cells)]) / edge**2).astype(np.float32)
+    return rows.reshape(2, 8 * low, low * edge), cells
 
 
 def eight_point(re, im):
@@ -59,11 +54,30 @@
     return out_re, out_im
 
 
-def prepare_kernel(
-    counts, cells, high, rest, assign, stations, time_slots, basis, image, route, back, pick, weights, wide, sums, *, slot_count
-):
+def transform_kernel(cells_hbm, row_turns, cell_turns, image, cells, high, rest, wide, sums, sem):
+    copy = pltpu.make_async_copy(cells_hbm, cells, sem)
+    copy.start()
     number = image.shape[1]
-    tiles, capacity = assign.shape
+    edge, span = cell_turns.shape[1:]
+    low = span // edge
+    cell_c, cell_s = cell_turns[0], cell_turns[1]
+    for m in range(8):
+        for k in range(low):
+            at = m * low + k
+            row_c, row_s = row_turns[0, at : at + 1, :], row_turns[1, at : at + 1, :]
+            c = row_c * cell_c - row_s * cell_s
+            s = row_s * cell_c + row_c * cell_s
+            c_top, s_top = c.astype(BF16), s.astype(BF16)
+            c_left = (c - c_top.astype(F32)).astype(BF16)
+            s_left = (s - s_top.astype(F32)).astype(BF16)
+            re = slice(k * edge, (k + 1) * edge)
+            im = slice(span + k * edge, span + (k + 1) * edge)
+            for held, cos_part, sin_part in ((high, c_top, s_top), (rest, c_left, s_left)):
+                held[m, re, :span] = cos_part
+                held[m, re, span:] = sin_part
+                held[m, im, :span] = -sin_part
+                held[m, im, span:] = cos_part
+    copy.wait()
     step = 16
 
     @pl.loop(0, number // step, unroll=2)
@@ -86,6 +100,11 @@
         right = jnp.concatenate([high[m], high[m], rest[m]], axis=0)
         image[m] = dot(left, right).astype(BF16)
 
+
+def prepare_kernel(counts, assign, stations, time_slots, basis, after, route, back, pick, weights, *, slot_count):
+    number = route.shape[0]
+    tiles, capacity = assign.shape
+
     per = 128 // capacity
     down = lax.broadcasted_iota(jnp.int32, (number, 128), 0)
     slot = lax.broadcasted_iota(jnp.int32, (1, capacity), 1)
@@ -107,9 +126,11 @@
         pick[which * number : (which + 1) * number, :] = hot.astype(BF16)
 
     terms = basis.shape[1]
+    edge = math.isqrt(basis.shape[2])
     for m in range(8):
-        cols = slice(m * 128, (m + 1) * 128)
-        b_re, b_im = basis[0, :, cols], basis[1, :, cols]
+        starts = [(8 * n + m) * edge for n in range(edge // 8)]
+        b_re = jnp.concatenate([basis[0, :, n : n + edge] for n in starts], axis=1)
+        b_im = jnp.concatenate([basis[1, :, n : n + edge] for n in starts], axis=1)
         weights[m, :terms, :128] = b_re
         weights[m, :terms, 128:] = b_im
         weights[m, terms:, :128] = -b_im
@@ -135,7 +156,16 @@
     return ar * br - ai * bi, ar * bi + ai * br
 
 
-def pack_kernel(me, coefs, tracks, *out):
+def pack_kernel(me, coefs_hbm, tracks_hbm, *refs):
+    out, (coefs, tracks, sems) = refs[:-3], refs[-3:]
+    copies = [
+        pltpu.make_async_copy(coefs_hbm, coefs, sems.at[0]),
+        pltpu.make_async_copy(tracks_hbm, tracks, sems.at[1]),
+    ]
+    for copy in copies:
+        copy.start()
+    for copy in copies:
+        copy.wait()
     capacity = tracks.shape[2]
     rows = coefs.shape[0]
     for r in range(len(out)):
@@ -173,20 +203,9 @@
     weights,
     freq,
     image,
-    payload,
-    table,
-    lanes,
-    coef,
-    wre,
-    wim,
-    pure,
-    puim,
-    zrow,
-    hre,
-    him,
-    zv,
-    interleaved,
+    *refs,
 ):
+    table, lanes, coef, wre, wim, pure, puim, zrow, hre, him, zv, interleaved = refs[-12:]
     number = image.shape[1]
     tiles, kinds3, capacity = lanes.shape
     slots = tiles * capacity
@@ -268,15 +287,16 @@
             wre[to, :] = i_re * g_re - i_im * g_im
             wim[to, :] = i_re * g_im + i_im * g_re
 
-    lane = lax.broadcasted_iota(jnp.int32, (8, 256), 1)
-    inner = (lane // 32) % 4
-    masks = [inner == j for j in range(4)]
     unroll = 16
 
     def one(g):
         at = pl.ds(pl.multiple_of(g * 8, 8), 8)
-        w = jnp.concatenate([wre[at, :], wim[at, :]], axis=1)
-        lhs = jnp.concatenate([jnp.where(k, w, 0.0) for k in masks], axis=0).astype(BF16)
+        w_re, w_im = wre[at, :], wim[at, :]
+        lhs = [
+            jnp.concatenate([w_re[:, n : n + 32], w_im[:, n : n + 32]], axis=1)
+            for n in range(0, 128, 32)
+        ]
+        lhs = jnp.concatenate(lhs, axis=0).astype(BF16)
         p_re, p_im = pure[at, :], puim[at, :]
         z = [jnp.broadcast_to(zrow[k, pl.ds(g, 1), :], (8, 128)) for k in range(6)]
         rr, ii, ri, ir = p_re * z[0], p_im * z[1], p_re * z[1], p_im * z[0]
@@ -288,7 +308,7 @@
         s = jnp.concatenate([lo_im, dn_im, p_im, up_im], axis=0).astype(BF16)
         top = jnp.concatenate([c, s], axis=1)
         low = jnp.concatenate([-s, c], axis=1)
-        rhs = jnp.concatenate([top] * 4 + [low] * 4, axis=0)
+        rhs = jnp.concatenate([top, low], axis=0)
         out = dot(lhs, rhs)
         h_re, h_im = out[24:32, :128], out[24:32, 128:]
         for j in (2, 1, 0):
@@ -316,7 +336,31 @@
     sent = dot(back[...], models)
     interleaved[pl.ds(0, slots, stride=2), :] = sent[:, :128]
     interleaved[pl.ds(1, slots, stride=2), :] = sent[:, 128:]
-    payload[...] = interleaved[...].astype(BF16)
+    along_z, in_plane = refs[: tiles // 4], refs[tiles // 4 : tiles // 4 + 4]
+    for r in range(tiles // 4):
+        for p in range(4):
+            start = pl.multiple_of((mine ^ (4 * r + p)) * (2 * capacity), capacity)
+            along_z[r][p] = interleaved[pl.ds(start, capacity), :].astype(BF16)
+            in_plane[p][r] = interleaved[pl.ds(start + capacity, capacity), :].astype(BF16)
+
+
+def turn_kernel(*refs):
+    count = refs[0].shape[0]
+    blocks, out = refs[:-count], refs[-count:]
+    for i, block in enumerate(blocks):
+        for j in range(count):
+            out[j][i] = block[j]
+
+
+def residual_kernel(me, observed, *refs):
+    arrived, residual = refs[:-1], refs[-1]
+    by_plane, by_z = arrived[:4], arrived[4:]
+    rows = by_plane[0].shape[1]
+    for r in range(len(by_z)):
+        for p in range(4):
+            source = me[0] ^ (4 * r + p)
+            residual[source, :rows, :] = observed[source, :rows, :] - by_plane[p][r].astype(F32)
+            residual[source, rows:, :] = observed[source, rows:, :] - by_z[r][p].astype(F32)
 
 
 def exchange(value, step, tiles):
@@ -351,68 +395,85 @@
     own_rows = beam_coefs.shape[0] * slot_count
     smem = pl.BlockSpec(memory_space=pltpu.SMEM)
     anywhere = pl.BlockSpec(memory_space=pl.ANY)
+    hbm = pl.BlockSpec(memory_space=pltpu.HBM)
     outer = tiles // 4
     me = lax.axis_index("tile").astype(jnp.int32).reshape(1)
     block = jax.ShapeDtypeStruct((2 * own_rows + 12 * steps, 128), BF16)
     packed = pl.pallas_call(
         pack_kernel,
         out_shape=[block] * outer,
-        in_specs=[smem, vmem, vmem],
+        in_specs=[smem, hbm, hbm],
         out_specs=[vmem] * outer,
+        scratch_shapes=[
+            pltpu.VMEM((own_rows, terms2), BF16),
+            pltpu.VMEM((tiles, 2 * steps, capacity), F32),
+            pltpu.SemaphoreType.DMA((2,)),
+        ],
+        compiler_params=pltpu.CompilerParams(vmem_limit_bytes=2 * MIB * (1 + tiles // 16)),
         name="pack",
     )(me, beam_coefs.reshape(own_rows, terms2), own_tracks)
     along = [packed[0]] + [exchange(packed[r], 4 * r, tiles) for r in range(1, outer)]
 
     cells = jnp.transpose(subgrids.reshape(number, 2, 8, 128), (0, 2, 1, 3))
     cells = cells.reshape(number * 16, 128)
-    basis = jnp.transpose(
-        beam_basis.reshape(2, terms2 // 2, 4, 8, edge), (0, 1, 3, 2, 4)
-    ).reshape(2, terms2 // 2, pixels)
-    high, rest = transform_matrices(edge)
-    image, route, back, pick, weights = pl.pallas_call(
+    row_turns, cell_turns = transform_tables(edge)
+    image = pl.pallas_call(
+        transform_kernel,
+        out_shape=jax.ShapeDtypeStruct((8, number, 256), BF16),
+        in_specs=[hbm] + [vmem] * 2,
+        out_specs=vmem,
+        scratch_shapes=[
+            pltpu.VMEM((number * 16, 128), BF16),
+            pltpu.VMEM((8, 256, 256), BF16),
+            pltpu.VMEM((8, 256, 256), BF16),
+            pltpu.VMEM((number * 16, 128), F32),
+            pltpu.VMEM((8, number, 512), BF16),
+            pltpu.SemaphoreType.DMA,
+        ],
+        compiler_params=pltpu.CompilerParams(vmem_limit_bytes=14 * MIB),
+        name="transform",
+    )(cells, jnp.asarray(row_turns), jnp.asarray(cell_turns))
+
+    near = pl.pallas_call(
+        stack_kernel,
+        out_shape=jax.ShapeDtypeStruct((outer,) + block.shape, BF16),
+        in_specs=[vmem] * outer + [anywhere],
+        out_specs=vmem,
+        compiler_params=pltpu.CompilerParams(vmem_limit_bytes=2 * MIB * (tiles // 16)),
+        name="stack",
+    )(*along, image)
+    over_y = exchange(near, 2, tiles)
+    over_core = exchange(near, 1, tiles)
+    over_both = exchange(over_y, 1, tiles)
+
+    route, back, pick, weights = pl.pallas_call(
         functools.partial(prepare_kernel, slot_count=slot_count),
         out_shape=[
-            jax.ShapeDtypeStruct((8, number, 256), BF16),
             jax.ShapeDtypeStruct((number, slots), BF16),
             jax.ShapeDtypeStruct((slots, number), BF16),
             jax.ShapeDtypeStruct((2 * number, tiles * own_rows), BF16),
             jax.ShapeDtypeStruct((8, terms2, 256), BF16),
         ],
-        in_specs=[smem] + [vmem] * 7,
-        out_specs=[vmem] * 5,
-        scratch_shapes=[
-            pltpu.VMEM((number * 16, 128), F32),
-            pltpu.VMEM((8, number, 512), BF16),
-        ],
-        compiler_params=pltpu.CompilerParams(vmem_limit_bytes=24 * 1024 * 1024),
+        in_specs=[smem] + [vmem] * 4 + [anywhere],
+        out_specs=[vmem] * 4,
+        compiler_params=pltpu.CompilerParams(vmem_limit_bytes=8 * MIB * (1 + tiles // 64)),
         name="prepare",
     )(
         counts,
-        cells,
-        jnp.asarray(high),
-        jnp.asarray(rest),
         assign[0],
         stations.T,
         time_slots.reshape(1, number),
-        basis,
+        beam_basis,
+        near,
     )
 
-    near = pl.pallas_call(
-        stack_kernel,
-        out_shape=jax.ShapeDtypeStruct((outer,) + block.shape, BF16),
-        in_specs=[vmem] * outer + [anywhere],
-        out_specs=vmem,
-        name="stack",
-    )(*along, image)
-    over_y = exchange(near, 2, tiles)
-    over_core = exchange(near, 1, tiles)
-    over_both = exchange(over_y, 1, tiles)
-
-    payload = pl.pallas_call(
+    for_z = jax.ShapeDtypeStruct((4, capacity, vis), BF16)
+    for_plane = jax.ShapeDtypeStruct((outer, capacity, vis), BF16)
+    models = pl.pallas_call(
         predict_kernel,
-        out_shape=jax.ShapeDtypeStruct((2 * slots, vis), BF16),
+        out_shape=[for_z] * outer + [for_plane] * 4,
         in_specs=[smem] + [vmem] * 10,
-        out_specs=vmem,
+        out_specs=[vmem] * (outer + 4),
         scratch_shapes=[
             pltpu.VMEM((tiles * own_rows, terms2), BF16),
             pltpu.VMEM((tiles, 6 * steps, capacity), F32),
@@ -427,7 +488,7 @@
             pltpu.VMEM((2, number, vis), F32),
             pltpu.VMEM((2 * slots, vis), F32),
         ],
-        compiler_params=pltpu.CompilerParams(vmem_limit_bytes=VMEM_LIMIT),
+        compiler_params=pltpu.CompilerParams(vmem_limit_bytes=20 * MIB * (1 + tiles // 64)),
         name="predict",
     )(
         me,
@@ -442,10 +503,32 @@
         frequencies.reshape(1, chan),
         image,
     )
-    arrived = lax.all_to_all(
-        payload.reshape(tiles, 2 * capacity, vis), "tile", split_axis=0, concat_axis=0, tiled=True
-    )
-    return observed - arrived.reshape(observed.shape).astype(F32)
+    def turned(blocks, out_shape):
+        return pl.pallas_call(
+            turn_kernel,
+            out_shape=out_shape,
+            in_specs=[vmem] * len(blocks),
+            out_specs=[vmem] * len(out_shape),
+            compiler_params=pltpu.CompilerParams(vmem_limit_bytes=2 * MIB),
+            name="turn",
+        )(*blocks)
+
+    first, second = models[:outer], models[outer:]
+    second = [second[0]] + [exchange(second[p], p, tiles) for p in range(1, 4)]
+    first = [first[0]] + [exchange(first[r], 4 * r, tiles) for r in range(1, outer)]
+    second = turned(second, [for_z] * outer)
+    second = [second[0]] + [exchange(second[r], 4 * r, tiles) for r in range(1, outer)]
+    first = turned(first, [for_plane] * 4)
+    first = [first[0]] + [exchange(first[p], p, tiles) for p in range(1, 4)]
+    residual = pl.pallas_call(
+        residual_kernel,
+        out_shape=jax.ShapeDtypeStruct((tiles, 2 * capacity, vis), F32),
+        in_specs=[smem] + [vmem] * (5 + outer),
+        out_specs=vmem,
+        compiler_params=pltpu.CompilerParams(vmem_limit_bytes=6 * MIB),
+        name="residual",
+    )(me, observed.reshape(tiles, 2 * capacity, vis), *first, *second)
+    return residual.reshape(observed.shape)
 
 
 def solution(mesh):

time: 64.3 us -> 51.9 us (0.81)
  blocking collectives: 20.3 us -> 0 us
  starting transfers between devices: 7.36 us -> 20 us
  waiting for transfers between devices: 5.62 us -> 13.9 us
  local copies, waits for them, and re-layouts: 12.2 us -> 4.16 us
  Pallas kernels: 17.1 us -> 13.4 us
  other arithmetic: 1.08 us -> 0 us
    all_to_all x1 -> x0, blocking collectives: 20.3 us -> none  [per_device(): lax.all_to_all(payload.reshape(tiles, 2 * capacity, vis), 'tile', split_a...]
    ppermute x6 -> x18, starting transfers between devices: 7.36 us -> 20 us  [exchange(): return lax.ppermute(value, 'tile', [(i, i ^ step) for i in range(tiles)])]
    ppermute x6 -> x18, waiting for transfers between devices: 5.62 us -> 13.9 us  [exchange(): return lax.ppermute(value, 'tile', [(i, i ^ step) for i in range(tiles)])]
    unnamed x39 -> x24, local copies, waits for them, and re-layouts: 11.9 us -> 4.16 us
    pallas_call x1, Pallas kernels: 1.53 us -> 0.01 us  [per_device(): pl.pallas_call(stack_kernel, out_shape=jax.ShapeDtypeStruct((outer,) + bl...]
    pallas_call x1, Pallas kernels: 2.8 us -> 1.58 us  [per_device(): pl.pallas_call(functools.partial(prepare_kernel, slot_count=slot_count),...]
    sub x1 -> x0, other arithmetic: 1.08 us -> none  [per_device(): return observed - arrived.reshape(observed.shape).astype(F32)]
    pallas_call x2 -> x6, Pallas kernels: 12.7 us -> 11.8 us  [the longest x1 8.01 us: per_device(): pl.pallas_call(predict_kernel, out_shape=[for_z] * outer + [for_plane] *...]
  transfers between devices with their start and end apart: 6 -> 18, of which waited for: 2 -> 4; matrix products, arithmetic and copies ran while one was open for 2% -> 0% of each run, Pallas kernels for 4% -> 8%
where the time goes in v6:
time: 51.9 us; the launch traced here: 51.6 us
  starting transfers between devices  20 us (39%)
  waiting for transfers between devices  13.9 us (27%)
  Pallas kernels  13.4 us (26%)
  local copies, waits for them, and re-layouts  4.16 us (8%)
    ppermute x18, starting transfers between devices, exchange(): return lax.ppermute(value, 'tile', [(i, i ^ step) for i in range(tiles)])  20 us
    ppermute x18, waiting for transfers between devices, exchange(): return lax.ppermute(value, 'tile', [(i, i ^ step) for i in range(tiles)])  13.9 us
    pallas_call x1, Pallas kernels, per_device(): pl.pallas_call(predict_kernel, out_shape=[for_z] * outer + [for_plane] *...  8.01 us
    unnamed x24, local copies, waits for them, and re-layouts  4.16 us
    pallas_call x1, Pallas kernels, per_device(): pl.pallas_call(transform_kernel, out_shape=jax.ShapeDtypeStruct((8, numbe...  2.47 us
    pallas_call x1, Pallas kernels, per_device(): pl.pallas_call(functools.partial(prepare_kernel, slot_count=slot_count),...  1.58 us
    pallas_call x1, Pallas kernels, per_device(): pl.pallas_call(residual_kernel, out_shape=jax.ShapeDtypeStruct((tiles, 2...  1.06 us
  transfers between devices with their start and end apart: 18, of which 4 were waited for; matrix products, arithmetic and copies ran while one was open for 0% of the time, Pallas kernels for 8%

profile of v6, /device:TPU:0, one launch (start us, length us, event | category | flops | bytes accessed | tf_op | source)
XLA Modules:
  0.0 51.6 jit_solution(13006533288093032220)
XLA Ops:
  0.0 0.0 copy-start.3
  0.0 0.8 %copy-done.3 = f32[1,16,64,2,4]{2,4,3,1,0:T(4,128)S(1)} copy-done((f32[1,16,64,2,4]{2,4,3,1,0:T(4,128)S(1)}, f32[1,16,64,2,4]{2,4,3,1,0:T(4,128)}, u32[]{:S(2)}) %copy-start.3) | copy-done | bytes 32792
  0.8 0.0 copy-start.6
  0.8 0.8 %copy-done.6 = bf16[8,8,256]{2,1,0:T(8,128)(2,1)S(1)} copy-done((bf16[8,8,256]{2,1,0:T(8,128)(2,1)S(1)}, bf16[8,8,256]{2,1,0:T(8,128)(2,1)}, u32[]{:S(2)}) %copy-start.6) | copy-done | bytes 32792
  1.6 0.0 copy-start.4
  1.6 0.0 copy-start.5
  1.6 0.2 pack.1
  1.8 3.1 %collective-permute-start = (bf16[176,128]{1,0:T(8,128)(2,1)S(1)}, bf16[176,128]{1,0:T(8,128)(2,1)S(1)}, u32[]{:S(2)}, u32[]{:S(2)}) collective-permute-start(bf16[176,128]{1,0:T(8,128)(2,1)S(1)} %get-tuple-element.30), channel_id=1, source_target_pairs={{0,4},{1,5},{2,6},{3,7},{4,0},{5,1},{6,2},{7,3},{8,12},{9,13},{10,... | collective-permute-start | bytes 135176 | tf_op jit(solution)/shard_map/ppermute | solution.py:367
  4.9 2.6 %collective-permute-start.1 = (bf16[176,128]{1,0:T(8,128)(2,1)S(1)}, bf16[176,128]{1,0:T(8,128)(2,1)S(1)}, u32[]{:S(2)}, u32[]{:S(2)}) collective-permute-start(bf16[176,128]{1,0:T(8,128)(2,1)S(1)} %get-tuple-element.31), channel_id=1, source_target_pairs={{0,8},{1,9},{2,10},{3,11},{4,12},{5,13},{6,14},{7,15},{8,0},{9,1},... | collective-permute-start | bytes 135176 | tf_op jit(solution)/shard_map/ppermute | solution.py:367
  7.5 0.0 collective-permute-start.2
  7.5 0.0 copy-done.4
  7.5 0.0 copy-done.5
  7.5 0.0 copy-start
  7.5 1.2 %copy-done = bf16[256,2,1024]{2,1,0:T(2,128)(2,1)S(1)} copy-done((bf16[256,2,1024]{2,1,0:T(2,128)(2,1)S(1)}, bf16[256,2,1024]{2,1,0:T(2,128)(2,1)}, u32[]{:S(2)}) %copy-start) | copy-done | bytes 1048600
  8.8 2.5 %transform.1.refs_4_.image = bf16[8,256,256]{2,1,0:T(8,128)(2,1)S(1)} custom-call(bf16[4096,128]{1,0:T(8,128)(2,1)S(1)} %bitcast.18, f32[2,32,128]{2,1,0:T(8,128)S(1)} %copy-done.5, f32[2,32,128]{2,1,0:T(8,128)S(1)} %copy-done.4), custom_call_target="tpu_custom_call" | custom-call | tf_op jit(solution)/shard_map/transform/pallas_call | solution.py:420
  11.2 0.0 collective-permute-done.refs_1_
  11.2 0.0 collective-permute-done.1.refs_2_
  11.3 2.1 %collective-permute-done.2.refs_3_ = bf16[176,128]{1,0:T(8,128)(2,1)S(1)} collective-permute-done((bf16[176,128]{1,0:T(8,128)(2,1)S(1)}, bf16[176,128]{1,0:T(8,128)(2,1)S(1)}, u32[]{:S(2)}, u32[]{:S(2)}) %collective-permute-start.2) | collective-permute-done | bytes 45088 | tf_op jit(solution)/shard_map/ppermute | solution.py:367
  13.4 0.0 copy-start.2
  13.4 0.0 copy-start.7
  13.4 1.6 %collective-permute-start.3 = (bf16[4,176,128]{2,1,0:T(8,128)(2,1)S(1)}, bf16[4,176,128]{2,1,0:T(8,128)(2,1)S(1)}, u32[]{:S(2)}, u32[]{:S(2)}) collective-permute-start(bf16[4,176,128]{2,1,0:T(8,128)(2,1)S(1)} %stack.1.after.near), channel_id=1, source_target_pairs={{0,2},{1,3},{2,0},{3,1},{4,6},{5,7},{6,4},{7,5},{8,10},{9,11},{10,... | collective-permute-start | bytes 540680 | tf_op jit(solution)/shard_map/ppermute | solution.py:367
  15.0 0.0 collective-permute-start.4
  15.0 4.0 %collective-permute-done.3.over_y = bf16[4,176,128]{2,1,0:T(8,128)(2,1)S(1)} collective-permute-done((bf16[4,176,128]{2,1,0:T(8,128)(2,1)S(1)}, bf16[4,176,128]{2,1,0:T(8,128)(2,1)S(1)}, u32[]{:S(2)}, u32[]{:S(2)}) %collective-permute-start.3) | collective-permute-done | bytes 180256 | tf_op jit(solution)/shard_map/ppermute | solution.py:367
  18.9 0.0 collective-permute-start.5
  18.9 0.0 copy-start.8
  18.9 0.0 copy-start.10
  19.0 0.0 copy-done.2
  19.0 0.0 copy-done.7
  19.0 0.7 %copy-done.8 = s32[256,2]{0,1:T(2,128)S(1)} copy-done((s32[256,2]{0,1:T(2,128)S(1)}, s32[256,2]{0,1:T(2,128)}, u32[]{:S(2)}) %copy-start.8) | copy-done | bytes 2072
  19.6 0.0 copy-done.9
  19.6 0.0 copy-done.10
  19.6 1.6 %prepare.1 = (bf16[256,1024]{1,0:T(8,128)(2,1)S(1)}, bf16[1024,256]{1,0:T(8,128)(2,1)S(1)}, bf16[512,1024]{1,0:T(8,128)(2,1)S(1)}, bf16[8,256,256]{2,1,0:T(8,128)(2,1)S(1)}) custom-call(s32[1,16]{1,0:T(1,128)S(1)} %copy-done.10, s32[16,64]{1,0:T(8,128)S(1)} %bitcast.22, s32[2,256]{1,0:T(2,128)S(1)} %bitcast.23, s32[1,256]{1,0:T(1,128)S(1)} %bitcast.24, ...), custom_call_target="tpu_custom_call" | custom-call | tf_op jit(solution)/shard_map/prepare/pallas_call | solution.py:449
  21.2 0.0 collective-permute-done.4.over_core
  21.2 0.0 collective-permute-done.5.over_both
  21.2 0.0 copy-start.11
  21.3 0.6 %copy-done.11 = f32[32]{0:T(128)S(1)} copy-done((f32[32]{0:T(128)S(1)}, f32[32]{0:T(128)}, u32[]{:S(2)}) %copy-start.11) | copy-done | bytes 152
  21.9 0.0 copy-start.1
  21.9 8.0 %predict.1 = (bf16[4,64,128]{2,1,0:T(8,128)(2,1)S(1)}, bf16[4,64,128]{2,1,0:T(8,128)(2,1)S(1)}, bf16[4,64,128]{2,1,0:T(8,128)(2,1)S(1)}, bf16[4,64,128]{2,1,0:T(...) custom-call(s32[1]{0:T(128)} %bitcast.me, ...), custom_call_target="tpu_custom_call" | custom-call | tf_op jit(solution)/shard_map/predict/pallas_call | solution.py:472
  29.9 0.1 collective-permute-start.6
  30.0 2.3 %collective-permute-start.7 = (bf16[4,64,128]{2,1,0:T(8,128)(2,1)S(1)}, bf16[4,64,128]{2,1,0:T(8,128)(2,1)S(1)}, u32[]{:S(2)}, u32[]{:S(2)}) collective-permute-start(bf16[4,64,128]{2,1,0:T(8,128)(2,1)S(1)} %get-tuple-element.39), channel_id=1, source_target_pairs={{0,8},{1,9},{2,10},{3,11},{4,12},{5,13},{6,14},{7,15},{8,0},{9,1},... | collective-permute-start | bytes 196616 | tf_op jit(solution)/shard_map/ppermute | solution.py:367
  32.3 2.1 %collective-permute-start.8 = (bf16[4,64,128]{2,1,0:T(8,128)(2,1)S(1)}, bf16[4,64,128]{2,1,0:T(8,128)(2,1)S(1)}, u32[]{:S(2)}, u32[]{:S(2)}) collective-permute-start(bf16[4,64,128]{2,1,0:T(8,128)(2,1)S(1)} %get-tuple-element.40), channel_id=1, source_target_pairs={{0,12},{1,13},{2,14},{3,15},{4,8},{5,9},{6,10},{7,11},{8,4},{9,5},... | collective-permute-start | bytes 196616 | tf_op jit(solution)/shard_map/ppermute | solution.py:367
  34.4 0.0 collective-permute-start.12
  34.4 1.5 %collective-permute-start.13 = (bf16[4,64,128]{2,1,0:T(8,128)(2,1)S(1)}, bf16[4,64,128]{2,1,0:T(8,128)(2,1)S(1)}, u32[]{:S(2)}, u32[]{:S(2)}) collective-permute-start(bf16[4,64,128]{2,1,0:T(8,128)(2,1)S(1)} %get-tuple-element.47), channel_id=1, source_target_pairs={{0,2},{1,3},{2,0},{3,1},{4,6},{5,7},{6,4},{7,5},{8,10},{9,11},{10,... | collective-permute-start | bytes 196616 | tf_op jit(solution)/shard_map/ppermute | solution.py:367
  35.9 0.0 collective-permute-done.6.refs_1_
  35.9 0.3 collective-permute-start.14
  36.2 2.5 %collective-permute-done.7.refs_2_ = bf16[4,64,128]{2,1,0:T(8,128)(2,1)S(1)} collective-permute-done((bf16[4,64,128]{2,1,0:T(8,128)(2,1)S(1)}, bf16[4,64,128]{2,1,0:T(8,128)(2,1)S(1)}, u32[]{:S(2)}, u32[]{:S(2)}) %collective-permute-start.7) | collective-permute-done | bytes 65568 | tf_op jit(solution)/shard_map/ppermute | solution.py:367
  38.7 0.0 collective-permute-done.8.refs_3_
  38.7 0.1 collective-permute-start.9
  38.8 1.6 %collective-permute-start.10 = (bf16[4,64,128]{2,1,0:T(8,128)(2,1)S(1)}, bf16[4,64,128]{2,1,0:T(8,128)(2,1)S(1)}, u32[]{:S(2)}, u32[]{:S(2)}) collective-permute-start(bf16[4,64,128]{2,1,0:T(8,128)(2,1)S(1)} %get-tuple-element.43), channel_id=1, source_target_pairs={{0,2},{1,3},{2,0},{3,1},{4,6},{5,7},{6,4},{7,5},{8,10},{9,11},{10,... | collective-permute-start | bytes 196616 | tf_op jit(solution)/shard_map/ppermute | solution.py:367
  40.4 0.0 collective-permute-done.12.refs_1_
  40.4 0.3 collective-permute-start.11
  40.7 0.0 collective-permute-done.13.refs_2_
  40.7 0.0 collective-permute-done.14.refs_3_
  40.7 1.7 %collective-permute-start.15 = (bf16[4,64,128]{2,1,0:T(8,128)(2,1)S(1)}, bf16[4,64,128]{2,1,0:T(8,128)(2,1)S(1)}, u32[]{:S(2)}, u32[]{:S(2)}) collective-permute-start(bf16[4,64,128]{2,1,0:T(8,128)(2,1)S(1)} %get-tuple-element.50), channel_id=1, source_target_pairs={{0,4},{1,5},{2,6},{3,7},{4,0},{5,1},{6,2},{7,3},{8,12},{9,13},{10,... | collective-permute-start | bytes 196616 | tf_op jit(solution)/shard_map/ppermute | solution.py:367
  42.4 0.7 %collective-permute-start.16 = (bf16[4,64,128]{2,1,0:T(8,128)(2,1)S(1)}, bf16[4,64,128]{2,1,0:T(8,128)(2,1)S(1)}, u32[]{:S(2)}, u32[]{:S(2)}) collective-permute-start(bf16[4,64,128]{2,1,0:T(8,128)(2,1)S(1)} %get-tuple-element.51), channel_id=1, source_target_pairs={{0,8},{1,9},{2,10},{3,11},{4,12},{5,13},{6,14},{7,15},{8,0},{9,1},... | collective-permute-start | bytes 196616 | tf_op jit(solution)/shard_map/ppermute | solution.py:367
  43.1 0.0 collective-permute-done.9.refs_1_
  43.1 2.1 %collective-permute-start.17 = (bf16[4,64,128]{2,1,0:T(8,128)(2,1)S(1)}, bf16[4,64,128]{2,1,0:T(8,128)(2,1)S(1)}, u32[]{:S(2)}, u32[]{:S(2)}) collective-permute-start(bf16[4,64,128]{2,1,0:T(8,128)(2,1)S(1)} %get-tuple-element.52), channel_id=1, source_target_pairs={{0,12},{1,13},{2,14},{3,15},{4,8},{5,9},{6,10},{7,11},{8,4},{9,5},... | collective-permute-start | bytes 196616 | tf_op jit(solution)/shard_map/ppermute | solution.py:367
  45.2 0.0 collective-permute-done.10.refs_2_
  45.2 0.0 collective-permute-done.11.refs_3_
  45.2 0.0 collective-permute-done.15.refs_5_
  45.2 5.4 %collective-permute-done.16.refs_6_ = bf16[4,64,128]{2,1,0:T(8,128)(2,1)S(1)} collective-permute-done((bf16[4,64,128]{2,1,0:T(8,128)(2,1)S(1)}, bf16[4,64,128]{2,1,0:T(8,128)(2,1)S(1)}, u32[]{:S(2)}, u32[]{:S(2)}) %collective-permute-start.16) | collective-permute-done | bytes 65568 | tf_op jit(solution)/shard_map/ppermute | solution.py:367
  50.5 0.0 collective-permute-done.17.refs_7_
  50.5 0.0 copy-done.1
  50.5 1.1 %residual.1 = f32[16,128,128]{2,1,0:T(8,128)} custom-call(s32[1]{0:T(128)} %bitcast.me, f32[16,128,128]{2,1,0:T(8,128)S(1)} %bitcast.19, bf16[4,64,128]{2,1,0:T(8,128)(2,1)S(1)} %get-tuple-element.41.refs_0_, bf16[4,64,128]{2,1,0:T(8,128)(2,1)S(1)} %collective-permute-done.9.refs_1_, bf16[4,64,128]{2,1,0:T(8,128)(2,1)S(1)} %collective-permute-done.10.refs_2_, ...), custom_call_target="tpu_custom_call" | custom-call | tf_op jit(solution)/shard_map/residual/pallas_call | solution.py:523
  (4 shorter events, 0.0 us)
Async XLA Ops:
  0.0 0.8 %copy-start.3 = (f32[1,16,64,2,4]{2,4,3,1,0:T(4,128)S(1)}, f32[1,16,64,2,4]{2,4,3,1,0:T(4,128)}, u32[]{:S(2)}) copy-start(f32[1,16,64,2,4]{2,4,3,1,0:T(4,128)} %param.20) | copy-start | bytes 98308
  0.8 0.8 %copy-start.6 = (bf16[8,8,256]{2,1,0:T(8,128)(2,1)S(1)}, bf16[8,8,256]{2,1,0:T(8,128)(2,1)}, u32[]{:S(2)}) copy-start(bf16[8,8,256]{2,1,0:T(8,128)(2,1)} %param.17) | copy-start | bytes 98308
  1.6 5.9 %copy-start.4 = (f32[2,32,128]{2,1,0:T(8,128)S(1)}, f32[2,32,128]{2,1,0:T(8,128)}, u32[]{:S(2)}) copy-start(f32[2,32,128]{2,1,0:T(8,128)} %constant.9.clone.cell_turns) | copy-start | bytes 98308
  1.6 5.9 %copy-start.5 = (f32[2,32,128]{2,1,0:T(8,128)S(1)}, f32[2,32,128]{2,1,0:T(8,128)}, u32[]{:S(2)}) copy-start(f32[2,32,128]{2,1,0:T(8,128)} %constant.8.clone.row_turns) | copy-start | bytes 98308
  1.8 9.4 %collective-permute-start = (bf16[176,128]{1,0:T(8,128)(2,1)S(1)}, bf16[176,128]{1,0:T(8,128)(2,1)S(1)}, u32[]{:S(2)}, u32[]{:S(2)}) collective-permute-start(bf16[176,128]{1,0:T(8,128)(2,1)S(1)} %get-tuple-element.30), channel_id=1, source_target_pairs={{0,4},{1,5},{2,6},{3,7},{4,0},{5,1},{6,2},{7,3},{8,12},{9,13},{10,... | collective-permute-start | bytes 135176 | tf_op jit(solution)/shard_map/ppermute | solution.py:367
  4.9 6.3 %collective-permute-start.1 = (bf16[176,128]{1,0:T(8,128)(2,1)S(1)}, bf16[176,128]{1,0:T(8,128)(2,1)S(1)}, u32[]{:S(2)}, u32[]{:S(2)}) collective-permute-start(bf16[176,128]{1,0:T(8,128)(2,1)S(1)} %get-tuple-element.31), channel_id=1, source_target_pairs={{0,8},{1,9},{2,10},{3,11},{4,12},{5,13},{6,14},{7,15},{8,0},{9,1},... | collective-permute-start | bytes 135176 | tf_op jit(solution)/shard_map/ppermute | solution.py:367
  7.5 5.8 %collective-permute-start.2 = (bf16[176,128]{1,0:T(8,128)(2,1)S(1)}, bf16[176,128]{1,0:T(8,128)(2,1)S(1)}, u32[]{:S(2)}, u32[]{:S(2)}) collective-permute-start(bf16[176,128]{1,0:T(8,128)(2,1)S(1)} %get-tuple-element.32), channel_id=1, source_target_pairs={{0,12},{1,13},{2,14},{3,15},{4,8},{5,9},{6,10},{7,11},{8,4},{9,5},... | collective-permute-start | bytes 135176 | tf_op jit(solution)/shard_map/ppermute | solution.py:367
  7.5 1.2 %copy-start = (bf16[256,2,1024]{2,1,0:T(2,128)(2,1)S(1)}, bf16[256,2,1024]{2,1,0:T(2,128)(2,1)}, u32[]{:S(2)}) copy-start(bf16[256,2,1024]{2,1,0:T(2,128)(2,1)} %param.12) | copy-start | bytes 3145732
  13.4 5.6 %copy-start.2 = (bf16[2,128,1024]{2,1,0:T(8,128)(2,1)S(1)}, bf16[2,128,1024]{2,1,0:T(8,128)(2,1)}, u32[]{:S(2)}) copy-start(bf16[2,128,1024]{2,1,0:T(8,128)(2,1)} %basis.1) | copy-start | bytes 1572868
  13.4 5.6 %copy-start.7 = (s32[1,16,64]{2,1,0:T(8,128)S(1)}, s32[1,16,64]{2,1,0:T(8,128)}, u32[]{:S(2)}) copy-start(s32[1,16,64]{2,1,0:T(8,128)} %param.15) | copy-start | bytes 12292
  13.4 5.6 %collective-permute-start.3 = (bf16[4,176,128]{2,1,0:T(8,128)(2,1)S(1)}, bf16[4,176,128]{2,1,0:T(8,128)(2,1)S(1)}, u32[]{:S(2)}, u32[]{:S(2)}) collective-permute-start(bf16[4,176,128]{2,1,0:T(8,128)(2,1)S(1)} %stack.1.after.near), channel_id=1, source_target_pairs={{0,2},{1,3},{2,0},{3,1},{4,6},{5,7},{6,4},{7,5},{8,10},{9,11},{10,... | collective-permute-start | bytes 540680 | tf_op jit(solution)/shard_map/ppermute | solution.py:367
  15.0 6.3 %collective-permute-start.4 = (bf16[4,176,128]{2,1,0:T(8,128)(2,1)S(1)}, bf16[4,176,128]{2,1,0:T(8,128)(2,1)S(1)}, u32[]{:S(2)}, u32[]{:S(2)}) collective-permute-start(bf16[4,176,128]{2,1,0:T(8,128)(2,1)S(1)} %stack.1.after.near), channel_id=1, source_target_pairs={{0,1},{1,0},{2,3},{3,2},{4,5},{5,4},{6,7},{7,6},{8,9},{9,8},{10,11... | collective-permute-start | bytes 540680 | tf_op jit(solution)/shard_map/ppermute | solution.py:367
  18.9 2.3 %collective-permute-start.5 = (bf16[4,176,128]{2,1,0:T(8,128)(2,1)S(1)}, bf16[4,176,128]{2,1,0:T(8,128)(2,1)S(1)}, u32[]{:S(2)}, u32[]{:S(2)}) collective-permute-start(bf16[4,176,128]{2,1,0:T(8,128)(2,1)S(1)} %collective-permute-done.3.over_y), channel_id=1, source_target_pairs={{0,1},{1,0},{2,3},{3,2},{4,5},{5,4},{6,7},{7,6},{8,9},{9,8},{10,11... | collective-permute-start | bytes 540680 | tf_op jit(solution)/shard_map/ppermute | solution.py:367
  18.9 0.7 %copy-start.8 = (s32[256,2]{0,1:T(2,128)S(1)}, s32[256,2]{0,1:T(2,128)}, u32[]{:S(2)}) copy-start(s32[256,2]{0,1:T(2,128)} %param.13) | copy-start | bytes 6148
  18.9 0.7 %copy-start.9 = (s32[256]{0:T(256)S(1)}, s32[256]{0:T(256)}, u32[]{:S(2)}) copy-start(s32[256]{0:T(256)} %param.14) | copy-start | bytes 3076
  18.9 0.7 %copy-start.10 = (s32[1,16]{1,0:T(1,128)S(1)}, s32[1,16]{1,0:T(1,128)}, u32[]{:S(2)}) copy-start(s32[1,16]{1,0:T(1,128)} %counts.1) | copy-start | bytes 196
  21.2 0.7 %copy-start.11 = (f32[32]{0:T(128)S(1)}, f32[32]{0:T(128)}, u32[]{:S(2)}) copy-start(f32[32]{0:T(128)} %param.19) | copy-start | bytes 388
  21.9 28.6 %copy-start.1 = (f32[1,16,64,2,128]{4,3,2,1,0:T(2,128)S(1)}, f32[1,16,64,2,128]{4,3,2,1,0:T(2,128)}, u32[]{:S(2)}) copy-start(f32[1,16,64,2,128]{4,3,2,1,0:T(2,128)} %param.21) | copy-start | bytes 3145732
  29.9 6.0 %collective-permute-start.6 = (bf16[4,64,128]{2,1,0:T(8,128)(2,1)S(1)}, bf16[4,64,128]{2,1,0:T(8,128)(2,1)S(1)}, u32[]{:S(2)}, u32[]{:S(2)}) collective-permute-start(bf16[4,64,128]{2,1,0:T(8,128)(2,1)S(1)} %get-tuple-element.38), channel_id=1, source_target_pairs={{0,4},{1,5},{2,6},{3,7},{4,0},{5,1},{6,2},{7,3},{8,12},{9,13},{10,... | collective-permute-start | bytes 196616 | tf_op jit(solution)/shard_map/ppermute | solution.py:367
  30.0 8.7 %collective-permute-start.7 = (bf16[4,64,128]{2,1,0:T(8,128)(2,1)S(1)}, bf16[4,64,128]{2,1,0:T(8,128)(2,1)S(1)}, u32[]{:S(2)}, u32[]{:S(2)}) collective-permute-start(bf16[4,64,128]{2,1,0:T(8,128)(2,1)S(1)} %get-tuple-element.39), channel_id=1, source_target_pairs={{0,8},{1,9},{2,10},{3,11},{4,12},{5,13},{6,14},{7,15},{8,0},{9,1},... | collective-permute-start | bytes 196616 | tf_op jit(solution)/shard_map/ppermute | solution.py:367
  32.3 6.4 %collective-permute-start.8 = (bf16[4,64,128]{2,1,0:T(8,128)(2,1)S(1)}, bf16[4,64,128]{2,1,0:T(8,128)(2,1)S(1)}, u32[]{:S(2)}, u32[]{:S(2)}) collective-permute-start(bf16[4,64,128]{2,1,0:T(8,128)(2,1)S(1)} %get-tuple-element.40), channel_id=1, source_target_pairs={{0,12},{1,13},{2,14},{3,15},{4,8},{5,9},{6,10},{7,11},{8,4},{9,5},... | collective-permute-start | bytes 196616 | tf_op jit(solution)/shard_map/ppermute | solution.py:367
  34.4 6.0 %collective-permute-start.12 = (bf16[4,64,128]{2,1,0:T(8,128)(2,1)S(1)}, bf16[4,64,128]{2,1,0:T(8,128)(2,1)S(1)}, u32[]{:S(2)}, u32[]{:S(2)}) collective-permute-start(bf16[4,64,128]{2,1,0:T(8,128)(2,1)S(1)} %get-tuple-element.46), channel_id=1, source_target_pairs={{0,1},{1,0},{2,3},{3,2},{4,5},{5,4},{6,7},{7,6},{8,9},{9,8},{10,11... | collective-permute-start | bytes 196616 | tf_op jit(solution)/shard_map/ppermute | solution.py:367
  34.4 6.3 %collective-permute-start.13 = (bf16[4,64,128]{2,1,0:T(8,128)(2,1)S(1)}, bf16[4,64,128]{2,1,0:T(8,128)(2,1)S(1)}, u32[]{:S(2)}, u32[]{:S(2)}) collective-permute-start(bf16[4,64,128]{2,1,0:T(8,128)(2,1)S(1)} %get-tuple-element.47), channel_id=1, source_target_pairs={{0,2},{1,3},{2,0},{3,1},{4,6},{5,7},{6,4},{7,5},{8,10},{9,11},{10,... | collective-permute-start | bytes 196616 | tf_op jit(solution)/shard_map/ppermute | solution.py:367
  35.9 4.8 %collective-permute-start.14 = (bf16[4,64,128]{2,1,0:T(8,128)(2,1)S(1)}, bf16[4,64,128]{2,1,0:T(8,128)(2,1)S(1)}, u32[]{:S(2)}, u32[]{:S(2)}) collective-permute-start(bf16[4,64,128]{2,1,0:T(8,128)(2,1)S(1)} %get-tuple-element.48), channel_id=1, source_target_pairs={{0,3},{1,2},{2,1},{3,0},{4,7},{5,6},{6,5},{7,4},{8,11},{9,10},{10,... | collective-permute-start | bytes 196616 | tf_op jit(solution)/shard_map/ppermute | solution.py:367
  38.7 4.4 %collective-permute-start.9 = (bf16[4,64,128]{2,1,0:T(8,128)(2,1)S(1)}, bf16[4,64,128]{2,1,0:T(8,128)(2,1)S(1)}, u32[]{:S(2)}, u32[]{:S(2)}) collective-permute-start(bf16[4,64,128]{2,1,0:T(8,128)(2,1)S(1)} %get-tuple-element.42), channel_id=1, source_target_pairs={{0,1},{1,0},{2,3},{3,2},{4,5},{5,4},{6,7},{7,6},{8,9},{9,8},{10,11... | collective-permute-start | bytes 196616 | tf_op jit(solution)/shard_map/ppermute | solution.py:367
  38.8 6.4 %collective-permute-start.10 = (bf16[4,64,128]{2,1,0:T(8,128)(2,1)S(1)}, bf16[4,64,128]{2,1,0:T(8,128)(2,1)S(1)}, u32[]{:S(2)}, u32[]{:S(2)}) collective-permute-start(bf16[4,64,128]{2,1,0:T(8,128)(2,1)S(1)} %get-tuple-element.43), channel_id=1, source_target_pairs={{0,2},{1,3},{2,0},{3,1},{4,6},{5,7},{6,4},{7,5},{8,10},{9,11},{10,... | collective-permute-start | bytes 196616 | tf_op jit(solution)/shard_map/ppermute | solution.py:367
  40.4 4.8 %collective-permute-start.11 = (bf16[4,64,128]{2,1,0:T(8,128)(2,1)S(1)}, bf16[4,64,128]{2,1,0:T(8,128)(2,1)S(1)}, u32[]{:S(2)}, u32[]{:S(2)}) collective-permute-start(bf16[4,64,128]{2,1,0:T(8,128)(2,1)S(1)} %get-tuple-element.44), channel_id=1, source_target_pairs={{0,3},{1,2},{2,1},{3,0},{4,7},{5,6},{6,5},{7,4},{8,11},{9,10},{10,... | collective-permute-start | bytes 196616 | tf_op jit(solution)/shard_map/ppermute | solution.py:367
  40.7 4.5 %collective-permute-start.15 = (bf16[4,64,128]{2,1,0:T(8,128)(2,1)S(1)}, bf16[4,64,128]{2,1,0:T(8,128)(2,1)S(1)}, u32[]{:S(2)}, u32[]{:S(2)}) collective-permute-start(bf16[4,64,128]{2,1,0:T(8,128)(2,1)S(1)} %get-tuple-element.50), channel_id=1, source_target_pairs={{0,4},{1,5},{2,6},{3,7},{4,0},{5,1},{6,2},{7,3},{8,12},{9,13},{10,... | collective-permute-start | bytes 196616 | tf_op jit(solution)/shard_map/ppermute | solution.py:367
  42.4 8.2 %collective-permute-start.16 = (bf16[4,64,128]{2,1,0:T(8,128)(2,1)S(1)}, bf16[4,64,128]{2,1,0:T(8,128)(2,1)S(1)}, u32[]{:S(2)}, u32[]{:S(2)}) collective-permute-start(bf16[4,64,128]{2,1,0:T(8,128)(2,1)S(1)} %get-tuple-element.51), channel_id=1, source_target_pairs={{0,8},{1,9},{2,10},{3,11},{4,12},{5,13},{6,14},{7,15},{8,0},{9,1},... | collective-permute-start | bytes 196616 | tf_op jit(solution)/shard_map/ppermute | solution.py:367
  43.1 7.4 %collective-permute-start.17 = (bf16[4,64,128]{2,1,0:T(8,128)(2,1)S(1)}, bf16[4,64,128]{2,1,0:T(8,128)(2,1)S(1)}, u32[]{:S(2)}, u32[]{:S(2)}) collective-permute-start(bf16[4,64,128]{2,1,0:T(8,128)(2,1)S(1)} %get-tuple-element.52), channel_id=1, source_target_pairs={{0,12},{1,13},{2,14},{3,15},{4,8},{5,9},{6,10},{7,11},{8,4},{9,5},... | collective-permute-start | bytes 196616 | tf_op jit(solution)/shard_map/ppermute | solution.py:367

commit v7 on v6

--- a/solution.py
+++ b/solution.py
@@ -101,9 +101,13 @@
         image[m] = dot(left, right).astype(BF16)
 
 
-def prepare_kernel(counts, assign, stations, time_slots, basis, after, route, back, pick, weights, *, slot_count):
+def prepare_kernel(
+    counts, assign, stations, time_slots, basis, freq, route, back, pick, weights, turns, *, slot_count
+):
     number = route.shape[0]
     tiles, capacity = assign.shape
+    scaled = freq[...] * (-1.0 / 32.0)
+    turns[...] = jnp.concatenate([scaled] * (turns.shape[1] // freq.shape[1]), axis=1)
 
     per = 128 // capacity
     down = lax.broadcasted_iota(jnp.int32, (number, 128), 0)
@@ -186,7 +190,7 @@
 
 
 def stack_kernel(*refs):
-    blocks, out = refs[:-2], refs[-1]
+    blocks, out = refs[:-3], refs[-1]
     for r, block in enumerate(blocks):
         out[r] = block[...]
 
@@ -201,7 +205,7 @@
     back,
     pick,
     weights,
-    freq,
+    turns,
     image,
     *refs,
 ):
@@ -210,9 +214,10 @@
     tiles, kinds3, capacity = lanes.shape
     slots = tiles * capacity
     rows_own = table.shape[0] // tiles
-    chan = freq.shape[1]
+    vis = turns.shape[1]
     kinds = kinds3 // 3
     steps = kinds // 2
+    chan = vis // steps
     mine = me[0]
 
     for arrived, flip in ((near, 0), (over_y, 2), (over_core, 1), (over_both, 3)):
@@ -241,11 +246,8 @@
     to_lane = lax.broadcasted_iota(jnp.int32, (4 * kinds, wide), 1) // chan
     spread = (from_row == to_lane).astype(F32).astype(BF16)
     uv = dot(per_sub, spread)
-    vis = steps * chan
-    fr = jnp.concatenate([freq[...]] * steps, axis=1)
-    scale = -1.0 / 32.0
-    ur, ui = unit_powers(uv[:, :vis] * fr * scale)
-    vr, vi = unit_powers(uv[:, vis:] * fr * scale)
+    ur, ui = unit_powers(uv[:, :vis] * turns[...])
+    vr, vi = unit_powers(uv[:, vis:] * turns[...])
 
     pure[pl.ds(0, number, stride=8), :] = jnp.ones_like(ur)
     puim[pl.ds(0, number, stride=8), :] = jnp.zeros_like(ur)
@@ -354,7 +356,7 @@
 
 def residual_kernel(me, observed, *refs):
     arrived, residual = refs[:-1], refs[-1]
-    by_plane, by_z = arrived[:4], arrived[4:]
+    by_z, by_plane = arrived[:-4], arrived[-4:]
     rows = by_plane[0].shape[1]
     for r in range(len(by_z)):
         for p in range(4):
@@ -409,7 +411,7 @@
             pltpu.VMEM((tiles, 2 * steps, capacity), F32),
             pltpu.SemaphoreType.DMA((2,)),
         ],
-        compiler_params=pltpu.CompilerParams(vmem_limit_bytes=2 * MIB * (1 + tiles // 16)),
+        compiler_params=pltpu.CompilerParams(vmem_limit_bytes=56 * MIB),
         name="pack",
     )(me, beam_coefs.reshape(own_rows, terms2), own_tracks)
     along = [packed[0]] + [exchange(packed[r], 4 * r, tiles) for r in range(1, outer)]
@@ -434,28 +436,17 @@
         name="transform",
     )(cells, jnp.asarray(row_turns), jnp.asarray(cell_turns))
 
-    near = pl.pallas_call(
-        stack_kernel,
-        out_shape=jax.ShapeDtypeStruct((outer,) + block.shape, BF16),
-        in_specs=[vmem] * outer + [anywhere],
-        out_specs=vmem,
-        compiler_params=pltpu.CompilerParams(vmem_limit_bytes=2 * MIB * (tiles // 16)),
-        name="stack",
-    )(*along, image)
-    over_y = exchange(near, 2, tiles)
-    over_core = exchange(near, 1, tiles)
-    over_both = exchange(over_y, 1, tiles)
-
-    route, back, pick, weights = pl.pallas_call(
+    route, back, pick, weights, turns = pl.pallas_call(
         functools.partial(prepare_kernel, slot_count=slot_count),
         out_shape=[
             jax.ShapeDtypeStruct((number, slots), BF16),
             jax.ShapeDtypeStruct((slots, number), BF16),
             jax.ShapeDtypeStruct((2 * number, tiles * own_rows), BF16),
             jax.ShapeDtypeStruct((8, terms2, 256), BF16),
+            jax.ShapeDtypeStruct((1, vis), F32),
         ],
-        in_specs=[smem] + [vmem] * 4 + [anywhere],
-        out_specs=[vmem] * 4,
+        in_specs=[smem] + [vmem] * 5,
+        out_specs=[vmem] * 5,
         compiler_params=pltpu.CompilerParams(vmem_limit_bytes=8 * MIB * (1 + tiles // 64)),
         name="prepare",
     )(
@@ -464,8 +455,20 @@
         stations.T,
         time_slots.reshape(1, number),
         beam_basis,
-        near,
+        frequencies.reshape(1, chan),
     )
+
+    near = pl.pallas_call(
+        stack_kernel,
+        out_shape=jax.ShapeDtypeStruct((outer,) + block.shape, BF16),
+        in_specs=[vmem] * outer + [anywhere] * 2,
+        out_specs=vmem,
+        compiler_params=pltpu.CompilerParams(vmem_limit_bytes=2 * MIB * (tiles // 16)),
+        name="stack",
+    )(*along, image, weights)
+    over_y = exchange(near, 2, tiles)
+    over_core = exchange(near, 1, tiles)
+    over_both = exchange(over_y, 1, tiles)
 
     for_z = jax.ShapeDtypeStruct((4, capacity, vis), BF16)
     for_plane = jax.ShapeDtypeStruct((outer, capacity, vis), BF16)
@@ -500,7 +503,7 @@
         back,
         pick,
         weights,
-        frequencies.reshape(1, chan),
+        turns,
         image,
     )
     def turned(blocks, out_shape):
@@ -527,7 +530,7 @@
         out_specs=vmem,
         compiler_params=pltpu.CompilerParams(vmem_limit_bytes=6 * MIB),
         name="residual",
-    )(me, observed.reshape(tiles, 2 * capacity, vis), *first, *second)
+    )(me, observed.reshape(tiles, 2 * capacity, vis), *second, *first)
     return residual.reshape(observed.shape)
 
 

time: 51.9 us -> 49.4 us (0.952)
  the two profiles are of different devices: /device:TPU:0 before, /device:TPU:17 now
where the time goes in v7:
time: 49.4 us; the launch traced here: 49.2 us
  starting transfers between devices  23.5 us (48%)
  Pallas kernels  14.8 us (30%)
  waiting for transfers between devices  8.82 us (18%)
  local copies, waits for them, and re-layouts  1.9 us (4%)
    ppermute x18, starting transfers between devices, exchange(): return lax.ppermute(value, 'tile', [(i, i ^ step) for i in range(tiles)])  23.5 us
    ppermute x18, waiting for transfers between devices, exchange(): return lax.ppermute(value, 'tile', [(i, i ^ step) for i in range(tiles)])  8.82 us
    pallas_call x1, Pallas kernels, per_device(): pl.pallas_call(predict_kernel, out_shape=[for_z] * outer + [for_plane] *...  8 us
    pallas_call x1, Pallas kernels, per_device(): pl.pallas_call(transform_kernel, out_shape=jax.ShapeDtypeStruct((8, numbe...  2.47 us
    unnamed x22, local copies, waits for them, and re-layouts  1.9 us
    pallas_call x1, Pallas kernels, per_device(): pl.pallas_call(pack_kernel, out_shape=[block] * outer, in_specs=[smem, hb...  1.62 us
    pallas_call x1, Pallas kernels, per_device(): pl.pallas_call(functools.partial(prepare_kernel, slot_count=slot_count),...  1.58 us
    pallas_call x1, Pallas kernels, per_device(): pl.pallas_call(residual_kernel, out_shape=jax.ShapeDtypeStruct((tiles, 2...  1.06 us
  transfers between devices with their start and end apart: 18, of which 6 were waited for; matrix products, arithmetic and copies ran while one was open for 0% of the time, Pallas kernels for 8%

profile of v7, /device:TPU:17, one launch (start us, length us, event | category | flops | bytes accessed | tf_op | source)
XLA Modules:
  0.0 49.2 jit_solution(15891578998212176218)
XLA Ops:
  0.0 0.0 copy-start.4
  0.0 0.0 copy-start.5
  0.0 1.6 %pack.1 = (bf16[176,128]{1,0:T(8,128)(2,1)}, bf16[176,128]{1,0:T(8,128)(2,1)}, bf16[176,128]{1,0:T(8,128)(2,1)}, bf16[176,128]{1,0:T(8,128)(2,1)}) custom-call(s32[1]{0:T(128)} %bitcast.me, bf16[64,256]{1,0:T(8,128)(2,1)} %bitcast.25, f32[16,8,64]{2,1,0:T(8,128)} %bitcast.24), custom_call_target="tpu_custom_call" | custom-call | tf_op jit(solution)/shard_map/pack/pallas_call | solution.py:404
  1.6 1.4 %collective-permute-start = (bf16[176,128]{1,0:T(8,128)(2,1)}, bf16[176,128]{1,0:T(8,128)(2,1)S(1)}, u32[]{:S(2)}, u32[]{:S(2)}) collective-permute-start(bf16[176,128]{1,0:T(8,128)(2,1)} %get-tuple-element.31), channel_id=1, source_target_pairs={{0,4},{1,5},{2,6},{3,7},{4,0},{5,1},{6,2},{7,3},{8,12},{9,13},{10,... | collective-permute-start | bytes 135176 | tf_op jit(solution)/shard_map/ppermute | solution.py:369
  3.0 0.1 collective-permute-start.1
  3.1 1.3 %collective-permute-start.2 = (bf16[176,128]{1,0:T(8,128)(2,1)}, bf16[176,128]{1,0:T(8,128)(2,1)S(1)}, u32[]{:S(2)}, u32[]{:S(2)}) collective-permute-start(bf16[176,128]{1,0:T(8,128)(2,1)} %get-tuple-element.33), channel_id=1, source_target_pairs={{0,12},{1,13},{2,14},{3,15},{4,8},{5,9},{6,10},{7,11},{8,4},{9,5},... | collective-permute-start | bytes 135176 | tf_op jit(solution)/shard_map/ppermute | solution.py:369
  4.4 0.0 copy-done.4
  4.4 0.0 copy-done.5
  4.4 0.0 copy-start
  4.4 1.2 %copy-done = bf16[256,2,1024]{2,1,0:T(2,128)(2,1)S(1)} copy-done((bf16[256,2,1024]{2,1,0:T(2,128)(2,1)S(1)}, bf16[256,2,1024]{2,1,0:T(2,128)(2,1)}, u32[]{:S(2)}) %copy-start) | copy-done | bytes 1048600
  5.6 0.0 copy-start.2
  5.6 0.0 copy-start.6
  5.6 0.0 copy-start.10
  5.6 2.5 %transform.1.refs_4_.image = bf16[8,256,256]{2,1,0:T(8,128)(2,1)S(1)} custom-call(bf16[4096,128]{1,0:T(8,128)(2,1)S(1)} %bitcast.18, f32[2,32,128]{2,1,0:T(8,128)S(1)} %copy-done.5, f32[2,32,128]{2,1,0:T(8,128)S(1)} %copy-done.4), custom_call_target="tpu_custom_call" | custom-call | tf_op jit(solution)/shard_map/transform/pallas_call | solution.py:422
  8.1 0.0 copy-start.7
  8.1 0.0 copy-start.8
  8.1 0.0 copy-start.9
  8.1 0.0 copy-done.2
  8.1 0.0 copy-done.6
  8.1 0.0 copy-done.10
  8.1 0.6 %copy-done.7 = s32[256,2]{0,1:T(2,128)S(1)} copy-done((s32[256,2]{0,1:T(2,128)S(1)}, s32[256,2]{0,1:T(2,128)}, u32[]{:S(2)}) %copy-start.7) | copy-done | bytes 2072
  8.8 0.0 copy-done.8
  8.8 0.0 copy-done.9
  8.8 0.0 copy-start.3
  8.8 1.6 %prepare.1 = (bf16[256,1024]{1,0:T(8,128)(2,1)S(1)}, bf16[1024,256]{1,0:T(8,128)(2,1)S(1)}, bf16[512,1024]{1,0:T(8,128)(2,1)S(1)}, bf16[8,256,256]{2,1,0:T(8,128)(2,1)S(1)}, f32[1,128]{1,0:T(1,128)S(1)}) custom-call(s32[1,16]{1,0:T(1,128)S(1)} %copy-done.9, s32[16,64]{1,0:T(8,128)S(1)} %bitcast.20, s32[2,256]{1,0:T(2,128)S(1)} %bitcast.21, ...), custom_call_target="tpu_custom_call" | custom-call | tf_op jit(solution)/shard_map/prepare/pallas_call | solution.py:439
  10.4 0.0 collective-permute-done.refs_1_
  10.4 0.0 collective-permute-done.1.refs_2_
  10.4 0.0 collective-permute-done.2.refs_3_
  10.4 0.0 copy-done.3
  10.4 1.3 %collective-permute-start.3 = (bf16[4,176,128]{2,1,0:T(8,128)(2,1)S(1)}, bf16[4,176,128]{2,1,0:T(8,128)(2,1)S(1)}, u32[]{:S(2)}, u32[]{:S(2)}) collective-permute-start(bf16[4,176,128]{2,1,0:T(8,128)(2,1)S(1)} %stack.1.near), channel_id=1, source_target_pairs={{0,2},{1,3},{2,0},{3,1},{4,6},{5,7},{6,4},{7,5},{8,10},{9,11},{10,... | collective-permute-start | bytes 540680 | tf_op jit(solution)/shard_map/ppermute | solution.py:369
  11.7 1.8 %collective-permute-start.4 = (bf16[4,176,128]{2,1,0:T(8,128)(2,1)S(1)}, bf16[4,176,128]{2,1,0:T(8,128)(2,1)S(1)}, u32[]{:S(2)}, u32[]{:S(2)}) collective-permute-start(bf16[4,176,128]{2,1,0:T(8,128)(2,1)S(1)} %stack.1.near), channel_id=1, source_target_pairs={{0,1},{1,0},{2,3},{3,2},{4,5},{5,4},{6,7},{7,6},{8,9},{9,8},{10,11... | collective-permute-start | bytes 540680 | tf_op jit(solution)/shard_map/ppermute | solution.py:369
  13.5 1.3 %collective-permute-done.3.over_y = bf16[4,176,128]{2,1,0:T(8,128)(2,1)S(1)} collective-permute-done((bf16[4,176,128]{2,1,0:T(8,128)(2,1)S(1)}, bf16[4,176,128]{2,1,0:T(8,128)(2,1)S(1)}, u32[]{:S(2)}, u32[]{:S(2)}) %collective-permute-start.3) | collective-permute-done | bytes 180256 | tf_op jit(solution)/shard_map/ppermute | solution.py:369
  14.8 2.7 %collective-permute-start.5 = (bf16[4,176,128]{2,1,0:T(8,128)(2,1)S(1)}, bf16[4,176,128]{2,1,0:T(8,128)(2,1)S(1)}, u32[]{:S(2)}, u32[]{:S(2)}) collective-permute-start(bf16[4,176,128]{2,1,0:T(8,128)(2,1)S(1)} %collective-permute-done.3.over_y), channel_id=1, source_target_pairs={{0,1},{1,0},{2,3},{3,2},{4,5},{5,4},{6,7},{7,6},{8,9},{9,8},{10,11... | collective-permute-start | bytes 540680 | tf_op jit(solution)/shard_map/ppermute | solution.py:369
  17.5 0.0 collective-permute-done.4.over_core
  17.5 1.0 %collective-permute-done.5.over_both = bf16[4,176,128]{2,1,0:T(8,128)(2,1)S(1)} collective-permute-done((bf16[4,176,128]{2,1,0:T(8,128)(2,1)S(1)}, bf16[4,176,128]{2,1,0:T(8,128)(2,1)S(1)}, u32[]{:S(2)}, u32[]{:S(2)}) %collective-permute-start.5) | collective-permute-done | bytes 180256 | tf_op jit(solution)/shard_map/ppermute | solution.py:369
  18.5 0.0 copy-start.1
  18.6 8.0 %predict.1 = (bf16[4,64,128]{2,1,0:T(8,128)(2,1)S(1)}, bf16[4,64,128]{2,1,0:T(8,128)(2,1)S(1)}, bf16[4,64,128]{2,1,0:T(8,128)(2,1)S(1)}, bf16[4,64,128]{2,1,0:T(...) custom-call(s32[1]{0:T(128)} %bitcast.me, ...), custom_call_target="tpu_custom_call" | custom-call | tf_op jit(solution)/shard_map/predict/pallas_call | solution.py:475
  26.6 0.4 collective-permute-start.6
  27.0 1.2 %collective-permute-start.7 = (bf16[4,64,128]{2,1,0:T(8,128)(2,1)S(1)}, bf16[4,64,128]{2,1,0:T(8,128)(2,1)S(1)}, u32[]{:S(2)}, u32[]{:S(2)}) collective-permute-start(bf16[4,64,128]{2,1,0:T(8,128)(2,1)S(1)} %get-tuple-element.41), channel_id=1, source_target_pairs={{0,2},{1,3},{2,0},{3,1},{4,6},{5,7},{6,4},{7,5},{8,10},{9,11},{10,... | collective-permute-start | bytes 196616 | tf_op jit(solution)/shard_map/ppermute | solution.py:369
  28.2 0.5 %collective-permute-start.8 = (bf16[4,64,128]{2,1,0:T(8,128)(2,1)S(1)}, bf16[4,64,128]{2,1,0:T(8,128)(2,1)S(1)}, u32[]{:S(2)}, u32[]{:S(2)}) collective-permute-start(bf16[4,64,128]{2,1,0:T(8,128)(2,1)S(1)} %get-tuple-element.42), channel_id=1, source_target_pairs={{0,3},{1,2},{2,1},{3,0},{4,7},{5,6},{6,5},{7,4},{8,11},{9,10},{10,... | collective-permute-start | bytes 196616 | tf_op jit(solution)/shard_map/ppermute | solution.py:369
  28.8 2.2 %collective-permute-start.12 = (bf16[4,64,128]{2,1,0:T(8,128)(2,1)S(1)}, bf16[4,64,128]{2,1,0:T(8,128)(2,1)S(1)}, u32[]{:S(2)}, u32[]{:S(2)}) collective-permute-start(bf16[4,64,128]{2,1,0:T(8,128)(2,1)S(1)} %get-tuple-element.48), channel_id=1, source_target_pairs={{0,4},{1,5},{2,6},{3,7},{4,0},{5,1},{6,2},{7,3},{8,12},{9,13},{10,... | collective-permute-start | bytes 196616 | tf_op jit(solution)/shard_map/ppermute | solution.py:369
  31.0 0.0 collective-permute-start.13
  31.0 0.0 collective-permute-done.6.refs_1_
  31.0 1.2 %collective-permute-start.14 = (bf16[4,64,128]{2,1,0:T(8,128)(2,1)S(1)}, bf16[4,64,128]{2,1,0:T(8,128)(2,1)S(1)}, u32[]{:S(2)}, u32[]{:S(2)}) collective-permute-start(bf16[4,64,128]{2,1,0:T(8,128)(2,1)S(1)} %get-tuple-element.50), channel_id=1, source_target_pairs={{0,12},{1,13},{2,14},{3,15},{4,8},{5,9},{6,10},{7,11},{8,4},{9,5},... | collective-permute-start | bytes 196616 | tf_op jit(solution)/shard_map/ppermute | solution.py:369
  32.2 0.0 collective-permute-done.7.refs_2_
  32.2 0.5 %collective-permute-done.8.refs_3_ = bf16[4,64,128]{2,1,0:T(8,128)(2,1)S(1)} collective-permute-done((bf16[4,64,128]{2,1,0:T(8,128)(2,1)S(1)}, bf16[4,64,128]{2,1,0:T(8,128)(2,1)S(1)}, u32[]{:S(2)}, u32[]{:S(2)}) %collective-permute-start.8) | collective-permute-done | bytes 65568 | tf_op jit(solution)/shard_map/ppermute | solution.py:369
  32.7 2.3 %collective-permute-start.9 = (bf16[4,64,128]{2,1,0:T(8,128)(2,1)S(1)}, bf16[4,64,128]{2,1,0:T(8,128)(2,1)S(1)}, u32[]{:S(2)}, u32[]{:S(2)}) collective-permute-start(bf16[4,64,128]{2,1,0:T(8,128)(2,1)S(1)} %get-tuple-element.44), channel_id=1, source_target_pairs={{0,4},{1,5},{2,6},{3,7},{4,0},{5,1},{6,2},{7,3},{8,12},{9,13},{10,... | collective-permute-start | bytes 196616 | tf_op jit(solution)/shard_map/ppermute | solution.py:369
  35.0 0.0 collective-permute-start.10
  35.0 0.0 collective-permute-done.12.refs_1_
  35.0 1.3 %collective-permute-start.11 = (bf16[4,64,128]{2,1,0:T(8,128)(2,1)S(1)}, bf16[4,64,128]{2,1,0:T(8,128)(2,1)S(1)}, u32[]{:S(2)}, u32[]{:S(2)}) collective-permute-start(bf16[4,64,128]{2,1,0:T(8,128)(2,1)S(1)} %get-tuple-element.46), channel_id=1, source_target_pairs={{0,12},{1,13},{2,14},{3,15},{4,8},{5,9},{6,10},{7,11},{8,4},{9,5},... | collective-permute-start | bytes 196616 | tf_op jit(solution)/shard_map/ppermute | solution.py:369
  36.2 0.0 collective-permute-done.13.refs_2_
  36.2 2.3 %collective-permute-done.14.refs_3_ = bf16[4,64,128]{2,1,0:T(8,128)(2,1)S(1)} collective-permute-done((bf16[4,64,128]{2,1,0:T(8,128)(2,1)S(1)}, bf16[4,64,128]{2,1,0:T(8,128)(2,1)S(1)}, u32[]{:S(2)}, u32[]{:S(2)}) %collective-permute-start.14) | collective-permute-done | bytes 65568 | tf_op jit(solution)/shard_map/ppermute | solution.py:369
  38.6 4.2 %collective-permute-start.15 = (bf16[4,64,128]{2,1,0:T(8,128)(2,1)S(1)}, bf16[4,64,128]{2,1,0:T(8,128)(2,1)S(1)}, u32[]{:S(2)}, u32[]{:S(2)}) collective-permute-start(bf16[4,64,128]{2,1,0:T(8,128)(2,1)S(1)} %get-tuple-element.52), channel_id=1, source_target_pairs={{0,1},{1,0},{2,3},{3,2},{4,5},{5,4},{6,7},{7,6},{8,9},{9,8},{10,11... | collective-permute-start | bytes 196616 | tf_op jit(solution)/shard_map/ppermute | solution.py:369
  42.8 1.3 %collective-permute-start.16 = (bf16[4,64,128]{2,1,0:T(8,128)(2,1)S(1)}, bf16[4,64,128]{2,1,0:T(8,128)(2,1)S(1)}, u32[]{:S(2)}, u32[]{:S(2)}) collective-permute-start(bf16[4,64,128]{2,1,0:T(8,128)(2,1)S(1)} %get-tuple-element.53), channel_id=1, source_target_pairs={{0,2},{1,3},{2,0},{3,1},{4,6},{5,7},{6,4},{7,5},{8,10},{9,11},{10,... | collective-permute-start | bytes 196616 | tf_op jit(solution)/shard_map/ppermute | solution.py:369
  44.1 0.0 collective-permute-done.9.refs_1_
  44.1 0.4 collective-permute-start.17
  44.5 0.0 collective-permute-done.10.refs_2_
  44.5 0.0 collective-permute-done.11.refs_3_
  44.5 0.0 collective-permute-done.15.refs_5_
  44.5 1.9 %collective-permute-done.16.refs_6_ = bf16[4,64,128]{2,1,0:T(8,128)(2,1)S(1)} collective-permute-done((bf16[4,64,128]{2,1,0:T(8,128)(2,1)S(1)}, bf16[4,64,128]{2,1,0:T(8,128)(2,1)S(1)}, u32[]{:S(2)}, u32[]{:S(2)}) %collective-permute-start.16) | collective-permute-done | bytes 65568 | tf_op jit(solution)/shard_map/ppermute | solution.py:369
  46.5 1.6 %collective-permute-done.17.refs_7_ = bf16[4,64,128]{2,1,0:T(8,128)(2,1)S(1)} collective-permute-done((bf16[4,64,128]{2,1,0:T(8,128)(2,1)S(1)}, bf16[4,64,128]{2,1,0:T(8,128)(2,1)S(1)}, u32[]{:S(2)}, u32[]{:S(2)}) %collective-permute-start.17) | collective-permute-done | bytes 65568 | tf_op jit(solution)/shard_map/ppermute | solution.py:369
  48.1 0.0 copy-done.1
  48.1 1.1 %residual.1 = f32[16,128,128]{2,1,0:T(8,128)} custom-call(s32[1]{0:T(128)} %bitcast.me, f32[16,128,128]{2,1,0:T(8,128)S(1)} %bitcast.19, bf16[4,64,128]{2,1,0:T(8,128)(2,1)S(1)} %get-tuple-element.43.refs_0_, bf16[4,64,128]{2,1,0:T(8,128)(2,1)S(1)} %collective-permute-done.9.refs_1_, bf16[4,64,128]{2,1,0:T(8,128)(2,1)S(1)} %collective-permute-done.10.refs_2_, ...), custom_call_target="tpu_custom_call" | custom-call | tf_op jit(solution)/shard_map/residual/pallas_call | solution.py:526
  (3 shorter events, 0.1 us)
Async XLA Ops:
  0.0 4.4 %copy-start.4 = (f32[2,32,128]{2,1,0:T(8,128)S(1)}, f32[2,32,128]{2,1,0:T(8,128)}, u32[]{:S(2)}) copy-start(f32[2,32,128]{2,1,0:T(8,128)} %constant.9.clone.cell_turns) | copy-start | bytes 98308
  0.0 4.4 %copy-start.5 = (f32[2,32,128]{2,1,0:T(8,128)S(1)}, f32[2,32,128]{2,1,0:T(8,128)}, u32[]{:S(2)}) copy-start(f32[2,32,128]{2,1,0:T(8,128)} %constant.8.clone.row_turns) | copy-start | bytes 98308
  1.6 8.7 %collective-permute-start = (bf16[176,128]{1,0:T(8,128)(2,1)}, bf16[176,128]{1,0:T(8,128)(2,1)S(1)}, u32[]{:S(2)}, u32[]{:S(2)}) collective-permute-start(bf16[176,128]{1,0:T(8,128)(2,1)} %get-tuple-element.31), channel_id=1, source_target_pairs={{0,4},{1,5},{2,6},{3,7},{4,0},{5,1},{6,2},{7,3},{8,12},{9,13},{10,... | collective-permute-start | bytes 135176 | tf_op jit(solution)/shard_map/ppermute | solution.py:369
  3.0 7.4 %collective-permute-start.1 = (bf16[176,128]{1,0:T(8,128)(2,1)}, bf16[176,128]{1,0:T(8,128)(2,1)S(1)}, u32[]{:S(2)}, u32[]{:S(2)}) collective-permute-start(bf16[176,128]{1,0:T(8,128)(2,1)} %get-tuple-element.32), channel_id=1, source_target_pairs={{0,8},{1,9},{2,10},{3,11},{4,12},{5,13},{6,14},{7,15},{8,0},{9,1},... | collective-permute-start | bytes 135176 | tf_op jit(solution)/shard_map/ppermute | solution.py:369
  3.1 7.3 %collective-permute-start.2 = (bf16[176,128]{1,0:T(8,128)(2,1)}, bf16[176,128]{1,0:T(8,128)(2,1)S(1)}, u32[]{:S(2)}, u32[]{:S(2)}) collective-permute-start(bf16[176,128]{1,0:T(8,128)(2,1)} %get-tuple-element.33), channel_id=1, source_target_pairs={{0,12},{1,13},{2,14},{3,15},{4,8},{5,9},{6,10},{7,11},{8,4},{9,5},... | collective-permute-start | bytes 135176 | tf_op jit(solution)/shard_map/ppermute | solution.py:369
  4.4 1.2 %copy-start = (bf16[256,2,1024]{2,1,0:T(2,128)(2,1)S(1)}, bf16[256,2,1024]{2,1,0:T(2,128)(2,1)}, u32[]{:S(2)}) copy-start(bf16[256,2,1024]{2,1,0:T(2,128)(2,1)} %param.12) | copy-start | bytes 3145732
  5.6 2.5 %copy-start.2 = (bf16[2,128,1024]{2,1,0:T(8,128)(2,1)S(1)}, bf16[2,128,1024]{2,1,0:T(8,128)(2,1)}, u32[]{:S(2)}) copy-start(bf16[2,128,1024]{2,1,0:T(8,128)(2,1)} %basis.1) | copy-start | bytes 1572868
  5.6 2.5 %copy-start.6 = (s32[1,16,64]{2,1,0:T(8,128)S(1)}, s32[1,16,64]{2,1,0:T(8,128)}, u32[]{:S(2)}) copy-start(s32[1,16,64]{2,1,0:T(8,128)} %param.15) | copy-start | bytes 12292
  5.6 2.5 %copy-start.10 = (f32[32]{0:T(128)S(1)}, f32[32]{0:T(128)}, u32[]{:S(2)}) copy-start(f32[32]{0:T(128)} %param.19) | copy-start | bytes 388
  8.1 0.7 %copy-start.7 = (s32[256,2]{0,1:T(2,128)S(1)}, s32[256,2]{0,1:T(2,128)}, u32[]{:S(2)}) copy-start(s32[256,2]{0,1:T(2,128)} %param.13) | copy-start | bytes 6148
  8.1 0.7 %copy-start.8 = (s32[256]{0:T(256)S(1)}, s32[256]{0:T(256)}, u32[]{:S(2)}) copy-start(s32[256]{0:T(256)} %param.14) | copy-start | bytes 3076
  8.1 0.7 %copy-start.9 = (s32[1,16]{1,0:T(1,128)S(1)}, s32[1,16]{1,0:T(1,128)}, u32[]{:S(2)}) copy-start(s32[1,16]{1,0:T(1,128)} %counts.1) | copy-start | bytes 196
  8.8 1.6 %copy-start.3 = (bf16[176,128]{1,0:T(8,128)(2,1)S(1)}, bf16[176,128]{1,0:T(8,128)(2,1)}, u32[]{:S(2)}) copy-start(bf16[176,128]{1,0:T(8,128)(2,1)} %get-tuple-element.30.refs_0_) | copy-start | bytes 135172
  10.4 4.4 %collective-permute-start.3 = (bf16[4,176,128]{2,1,0:T(8,128)(2,1)S(1)}, bf16[4,176,128]{2,1,0:T(8,128)(2,1)S(1)}, u32[]{:S(2)}, u32[]{:S(2)}) collective-permute-start(bf16[4,176,128]{2,1,0:T(8,128)(2,1)S(1)} %stack.1.near), channel_id=1, source_target_pairs={{0,2},{1,3},{2,0},{3,1},{4,6},{5,7},{6,4},{7,5},{8,10},{9,11},{10,... | collective-permute-start | bytes 540680 | tf_op jit(solution)/shard_map/ppermute | solution.py:369
  11.7 5.8 %collective-permute-start.4 = (bf16[4,176,128]{2,1,0:T(8,128)(2,1)S(1)}, bf16[4,176,128]{2,1,0:T(8,128)(2,1)S(1)}, u32[]{:S(2)}, u32[]{:S(2)}) collective-permute-start(bf16[4,176,128]{2,1,0:T(8,128)(2,1)S(1)} %stack.1.near), channel_id=1, source_target_pairs={{0,1},{1,0},{2,3},{3,2},{4,5},{5,4},{6,7},{7,6},{8,9},{9,8},{10,11... | collective-permute-start | bytes 540680 | tf_op jit(solution)/shard_map/ppermute | solution.py:369
  14.8 3.7 %collective-permute-start.5 = (bf16[4,176,128]{2,1,0:T(8,128)(2,1)S(1)}, bf16[4,176,128]{2,1,0:T(8,128)(2,1)S(1)}, u32[]{:S(2)}, u32[]{:S(2)}) collective-permute-start(bf16[4,176,128]{2,1,0:T(8,128)(2,1)S(1)} %collective-permute-done.3.over_y), channel_id=1, source_target_pairs={{0,1},{1,0},{2,3},{3,2},{4,5},{5,4},{6,7},{7,6},{8,9},{9,8},{10,11... | collective-permute-start | bytes 540680 | tf_op jit(solution)/shard_map/ppermute | solution.py:369
  18.5 29.6 %copy-start.1 = (f32[1,16,64,2,128]{4,3,2,1,0:T(2,128)S(1)}, f32[1,16,64,2,128]{4,3,2,1,0:T(2,128)}, u32[]{:S(2)}) copy-start(f32[1,16,64,2,128]{4,3,2,1,0:T(2,128)} %param.21) | copy-start | bytes 3145732
  26.6 4.4 %collective-permute-start.6 = (bf16[4,64,128]{2,1,0:T(8,128)(2,1)S(1)}, bf16[4,64,128]{2,1,0:T(8,128)(2,1)S(1)}, u32[]{:S(2)}, u32[]{:S(2)}) collective-permute-start(bf16[4,64,128]{2,1,0:T(8,128)(2,1)S(1)} %get-tuple-element.40), channel_id=1, source_target_pairs={{0,1},{1,0},{2,3},{3,2},{4,5},{5,4},{6,7},{7,6},{8,9},{9,8},{10,11... | collective-permute-start | bytes 196616 | tf_op jit(solution)/shard_map/ppermute | solution.py:369
  27.0 5.2 %collective-permute-start.7 = (bf16[4,64,128]{2,1,0:T(8,128)(2,1)S(1)}, bf16[4,64,128]{2,1,0:T(8,128)(2,1)S(1)}, u32[]{:S(2)}, u32[]{:S(2)}) collective-permute-start(bf16[4,64,128]{2,1,0:T(8,128)(2,1)S(1)} %get-tuple-element.41), channel_id=1, source_target_pairs={{0,2},{1,3},{2,0},{3,1},{4,6},{5,7},{6,4},{7,5},{8,10},{9,11},{10,... | collective-permute-start | bytes 196616 | tf_op jit(solution)/shard_map/ppermute | solution.py:369
  28.2 4.4 %collective-permute-start.8 = (bf16[4,64,128]{2,1,0:T(8,128)(2,1)S(1)}, bf16[4,64,128]{2,1,0:T(8,128)(2,1)S(1)}, u32[]{:S(2)}, u32[]{:S(2)}) collective-permute-start(bf16[4,64,128]{2,1,0:T(8,128)(2,1)S(1)} %get-tuple-element.42), channel_id=1, source_target_pairs={{0,3},{1,2},{2,1},{3,0},{4,7},{5,6},{6,5},{7,4},{8,11},{9,10},{10,... | collective-permute-start | bytes 196616 | tf_op jit(solution)/shard_map/ppermute | solution.py:369
  28.8 6.2 %collective-permute-start.12 = (bf16[4,64,128]{2,1,0:T(8,128)(2,1)S(1)}, bf16[4,64,128]{2,1,0:T(8,128)(2,1)S(1)}, u32[]{:S(2)}, u32[]{:S(2)}) collective-permute-start(bf16[4,64,128]{2,1,0:T(8,128)(2,1)S(1)} %get-tuple-element.48), channel_id=1, source_target_pairs={{0,4},{1,5},{2,6},{3,7},{4,0},{5,1},{6,2},{7,3},{8,12},{9,13},{10,... | collective-permute-start | bytes 196616 | tf_op jit(solution)/shard_map/ppermute | solution.py:369
  31.0 5.2 %collective-permute-start.13 = (bf16[4,64,128]{2,1,0:T(8,128)(2,1)S(1)}, bf16[4,64,128]{2,1,0:T(8,128)(2,1)S(1)}, u32[]{:S(2)}, u32[]{:S(2)}) collective-permute-start(bf16[4,64,128]{2,1,0:T(8,128)(2,1)S(1)} %get-tuple-element.49), channel_id=1, source_target_pairs={{0,8},{1,9},{2,10},{3,11},{4,12},{5,13},{6,14},{7,15},{8,0},{9,1},... | collective-permute-start | bytes 196616 | tf_op jit(solution)/shard_map/ppermute | solution.py:369
  31.0 7.6 %collective-permute-start.14 = (bf16[4,64,128]{2,1,0:T(8,128)(2,1)S(1)}, bf16[4,64,128]{2,1,0:T(8,128)(2,1)S(1)}, u32[]{:S(2)}, u32[]{:S(2)}) collective-permute-start(bf16[4,64,128]{2,1,0:T(8,128)(2,1)S(1)} %get-tuple-element.50), channel_id=1, source_target_pairs={{0,12},{1,13},{2,14},{3,15},{4,8},{5,9},{6,10},{7,11},{8,4},{9,5},... | collective-permute-start | bytes 196616 | tf_op jit(solution)/shard_map/ppermute | solution.py:369
  32.7 11.4 %collective-permute-start.9 = (bf16[4,64,128]{2,1,0:T(8,128)(2,1)S(1)}, bf16[4,64,128]{2,1,0:T(8,128)(2,1)S(1)}, u32[]{:S(2)}, u32[]{:S(2)}) collective-permute-start(bf16[4,64,128]{2,1,0:T(8,128)(2,1)S(1)} %get-tuple-element.44), channel_id=1, source_target_pairs={{0,4},{1,5},{2,6},{3,7},{4,0},{5,1},{6,2},{7,3},{8,12},{9,13},{10,... | collective-permute-start | bytes 196616 | tf_op jit(solution)/shard_map/ppermute | solution.py:369
  35.0 9.6 %collective-permute-start.10 = (bf16[4,64,128]{2,1,0:T(8,128)(2,1)S(1)}, bf16[4,64,128]{2,1,0:T(8,128)(2,1)S(1)}, u32[]{:S(2)}, u32[]{:S(2)}) collective-permute-start(bf16[4,64,128]{2,1,0:T(8,128)(2,1)S(1)} %get-tuple-element.45), channel_id=1, source_target_pairs={{0,8},{1,9},{2,10},{3,11},{4,12},{5,13},{6,14},{7,15},{8,0},{9,1},... | collective-permute-start | bytes 196616 | tf_op jit(solution)/shard_map/ppermute | solution.py:369
  35.0 9.6 %collective-permute-start.11 = (bf16[4,64,128]{2,1,0:T(8,128)(2,1)S(1)}, bf16[4,64,128]{2,1,0:T(8,128)(2,1)S(1)}, u32[]{:S(2)}, u32[]{:S(2)}) collective-permute-start(bf16[4,64,128]{2,1,0:T(8,128)(2,1)S(1)} %get-tuple-element.46), channel_id=1, source_target_pairs={{0,12},{1,13},{2,14},{3,15},{4,8},{5,9},{6,10},{7,11},{8,4},{9,5},... | collective-permute-start | bytes 196616 | tf_op jit(solution)/shard_map/ppermute | solution.py:369
  38.6 5.9 %collective-permute-start.15 = (bf16[4,64,128]{2,1,0:T(8,128)(2,1)S(1)}, bf16[4,64,128]{2,1,0:T(8,128)(2,1)S(1)}, u32[]{:S(2)}, u32[]{:S(2)}) collective-permute-start(bf16[4,64,128]{2,1,0:T(8,128)(2,1)S(1)} %get-tuple-element.52), channel_id=1, source_target_pairs={{0,1},{1,0},{2,3},{3,2},{4,5},{5,4},{6,7},{7,6},{8,9},{9,8},{10,11... | collective-permute-start | bytes 196616 | tf_op jit(solution)/shard_map/ppermute | solution.py:369
  42.8 3.7 %collective-permute-start.16 = (bf16[4,64,128]{2,1,0:T(8,128)(2,1)S(1)}, bf16[4,64,128]{2,1,0:T(8,128)(2,1)S(1)}, u32[]{:S(2)}, u32[]{:S(2)}) collective-permute-start(bf16[4,64,128]{2,1,0:T(8,128)(2,1)S(1)} %get-tuple-element.53), channel_id=1, source_target_pairs={{0,2},{1,3},{2,0},{3,1},{4,6},{5,7},{6,4},{7,5},{8,10},{9,11},{10,... | collective-permute-start | bytes 196616 | tf_op jit(solution)/shard_map/ppermute | solution.py:369
  44.1 4.0 %collective-permute-start.17 = (bf16[4,64,128]{2,1,0:T(8,128)(2,1)S(1)}, bf16[4,64,128]{2,1,0:T(8,128)(2,1)S(1)}, u32[]{:S(2)}, u32[]{:S(2)}) collective-permute-start(bf16[4,64,128]{2,1,0:T(8,128)(2,1)S(1)} %get-tuple-element.54), channel_id=1, source_target_pairs={{0,3},{1,2},{2,1},{3,0},{4,7},{5,6},{6,5},{7,4},{8,11},{9,10},{10,... | collective-permute-start | bytes 196616 | tf_op jit(solution)/shard_map/ppermute | solution.py:369

commit v8 on v7

--- a/solution.py
+++ b/solution.py
@@ -54,7 +54,7 @@
     return out_re, out_im
 
 
-def transform_kernel(cells_hbm, row_turns, cell_turns, image, cells, high, rest, wide, sums, sem):
+def transform_kernel(cells_hbm, row_turns, cell_turns, after, image, cells, high, rest, wide, sums, sem):
     copy = pltpu.make_async_copy(cells_hbm, cells, sem)
     copy.start()
     number = image.shape[1]
@@ -190,9 +190,13 @@
 
 
 def stack_kernel(*refs):
-    blocks, out = refs[:-3], refs[-1]
-    for r, block in enumerate(blocks):
+    blocks, out = refs[:-2], refs[-1]
+    for r, block in enumerate(blocks[::-1]):
         out[r] = block[...]
+
+
+def relay_kernel(block, after, out):
+    out[...] = block[...]
 
 
 def predict_kernel(
@@ -289,7 +293,7 @@
             wre[to, :] = i_re * g_re - i_im * g_im
             wim[to, :] = i_re * g_im + i_im * g_re
 
-    unroll = 16
+    unroll = 32
 
     def one(g):
         at = pl.ds(pl.multiple_of(g * 8, 8), 8)
@@ -349,14 +353,14 @@
 def turn_kernel(*refs):
     count = refs[0].shape[0]
     blocks, out = refs[:-count], refs[-count:]
-    for i, block in enumerate(blocks):
+    for i, block in enumerate(blocks[::-1]):
         for j in range(count):
             out[j][i] = block[j]
 
 
 def residual_kernel(me, observed, *refs):
     arrived, residual = refs[:-1], refs[-1]
-    by_z, by_plane = arrived[:-4], arrived[-4:]
+    by_z, by_plane = arrived[:-4][::-1], arrived[-4:]
     rows = by_plane[0].shape[1]
     for r in range(len(by_z)):
         for p in range(4):
@@ -416,26 +420,6 @@
     )(me, beam_coefs.reshape(own_rows, terms2), own_tracks)
     along = [packed[0]] + [exchange(packed[r], 4 * r, tiles) for r in range(1, outer)]
 
-    cells = jnp.transpose(subgrids.reshape(number, 2, 8, 128), (0, 2, 1, 3))
-    cells = cells.reshape(number * 16, 128)
-    row_turns, cell_turns = transform_tables(edge)
-    image = pl.pallas_call(
-        transform_kernel,
-        out_shape=jax.ShapeDtypeStruct((8, number, 256), BF16),
-        in_specs=[hbm] + [vmem] * 2,
-        out_specs=vmem,
-        scratch_shapes=[
-            pltpu.VMEM((number * 16, 128), BF16),
-            pltpu.VMEM((8, 256, 256), BF16),
-            pltpu.VMEM((8, 256, 256), BF16),
-            pltpu.VMEM((number * 16, 128), F32),
-            pltpu.VMEM((8, number, 512), BF16),
-            pltpu.SemaphoreType.DMA,
-        ],
-        compiler_params=pltpu.CompilerParams(vmem_limit_bytes=14 * MIB),
-        name="transform",
-    )(cells, jnp.asarray(row_turns), jnp.asarray(cell_turns))
-
     route, back, pick, weights, turns = pl.pallas_call(
         functools.partial(prepare_kernel, slot_count=slot_count),
         out_shape=[
@@ -461,14 +445,42 @@
     near = pl.pallas_call(
         stack_kernel,
         out_shape=jax.ShapeDtypeStruct((outer,) + block.shape, BF16),
-        in_specs=[vmem] * outer + [anywhere] * 2,
+        in_specs=[vmem] * outer + [anywhere],
         out_specs=vmem,
         compiler_params=pltpu.CompilerParams(vmem_limit_bytes=2 * MIB * (tiles // 16)),
         name="stack",
-    )(*along, image, weights)
+    )(*along[::-1], weights)
+    over_core = exchange(near, 1, tiles)
     over_y = exchange(near, 2, tiles)
-    over_core = exchange(near, 1, tiles)
-    over_both = exchange(over_y, 1, tiles)
+    cells = jnp.transpose(subgrids.reshape(number, 2, 8, 128), (0, 2, 1, 3))
+    cells = cells.reshape(number * 16, 128)
+    row_turns, cell_turns = transform_tables(edge)
+    image = pl.pallas_call(
+        transform_kernel,
+        out_shape=jax.ShapeDtypeStruct((8, number, 256), BF16),
+        in_specs=[hbm] + [vmem] * 2 + [anywhere],
+        out_specs=vmem,
+        scratch_shapes=[
+            pltpu.VMEM((number * 16, 128), BF16),
+            pltpu.VMEM((8, 256, 256), BF16),
+            pltpu.VMEM((8, 256, 256), BF16),
+            pltpu.VMEM((number * 16, 128), F32),
+            pltpu.VMEM((8, number, 512), BF16),
+            pltpu.SemaphoreType.DMA,
+        ],
+        compiler_params=pltpu.CompilerParams(vmem_limit_bytes=14 * MIB),
+        name="transform",
+    )(cells, jnp.asarray(row_turns), jnp.asarray(cell_turns), near)
+
+    over_both = pl.pallas_call(
+        relay_kernel,
+        out_shape=jax.ShapeDtypeStruct(over_y.shape, BF16),
+        in_specs=[vmem, anywhere],
+        out_specs=vmem,
+        compiler_params=pltpu.CompilerParams(vmem_limit_bytes=2 * MIB * (tiles // 16)),
+        name="relay",
+    )(over_y, image)
+    over_both = exchange(over_both, 1, tiles)
 
     for_z = jax.ShapeDtypeStruct((4, capacity, vis), BF16)
     for_plane = jax.ShapeDtypeStruct((outer, capacity, vis), BF16)
@@ -514,7 +526,7 @@
             out_specs=[vmem] * len(out_shape),
             compiler_params=pltpu.CompilerParams(vmem_limit_bytes=2 * MIB),
             name="turn",
-        )(*blocks)
+        )(*blocks[::-1])
 
     first, second = models[:outer], models[outer:]
     second = [second[0]] + [exchange(second[p], p, tiles) for p in range(1, 4)]
@@ -530,7 +542,7 @@
         out_specs=vmem,
         compiler_params=pltpu.CompilerParams(vmem_limit_bytes=6 * MIB),
         name="residual",
-    )(me, observed.reshape(tiles, 2 * capacity, vis), *second, *first)
+    )(me, observed.reshape(tiles, 2 * capacity, vis), *second[::-1], *first)
     return residual.reshape(observed.shape)
 
 

time: 49.4 us -> 47.8 us (0.968)
  the two profiles are of different devices: /device:TPU:17 before, /device:TPU:0 now
where the time goes in v8:
time: 47.8 us; the launch traced here: 47.5 us
  starting transfers between devices  20.3 us (42%)
  Pallas kernels  13.2 us (28%)
  waiting for transfers between devices  8.64 us (18%)
  local copies, waits for them, and re-layouts  5.2 us (11%)
    ppermute x18, starting transfers between devices, exchange(): return lax.ppermute(value, 'tile', [(i, i ^ step) for i in range(tiles)])  20.3 us
    ppermute x18, waiting for transfers between devices, exchange(): return lax.ppermute(value, 'tile', [(i, i ^ step) for i in range(tiles)])  8.64 us
    pallas_call x1, Pallas kernels, per_device(): pl.pallas_call(predict_kernel, out_shape=[for_z] * outer + [for_plane] *...  6.33 us
    unnamed x22, local copies, waits for them, and re-layouts  5.2 us
    pallas_call x1, Pallas kernels, per_device(): pl.pallas_call(transform_kernel, out_shape=jax.ShapeDtypeStruct((8, numbe...  2.48 us
    pallas_call x1, Pallas kernels, per_device(): pl.pallas_call(pack_kernel, out_shape=[block] * outer, in_specs=[smem, hb...  1.7 us
    pallas_call x1, Pallas kernels, per_device(): pl.pallas_call(functools.partial(prepare_kernel, slot_count=slot_count),...  1.58 us
    pallas_call x1, Pallas kernels, per_device(): pl.pallas_call(residual_kernel, out_shape=jax.ShapeDtypeStruct((tiles, 2...  1.07 us
  transfers between devices with their start and end apart: 18, of which 6 were waited for; matrix products, arithmetic and copies ran while one was open for 0% of the time, Pallas kernels for 9%

profile of v8, /device:TPU:0, one launch (start us, length us, event | category | flops | bytes accessed | tf_op | source)
XLA Modules:
  0.0 47.5 jit_solution(2994011365923677502)
XLA Ops:
  0.0 0.0 copy-start
  0.0 1.7 %pack.1 = (bf16[176,128]{1,0:T(8,128)(2,1)}, bf16[176,128]{1,0:T(8,128)(2,1)}, bf16[176,128]{1,0:T(8,128)(2,1)}, bf16[176,128]{1,0:T(8,128)(2,1)}) custom-call(s32[1]{0:T(128)} %bitcast.me, bf16[64,256]{1,0:T(8,128)(2,1)} %bitcast.25, f32[16,8,64]{2,1,0:T(8,128)} %bitcast.24), custom_call_target="tpu_custom_call" | custom-call | tf_op jit(solution)/shard_map/pack/pallas_call | solution.py:408
  1.7 5.1 %collective-permute-start = (bf16[176,128]{1,0:T(8,128)(2,1)}, bf16[176,128]{1,0:T(8,128)(2,1)S(1)}, u32[]{:S(2)}, u32[]{:S(2)}) collective-permute-start(bf16[176,128]{1,0:T(8,128)(2,1)} %get-tuple-element.30), channel_id=1, source_target_pairs={{0,12},{1,13},{2,14},{3,15},{4,8},{5,9},{6,10},{7,11},{8,4},{9,5},... | collective-permute-start | bytes 135176 | tf_op jit(solution)/shard_map/ppermute | solution.py:373
  6.8 0.0 collective-permute-start.1
  6.8 0.6 %collective-permute-start.2 = (bf16[176,128]{1,0:T(8,128)(2,1)}, bf16[176,128]{1,0:T(8,128)(2,1)S(1)}, u32[]{:S(2)}, u32[]{:S(2)}) collective-permute-start(bf16[176,128]{1,0:T(8,128)(2,1)} %get-tuple-element.32), channel_id=1, source_target_pairs={{0,4},{1,5},{2,6},{3,7},{4,0},{5,1},{6,2},{7,3},{8,12},{9,13},{10,... | collective-permute-start | bytes 135176 | tf_op jit(solution)/shard_map/ppermute | solution.py:373
  7.5 0.0 copy-start.2
  7.5 1.0 %copy-done.2 = bf16[2,128,1024]{2,1,0:T(8,128)(2,1)S(1)} copy-done((bf16[2,128,1024]{2,1,0:T(8,128)(2,1)S(1)}, bf16[2,128,1024]{2,1,0:T(8,128)(2,1)}, u32[]{:S(2)}) %copy-start.2) | copy-done | bytes 524312
  8.5 0.0 copy-start.6
  8.5 0.7 %copy-done.6 = s32[1,16,64]{2,1,0:T(8,128)S(1)} copy-done((s32[1,16,64]{2,1,0:T(8,128)S(1)}, s32[1,16,64]{2,1,0:T(8,128)}, u32[]{:S(2)}) %copy-start.6) | copy-done | bytes 4120
  9.2 0.0 copy-start.7
  9.2 0.7 %copy-done.7 = s32[256,2]{0,1:T(2,128)S(1)} copy-done((s32[256,2]{0,1:T(2,128)S(1)}, s32[256,2]{0,1:T(2,128)}, u32[]{:S(2)}) %copy-start.7) | copy-done | bytes 2072
  9.9 0.0 copy-start.8
  9.9 0.7 %copy-done.8 = s32[256]{0:T(256)S(1)} copy-done((s32[256]{0:T(256)S(1)}, s32[256]{0:T(256)}, u32[]{:S(2)}) %copy-start.8) | copy-done | bytes 1048
  10.6 0.0 copy-start.9
  10.6 0.7 %copy-done.9 = s32[1,16]{1,0:T(1,128)S(1)} copy-done((s32[1,16]{1,0:T(1,128)S(1)}, s32[1,16]{1,0:T(1,128)}, u32[]{:S(2)}) %copy-start.9) | copy-done | bytes 88
  11.2 0.0 copy-start.10
  11.2 0.7 %copy-done.10 = f32[32]{0:T(128)S(1)} copy-done((f32[32]{0:T(128)S(1)}, f32[32]{0:T(128)}, u32[]{:S(2)}) %copy-start.10) | copy-done | bytes 152
  11.9 1.6 %prepare.1 = (bf16[256,1024]{1,0:T(8,128)(2,1)S(1)}, bf16[1024,256]{1,0:T(8,128)(2,1)S(1)}, bf16[512,1024]{1,0:T(8,128)(2,1)S(1)}, bf16[8,256,256]{2,1,0:T(8,128)(2,1)S(1)}, f32[1,128]{1,0:T(1,128)S(1)}) custom-call(s32[1,16]{1,0:T(1,128)S(1)} %copy-done.9, s32[16,64]{1,0:T(8,128)S(1)} %bitcast.20, s32[2,256]{1,0:T(2,128)S(1)} %bitcast.21, ...), custom_call_target="tpu_custom_call" | custom-call | tf_op jit(solution)/shard_map/prepare/pallas_call | solution.py:423
  13.5 0.0 collective-permute-done.refs_0_
  13.5 0.0 collective-permute-done.1.refs_1_
  13.5 0.0 collective-permute-done.2.refs_2_
  13.5 0.0 copy-start.3
  13.5 0.8 %copy-done.3 = bf16[176,128]{1,0:T(8,128)(2,1)S(1)} copy-done((bf16[176,128]{1,0:T(8,128)(2,1)S(1)}, bf16[176,128]{1,0:T(8,128)(2,1)}, u32[]{:S(2)}) %copy-start.3) | copy-done | bytes 45080
  14.3 0.0 copy-start.4
  14.3 0.0 copy-start.5
  14.3 1.7 %collective-permute-start.3 = (bf16[4,176,128]{2,1,0:T(8,128)(2,1)S(1)}, bf16[4,176,128]{2,1,0:T(8,128)(2,1)S(1)}, u32[]{:S(2)}, u32[]{:S(2)}) collective-permute-start(bf16[4,176,128]{2,1,0:T(8,128)(2,1)S(1)} %stack.1.after.near), channel_id=1, source_target_pairs={{0,2},{1,3},{2,0},{3,1},{4,6},{5,7},{6,4},{7,5},{8,10},{9,11},{10,... | collective-permute-start | bytes 540680 | tf_op jit(solution)/shard_map/ppermute | solution.py:373
  16.0 0.0 collective-permute-start.4
  16.0 0.0 copy-done
  16.0 0.0 copy-done.4
  16.1 0.0 copy-done.5
  16.1 2.5 %transform.1.after.image = bf16[8,256,256]{2,1,0:T(8,128)(2,1)S(1)} custom-call(bf16[4096,128]{1,0:T(8,128)(2,1)S(1)} %bitcast.18, f32[2,32,128]{2,1,0:T(8,128)S(1)} %copy-done.5, f32[2,32,128]{2,1,0:T(8,128)S(1)} %copy-done.4, bf16[4,176,128]{2,1,0:T(8,128)(2,1)S(1)} %stack.1.after.near), custom_call_target="tpu_custom_call" | custom-call | tf_op jit(solution)/shard_map/transform/pallas_call | solution.py:458
  18.5 1.6 %collective-permute-done.3.block.over_y = bf16[4,176,128]{2,1,0:T(8,128)(2,1)S(1)} collective-permute-done((bf16[4,176,128]{2,1,0:T(8,128)(2,1)S(1)}, bf16[4,176,128]{2,1,0:T(8,128)(2,1)S(1)}, u32[]{:S(2)}, u32[]{:S(2)}) %collective-permute-start.3) | collective-permute-done | bytes 180256 | tf_op jit(solution)/shard_map/ppermute | solution.py:373
  20.1 0.1 collective-permute-start.5
  20.2 0.0 collective-permute-done.4.over_core
  20.2 1.4 %collective-permute-done.5.over_both = bf16[4,176,128]{2,1,0:T(8,128)(2,1)S(1)} collective-permute-done((bf16[4,176,128]{2,1,0:T(8,128)(2,1)S(1)}, bf16[4,176,128]{2,1,0:T(8,128)(2,1)S(1)}, u32[]{:S(2)}, u32[]{:S(2)}) %collective-permute-start.5) | collective-permute-done | bytes 180256 | tf_op jit(solution)/shard_map/ppermute | solution.py:373
  21.6 0.0 copy-start.1
  21.6 6.3 %predict.1 = (bf16[4,64,128]{2,1,0:T(8,128)(2,1)S(1)}, bf16[4,64,128]{2,1,0:T(8,128)(2,1)S(1)}, bf16[4,64,128]{2,1,0:T(8,128)(2,1)S(1)}, bf16[4,64,128]{2,1,0:T(...) custom-call(s32[1]{0:T(128)} %bitcast.me, ...), custom_call_target="tpu_custom_call" | custom-call | tf_op jit(solution)/shard_map/predict/pallas_call | solution.py:487
  27.9 1.3 %collective-permute-start.6 = (bf16[4,64,128]{2,1,0:T(8,128)(2,1)S(1)}, bf16[4,64,128]{2,1,0:T(8,128)(2,1)S(1)}, u32[]{:S(2)}, u32[]{:S(2)}) collective-permute-start(bf16[4,64,128]{2,1,0:T(8,128)(2,1)S(1)} %get-tuple-element.39), channel_id=1, source_target_pairs={{0,3},{1,2},{2,1},{3,0},{4,7},{5,6},{6,5},{7,4},{8,11},{9,10},{10,... | collective-permute-start | bytes 196616 | tf_op jit(solution)/shard_map/ppermute | solution.py:373
  29.3 0.5 %collective-permute-start.7 = (bf16[4,64,128]{2,1,0:T(8,128)(2,1)S(1)}, bf16[4,64,128]{2,1,0:T(8,128)(2,1)S(1)}, u32[]{:S(2)}, u32[]{:S(2)}) collective-permute-start(bf16[4,64,128]{2,1,0:T(8,128)(2,1)S(1)} %get-tuple-element.40), channel_id=1, source_target_pairs={{0,2},{1,3},{2,0},{3,1},{4,6},{5,7},{6,4},{7,5},{8,10},{9,11},{10,... | collective-permute-start | bytes 196616 | tf_op jit(solution)/shard_map/ppermute | solution.py:373
  29.8 0.1 collective-permute-start.8
  29.9 3.5 %collective-permute-start.12 = (bf16[4,64,128]{2,1,0:T(8,128)(2,1)S(1)}, bf16[4,64,128]{2,1,0:T(8,128)(2,1)S(1)}, u32[]{:S(2)}, u32[]{:S(2)}) collective-permute-start(bf16[4,64,128]{2,1,0:T(8,128)(2,1)S(1)} %get-tuple-element.47), channel_id=1, source_target_pairs={{0,12},{1,13},{2,14},{3,15},{4,8},{5,9},{6,10},{7,11},{8,4},{9,5},... | collective-permute-start | bytes 196616 | tf_op jit(solution)/shard_map/ppermute | solution.py:373
  33.4 0.0 collective-permute-start.13
  33.4 0.0 collective-permute-done.6.refs_0_
  33.4 0.9 %collective-permute-start.14 = (bf16[4,64,128]{2,1,0:T(8,128)(2,1)S(1)}, bf16[4,64,128]{2,1,0:T(8,128)(2,1)S(1)}, u32[]{:S(2)}, u32[]{:S(2)}) collective-permute-start(bf16[4,64,128]{2,1,0:T(8,128)(2,1)S(1)} %get-tuple-element.49), channel_id=1, source_target_pairs={{0,4},{1,5},{2,6},{3,7},{4,0},{5,1},{6,2},{7,3},{8,12},{9,13},{10,... | collective-permute-start | bytes 196616 | tf_op jit(solution)/shard_map/ppermute | solution.py:373
  34.3 0.0 collective-permute-done.7.refs_1_
  34.3 0.0 collective-permute-done.8.refs_2_
  34.3 3.6 %collective-permute-start.9 = (bf16[4,64,128]{2,1,0:T(8,128)(2,1)S(1)}, bf16[4,64,128]{2,1,0:T(8,128)(2,1)S(1)}, u32[]{:S(2)}, u32[]{:S(2)}) collective-permute-start(bf16[4,64,128]{2,1,0:T(8,128)(2,1)S(1)} %get-tuple-element.43), channel_id=1, source_target_pairs={{0,12},{1,13},{2,14},{3,15},{4,8},{5,9},{6,10},{7,11},{8,4},{9,5},... | collective-permute-start | bytes 196616 | tf_op jit(solution)/shard_map/ppermute | solution.py:373
  37.9 0.0 collective-permute-start.10
  37.9 0.0 collective-permute-done.12.refs_0_
  37.9 0.9 %collective-permute-start.11 = (bf16[4,64,128]{2,1,0:T(8,128)(2,1)S(1)}, bf16[4,64,128]{2,1,0:T(8,128)(2,1)S(1)}, u32[]{:S(2)}, u32[]{:S(2)}) collective-permute-start(bf16[4,64,128]{2,1,0:T(8,128)(2,1)S(1)} %get-tuple-element.45), channel_id=1, source_target_pairs={{0,4},{1,5},{2,6},{3,7},{4,0},{5,1},{6,2},{7,3},{8,12},{9,13},{10,... | collective-permute-start | bytes 196616 | tf_op jit(solution)/shard_map/ppermute | solution.py:373
  38.8 1.9 %collective-permute-done.13.refs_1_ = bf16[4,64,128]{2,1,0:T(8,128)(2,1)S(1)} collective-permute-done((bf16[4,64,128]{2,1,0:T(8,128)(2,1)S(1)}, bf16[4,64,128]{2,1,0:T(8,128)(2,1)S(1)}, u32[]{:S(2)}, u32[]{:S(2)}) %collective-permute-start.13) | collective-permute-done | bytes 65568 | tf_op jit(solution)/shard_map/ppermute | solution.py:373
  40.7 0.0 collective-permute-done.14.refs_2_
  40.7 0.1 collective-permute-start.15
  40.8 1.5 %collective-permute-start.16 = (bf16[4,64,128]{2,1,0:T(8,128)(2,1)S(1)}, bf16[4,64,128]{2,1,0:T(8,128)(2,1)S(1)}, u32[]{:S(2)}, u32[]{:S(2)}) collective-permute-start(bf16[4,64,128]{2,1,0:T(8,128)(2,1)S(1)} %get-tuple-element.53), channel_id=1, source_target_pairs={{0,2},{1,3},{2,0},{3,1},{4,6},{5,7},{6,4},{7,5},{8,10},{9,11},{10,... | collective-permute-start | bytes 196616 | tf_op jit(solution)/shard_map/ppermute | solution.py:373
  42.4 0.0 collective-permute-done.9.refs_0_
  42.4 0.3 collective-permute-start.17
  42.7 2.3 %collective-permute-done.10.refs_1_ = bf16[4,64,128]{2,1,0:T(8,128)(2,1)S(1)} collective-permute-done((bf16[4,64,128]{2,1,0:T(8,128)(2,1)S(1)}, bf16[4,64,128]{2,1,0:T(8,128)(2,1)S(1)}, u32[]{:S(2)}, u32[]{:S(2)}) %collective-permute-start.10) | collective-permute-done | bytes 65568 | tf_op jit(solution)/shard_map/ppermute | solution.py:373
  45.0 0.0 collective-permute-done.11.refs_2_
  45.0 0.0 collective-permute-done.15.refs_5_
  45.0 0.3 collective-permute-done.16.refs_6_
  45.3 1.1 %collective-permute-done.17.refs_7_ = bf16[4,64,128]{2,1,0:T(8,128)(2,1)S(1)} collective-permute-done((bf16[4,64,128]{2,1,0:T(8,128)(2,1)S(1)}, bf16[4,64,128]{2,1,0:T(8,128)(2,1)S(1)}, u32[]{:S(2)}, u32[]{:S(2)}) %collective-permute-start.17) | collective-permute-done | bytes 65568 | tf_op jit(solution)/shard_map/ppermute | solution.py:373
  46.4 0.0 copy-done.1
  46.4 1.1 %residual.1 = f32[16,128,128]{2,1,0:T(8,128)} custom-call(s32[1]{0:T(128)} %bitcast.me, f32[16,128,128]{2,1,0:T(8,128)S(1)} %bitcast.19, bf16[4,64,128]{2,1,0:T(8,128)(2,1)S(1)} %collective-permute-done.9.refs_0_, bf16[4,64,128]{2,1,0:T(8,128)(2,1)S(1)} %collective-permute-done.10.refs_1_, bf16[4,64,128]{2,1,0:T(8,128)(2,1)S(1)} %collective-permute-done.11.refs_2_, ...), custom_call_target="tpu_custom_call" | custom-call | tf_op jit(solution)/shard_map/residual/pallas_call | solution.py:538
  (4 shorter events, 0.1 us)
Async XLA Ops:
  0.0 16.0 %copy-start = (bf16[256,2,1024]{2,1,0:T(2,128)(2,1)S(1)}, bf16[256,2,1024]{2,1,0:T(2,128)(2,1)}, u32[]{:S(2)}) copy-start(bf16[256,2,1024]{2,1,0:T(2,128)(2,1)} %param.12) | copy-start | bytes 3145732
  1.7 11.8 %collective-permute-start = (bf16[176,128]{1,0:T(8,128)(2,1)}, bf16[176,128]{1,0:T(8,128)(2,1)S(1)}, u32[]{:S(2)}, u32[]{:S(2)}) collective-permute-start(bf16[176,128]{1,0:T(8,128)(2,1)} %get-tuple-element.30), channel_id=1, source_target_pairs={{0,12},{1,13},{2,14},{3,15},{4,8},{5,9},{6,10},{7,11},{8,4},{9,5},... | collective-permute-start | bytes 135176 | tf_op jit(solution)/shard_map/ppermute | solution.py:373
  6.8 6.7 %collective-permute-start.1 = (bf16[176,128]{1,0:T(8,128)(2,1)}, bf16[176,128]{1,0:T(8,128)(2,1)S(1)}, u32[]{:S(2)}, u32[]{:S(2)}) collective-permute-start(bf16[176,128]{1,0:T(8,128)(2,1)} %get-tuple-element.31), channel_id=1, source_target_pairs={{0,8},{1,9},{2,10},{3,11},{4,12},{5,13},{6,14},{7,15},{8,0},{9,1},... | collective-permute-start | bytes 135176 | tf_op jit(solution)/shard_map/ppermute | solution.py:373
  6.8 6.7 %collective-permute-start.2 = (bf16[176,128]{1,0:T(8,128)(2,1)}, bf16[176,128]{1,0:T(8,128)(2,1)S(1)}, u32[]{:S(2)}, u32[]{:S(2)}) collective-permute-start(bf16[176,128]{1,0:T(8,128)(2,1)} %get-tuple-element.32), channel_id=1, source_target_pairs={{0,4},{1,5},{2,6},{3,7},{4,0},{5,1},{6,2},{7,3},{8,12},{9,13},{10,... | collective-permute-start | bytes 135176 | tf_op jit(solution)/shard_map/ppermute | solution.py:373
  7.5 1.0 %copy-start.2 = (bf16[2,128,1024]{2,1,0:T(8,128)(2,1)S(1)}, bf16[2,128,1024]{2,1,0:T(8,128)(2,1)}, u32[]{:S(2)}) copy-start(bf16[2,128,1024]{2,1,0:T(8,128)(2,1)} %basis.1) | copy-start | bytes 1572868
  8.5 0.7 %copy-start.6 = (s32[1,16,64]{2,1,0:T(8,128)S(1)}, s32[1,16,64]{2,1,0:T(8,128)}, u32[]{:S(2)}) copy-start(s32[1,16,64]{2,1,0:T(8,128)} %param.15) | copy-start | bytes 12292
  9.2 0.7 %copy-start.7 = (s32[256,2]{0,1:T(2,128)S(1)}, s32[256,2]{0,1:T(2,128)}, u32[]{:S(2)}) copy-start(s32[256,2]{0,1:T(2,128)} %param.13) | copy-start | bytes 6148
  9.9 0.7 %copy-start.8 = (s32[256]{0:T(256)S(1)}, s32[256]{0:T(256)}, u32[]{:S(2)}) copy-start(s32[256]{0:T(256)} %param.14) | copy-start | bytes 3076
  10.6 0.7 %copy-start.9 = (s32[1,16]{1,0:T(1,128)S(1)}, s32[1,16]{1,0:T(1,128)}, u32[]{:S(2)}) copy-start(s32[1,16]{1,0:T(1,128)} %counts.1) | copy-start | bytes 196
  11.2 0.7 %copy-start.10 = (f32[32]{0:T(128)S(1)}, f32[32]{0:T(128)}, u32[]{:S(2)}) copy-start(f32[32]{0:T(128)} %param.19) | copy-start | bytes 388
  13.5 0.8 %copy-start.3 = (bf16[176,128]{1,0:T(8,128)(2,1)S(1)}, bf16[176,128]{1,0:T(8,128)(2,1)}, u32[]{:S(2)}) copy-start(bf16[176,128]{1,0:T(8,128)(2,1)} %get-tuple-element.33.refs_3_) | copy-start | bytes 135172
  14.3 1.8 %copy-start.4 = (f32[2,32,128]{2,1,0:T(8,128)S(1)}, f32[2,32,128]{2,1,0:T(8,128)}, u32[]{:S(2)}) copy-start(f32[2,32,128]{2,1,0:T(8,128)} %constant.9.clone.cell_turns) | copy-start | bytes 98308
  14.3 1.8 %copy-start.5 = (f32[2,32,128]{2,1,0:T(8,128)S(1)}, f32[2,32,128]{2,1,0:T(8,128)}, u32[]{:S(2)}) copy-start(f32[2,32,128]{2,1,0:T(8,128)} %constant.8.clone.row_turns) | copy-start | bytes 98308
  14.3 5.8 %collective-permute-start.3 = (bf16[4,176,128]{2,1,0:T(8,128)(2,1)S(1)}, bf16[4,176,128]{2,1,0:T(8,128)(2,1)S(1)}, u32[]{:S(2)}, u32[]{:S(2)}) collective-permute-start(bf16[4,176,128]{2,1,0:T(8,128)(2,1)S(1)} %stack.1.after.near), channel_id=1, source_target_pairs={{0,2},{1,3},{2,0},{3,1},{4,6},{5,7},{6,4},{7,5},{8,10},{9,11},{10,... | collective-permute-start | bytes 540680 | tf_op jit(solution)/shard_map/ppermute | solution.py:373
  16.0 4.2 %collective-permute-start.4 = (bf16[4,176,128]{2,1,0:T(8,128)(2,1)S(1)}, bf16[4,176,128]{2,1,0:T(8,128)(2,1)S(1)}, u32[]{:S(2)}, u32[]{:S(2)}) collective-permute-start(bf16[4,176,128]{2,1,0:T(8,128)(2,1)S(1)} %stack.1.after.near), channel_id=1, source_target_pairs={{0,1},{1,0},{2,3},{3,2},{4,5},{5,4},{6,7},{7,6},{8,9},{9,8},{10,11... | collective-permute-start | bytes 540680 | tf_op jit(solution)/shard_map/ppermute | solution.py:373
  20.1 1.5 %collective-permute-start.5 = (bf16[4,176,128]{2,1,0:T(8,128)(2,1)S(1)}, bf16[4,176,128]{2,1,0:T(8,128)(2,1)S(1)}, u32[]{:S(2)}, u32[]{:S(2)}) collective-permute-start(bf16[4,176,128]{2,1,0:T(8,128)(2,1)S(1)} %relay.1), channel_id=1, source_target_pairs={{0,1},{1,0},{2,3},{3,2},{4,5},{5,4},{6,7},{7,6},{8,9},{9,8},{10,11... | collective-permute-start | bytes 540680 | tf_op jit(solution)/shard_map/ppermute | solution.py:373
  21.6 24.8 %copy-start.1 = (f32[1,16,64,2,128]{4,3,2,1,0:T(2,128)S(1)}, f32[1,16,64,2,128]{4,3,2,1,0:T(2,128)}, u32[]{:S(2)}) copy-start(f32[1,16,64,2,128]{4,3,2,1,0:T(2,128)} %param.21) | copy-start | bytes 3145732
  27.9 5.4 %collective-permute-start.6 = (bf16[4,64,128]{2,1,0:T(8,128)(2,1)S(1)}, bf16[4,64,128]{2,1,0:T(8,128)(2,1)S(1)}, u32[]{:S(2)}, u32[]{:S(2)}) collective-permute-start(bf16[4,64,128]{2,1,0:T(8,128)(2,1)S(1)} %get-tuple-element.39), channel_id=1, source_target_pairs={{0,3},{1,2},{2,1},{3,0},{4,7},{5,6},{6,5},{7,4},{8,11},{9,10},{10,... | collective-permute-start | bytes 196616 | tf_op jit(solution)/shard_map/ppermute | solution.py:373
  29.3 5.0 %collective-permute-start.7 = (bf16[4,64,128]{2,1,0:T(8,128)(2,1)S(1)}, bf16[4,64,128]{2,1,0:T(8,128)(2,1)S(1)}, u32[]{:S(2)}, u32[]{:S(2)}) collective-permute-start(bf16[4,64,128]{2,1,0:T(8,128)(2,1)S(1)} %get-tuple-element.40), channel_id=1, source_target_pairs={{0,2},{1,3},{2,0},{3,1},{4,6},{5,7},{6,4},{7,5},{8,10},{9,11},{10,... | collective-permute-start | bytes 196616 | tf_op jit(solution)/shard_map/ppermute | solution.py:373
  29.8 4.5 %collective-permute-start.8 = (bf16[4,64,128]{2,1,0:T(8,128)(2,1)S(1)}, bf16[4,64,128]{2,1,0:T(8,128)(2,1)S(1)}, u32[]{:S(2)}, u32[]{:S(2)}) collective-permute-start(bf16[4,64,128]{2,1,0:T(8,128)(2,1)S(1)} %get-tuple-element.41), channel_id=1, source_target_pairs={{0,1},{1,0},{2,3},{3,2},{4,5},{5,4},{6,7},{7,6},{8,9},{9,8},{10,11... | collective-permute-start | bytes 196616 | tf_op jit(solution)/shard_map/ppermute | solution.py:373
  29.9 8.0 %collective-permute-start.12 = (bf16[4,64,128]{2,1,0:T(8,128)(2,1)S(1)}, bf16[4,64,128]{2,1,0:T(8,128)(2,1)S(1)}, u32[]{:S(2)}, u32[]{:S(2)}) collective-permute-start(bf16[4,64,128]{2,1,0:T(8,128)(2,1)S(1)} %get-tuple-element.47), channel_id=1, source_target_pairs={{0,12},{1,13},{2,14},{3,15},{4,8},{5,9},{6,10},{7,11},{8,4},{9,5},... | collective-permute-start | bytes 196616 | tf_op jit(solution)/shard_map/ppermute | solution.py:373
  33.4 7.3 %collective-permute-start.13 = (bf16[4,64,128]{2,1,0:T(8,128)(2,1)S(1)}, bf16[4,64,128]{2,1,0:T(8,128)(2,1)S(1)}, u32[]{:S(2)}, u32[]{:S(2)}) collective-permute-start(bf16[4,64,128]{2,1,0:T(8,128)(2,1)S(1)} %get-tuple-element.48), channel_id=1, source_target_pairs={{0,8},{1,9},{2,10},{3,11},{4,12},{5,13},{6,14},{7,15},{8,0},{9,1},... | collective-permute-start | bytes 196616 | tf_op jit(solution)/shard_map/ppermute | solution.py:373
  33.4 7.3 %collective-permute-start.14 = (bf16[4,64,128]{2,1,0:T(8,128)(2,1)S(1)}, bf16[4,64,128]{2,1,0:T(8,128)(2,1)S(1)}, u32[]{:S(2)}, u32[]{:S(2)}) collective-permute-start(bf16[4,64,128]{2,1,0:T(8,128)(2,1)S(1)} %get-tuple-element.49), channel_id=1, source_target_pairs={{0,4},{1,5},{2,6},{3,7},{4,0},{5,1},{6,2},{7,3},{8,12},{9,13},{10,... | collective-permute-start | bytes 196616 | tf_op jit(solution)/shard_map/ppermute | solution.py:373
  34.3 8.1 %collective-permute-start.9 = (bf16[4,64,128]{2,1,0:T(8,128)(2,1)S(1)}, bf16[4,64,128]{2,1,0:T(8,128)(2,1)S(1)}, u32[]{:S(2)}, u32[]{:S(2)}) collective-permute-start(bf16[4,64,128]{2,1,0:T(8,128)(2,1)S(1)} %get-tuple-element.43), channel_id=1, source_target_pairs={{0,12},{1,13},{2,14},{3,15},{4,8},{5,9},{6,10},{7,11},{8,4},{9,5},... | collective-permute-start | bytes 196616 | tf_op jit(solution)/shard_map/ppermute | solution.py:373
  37.9 7.1 %collective-permute-start.10 = (bf16[4,64,128]{2,1,0:T(8,128)(2,1)S(1)}, bf16[4,64,128]{2,1,0:T(8,128)(2,1)S(1)}, u32[]{:S(2)}, u32[]{:S(2)}) collective-permute-start(bf16[4,64,128]{2,1,0:T(8,128)(2,1)S(1)} %get-tuple-element.44), channel_id=1, source_target_pairs={{0,8},{1,9},{2,10},{3,11},{4,12},{5,13},{6,14},{7,15},{8,0},{9,1},... | collective-permute-start | bytes 196616 | tf_op jit(solution)/shard_map/ppermute | solution.py:373
  37.9 7.1 %collective-permute-start.11 = (bf16[4,64,128]{2,1,0:T(8,128)(2,1)S(1)}, bf16[4,64,128]{2,1,0:T(8,128)(2,1)S(1)}, u32[]{:S(2)}, u32[]{:S(2)}) collective-permute-start(bf16[4,64,128]{2,1,0:T(8,128)(2,1)S(1)} %get-tuple-element.45), channel_id=1, source_target_pairs={{0,4},{1,5},{2,6},{3,7},{4,0},{5,1},{6,2},{7,3},{8,12},{9,13},{10,... | collective-permute-start | bytes 196616 | tf_op jit(solution)/shard_map/ppermute | solution.py:373
  40.7 4.2 %collective-permute-start.15 = (bf16[4,64,128]{2,1,0:T(8,128)(2,1)S(1)}, bf16[4,64,128]{2,1,0:T(8,128)(2,1)S(1)}, u32[]{:S(2)}, u32[]{:S(2)}) collective-permute-start(bf16[4,64,128]{2,1,0:T(8,128)(2,1)S(1)} %get-tuple-element.52), channel_id=1, source_target_pairs={{0,1},{1,0},{2,3},{3,2},{4,5},{5,4},{6,7},{7,6},{8,9},{9,8},{10,11... | collective-permute-start | bytes 196616 | tf_op jit(solution)/shard_map/ppermute | solution.py:373
  40.8 4.5 %collective-permute-start.16 = (bf16[4,64,128]{2,1,0:T(8,128)(2,1)S(1)}, bf16[4,64,128]{2,1,0:T(8,128)(2,1)S(1)}, u32[]{:S(2)}, u32[]{:S(2)}) collective-permute-start(bf16[4,64,128]{2,1,0:T(8,128)(2,1)S(1)} %get-tuple-element.53), channel_id=1, source_target_pairs={{0,2},{1,3},{2,0},{3,1},{4,6},{5,7},{6,4},{7,5},{8,10},{9,11},{10,... | collective-permute-start | bytes 196616 | tf_op jit(solution)/shard_map/ppermute | solution.py:373
  42.4 4.0 %collective-permute-start.17 = (bf16[4,64,128]{2,1,0:T(8,128)(2,1)S(1)}, bf16[4,64,128]{2,1,0:T(8,128)(2,1)S(1)}, u32[]{:S(2)}, u32[]{:S(2)}) collective-permute-start(bf16[4,64,128]{2,1,0:T(8,128)(2,1)S(1)} %get-tuple-element.54), channel_id=1, source_target_pairs={{0,3},{1,2},{2,1},{3,0},{4,7},{5,6},{6,5},{7,4},{8,11},{9,10},{10,... | collective-permute-start | bytes 196616 | tf_op jit(solution)/shard_map/ppermute | solution.py:373

commit v9 on v7

--- a/solution.py
+++ b/solution.py
@@ -80,7 +80,7 @@
     copy.wait()
     step = 16
 
-    @pl.loop(0, number // step, unroll=2)
+    @pl.loop(0, number // step, unroll=8)
     def _(n):
         rows = pl.ds(pl.multiple_of(n * step, step), step)
         span = pl.ds(pl.multiple_of(n * step * 16, step * 16), step * 16)
@@ -102,7 +102,7 @@
 
 
 def prepare_kernel(
-    counts, assign, stations, time_slots, basis, freq, route, back, pick, weights, turns, *, slot_count
+    counts, assign, stations, time_slots, basis, freq, after, route, back, pick, weights, turns, *, slot_count
 ):
     number = route.shape[0]
     tiles, capacity = assign.shape
@@ -189,10 +189,20 @@
         out[r][2 * rows :, :] = pieces.astype(BF16)
 
 
-def stack_kernel(*refs):
-    blocks, out = refs[:-3], refs[-1]
-    for r, block in enumerate(blocks):
-        out[r] = block[...]
+def stack_kernel(me, *refs):
+    blocks, near, for_y = refs[:-3], refs[-2], refs[-1]
+    pair = near.shape[1] - for_y.shape[1]
+    table = for_y.shape[1] - pair
+    for r, block in enumerate(blocks[::-1]):
+        near[r] = block[...]
+        tracks = block[table:, :].astype(F32)
+        tracks = jnp.where(me[0] & 2 == 0, tracks[pair:, :], tracks[:pair, :])
+        for_y[r, :table, :] = block[:table, :]
+        for_y[r, table:, :] = tracks.astype(BF16)
+
+
+def relay_kernel(block, after, out):
+    out[...] = block[...]
 
 
 def predict_kernel(
@@ -227,7 +237,8 @@
             table[at, :128] = arrived[r, :rows_own, :]
             table[at, 128:] = arrived[r, rows_own : 2 * rows_own, :]
             piece = arrived[r, 2 * rows_own :, :].astype(F32)
-            piece = jnp.where(mine & 2 == 0, piece[:kinds3, :], piece[kinds3:, :])
+            if piece.shape[0] > kinds3:
+                piece = jnp.where(mine & 2 == 0, piece[:kinds3, :], piece[kinds3:, :])
             moved = jnp.where(mine & 1 == 0, piece, pltpu.roll(piece, 128 - capacity, 1))
             lanes[owner] = moved[:, :capacity]
     per = 128 // capacity
@@ -289,7 +300,7 @@
             wre[to, :] = i_re * g_re - i_im * g_im
             wim[to, :] = i_re * g_im + i_im * g_re
 
-    unroll = 16
+    unroll = 64
 
     def one(g):
         at = pl.ds(pl.multiple_of(g * 8, 8), 8)
@@ -349,14 +360,14 @@
 def turn_kernel(*refs):
     count = refs[0].shape[0]
     blocks, out = refs[:-count], refs[-count:]
-    for i, block in enumerate(blocks):
+    for i, block in enumerate(blocks[::-1]):
         for j in range(count):
             out[j][i] = block[j]
 
 
 def residual_kernel(me, observed, *refs):
     arrived, residual = refs[:-1], refs[-1]
-    by_z, by_plane = arrived[:-4], arrived[-4:]
+    by_z, by_plane = arrived[:-4][::-1], arrived[-4:]
     rows = by_plane[0].shape[1]
     for r in range(len(by_z)):
         for p in range(4):
@@ -436,6 +447,19 @@
         name="transform",
     )(cells, jnp.asarray(row_turns), jnp.asarray(cell_turns))
 
+    near, for_y = pl.pallas_call(
+        stack_kernel,
+        out_shape=[
+            jax.ShapeDtypeStruct((outer,) + block.shape, BF16),
+            jax.ShapeDtypeStruct((outer, 2 * own_rows + 6 * steps, 128), BF16),
+        ],
+        in_specs=[smem] + [vmem] * outer + [anywhere],
+        out_specs=[vmem] * 2,
+        compiler_params=pltpu.CompilerParams(vmem_limit_bytes=3 * MIB * (tiles // 16)),
+        name="stack",
+    )(me, *along[::-1], image)
+    over_core = exchange(near, 1, tiles)
+    over_y = exchange(for_y, 2, tiles)
     route, back, pick, weights, turns = pl.pallas_call(
         functools.partial(prepare_kernel, slot_count=slot_count),
         out_shape=[
@@ -445,7 +469,7 @@
             jax.ShapeDtypeStruct((8, terms2, 256), BF16),
             jax.ShapeDtypeStruct((1, vis), F32),
         ],
-        in_specs=[smem] + [vmem] * 5,
+        in_specs=[smem] + [vmem] * 5 + [anywhere],
         out_specs=[vmem] * 5,
         compiler_params=pltpu.CompilerParams(vmem_limit_bytes=8 * MIB * (1 + tiles // 64)),
         name="prepare",
@@ -456,19 +480,18 @@
         time_slots.reshape(1, number),
         beam_basis,
         frequencies.reshape(1, chan),
+        near,
     )
 
-    near = pl.pallas_call(
-        stack_kernel,
-        out_shape=jax.ShapeDtypeStruct((outer,) + block.shape, BF16),
-        in_specs=[vmem] * outer + [anywhere] * 2,
+    over_both = pl.pallas_call(
+        relay_kernel,
+        out_shape=jax.ShapeDtypeStruct(over_y.shape, BF16),
+        in_specs=[vmem, anywhere],
         out_specs=vmem,
         compiler_params=pltpu.CompilerParams(vmem_limit_bytes=2 * MIB * (tiles // 16)),
-        name="stack",
-    )(*along, image, weights)
-    over_y = exchange(near, 2, tiles)
-    over_core = exchange(near, 1, tiles)
-    over_both = exchange(over_y, 1, tiles)
+        name="relay",
+    )(over_y, weights)
+    over_both = exchange(over_both, 1, tiles)
 
     for_z = jax.ShapeDtypeStruct((4, capacity, vis), BF16)
     for_plane = jax.ShapeDtypeStruct((outer, capacity, vis), BF16)
@@ -514,7 +537,7 @@
             out_specs=[vmem] * len(out_shape),
             compiler_params=pltpu.CompilerParams(vmem_limit_bytes=2 * MIB),
             name="turn",
-        )(*blocks)
+        )(*blocks[::-1])
 
     first, second = models[:outer], models[outer:]
     second = [second[0]] + [exchange(second[p], p, tiles) for p in range(1, 4)]
@@ -530,7 +553,7 @@
         out_specs=vmem,
         compiler_params=pltpu.CompilerParams(vmem_limit_bytes=6 * MIB),
         name="residual",
-    )(me, observed.reshape(tiles, 2 * capacity, vis), *second, *first)
+    )(me, observed.reshape(tiles, 2 * capacity, vis), *second[::-1], *first)
     return residual.reshape(observed.shape)
 
 

time: 49.4 us -> 43.8 us (0.89)
  the two profiles are of different devices: /device:TPU:17 before, /device:TPU:0 now
where the time goes in v9:
time: 43.8 us; the launch traced here: 43.5 us
  starting transfers between devices  20.1 us (46%)
  Pallas kernels  12.6 us (29%)
  waiting for transfers between devices  8.64 us (20%)
  local copies, waits for them, and re-layouts  1.92 us (4%)
    ppermute x18, starting transfers between devices, exchange(): return lax.ppermute(value, 'tile', [(i, i ^ step) for i in range(tiles)])  20.1 us
    ppermute x18, waiting for transfers between devices, exchange(): return lax.ppermute(value, 'tile', [(i, i ^ step) for i in range(tiles)])  8.64 us
    pallas_call x1, Pallas kernels, per_device(): pl.pallas_call(predict_kernel, out_shape=[for_z] * outer + [for_plane] *...  5.83 us
    pallas_call x1, Pallas kernels, per_device(): pl.pallas_call(transform_kernel, out_shape=jax.ShapeDtypeStruct((8, numbe...  2.44 us
    unnamed x22, local copies, waits for them, and re-layouts  1.92 us
    pallas_call x1, Pallas kernels, per_device(): pl.pallas_call(pack_kernel, out_shape=[block] * outer, in_specs=[smem, hb...  1.63 us
    pallas_call x1, Pallas kernels, per_device(): pl.pallas_call(functools.partial(prepare_kernel, slot_count=slot_count),...  1.58 us
    pallas_call x1, Pallas kernels, per_device(): pl.pallas_call(residual_kernel, out_shape=jax.ShapeDtypeStruct((tiles, 2...  1.06 us
  transfers between devices with their start and end apart: 18, of which 7 were waited for; matrix products, arithmetic and copies ran while one was open for 0% of the time, Pallas kernels for 9%

profile of v9, /device:TPU:0, one launch (start us, length us, event | category | flops | bytes accessed | tf_op | source)
XLA Modules:
  0.0 43.5 jit_solution(2591324711528399698)
XLA Ops:
  0.0 0.0 copy-start.4
  0.0 0.0 copy-start.5
  0.0 1.6 %pack.1 = (bf16[176,128]{1,0:T(8,128)(2,1)}, bf16[176,128]{1,0:T(8,128)(2,1)}, bf16[176,128]{1,0:T(8,128)(2,1)}, bf16[176,128]{1,0:T(8,128)(2,1)}) custom-call(s32[1]{0:T(128)} %bitcast.me, bf16[64,256]{1,0:T(8,128)(2,1)} %bitcast.25, f32[16,8,64]{2,1,0:T(8,128)} %bitcast.24), custom_call_target="tpu_custom_call" | custom-call | tf_op jit(solution)/shard_map/pack/pallas_call | solution.py:415
  1.6 5.1 %collective-permute-start = (bf16[176,128]{1,0:T(8,128)(2,1)}, bf16[176,128]{1,0:T(8,128)(2,1)S(1)}, u32[]{:S(2)}, u32[]{:S(2)}) collective-permute-start(bf16[176,128]{1,0:T(8,128)(2,1)} %get-tuple-element.32), channel_id=1, source_target_pairs={{0,12},{1,13},{2,14},{3,15},{4,8},{5,9},{6,10},{7,11},{8,4},{9,5},... | collective-permute-start | bytes 135176 | tf_op jit(solution)/shard_map/ppermute | solution.py:380
  6.8 0.0 collective-permute-start.1
  6.8 0.6 %collective-permute-start.2 = (bf16[176,128]{1,0:T(8,128)(2,1)}, bf16[176,128]{1,0:T(8,128)(2,1)S(1)}, u32[]{:S(2)}, u32[]{:S(2)}) collective-permute-start(bf16[176,128]{1,0:T(8,128)(2,1)} %get-tuple-element.34), channel_id=1, source_target_pairs={{0,4},{1,5},{2,6},{3,7},{4,0},{5,1},{6,2},{7,3},{8,12},{9,13},{10,... | collective-permute-start | bytes 135176 | tf_op jit(solution)/shard_map/ppermute | solution.py:380
  7.4 0.0 copy-done.4
  7.4 0.0 copy-done.5
  7.4 0.0 copy-start
  7.4 1.2 %copy-done = bf16[256,2,1024]{2,1,0:T(2,128)(2,1)S(1)} copy-done((bf16[256,2,1024]{2,1,0:T(2,128)(2,1)S(1)}, bf16[256,2,1024]{2,1,0:T(2,128)(2,1)}, u32[]{:S(2)}) %copy-start) | copy-done | bytes 1048600
  8.6 0.0 copy-start.3
  8.6 2.4 %transform.1.refs_4_.image = bf16[8,256,256]{2,1,0:T(8,128)(2,1)S(1)} custom-call(bf16[4096,128]{1,0:T(8,128)(2,1)S(1)} %bitcast.18, f32[2,32,128]{2,1,0:T(8,128)S(1)} %copy-done.5, f32[2,32,128]{2,1,0:T(8,128)S(1)} %copy-done.4), custom_call_target="tpu_custom_call" | custom-call | tf_op jit(solution)/shard_map/transform/pallas_call | solution.py:433
  11.1 0.0 collective-permute-done.refs_0_
  11.1 0.8 %collective-permute-done.1.refs_1_ = bf16[176,128]{1,0:T(8,128)(2,1)S(1)} collective-permute-done((bf16[176,128]{1,0:T(8,128)(2,1)}, bf16[176,128]{1,0:T(8,128)(2,1)S(1)}, u32[]{:S(2)}, u32[]{:S(2)}) %collective-permute-start.1) | collective-permute-done | bytes 45088 | tf_op jit(solution)/shard_map/ppermute | solution.py:380
  11.9 0.0 collective-permute-done.2.refs_2_
  11.9 0.0 copy-done.3
  11.9 0.0 copy-start.2
  11.9 0.0 copy-start.9
  11.9 0.0 copy-start.10
  12.0 0.0 copy-start.6
  12.0 1.6 %collective-permute-start.3 = (bf16[4,152,128]{2,1,0:T(8,128)(2,1)S(1)}, bf16[4,152,128]{2,1,0:T(8,128)(2,1)S(1)}, u32[]{:S(2)}, u32[]{:S(2)}) collective-permute-start(bf16[4,152,128]{2,1,0:T(8,128)(2,1)S(1)} %get-tuple-element.37), channel_id=1, source_target_pairs={{0,2},{1,3},{2,0},{3,1},{4,6},{5,7},{6,4},{7,5},{8,10},{9,11},{10,... | collective-permute-start | bytes 466952 | tf_op jit(solution)/shard_map/ppermute | solution.py:380
  13.6 0.0 collective-permute-start.4
  13.6 0.0 copy-start.7
  13.6 0.0 copy-start.8
  13.6 0.0 copy-done.2
  13.6 0.0 copy-done.9
  13.6 0.0 copy-done.10
  13.6 0.0 copy-done.6
  13.6 0.6 %copy-done.7 = s32[256,2]{0,1:T(2,128)S(1)} copy-done((s32[256,2]{0,1:T(2,128)S(1)}, s32[256,2]{0,1:T(2,128)}, u32[]{:S(2)}) %copy-start.7) | copy-done | bytes 2072
  14.3 0.0 copy-done.8
  14.3 1.6 %prepare.1 = (bf16[256,1024]{1,0:T(8,128)(2,1)S(1)}, bf16[1024,256]{1,0:T(8,128)(2,1)S(1)}, bf16[512,1024]{1,0:T(8,128)(2,1)S(1)}, bf16[8,256,256]{2,1,0:T(8,128)(2,1)S(1)}, f32[1,128]{1,0:T(1,128)S(1)}) custom-call(s32[1,16]{1,0:T(1,128)S(1)} %copy-done.9, s32[16,64]{1,0:T(8,128)S(1)} %bitcast.20, s32[2,256]{1,0:T(2,128)S(1)} %bitcast.21, ...), custom_call_target="tpu_custom_call" | custom-call | tf_op jit(solution)/shard_map/prepare/pallas_call | solution.py:463
  15.9 1.4 %collective-permute-done.3.block.over_y = bf16[4,152,128]{2,1,0:T(8,128)(2,1)S(1)} collective-permute-done((bf16[4,152,128]{2,1,0:T(8,128)(2,1)S(1)}, bf16[4,152,128]{2,1,0:T(8,128)(2,1)S(1)}, u32[]{:S(2)}, u32[]{:S(2)}) %collective-permute-start.3) | collective-permute-done | bytes 155680 | tf_op jit(solution)/shard_map/ppermute | solution.py:380
  17.3 0.1 collective-permute-start.5
  17.4 0.0 collective-permute-done.4.over_core
  17.4 1.4 %collective-permute-done.5.over_both = bf16[4,152,128]{2,1,0:T(8,128)(2,1)S(1)} collective-permute-done((bf16[4,152,128]{2,1,0:T(8,128)(2,1)S(1)}, bf16[4,152,128]{2,1,0:T(8,128)(2,1)S(1)}, u32[]{:S(2)}, u32[]{:S(2)}) %collective-permute-start.5) | collective-permute-done | bytes 155680 | tf_op jit(solution)/shard_map/ppermute | solution.py:380
  18.8 0.0 copy-start.1
  18.8 5.8 %predict.1 = (bf16[4,64,128]{2,1,0:T(8,128)(2,1)S(1)}, bf16[4,64,128]{2,1,0:T(8,128)(2,1)S(1)}, bf16[4,64,128]{2,1,0:T(8,128)(2,1)S(1)}, bf16[4,64,128]{2,1,0:T(...) custom-call(s32[1]{0:T(128)} %bitcast.me, ...), custom_call_target="tpu_custom_call" | custom-call | tf_op jit(solution)/shard_map/predict/pallas_call | solution.py:498
  24.6 1.3 %collective-permute-start.6 = (bf16[4,64,128]{2,1,0:T(8,128)(2,1)S(1)}, bf16[4,64,128]{2,1,0:T(8,128)(2,1)S(1)}, u32[]{:S(2)}, u32[]{:S(2)}) collective-permute-start(bf16[4,64,128]{2,1,0:T(8,128)(2,1)S(1)} %get-tuple-element.43), channel_id=1, source_target_pairs={{0,3},{1,2},{2,1},{3,0},{4,7},{5,6},{6,5},{7,4},{8,11},{9,10},{10,... | collective-permute-start | bytes 196616 | tf_op jit(solution)/shard_map/ppermute | solution.py:380
  25.9 0.5 %collective-permute-start.7 = (bf16[4,64,128]{2,1,0:T(8,128)(2,1)S(1)}, bf16[4,64,128]{2,1,0:T(8,128)(2,1)S(1)}, u32[]{:S(2)}, u32[]{:S(2)}) collective-permute-start(bf16[4,64,128]{2,1,0:T(8,128)(2,1)S(1)} %get-tuple-element.44), channel_id=1, source_target_pairs={{0,2},{1,3},{2,0},{3,1},{4,6},{5,7},{6,4},{7,5},{8,10},{9,11},{10,... | collective-permute-start | bytes 196616 | tf_op jit(solution)/shard_map/ppermute | solution.py:380
  26.5 0.1 collective-permute-start.8
  26.5 3.0 %collective-permute-start.12 = (bf16[4,64,128]{2,1,0:T(8,128)(2,1)S(1)}, bf16[4,64,128]{2,1,0:T(8,128)(2,1)S(1)}, u32[]{:S(2)}, u32[]{:S(2)}) collective-permute-start(bf16[4,64,128]{2,1,0:T(8,128)(2,1)S(1)} %get-tuple-element.51), channel_id=1, source_target_pairs={{0,12},{1,13},{2,14},{3,15},{4,8},{5,9},{6,10},{7,11},{8,4},{9,5},... | collective-permute-start | bytes 196616 | tf_op jit(solution)/shard_map/ppermute | solution.py:380
  29.5 0.0 collective-permute-start.13
  29.5 0.0 collective-permute-done.6.refs_0_
  29.5 1.4 %collective-permute-start.14 = (bf16[4,64,128]{2,1,0:T(8,128)(2,1)S(1)}, bf16[4,64,128]{2,1,0:T(8,128)(2,1)S(1)}, u32[]{:S(2)}, u32[]{:S(2)}) collective-permute-start(bf16[4,64,128]{2,1,0:T(8,128)(2,1)S(1)} %get-tuple-element.53), channel_id=1, source_target_pairs={{0,4},{1,5},{2,6},{3,7},{4,0},{5,1},{6,2},{7,3},{8,12},{9,13},{10,... | collective-permute-start | bytes 196616 | tf_op jit(solution)/shard_map/ppermute | solution.py:380
  30.9 0.0 collective-permute-done.7.refs_1_
  30.9 0.0 collective-permute-done.8.refs_2_
  31.0 3.0 %collective-permute-start.9 = (bf16[4,64,128]{2,1,0:T(8,128)(2,1)S(1)}, bf16[4,64,128]{2,1,0:T(8,128)(2,1)S(1)}, u32[]{:S(2)}, u32[]{:S(2)}) collective-permute-start(bf16[4,64,128]{2,1,0:T(8,128)(2,1)S(1)} %get-tuple-element.47), channel_id=1, source_target_pairs={{0,12},{1,13},{2,14},{3,15},{4,8},{5,9},{6,10},{7,11},{8,4},{9,5},... | collective-permute-start | bytes 196616 | tf_op jit(solution)/shard_map/ppermute | solution.py:380
  34.0 0.0 collective-permute-start.10
  34.0 0.0 collective-permute-done.12.refs_0_
  34.0 1.4 %collective-permute-start.11 = (bf16[4,64,128]{2,1,0:T(8,128)(2,1)S(1)}, bf16[4,64,128]{2,1,0:T(8,128)(2,1)S(1)}, u32[]{:S(2)}, u32[]{:S(2)}) collective-permute-start(bf16[4,64,128]{2,1,0:T(8,128)(2,1)S(1)} %get-tuple-element.49), channel_id=1, source_target_pairs={{0,4},{1,5},{2,6},{3,7},{4,0},{5,1},{6,2},{7,3},{8,12},{9,13},{10,... | collective-permute-start | bytes 196616 | tf_op jit(solution)/shard_map/ppermute | solution.py:380
  35.4 1.3 %collective-permute-done.13.refs_1_ = bf16[4,64,128]{2,1,0:T(8,128)(2,1)S(1)} collective-permute-done((bf16[4,64,128]{2,1,0:T(8,128)(2,1)S(1)}, bf16[4,64,128]{2,1,0:T(8,128)(2,1)S(1)}, u32[]{:S(2)}, u32[]{:S(2)}) %collective-permute-start.13) | collective-permute-done | bytes 65568 | tf_op jit(solution)/shard_map/ppermute | solution.py:380
  36.7 0.0 collective-permute-done.14.refs_2_
  36.7 0.1 collective-permute-start.15
  36.8 1.6 %collective-permute-start.16 = (bf16[4,64,128]{2,1,0:T(8,128)(2,1)S(1)}, bf16[4,64,128]{2,1,0:T(8,128)(2,1)S(1)}, u32[]{:S(2)}, u32[]{:S(2)}) collective-permute-start(bf16[4,64,128]{2,1,0:T(8,128)(2,1)S(1)} %get-tuple-element.57), channel_id=1, source_target_pairs={{0,2},{1,3},{2,0},{3,1},{4,6},{5,7},{6,4},{7,5},{8,10},{9,11},{10,... | collective-permute-start | bytes 196616 | tf_op jit(solution)/shard_map/ppermute | solution.py:380
  38.3 0.0 collective-permute-done.9.refs_0_
  38.4 0.3 collective-permute-start.17
  38.6 2.6 %collective-permute-done.10.refs_1_ = bf16[4,64,128]{2,1,0:T(8,128)(2,1)S(1)} collective-permute-done((bf16[4,64,128]{2,1,0:T(8,128)(2,1)S(1)}, bf16[4,64,128]{2,1,0:T(8,128)(2,1)S(1)}, u32[]{:S(2)}, u32[]{:S(2)}) %collective-permute-start.10) | collective-permute-done | bytes 65568 | tf_op jit(solution)/shard_map/ppermute | solution.py:380
  41.2 0.0 collective-permute-done.11.refs_2_
  41.2 0.0 collective-permute-done.15.refs_5_
  41.2 0.1 collective-permute-done.16.refs_6_
  41.3 1.1 %collective-permute-done.17.refs_7_ = bf16[4,64,128]{2,1,0:T(8,128)(2,1)S(1)} collective-permute-done((bf16[4,64,128]{2,1,0:T(8,128)(2,1)S(1)}, bf16[4,64,128]{2,1,0:T(8,128)(2,1)S(1)}, u32[]{:S(2)}, u32[]{:S(2)}) %collective-permute-start.17) | collective-permute-done | bytes 65568 | tf_op jit(solution)/shard_map/ppermute | solution.py:380
  42.4 0.0 copy-done.1
  42.4 1.1 %residual.1 = f32[16,128,128]{2,1,0:T(8,128)} custom-call(s32[1]{0:T(128)} %bitcast.me, f32[16,128,128]{2,1,0:T(8,128)S(1)} %bitcast.19, bf16[4,64,128]{2,1,0:T(8,128)(2,1)S(1)} %collective-permute-done.9.refs_0_, bf16[4,64,128]{2,1,0:T(8,128)(2,1)S(1)} %collective-permute-done.10.refs_1_, bf16[4,64,128]{2,1,0:T(8,128)(2,1)S(1)} %collective-permute-done.11.refs_2_, ...), custom_call_target="tpu_custom_call" | custom-call | tf_op jit(solution)/shard_map/residual/pallas_call | solution.py:549
  (4 shorter events, 0.1 us)
Async XLA Ops:
  0.0 7.4 %copy-start.4 = (f32[2,32,128]{2,1,0:T(8,128)S(1)}, f32[2,32,128]{2,1,0:T(8,128)}, u32[]{:S(2)}) copy-start(f32[2,32,128]{2,1,0:T(8,128)} %constant.9.clone.cell_turns) | copy-start | bytes 98308
  0.0 7.4 %copy-start.5 = (f32[2,32,128]{2,1,0:T(8,128)S(1)}, f32[2,32,128]{2,1,0:T(8,128)}, u32[]{:S(2)}) copy-start(f32[2,32,128]{2,1,0:T(8,128)} %constant.8.clone.row_turns) | copy-start | bytes 98308
  1.6 9.4 %collective-permute-start = (bf16[176,128]{1,0:T(8,128)(2,1)}, bf16[176,128]{1,0:T(8,128)(2,1)S(1)}, u32[]{:S(2)}, u32[]{:S(2)}) collective-permute-start(bf16[176,128]{1,0:T(8,128)(2,1)} %get-tuple-element.32), channel_id=1, source_target_pairs={{0,12},{1,13},{2,14},{3,15},{4,8},{5,9},{6,10},{7,11},{8,4},{9,5},... | collective-permute-start | bytes 135176 | tf_op jit(solution)/shard_map/ppermute | solution.py:380
  6.8 5.2 %collective-permute-start.1 = (bf16[176,128]{1,0:T(8,128)(2,1)}, bf16[176,128]{1,0:T(8,128)(2,1)S(1)}, u32[]{:S(2)}, u32[]{:S(2)}) collective-permute-start(bf16[176,128]{1,0:T(8,128)(2,1)} %get-tuple-element.33), channel_id=1, source_target_pairs={{0,8},{1,9},{2,10},{3,11},{4,12},{5,13},{6,14},{7,15},{8,0},{9,1},... | collective-permute-start | bytes 135176 | tf_op jit(solution)/shard_map/ppermute | solution.py:380
  6.8 5.2 %collective-permute-start.2 = (bf16[176,128]{1,0:T(8,128)(2,1)}, bf16[176,128]{1,0:T(8,128)(2,1)S(1)}, u32[]{:S(2)}, u32[]{:S(2)}) collective-permute-start(bf16[176,128]{1,0:T(8,128)(2,1)} %get-tuple-element.34), channel_id=1, source_target_pairs={{0,4},{1,5},{2,6},{3,7},{4,0},{5,1},{6,2},{7,3},{8,12},{9,13},{10,... | collective-permute-start | bytes 135176 | tf_op jit(solution)/shard_map/ppermute | solution.py:380
  7.4 1.2 %copy-start = (bf16[256,2,1024]{2,1,0:T(2,128)(2,1)S(1)}, bf16[256,2,1024]{2,1,0:T(2,128)(2,1)}, u32[]{:S(2)}) copy-start(bf16[256,2,1024]{2,1,0:T(2,128)(2,1)} %param.12) | copy-start | bytes 3145732
  8.6 3.3 %copy-start.3 = (bf16[176,128]{1,0:T(8,128)(2,1)S(1)}, bf16[176,128]{1,0:T(8,128)(2,1)}, u32[]{:S(2)}) copy-start(bf16[176,128]{1,0:T(8,128)(2,1)} %get-tuple-element.35.refs_3_) | copy-start | bytes 135172
  11.9 1.7 %copy-start.2 = (bf16[2,128,1024]{2,1,0:T(8,128)(2,1)S(1)}, bf16[2,128,1024]{2,1,0:T(8,128)(2,1)}, u32[]{:S(2)}) copy-start(bf16[2,128,1024]{2,1,0:T(8,128)(2,1)} %basis.1) | copy-start | bytes 1572868
  11.9 1.7 %copy-start.9 = (s32[1,16]{1,0:T(1,128)S(1)}, s32[1,16]{1,0:T(1,128)}, u32[]{:S(2)}) copy-start(s32[1,16]{1,0:T(1,128)} %counts.1) | copy-start | bytes 196
  11.9 1.7 %copy-start.10 = (f32[32]{0:T(128)S(1)}, f32[32]{0:T(128)}, u32[]{:S(2)}) copy-start(f32[32]{0:T(128)} %param.19) | copy-start | bytes 388
  12.0 1.6 %copy-start.6 = (s32[1,16,64]{2,1,0:T(8,128)S(1)}, s32[1,16,64]{2,1,0:T(8,128)}, u32[]{:S(2)}) copy-start(s32[1,16,64]{2,1,0:T(8,128)} %param.15) | copy-start | bytes 12292
  12.0 5.3 %collective-permute-start.3 = (bf16[4,152,128]{2,1,0:T(8,128)(2,1)S(1)}, bf16[4,152,128]{2,1,0:T(8,128)(2,1)S(1)}, u32[]{:S(2)}, u32[]{:S(2)}) collective-permute-start(bf16[4,152,128]{2,1,0:T(8,128)(2,1)S(1)} %get-tuple-element.37), channel_id=1, source_target_pairs={{0,2},{1,3},{2,0},{3,1},{4,6},{5,7},{6,4},{7,5},{8,10},{9,11},{10,... | collective-permute-start | bytes 466952 | tf_op jit(solution)/shard_map/ppermute | solution.py:380
  13.6 3.8 %collective-permute-start.4 = (bf16[4,176,128]{2,1,0:T(8,128)(2,1)S(1)}, bf16[4,176,128]{2,1,0:T(8,128)(2,1)S(1)}, u32[]{:S(2)}, u32[]{:S(2)}) collective-permute-start(bf16[4,176,128]{2,1,0:T(8,128)(2,1)S(1)} %get-tuple-element.36.after.near), channel_id=1, source_target_pairs={{0,1},{1,0},{2,3},{3,2},{4,5},{5,4},{6,7},{7,6},{8,9},{9,8},{10,11... | collective-permute-start | bytes 540680 | tf_op jit(solution)/shard_map/ppermute | solution.py:380
  13.6 0.7 %copy-start.7 = (s32[256,2]{0,1:T(2,128)S(1)}, s32[256,2]{0,1:T(2,128)}, u32[]{:S(2)}) copy-start(s32[256,2]{0,1:T(2,128)} %param.13) | copy-start | bytes 6148
  13.6 0.7 %copy-start.8 = (s32[256]{0:T(256)S(1)}, s32[256]{0:T(256)}, u32[]{:S(2)}) copy-start(s32[256]{0:T(256)} %param.14) | copy-start | bytes 3076
  17.3 1.4 %collective-permute-start.5 = (bf16[4,152,128]{2,1,0:T(8,128)(2,1)S(1)}, bf16[4,152,128]{2,1,0:T(8,128)(2,1)S(1)}, u32[]{:S(2)}, u32[]{:S(2)}) collective-permute-start(bf16[4,152,128]{2,1,0:T(8,128)(2,1)S(1)} %relay.1), channel_id=1, source_target_pairs={{0,1},{1,0},{2,3},{3,2},{4,5},{5,4},{6,7},{7,6},{8,9},{9,8},{10,11... | collective-permute-start | bytes 466952 | tf_op jit(solution)/shard_map/ppermute | solution.py:380
  18.8 23.6 %copy-start.1 = (f32[1,16,64,2,128]{4,3,2,1,0:T(2,128)S(1)}, f32[1,16,64,2,128]{4,3,2,1,0:T(2,128)}, u32[]{:S(2)}) copy-start(f32[1,16,64,2,128]{4,3,2,1,0:T(2,128)} %param.21) | copy-start | bytes 3145732
  24.6 4.9 %collective-permute-start.6 = (bf16[4,64,128]{2,1,0:T(8,128)(2,1)S(1)}, bf16[4,64,128]{2,1,0:T(8,128)(2,1)S(1)}, u32[]{:S(2)}, u32[]{:S(2)}) collective-permute-start(bf16[4,64,128]{2,1,0:T(8,128)(2,1)S(1)} %get-tuple-element.43), channel_id=1, source_target_pairs={{0,3},{1,2},{2,1},{3,0},{4,7},{5,6},{6,5},{7,4},{8,11},{9,10},{10,... | collective-permute-start | bytes 196616 | tf_op jit(solution)/shard_map/ppermute | solution.py:380
  25.9 5.0 %collective-permute-start.7 = (bf16[4,64,128]{2,1,0:T(8,128)(2,1)S(1)}, bf16[4,64,128]{2,1,0:T(8,128)(2,1)S(1)}, u32[]{:S(2)}, u32[]{:S(2)}) collective-permute-start(bf16[4,64,128]{2,1,0:T(8,128)(2,1)S(1)} %get-tuple-element.44), channel_id=1, source_target_pairs={{0,2},{1,3},{2,0},{3,1},{4,6},{5,7},{6,4},{7,5},{8,10},{9,11},{10,... | collective-permute-start | bytes 196616 | tf_op jit(solution)/shard_map/ppermute | solution.py:380
  26.5 4.5 %collective-permute-start.8 = (bf16[4,64,128]{2,1,0:T(8,128)(2,1)S(1)}, bf16[4,64,128]{2,1,0:T(8,128)(2,1)S(1)}, u32[]{:S(2)}, u32[]{:S(2)}) collective-permute-start(bf16[4,64,128]{2,1,0:T(8,128)(2,1)S(1)} %get-tuple-element.45), channel_id=1, source_target_pairs={{0,1},{1,0},{2,3},{3,2},{4,5},{5,4},{6,7},{7,6},{8,9},{9,8},{10,11... | collective-permute-start | bytes 196616 | tf_op jit(solution)/shard_map/ppermute | solution.py:380
  26.5 7.5 %collective-permute-start.12 = (bf16[4,64,128]{2,1,0:T(8,128)(2,1)S(1)}, bf16[4,64,128]{2,1,0:T(8,128)(2,1)S(1)}, u32[]{:S(2)}, u32[]{:S(2)}) collective-permute-start(bf16[4,64,128]{2,1,0:T(8,128)(2,1)S(1)} %get-tuple-element.51), channel_id=1, source_target_pairs={{0,12},{1,13},{2,14},{3,15},{4,8},{5,9},{6,10},{7,11},{8,4},{9,5},... | collective-permute-start | bytes 196616 | tf_op jit(solution)/shard_map/ppermute | solution.py:380
  29.5 7.2 %collective-permute-start.13 = (bf16[4,64,128]{2,1,0:T(8,128)(2,1)S(1)}, bf16[4,64,128]{2,1,0:T(8,128)(2,1)S(1)}, u32[]{:S(2)}, u32[]{:S(2)}) collective-permute-start(bf16[4,64,128]{2,1,0:T(8,128)(2,1)S(1)} %get-tuple-element.52), channel_id=1, source_target_pairs={{0,8},{1,9},{2,10},{3,11},{4,12},{5,13},{6,14},{7,15},{8,0},{9,1},... | collective-permute-start | bytes 196616 | tf_op jit(solution)/shard_map/ppermute | solution.py:380
  29.5 7.2 %collective-permute-start.14 = (bf16[4,64,128]{2,1,0:T(8,128)(2,1)S(1)}, bf16[4,64,128]{2,1,0:T(8,128)(2,1)S(1)}, u32[]{:S(2)}, u32[]{:S(2)}) collective-permute-start(bf16[4,64,128]{2,1,0:T(8,128)(2,1)S(1)} %get-tuple-element.53), channel_id=1, source_target_pairs={{0,4},{1,5},{2,6},{3,7},{4,0},{5,1},{6,2},{7,3},{8,12},{9,13},{10,... | collective-permute-start | bytes 196616 | tf_op jit(solution)/shard_map/ppermute | solution.py:380
  31.0 7.4 %collective-permute-start.9 = (bf16[4,64,128]{2,1,0:T(8,128)(2,1)S(1)}, bf16[4,64,128]{2,1,0:T(8,128)(2,1)S(1)}, u32[]{:S(2)}, u32[]{:S(2)}) collective-permute-start(bf16[4,64,128]{2,1,0:T(8,128)(2,1)S(1)} %get-tuple-element.47), channel_id=1, source_target_pairs={{0,12},{1,13},{2,14},{3,15},{4,8},{5,9},{6,10},{7,11},{8,4},{9,5},... | collective-permute-start | bytes 196616 | tf_op jit(solution)/shard_map/ppermute | solution.py:380
  34.0 7.2 %collective-permute-start.10 = (bf16[4,64,128]{2,1,0:T(8,128)(2,1)S(1)}, bf16[4,64,128]{2,1,0:T(8,128)(2,1)S(1)}, u32[]{:S(2)}, u32[]{:S(2)}) collective-permute-start(bf16[4,64,128]{2,1,0:T(8,128)(2,1)S(1)} %get-tuple-element.48), channel_id=1, source_target_pairs={{0,8},{1,9},{2,10},{3,11},{4,12},{5,13},{6,14},{7,15},{8,0},{9,1},... | collective-permute-start | bytes 196616 | tf_op jit(solution)/shard_map/ppermute | solution.py:380
  34.0 7.2 %collective-permute-start.11 = (bf16[4,64,128]{2,1,0:T(8,128)(2,1)S(1)}, bf16[4,64,128]{2,1,0:T(8,128)(2,1)S(1)}, u32[]{:S(2)}, u32[]{:S(2)}) collective-permute-start(bf16[4,64,128]{2,1,0:T(8,128)(2,1)S(1)} %get-tuple-element.49), channel_id=1, source_target_pairs={{0,4},{1,5},{2,6},{3,7},{4,0},{5,1},{6,2},{7,3},{8,12},{9,13},{10,... | collective-permute-start | bytes 196616 | tf_op jit(solution)/shard_map/ppermute | solution.py:380
  36.7 4.5 %collective-permute-start.15 = (bf16[4,64,128]{2,1,0:T(8,128)(2,1)S(1)}, bf16[4,64,128]{2,1,0:T(8,128)(2,1)S(1)}, u32[]{:S(2)}, u32[]{:S(2)}) collective-permute-start(bf16[4,64,128]{2,1,0:T(8,128)(2,1)S(1)} %get-tuple-element.56), channel_id=1, source_target_pairs={{0,1},{1,0},{2,3},{3,2},{4,5},{5,4},{6,7},{7,6},{8,9},{9,8},{10,11... | collective-permute-start | bytes 196616 | tf_op jit(solution)/shard_map/ppermute | solution.py:380
  36.8 4.5 %collective-permute-start.16 = (bf16[4,64,128]{2,1,0:T(8,128)(2,1)S(1)}, bf16[4,64,128]{2,1,0:T(8,128)(2,1)S(1)}, u32[]{:S(2)}, u32[]{:S(2)}) collective-permute-start(bf16[4,64,128]{2,1,0:T(8,128)(2,1)S(1)} %get-tuple-element.57), channel_id=1, source_target_pairs={{0,2},{1,3},{2,0},{3,1},{4,6},{5,7},{6,4},{7,5},{8,10},{9,11},{10,... | collective-permute-start | bytes 196616 | tf_op jit(solution)/shard_map/ppermute | solution.py:380
  38.4 4.0 %collective-permute-start.17 = (bf16[4,64,128]{2,1,0:T(8,128)(2,1)S(1)}, bf16[4,64,128]{2,1,0:T(8,128)(2,1)S(1)}, u32[]{:S(2)}, u32[]{:S(2)}) collective-permute-start(bf16[4,64,128]{2,1,0:T(8,128)(2,1)S(1)} %get-tuple-element.58), channel_id=1, source_target_pairs={{0,3},{1,2},{2,1},{3,0},{4,7},{5,6},{6,5},{7,4},{8,11},{9,10},{10,... | collective-permute-start | bytes 196616 | tf_op jit(solution)/shard_map/ppermute | solution.py:380

commit v10 on v9

--- a/solution.py
+++ b/solution.py
@@ -101,11 +101,18 @@
         image[m] = dot(left, right).astype(BF16)
 
 
+def relative(mine, place, tiles):
+    outer = tiles // 4
+    return mine ^ (4 * (place % outer) + place // outer)
+
+
 def prepare_kernel(
-    counts, assign, stations, time_slots, basis, freq, after, route, back, pick, weights, turns, *, slot_count
+    me, counts, assign, stations, time_slots, basis, freq, after, route, back, pick, weights, turns, *, slot_count
 ):
     number = route.shape[0]
     tiles, capacity = assign.shape
+    outer = tiles // 4
+    mine = me[0]
     scaled = freq[...] * (-1.0 / 32.0)
     turns[...] = jnp.concatenate([scaled] * (turns.shape[1] // freq.shape[1]), axis=1)
 
@@ -113,16 +120,20 @@
     down = lax.broadcasted_iota(jnp.int32, (number, 128), 0)
     slot = lax.broadcasted_iota(jnp.int32, (1, capacity), 1)
     for n in range(tiles // per):
-        chosen = [
-            jnp.where(slot < counts[0, d], assign[d : d + 1, :], -1)
-            for d in range(n * per, (n + 1) * per)
-        ]
+        chosen = []
+        for place in range(n * per, (n + 1) * per):
+            d = relative(mine, place, tiles)
+            chosen.append(jnp.where(slot < counts[0, d], assign[pl.ds(d, 1), :], -1))
         hot = (jnp.concatenate(chosen, axis=1) == down).astype(F32)
         route[:, n * 128 : (n + 1) * 128] = hot.astype(BF16)
         back[n * 128 : (n + 1) * 128, :] = hot.T.astype(BF16)
 
-    index = (stations[...] * slot_count + time_slots[...]).astype(F32)
-    index = jnp.concatenate([index, jnp.zeros((6, number), F32)], axis=0).T
+    rows_own = pick.shape[1] // tiles
+    each = rows_own // slot_count
+    away = (stations[...] // each) ^ mine
+    place = away % 4 * outer + away // 4
+    index = place * rows_own + stations[...] % each * slot_count + time_slots[...]
+    index = jnp.concatenate([index.astype(F32), jnp.zeros((6, number), F32)], axis=0).T
     index = index.astype(jnp.int32)
     across = lax.broadcasted_iota(jnp.int32, (number, pick.shape[1]), 1)
     for which in range(2):
@@ -161,7 +172,7 @@
 
 
 def pack_kernel(me, coefs_hbm, tracks_hbm, *refs):
-    out, (coefs, tracks, sems) = refs[:-3], refs[-3:]
+    out, for_y, coefs, tracks, sems = refs[:-4], *refs[-4:]
     copies = [
         pltpu.make_async_copy(coefs_hbm, coefs, sems.at[0]),
         pltpu.make_async_copy(tracks_hbm, tracks, sems.at[1]),
@@ -177,9 +188,8 @@
         kept = []
         for k in (0, 2):
             tr = jnp.concatenate([tracks[plane * 4 + k], tracks[plane * 4 + k + 1]], axis=1)
-            t_hi = tr.astype(BF16).astype(F32)
-            t_mid = (tr - t_hi).astype(BF16).astype(F32)
-            kept += [t_hi, t_mid, tr - t_hi - t_mid]
+            top = tr.astype(BF16).astype(F32)
+            kept += [top, tr - top]
         pieces = jnp.concatenate(kept, axis=0)
         if 2 * capacity < 128:
             blank = jnp.zeros((pieces.shape[0], 128 - 2 * capacity), F32)
@@ -187,29 +197,61 @@
         out[r][:rows, :] = coefs[:, :128]
         out[r][rows : 2 * rows, :] = coefs[:, 128:]
         out[r][2 * rows :, :] = pieces.astype(BF16)
+        if r == 0:
+            for_y[:rows, :] = coefs[:, :128]
+            for_y[rows : 2 * rows, :] = coefs[:, 128:]
+            for_y[2 * rows :, :] = own_pair(pieces, me[0] ^ 2).astype(BF16)
+
+
+def own_pair(pieces, device):
+    half = pieces.shape[0] // 2
+    return jnp.where(device & 2 == 0, pieces[:half, :], pieces[half:, :])
 
 
 def stack_kernel(me, *refs):
-    blocks, near, for_y = refs[:-3], refs[-2], refs[-1]
-    pair = near.shape[1] - for_y.shape[1]
-    table = for_y.shape[1] - pair
+    blocks, near, for_y = refs[:-4], refs[-2], refs[-1]
+    table = 2 * for_y.shape[1] - near.shape[1]
     for r, block in enumerate(blocks[::-1]):
         near[r] = block[...]
-        tracks = block[table:, :].astype(F32)
-        tracks = jnp.where(me[0] & 2 == 0, tracks[pair:, :], tracks[:pair, :])
-        for_y[r, :table, :] = block[:table, :]
-        for_y[r, table:, :] = tracks.astype(BF16)
-
-
-def relay_kernel(block, after, out):
-    out[...] = block[...]
+        if r > 0:
+            for_y[r - 1, :table, :] = block[:table, :]
+            tracks = own_pair(block[table:, :].astype(F32), me[0] ^ 2)
+            for_y[r - 1, table:, :] = tracks.astype(BF16)
+
+
+def relay_kernel(own, others, after, out):
+    out[0] = own[...]
+    for r in range(others.shape[0]):
+        out[r + 1] = others[r]
+
+
+def unpacked(mine, groups, table, rows_own, capacity):
+    kept = []
+    for arrived in groups:
+        for r in range(arrived.shape[0]):
+            at = slice(len(kept) * rows_own, (len(kept) + 1) * rows_own)
+            table[at, :128] = arrived[r, :rows_own, :]
+            table[at, 128:] = arrived[r, rows_own : 2 * rows_own, :]
+            piece = arrived[r, 2 * rows_own :, :].astype(F32)
+            if arrived.shape[1] == groups[0].shape[1] and len(groups) > 1:
+                piece = own_pair(piece, mine)
+            moved = jnp.where(mine & 1 == 0, piece, pltpu.roll(piece, 128 - capacity, 1))
+            kept.append(moved[:, :capacity])
+    per = 128 // capacity
+    tiles = [jnp.concatenate(kept[n : n + per], axis=1) for n in range(0, len(kept), per)]
+    return jnp.concatenate(tiles, axis=1).astype(BF16)
+
+
+def early_kernel(me, near, over_core, over_y, route, pick, coef, per_sub, table, *, capacity):
+    places = 3 * near.shape[0]
+    rows = table.shape[0]
+    pieces = unpacked(me[0], (near, over_core, over_y), table, rows // places, capacity)
+    coef[...] = dot(pick[:, :rows], table[...]).astype(BF16)
+    per_sub[...] = dot(route[:, : places * capacity], pieces, NT)
 
 
 def predict_kernel(
     me,
-    near,
-    over_y,
-    over_core,
     over_both,
     route,
     back,
@@ -217,44 +259,27 @@
     weights,
     turns,
     image,
+    coef_early,
+    per_sub_early,
     *refs,
 ):
-    table, lanes, coef, wre, wim, pure, puim, zrow, hre, him, zv, interleaved = refs[-12:]
+    table, coef, wre, wim, pure, puim, zrow, hre, him, zv, interleaved = refs[-11:]
     number = image.shape[1]
-    tiles, kinds3, capacity = lanes.shape
-    slots = tiles * capacity
-    rows_own = table.shape[0] // tiles
+    slots = back.shape[0]
+    outer = over_both.shape[0]
+    capacity = slots // (4 * outer)
+    rows = table.shape[0]
     vis = turns.shape[1]
-    kinds = kinds3 // 3
+    kinds = per_sub_early.shape[1] // 2
     steps = kinds // 2
     chan = vis // steps
-    mine = me[0]
-
-    for arrived, flip in ((near, 0), (over_y, 2), (over_core, 1), (over_both, 3)):
-        for r in range(arrived.shape[0]):
-            owner = mine ^ (4 * r + flip)
-            at = pl.ds(pl.multiple_of(owner * rows_own, rows_own), rows_own)
-            table[at, :128] = arrived[r, :rows_own, :]
-            table[at, 128:] = arrived[r, rows_own : 2 * rows_own, :]
-            piece = arrived[r, 2 * rows_own :, :].astype(F32)
-            if piece.shape[0] > kinds3:
-                piece = jnp.where(mine & 2 == 0, piece[:kinds3, :], piece[kinds3:, :])
-            moved = jnp.where(mine & 1 == 0, piece, pltpu.roll(piece, 128 - capacity, 1))
-            lanes[owner] = moved[:, :capacity]
-    per = 128 // capacity
-    pieces = jnp.concatenate(
-        [
-            jnp.concatenate([lanes[d] for d in range(n * per, (n + 1) * per)], axis=1)
-            for n in range(tiles // per)
-        ],
-        axis=1,
-    )
-    pieces = jnp.concatenate([pieces, jnp.zeros((kinds, slots), F32)], axis=0).astype(BF16)
-
-    per_sub = dot(route[...], pieces, NT).astype(BF16)
+    pieces = unpacked(me[0], (over_both,), table, rows // outer, capacity)
+
+    per_sub = per_sub_early[...] + dot(route[:, slots - outer * capacity :], pieces, NT)
+    per_sub = per_sub.astype(BF16)
     wide = 2 * steps * chan
-    from_row = lax.broadcasted_iota(jnp.int32, (4 * kinds, wide), 0) % kinds
-    to_lane = lax.broadcasted_iota(jnp.int32, (4 * kinds, wide), 1) // chan
+    from_row = lax.broadcasted_iota(jnp.int32, (2 * kinds, wide), 0) % kinds
+    to_lane = lax.broadcasted_iota(jnp.int32, (2 * kinds, wide), 1) // chan
     spread = (from_row == to_lane).astype(F32).astype(BF16)
     uv = dot(per_sub, spread)
     ur, ui = unit_powers(uv[:, :vis] * turns[...])
@@ -283,7 +308,8 @@
     zrow[4] = cr
     zrow[5] = ci
 
-    coef[...] = dot(pick[...], table[...]).astype(BF16)
+    last = dot(pick[:, pick.shape[1] - rows :], table[...])
+    coef[...] = (coef_early[...].astype(F32) + last).astype(BF16)
 
     block = 32
     for m in range(8):
@@ -300,7 +326,7 @@
             wre[to, :] = i_re * g_re - i_im * g_im
             wim[to, :] = i_re * g_im + i_im * g_re
 
-    unroll = 64
+    unroll = 128
 
     def one(g):
         at = pl.ds(pl.multiple_of(g * 8, 8), 8)
@@ -349,12 +375,12 @@
     sent = dot(back[...], models)
     interleaved[pl.ds(0, slots, stride=2), :] = sent[:, :128]
     interleaved[pl.ds(1, slots, stride=2), :] = sent[:, 128:]
-    along_z, in_plane = refs[: tiles // 4], refs[tiles // 4 : tiles // 4 + 4]
-    for r in range(tiles // 4):
+    along_z, in_plane = refs[:outer], refs[outer : outer + 4]
+    for r in range(outer):
         for p in range(4):
-            start = pl.multiple_of((mine ^ (4 * r + p)) * (2 * capacity), capacity)
-            along_z[r][p] = interleaved[pl.ds(start, capacity), :].astype(BF16)
-            in_plane[p][r] = interleaved[pl.ds(start + capacity, capacity), :].astype(BF16)
+            start = (p * outer + r) * (2 * capacity)
+            along_z[r][p] = interleaved[start : start + capacity, :].astype(BF16)
+            in_plane[p][r] = interleaved[start + capacity : start + 2 * capacity, :].astype(BF16)
 
 
 def turn_kernel(*refs):
@@ -365,15 +391,28 @@
             out[j][i] = block[j]
 
 
-def residual_kernel(me, observed, *refs):
-    arrived, residual = refs[:-1], refs[-1]
-    by_z, by_plane = arrived[:-4][::-1], arrived[-4:]
-    rows = by_plane[0].shape[1]
+def residual_second(me, observed, *refs):
+    by_z, (out, kept, sem) = refs[:-3][::-1], refs[-3:]
+    rows = kept.shape[1]
     for r in range(len(by_z)):
         for p in range(4):
             source = me[0] ^ (4 * r + p)
-            residual[source, :rows, :] = observed[source, :rows, :] - by_plane[p][r].astype(F32)
-            residual[source, rows:, :] = observed[source, rows:, :] - by_z[r][p].astype(F32)
+            kept[source] = observed[source, rows:, :] - by_z[r][p].astype(F32)
+    copy = pltpu.make_async_copy(kept, out.at[:, rows:, :], sem)
+    copy.start()
+    copy.wait()
+
+
+def residual_first(me, observed, second, *refs):
+    by_plane, (out, kept, sem) = refs[:-3], refs[-3:]
+    rows = kept.shape[1]
+    for p in range(4):
+        for r in range(by_plane[p].shape[0]):
+            source = me[0] ^ (4 * r + p)
+            kept[source] = observed[source, :rows, :] - by_plane[p][r].astype(F32)
+    copy = pltpu.make_async_copy(kept, out.at[:, :rows, :], sem)
+    copy.start()
+    copy.wait()
 
 
 def exchange(value, step, tiles):
@@ -411,12 +450,13 @@
     hbm = pl.BlockSpec(memory_space=pltpu.HBM)
     outer = tiles // 4
     me = lax.axis_index("tile").astype(jnp.int32).reshape(1)
-    block = jax.ShapeDtypeStruct((2 * own_rows + 12 * steps, 128), BF16)
-    packed = pl.pallas_call(
+    block = jax.ShapeDtypeStruct((2 * own_rows + 8 * steps, 128), BF16)
+    block_y = jax.ShapeDtypeStruct((2 * own_rows + 4 * steps, 128), BF16)
+    *packed, own_y = pl.pallas_call(
         pack_kernel,
-        out_shape=[block] * outer,
+        out_shape=[block] * outer + [block_y],
         in_specs=[smem, hbm, hbm],
-        out_specs=[vmem] * outer,
+        out_specs=[vmem] * (outer + 1),
         scratch_shapes=[
             pltpu.VMEM((own_rows, terms2), BF16),
             pltpu.VMEM((tiles, 2 * steps, capacity), F32),
@@ -426,6 +466,7 @@
         name="pack",
     )(me, beam_coefs.reshape(own_rows, terms2), own_tracks)
     along = [packed[0]] + [exchange(packed[r], 4 * r, tiles) for r in range(1, outer)]
+    own_over_y = exchange(own_y, 2, tiles)
 
     cells = jnp.transpose(subgrids.reshape(number, 2, 8, 128), (0, 2, 1, 3))
     cells = cells.reshape(number * 16, 128)
@@ -451,13 +492,13 @@
         stack_kernel,
         out_shape=[
             jax.ShapeDtypeStruct((outer,) + block.shape, BF16),
-            jax.ShapeDtypeStruct((outer, 2 * own_rows + 6 * steps, 128), BF16),
+            jax.ShapeDtypeStruct((outer - 1,) + block_y.shape, BF16),
         ],
-        in_specs=[smem] + [vmem] * outer + [anywhere],
+        in_specs=[smem] + [vmem] * outer + [anywhere] * 2,
         out_specs=[vmem] * 2,
         compiler_params=pltpu.CompilerParams(vmem_limit_bytes=3 * MIB * (tiles // 16)),
         name="stack",
-    )(me, *along[::-1], image)
+    )(me, *along[::-1], own_over_y, image)
     over_core = exchange(near, 1, tiles)
     over_y = exchange(for_y, 2, tiles)
     route, back, pick, weights, turns = pl.pallas_call(
@@ -469,11 +510,12 @@
             jax.ShapeDtypeStruct((8, terms2, 256), BF16),
             jax.ShapeDtypeStruct((1, vis), F32),
         ],
-        in_specs=[smem] + [vmem] * 5 + [anywhere],
+        in_specs=[smem] * 2 + [vmem] * 5 + [anywhere],
         out_specs=[vmem] * 5,
         compiler_params=pltpu.CompilerParams(vmem_limit_bytes=8 * MIB * (1 + tiles // 64)),
         name="prepare",
     )(
+        me,
         counts,
         assign[0],
         stations.T,
@@ -483,26 +525,37 @@
         near,
     )
 
-    over_both = pl.pallas_call(
+    over_y = pl.pallas_call(
         relay_kernel,
-        out_shape=jax.ShapeDtypeStruct(over_y.shape, BF16),
-        in_specs=[vmem, anywhere],
+        out_shape=jax.ShapeDtypeStruct((outer,) + block_y.shape, BF16),
+        in_specs=[vmem, vmem, anywhere],
         out_specs=vmem,
         compiler_params=pltpu.CompilerParams(vmem_limit_bytes=2 * MIB * (tiles // 16)),
         name="relay",
-    )(over_y, weights)
-    over_both = exchange(over_both, 1, tiles)
+    )(own_over_y, over_y, weights)
+    over_both = exchange(over_y, 1, tiles)
+    coef_early, per_sub_early = pl.pallas_call(
+        functools.partial(early_kernel, capacity=capacity),
+        out_shape=[
+            jax.ShapeDtypeStruct((2 * number, terms2), BF16),
+            jax.ShapeDtypeStruct((number, 4 * steps), F32),
+        ],
+        in_specs=[smem] + [vmem] * 5,
+        out_specs=[vmem] * 2,
+        scratch_shapes=[pltpu.VMEM((3 * outer * own_rows, terms2), BF16)],
+        compiler_params=pltpu.CompilerParams(vmem_limit_bytes=8 * MIB * (1 + tiles // 64)),
+        name="early",
+    )(me, near, over_core, over_y, route, pick)
 
     for_z = jax.ShapeDtypeStruct((4, capacity, vis), BF16)
     for_plane = jax.ShapeDtypeStruct((outer, capacity, vis), BF16)
     models = pl.pallas_call(
         predict_kernel,
         out_shape=[for_z] * outer + [for_plane] * 4,
-        in_specs=[smem] + [vmem] * 10,
+        in_specs=[smem] + [vmem] * 9,
         out_specs=[vmem] * (outer + 4),
         scratch_shapes=[
-            pltpu.VMEM((tiles * own_rows, terms2), BF16),
-            pltpu.VMEM((tiles, 6 * steps, capacity), F32),
+            pltpu.VMEM((outer * own_rows, terms2), BF16),
             pltpu.VMEM((2 * number, terms2), BF16),
             pltpu.VMEM((number * 8, 128), F32),
             pltpu.VMEM((number * 8, 128), F32),
@@ -518,9 +571,6 @@
         name="predict",
     )(
         me,
-        near,
-        over_y,
-        over_core,
         over_both,
         route,
         back,
@@ -528,6 +578,8 @@
         weights,
         turns,
         image,
+        coef_early,
+        per_sub_early,
     )
     def turned(blocks, out_shape):
         return pl.pallas_call(
@@ -546,14 +598,23 @@
     second = [second[0]] + [exchange(second[r], 4 * r, tiles) for r in range(1, outer)]
     first = turned(first, [for_plane] * 4)
     first = [first[0]] + [exchange(first[p], p, tiles) for p in range(1, 4)]
-    residual = pl.pallas_call(
-        residual_kernel,
-        out_shape=jax.ShapeDtypeStruct((tiles, 2 * capacity, vis), F32),
-        in_specs=[smem] + [vmem] * (5 + outer),
-        out_specs=vmem,
+    ours = observed.reshape(tiles, 2 * capacity, vis)
+    finish = functools.partial(
+        pl.pallas_call,
+        out_shape=jax.ShapeDtypeStruct(ours.shape, F32),
+        out_specs=anywhere,
+        scratch_shapes=[pltpu.VMEM((tiles, capacity, vis), F32), pltpu.SemaphoreType.DMA],
         compiler_params=pltpu.CompilerParams(vmem_limit_bytes=6 * MIB),
-        name="residual",
-    )(me, observed.reshape(tiles, 2 * capacity, vis), *second[::-1], *first)
+    )
+    residual = finish(
+        residual_second, in_specs=[smem] + [vmem] * (1 + outer), name="residual_second"
+    )(me, ours, *second[::-1])
+    residual = finish(
+        residual_first,
+        in_specs=[smem, vmem, anywhere] + [vmem] * 4,
+        input_output_aliases={2: 0},
+        name="residual_first",
+    )(me, ours, residual, *first)
     return residual.reshape(observed.shape)
 
 

time: 43.8 us -> 43.3 us (0.989)
    pallas_call x3 -> x5, Pallas kernels: 2.7 us -> 3.9 us  [the longest x1 1.63 us: per_device(): pl.pallas_call(pack_kernel, out_shape=[block] * outer + [block_y], in_spe...]
    pallas_call x1, Pallas kernels: 5.83 us -> 4.9 us  [per_device(): pl.pallas_call(predict_kernel, out_shape=[for_z] * outer + [for_plane] *...]
    ppermute x18 -> x19, waiting for transfers between devices: 8.64 us -> 8.22 us  [exchange(): return lax.ppermute(value, 'tile', [(i, i ^ step) for i in range(tiles)])]
    ppermute x18 -> x19, starting transfers between devices: 20.1 us -> 19.8 us  [exchange(): return lax.ppermute(value, 'tile', [(i, i ^ step) for i in range(tiles)])]
  transfers between devices with their start and end apart: 18 -> 19, of which waited for: 7 -> 6; matrix products, arithmetic and copies ran while one was open for 0% -> 0% of each run, Pallas kernels for 9% -> 13%
where the time goes in v10:
time: 43.3 us; the launch traced here: 43.1 us
  starting transfers between devices  19.8 us (46%)
  Pallas kernels  12.9 us (30%)
  waiting for transfers between devices  8.22 us (19%)
  local copies, waits for them, and re-layouts  1.99 us (5%)
    ppermute x19, starting transfers between devices, exchange(): return lax.ppermute(value, 'tile', [(i, i ^ step) for i in range(tiles)])  19.8 us
    ppermute x19, waiting for transfers between devices, exchange(): return lax.ppermute(value, 'tile', [(i, i ^ step) for i in range(tiles)])  8.22 us
    pallas_call x1, Pallas kernels, per_device(): pl.pallas_call(predict_kernel, out_shape=[for_z] * outer + [for_plane] *...  4.9 us
    pallas_call x1, Pallas kernels, per_device(): pl.pallas_call(transform_kernel, out_shape=jax.ShapeDtypeStruct((8, numbe...  2.44 us
    unnamed x22, local copies, waits for them, and re-layouts  1.99 us
    pallas_call x1, Pallas kernels, per_device(): pl.pallas_call(pack_kernel, out_shape=[block] * outer + [block_y], in_spe...  1.63 us
    pallas_call x1, Pallas kernels, per_device(): pl.pallas_call(functools.partial(prepare_kernel, slot_count=slot_count),...  1.59 us
  transfers between devices with their start and end apart: 19, of which 6 were waited for; matrix products, arithmetic and copies ran while one was open for 0% of the time, Pallas kernels for 13%

profile of v10, /device:TPU:0, one launch (start us, length us, event | category | flops | bytes accessed | tf_op | source)
XLA Modules:
  0.0 43.1 jit_solution(10621546687848741864)
XLA Ops:
  0.0 0.0 copy-start.4
  0.0 0.0 copy-start.5
  0.0 1.6 %pack.1 = (bf16[160,128]{1,0:T(8,128)(2,1)}, bf16[160,128]{1,0:T(8,128)(2,1)}, bf16[160,128]{1,0:T(8,128)(2,1)}, bf16[160,128]{1,0:T(8,128)(2,1)}, bf16[144,128]{1,0:T(8,128)(2,1)}) custom-call(s32[1]{0:T(128)} %bitcast.me, bf16[64,256]{1,0:T(8,128)(2,1)} %bitcast.26, f32[16,8,64]{2,1,0:T(8,128)} %bitcast.25), custom_call_target="tpu_custom_call" | custom-call | tf_op jit(solution)/shard_map/pack/pallas_call | solution.py:455
  1.6 5.1 %collective-permute-start.1 = (bf16[160,128]{1,0:T(8,128)(2,1)}, bf16[160,128]{1,0:T(8,128)(2,1)S(1)}, u32[]{:S(2)}, u32[]{:S(2)}) collective-permute-start(bf16[160,128]{1,0:T(8,128)(2,1)} %get-tuple-element.36), channel_id=1, source_target_pairs={{0,12},{1,13},{2,14},{3,15},{4,8},{5,9},{6,10},{7,11},{8,4},{9,5},... | collective-permute-start | bytes 122888 | tf_op jit(solution)/shard_map/ppermute | solution.py:419
  6.8 0.0 collective-permute-start.2
  6.8 0.6 %collective-permute-start.3 = (bf16[160,128]{1,0:T(8,128)(2,1)}, bf16[160,128]{1,0:T(8,128)(2,1)S(1)}, u32[]{:S(2)}, u32[]{:S(2)}) collective-permute-start(bf16[160,128]{1,0:T(8,128)(2,1)} %get-tuple-element.38), channel_id=1, source_target_pairs={{0,4},{1,5},{2,6},{3,7},{4,0},{5,1},{6,2},{7,3},{8,12},{9,13},{10,... | collective-permute-start | bytes 122888 | tf_op jit(solution)/shard_map/ppermute | solution.py:419
  7.4 1.7 %collective-permute-start = (bf16[144,128]{1,0:T(8,128)(2,1)}, bf16[144,128]{1,0:T(8,128)(2,1)S(1)}, u32[]{:S(2)}, u32[]{:S(2)}) collective-permute-start(bf16[144,128]{1,0:T(8,128)(2,1)} %get-tuple-element.35), channel_id=1, source_target_pairs={{0,2},{1,3},{2,0},{3,1},{4,6},{5,7},{6,4},{7,5},{8,10},{9,11},{10,... | collective-permute-start | bytes 110600 | tf_op jit(solution)/shard_map/ppermute | solution.py:419
  9.1 0.0 copy-done.4
  9.1 0.0 copy-done.5
  9.1 1.2 %copy-done.1 = bf16[256,2,1024]{2,1,0:T(2,128)(2,1)S(1)} copy-done((bf16[256,2,1024]{2,1,0:T(2,128)(2,1)S(1)}, bf16[256,2,1024]{2,1,0:T(2,128)(2,1)}, u32[]{:S(2)}) %copy-start.1) | copy-done | bytes 1048600
  10.3 0.0 copy-start.3
  10.3 2.4 %transform.1.refs_5_.image = bf16[8,256,256]{2,1,0:T(8,128)(2,1)S(1)} custom-call(bf16[4096,128]{1,0:T(8,128)(2,1)S(1)} %bitcast.20, f32[2,32,128]{2,1,0:T(8,128)S(1)} %copy-done.5, f32[2,32,128]{2,1,0:T(8,128)S(1)} %copy-done.4), custom_call_target="tpu_custom_call" | custom-call | tf_op jit(solution)/shard_map/transform/pallas_call | solution.py:474
  12.7 0.0 collective-permute-done.refs_4_.own
  12.8 0.0 collective-permute-done.1.refs_0_
  12.8 0.0 collective-permute-done.2.refs_1_
  12.8 0.0 collective-permute-done.3.refs_2_
  12.8 0.0 copy-done.3
  12.8 0.0 copy-start.2
  12.8 0.0 copy-start.9
  12.8 0.0 copy-start.10
  12.9 0.0 copy-start.6
  12.9 0.7 %collective-permute-start.4 = (bf16[3,144,128]{2,1,0:T(8,128)(2,1)S(1)}, bf16[3,144,128]{2,1,0:T(8,128)(2,1)S(1)}, u32[]{:S(2)}, u32[]{:S(2)}) collective-permute-start(bf16[3,144,128]{2,1,0:T(8,128)(2,1)S(1)} %get-tuple-element.40), channel_id=1, source_target_pairs={{0,2},{1,3},{2,0},{3,1},{4,6},{5,7},{6,4},{7,5},{8,10},{9,11},{10,... | collective-permute-start | bytes 331784 | tf_op jit(solution)/shard_map/ppermute | solution.py:419
  13.5 0.0 collective-permute-start.6
  13.5 0.0 copy-start.7
  13.6 0.3 copy-done.2
  13.8 0.0 copy-done.9
  13.8 0.0 copy-done.10
  13.9 0.0 copy-done.6
  13.9 0.4 copy-done.7
  14.3 0.0 copy-done.8
  14.3 1.6 %prepare.1 = (bf16[256,1024]{1,0:T(8,128)(2,1)S(1)}, bf16[1024,256]{1,0:T(8,128)(2,1)S(1)}, bf16[512,1024]{1,0:T(8,128)(2,1)S(1)}, bf16[8,256,256]{2,1,0:T(8,128)(2,1)S(1)}, f32[1,128]{1,0:T(1,128)S(1)}) custom-call(s32[1]{0:T(128)} %bitcast.me, s32[1,16]{1,0:T(1,128)S(1)} %copy-done.9, s32[16,64]{1,0:T(8,128)S(1)} %bitcast.21, s32[2,256]{1,0:T(2,128)S(1)} %bitcast.22, ...), custom_call_target="tpu_custom_call" | custom-call | tf_op jit(solution)/shard_map/prepare/pallas_call | solution.py:504
  15.9 1.8 %collective-permute-done.4.others = bf16[3,144,128]{2,1,0:T(8,128)(2,1)S(1)} collective-permute-done((bf16[3,144,128]{2,1,0:T(8,128)(2,1)S(1)}, bf16[3,144,128]{2,1,0:T(8,128)(2,1)S(1)}, u32[]{:S(2)}, u32[]{:S(2)}) %collective-permute-start.4) | collective-permute-done | bytes 110624 | tf_op jit(solution)/shard_map/ppermute | solution.py:419
  17.7 0.1 collective-permute-start.5
  17.8 0.0 collective-permute-done.6.over_core
  17.8 0.5 %early.1 = (bf16[512,256]{1,0:T(8,128)(2,1)S(1)}, f32[256,16]{1,0:T(8,128)S(1)}) custom-call(s32[1]{0:T(128)} %bitcast.me, bf16[4,160,128]{2,1,0:T(8,128)(2,1)S(1)} %get-tuple-element.41.after.near, bf16[4,160,128]{2,1,0:T(8,128)(2,1)S(1)} %collective-permute-done.6.over_core, bf16[4,144,128]{2,1,0:T(8,128)(2,1)S(1)} %relay.1.over_y, ...), custom_call_target="tpu_custom_call" | custom-call | tf_op jit(solution)/shard_map/early/pallas_call | solution.py:537
  18.3 0.8 %collective-permute-done.5.over_both = bf16[4,144,128]{2,1,0:T(8,128)(2,1)S(1)} collective-permute-done((bf16[4,144,128]{2,1,0:T(8,128)(2,1)S(1)}, bf16[4,144,128]{2,1,0:T(8,128)(2,1)S(1)}, u32[]{:S(2)}, u32[]{:S(2)}) %collective-permute-start.5) | collective-permute-done | bytes 147488 | tf_op jit(solution)/shard_map/ppermute | solution.py:419
  19.2 4.9 %predict.1 = (bf16[4,64,128]{2,1,0:T(8,128)(2,1)S(1)}, bf16[4,64,128]{2,1,0:T(8,128)(2,1)S(1)}, bf16[4,64,128]{2,1,0:T(8,128)(2,1)S(1)}, bf16[4,64,128]{2,1,0:T(...) custom-call(s32[1]{0:T(128)} %bitcast.me, ...), custom_call_target="tpu_custom_call" | custom-call | tf_op jit(solution)/shard_map/predict/pallas_call | solution.py:552
  24.1 0.4 collective-permute-start.7
  24.5 1.4 %collective-permute-start.8 = (bf16[4,64,128]{2,1,0:T(8,128)(2,1)S(1)}, bf16[4,64,128]{2,1,0:T(8,128)(2,1)S(1)}, u32[]{:S(2)}, u32[]{:S(2)}) collective-permute-start(bf16[4,64,128]{2,1,0:T(8,128)(2,1)S(1)} %get-tuple-element.50), channel_id=1, source_target_pairs={{0,2},{1,3},{2,0},{3,1},{4,6},{5,7},{6,4},{7,5},{8,10},{9,11},{10,... | collective-permute-start | bytes 196616 | tf_op jit(solution)/shard_map/ppermute | solution.py:419
  25.9 0.1 collective-permute-start.9
  26.0 3.6 %collective-permute-start.13 = (bf16[4,64,128]{2,1,0:T(8,128)(2,1)S(1)}, bf16[4,64,128]{2,1,0:T(8,128)(2,1)S(1)}, u32[]{:S(2)}, u32[]{:S(2)}) collective-permute-start(bf16[4,64,128]{2,1,0:T(8,128)(2,1)S(1)} %get-tuple-element.57), channel_id=1, source_target_pairs={{0,12},{1,13},{2,14},{3,15},{4,8},{5,9},{6,10},{7,11},{8,4},{9,5},... | collective-permute-start | bytes 196616 | tf_op jit(solution)/shard_map/ppermute | solution.py:419
  29.6 0.0 collective-permute-start.14
  29.6 0.0 collective-permute-done.7.refs_0_
  29.6 0.8 %collective-permute-start.15 = (bf16[4,64,128]{2,1,0:T(8,128)(2,1)S(1)}, bf16[4,64,128]{2,1,0:T(8,128)(2,1)S(1)}, u32[]{:S(2)}, u32[]{:S(2)}) collective-permute-start(bf16[4,64,128]{2,1,0:T(8,128)(2,1)S(1)} %get-tuple-element.59), channel_id=1, source_target_pairs={{0,4},{1,5},{2,6},{3,7},{4,0},{5,1},{6,2},{7,3},{8,12},{9,13},{10,... | collective-permute-start | bytes 196616 | tf_op jit(solution)/shard_map/ppermute | solution.py:419
  30.4 0.0 collective-permute-done.8.refs_1_
  30.4 0.0 collective-permute-done.9.refs_2_
  30.4 3.7 %collective-permute-start.10 = (bf16[4,64,128]{2,1,0:T(8,128)(2,1)S(1)}, bf16[4,64,128]{2,1,0:T(8,128)(2,1)S(1)}, u32[]{:S(2)}, u32[]{:S(2)}) collective-permute-start(bf16[4,64,128]{2,1,0:T(8,128)(2,1)S(1)} %get-tuple-element.53), channel_id=1, source_target_pairs={{0,12},{1,13},{2,14},{3,15},{4,8},{5,9},{6,10},{7,11},{8,4},{9,5},... | collective-permute-start | bytes 196616 | tf_op jit(solution)/shard_map/ppermute | solution.py:419
  34.1 0.0 collective-permute-start.11
  34.1 0.0 collective-permute-done.13.refs_0_
  34.1 0.8 %collective-permute-start.12 = (bf16[4,64,128]{2,1,0:T(8,128)(2,1)S(1)}, bf16[4,64,128]{2,1,0:T(8,128)(2,1)S(1)}, u32[]{:S(2)}, u32[]{:S(2)}) collective-permute-start(bf16[4,64,128]{2,1,0:T(8,128)(2,1)S(1)} %get-tuple-element.55), channel_id=1, source_target_pairs={{0,4},{1,5},{2,6},{3,7},{4,0},{5,1},{6,2},{7,3},{8,12},{9,13},{10,... | collective-permute-start | bytes 196616 | tf_op jit(solution)/shard_map/ppermute | solution.py:419
  34.9 1.3 %collective-permute-done.14.refs_1_ = bf16[4,64,128]{2,1,0:T(8,128)(2,1)S(1)} collective-permute-done((bf16[4,64,128]{2,1,0:T(8,128)(2,1)S(1)}, bf16[4,64,128]{2,1,0:T(8,128)(2,1)S(1)}, u32[]{:S(2)}, u32[]{:S(2)}) %collective-permute-start.14) | collective-permute-done | bytes 65568 | tf_op jit(solution)/shard_map/ppermute | solution.py:419
  36.2 0.0 collective-permute-done.15.refs_2_
  36.2 0.1 collective-permute-start.16
  36.3 0.7 %collective-permute-start.17 = (bf16[4,64,128]{2,1,0:T(8,128)(2,1)S(1)}, bf16[4,64,128]{2,1,0:T(8,128)(2,1)S(1)}, u32[]{:S(2)}, u32[]{:S(2)}) collective-permute-start(bf16[4,64,128]{2,1,0:T(8,128)(2,1)S(1)} %get-tuple-element.63), channel_id=1, source_target_pairs={{0,2},{1,3},{2,0},{3,1},{4,6},{5,7},{6,4},{7,5},{8,10},{9,11},{10,... | collective-permute-start | bytes 196616 | tf_op jit(solution)/shard_map/ppermute | solution.py:419
  37.0 1.1 %collective-permute-done.10.refs_0_ = bf16[4,64,128]{2,1,0:T(8,128)(2,1)S(1)} collective-permute-done((bf16[4,64,128]{2,1,0:T(8,128)(2,1)S(1)}, bf16[4,64,128]{2,1,0:T(8,128)(2,1)S(1)}, u32[]{:S(2)}, u32[]{:S(2)}) %collective-permute-start.10) | collective-permute-done | bytes 65568 | tf_op jit(solution)/shard_map/ppermute | solution.py:419
  38.0 0.1 collective-permute-start.18
  38.2 2.8 %collective-permute-done.11.refs_1_ = bf16[4,64,128]{2,1,0:T(8,128)(2,1)S(1)} collective-permute-done((bf16[4,64,128]{2,1,0:T(8,128)(2,1)S(1)}, bf16[4,64,128]{2,1,0:T(8,128)(2,1)S(1)}, u32[]{:S(2)}, u32[]{:S(2)}) %collective-permute-start.11) | collective-permute-done | bytes 65568 | tf_op jit(solution)/shard_map/ppermute | solution.py:419
  41.0 0.0 collective-permute-done.12.refs_2_
  41.0 0.0 copy-done
  41.0 0.9 %residual_second.1.second = f32[16,128,128]{2,1,0:T(8,128)} custom-call(s32[1]{0:T(128)} %bitcast.me, f32[16,128,128]{2,1,0:T(8,128)S(1)} %bitcast.18, bf16[4,64,128]{2,1,0:T(8,128)(2,1)S(1)} %collective-permute-done.10.refs_0_, bf16[4,64,128]{2,1,0:T(8,128)(2,1)S(1)} %collective-permute-done.11.refs_1_, ...), custom_call_target="tpu_custom_call" | custom-call | tf_op jit(solution)/shard_map/residual_second/pallas_call | solution.py:609
  41.8 0.0 collective-permute-done.16.refs_1_
  41.9 0.0 collective-permute-done.17.refs_2_
  41.9 0.3 collective-permute-done.18.refs_3_
  42.2 0.9 %residual_first.1 = f32[16,128,128]{2,1,0:T(8,128)} custom-call(s32[1]{0:T(128)} %bitcast.me, f32[16,128,128]{2,1,0:T(8,128)S(1)} %bitcast.19, f32[16,128,128]{2,1,0:T(8,128)} %residual_second.1.second, bf16[4,64,128]{2,1,0:T(8,128)(2,1)S(1)} %get-tuple-element.61.refs_0_, ...), custom_call_target="tpu_custom_call", output_to_operand_aliasing={{}: (2, {})} | custom-call | tf_op jit(solution)/shard_map/residual_first/pallas_call | solution.py:612
  (7 shorter events, 0.1 us)
Async XLA Ops:
  0.0 9.1 %copy-start.4 = (f32[2,32,128]{2,1,0:T(8,128)S(1)}, f32[2,32,128]{2,1,0:T(8,128)}, u32[]{:S(2)}) copy-start(f32[2,32,128]{2,1,0:T(8,128)} %constant.9.clone.cell_turns) | copy-start | bytes 98308
  0.0 9.1 %copy-start.5 = (f32[2,32,128]{2,1,0:T(8,128)S(1)}, f32[2,32,128]{2,1,0:T(8,128)}, u32[]{:S(2)}) copy-start(f32[2,32,128]{2,1,0:T(8,128)} %constant.8.clone.row_turns) | copy-start | bytes 98308
  1.6 11.1 %collective-permute-start.1 = (bf16[160,128]{1,0:T(8,128)(2,1)}, bf16[160,128]{1,0:T(8,128)(2,1)S(1)}, u32[]{:S(2)}, u32[]{:S(2)}) collective-permute-start(bf16[160,128]{1,0:T(8,128)(2,1)} %get-tuple-element.36), channel_id=1, source_target_pairs={{0,12},{1,13},{2,14},{3,15},{4,8},{5,9},{6,10},{7,11},{8,4},{9,5},... | collective-permute-start | bytes 122888 | tf_op jit(solution)/shard_map/ppermute | solution.py:419
  6.8 6.0 %collective-permute-start.2 = (bf16[160,128]{1,0:T(8,128)(2,1)}, bf16[160,128]{1,0:T(8,128)(2,1)S(1)}, u32[]{:S(2)}, u32[]{:S(2)}) collective-permute-start(bf16[160,128]{1,0:T(8,128)(2,1)} %get-tuple-element.37), channel_id=1, source_target_pairs={{0,8},{1,9},{2,10},{3,11},{4,12},{5,13},{6,14},{7,15},{8,0},{9,1},... | collective-permute-start | bytes 122888 | tf_op jit(solution)/shard_map/ppermute | solution.py:419
  6.8 6.0 %collective-permute-start.3 = (bf16[160,128]{1,0:T(8,128)(2,1)}, bf16[160,128]{1,0:T(8,128)(2,1)S(1)}, u32[]{:S(2)}, u32[]{:S(2)}) collective-permute-start(bf16[160,128]{1,0:T(8,128)(2,1)} %get-tuple-element.38), channel_id=1, source_target_pairs={{0,4},{1,5},{2,6},{3,7},{4,0},{5,1},{6,2},{7,3},{8,12},{9,13},{10,... | collective-permute-start | bytes 122888 | tf_op jit(solution)/shard_map/ppermute | solution.py:419
  7.4 5.4 %collective-permute-start = (bf16[144,128]{1,0:T(8,128)(2,1)}, bf16[144,128]{1,0:T(8,128)(2,1)S(1)}, u32[]{:S(2)}, u32[]{:S(2)}) collective-permute-start(bf16[144,128]{1,0:T(8,128)(2,1)} %get-tuple-element.35), channel_id=1, source_target_pairs={{0,2},{1,3},{2,0},{3,1},{4,6},{5,7},{6,4},{7,5},{8,10},{9,11},{10,... | collective-permute-start | bytes 110600 | tf_op jit(solution)/shard_map/ppermute | solution.py:419
  9.1 1.2 %copy-start.1 = (bf16[256,2,1024]{2,1,0:T(2,128)(2,1)S(1)}, bf16[256,2,1024]{2,1,0:T(2,128)(2,1)}, u32[]{:S(2)}) copy-start(bf16[256,2,1024]{2,1,0:T(2,128)(2,1)} %param.12) | copy-start | bytes 3145732
  10.3 2.5 %copy-start.3 = (bf16[160,128]{1,0:T(8,128)(2,1)S(1)}, bf16[160,128]{1,0:T(8,128)(2,1)}, u32[]{:S(2)}) copy-start(bf16[160,128]{1,0:T(8,128)(2,1)} %get-tuple-element.39.refs_3_) | copy-start | bytes 122884
  12.8 1.0 %copy-start.2 = (bf16[2,128,1024]{2,1,0:T(8,128)(2,1)S(1)}, bf16[2,128,1024]{2,1,0:T(8,128)(2,1)}, u32[]{:S(2)}) copy-start(bf16[2,128,1024]{2,1,0:T(8,128)(2,1)} %basis.1) | copy-start | bytes 1572868
  12.8 1.0 %copy-start.9 = (s32[1,16]{1,0:T(1,128)S(1)}, s32[1,16]{1,0:T(1,128)}, u32[]{:S(2)}) copy-start(s32[1,16]{1,0:T(1,128)} %counts.1) | copy-start | bytes 196
  12.8 1.0 %copy-start.10 = (f32[32]{0:T(128)S(1)}, f32[32]{0:T(128)}, u32[]{:S(2)}) copy-start(f32[32]{0:T(128)} %param.19) | copy-start | bytes 388
  12.9 1.0 %copy-start.6 = (s32[1,16,64]{2,1,0:T(8,128)S(1)}, s32[1,16,64]{2,1,0:T(8,128)}, u32[]{:S(2)}) copy-start(s32[1,16,64]{2,1,0:T(8,128)} %param.15) | copy-start | bytes 12292
  12.9 4.8 %collective-permute-start.4 = (bf16[3,144,128]{2,1,0:T(8,128)(2,1)S(1)}, bf16[3,144,128]{2,1,0:T(8,128)(2,1)S(1)}, u32[]{:S(2)}, u32[]{:S(2)}) collective-permute-start(bf16[3,144,128]{2,1,0:T(8,128)(2,1)S(1)} %get-tuple-element.40), channel_id=1, source_target_pairs={{0,2},{1,3},{2,0},{3,1},{4,6},{5,7},{6,4},{7,5},{8,10},{9,11},{10,... | collective-permute-start | bytes 331784 | tf_op jit(solution)/shard_map/ppermute | solution.py:419
  13.5 4.3 %collective-permute-start.6 = (bf16[4,160,128]{2,1,0:T(8,128)(2,1)S(1)}, bf16[4,160,128]{2,1,0:T(8,128)(2,1)S(1)}, u32[]{:S(2)}, u32[]{:S(2)}) collective-permute-start(bf16[4,160,128]{2,1,0:T(8,128)(2,1)S(1)} %get-tuple-element.41.after.near), channel_id=1, source_target_pairs={{0,1},{1,0},{2,3},{3,2},{4,5},{5,4},{6,7},{7,6},{8,9},{9,8},{10,11... | collective-permute-start | bytes 491528 | tf_op jit(solution)/shard_map/ppermute | solution.py:419
  13.5 0.7 %copy-start.7 = (s32[256,2]{0,1:T(2,128)S(1)}, s32[256,2]{0,1:T(2,128)}, u32[]{:S(2)}) copy-start(s32[256,2]{0,1:T(2,128)} %param.13) | copy-start | bytes 6148
  13.6 0.7 %copy-start.8 = (s32[256]{0:T(256)S(1)}, s32[256]{0:T(256)}, u32[]{:S(2)}) copy-start(s32[256]{0:T(256)} %param.14) | copy-start | bytes 3076
  17.7 1.4 %collective-permute-start.5 = (bf16[4,144,128]{2,1,0:T(8,128)(2,1)S(1)}, bf16[4,144,128]{2,1,0:T(8,128)(2,1)S(1)}, u32[]{:S(2)}, u32[]{:S(2)}) collective-permute-start(bf16[4,144,128]{2,1,0:T(8,128)(2,1)S(1)} %relay.1.over_y), channel_id=1, source_target_pairs={{0,1},{1,0},{2,3},{3,2},{4,5},{5,4},{6,7},{7,6},{8,9},{9,8},{10,11... | collective-permute-start | bytes 442376 | tf_op jit(solution)/shard_map/ppermute | solution.py:419
  19.2 21.8 %copy-start = (f32[1,16,64,2,128]{4,3,2,1,0:T(2,128)S(1)}, f32[1,16,64,2,128]{4,3,2,1,0:T(2,128)}, u32[]{:S(2)}) copy-start(f32[1,16,64,2,128]{4,3,2,1,0:T(2,128)} %param.21) | copy-start | bytes 3145732
  24.1 5.5 %collective-permute-start.7 = (bf16[4,64,128]{2,1,0:T(8,128)(2,1)S(1)}, bf16[4,64,128]{2,1,0:T(8,128)(2,1)S(1)}, u32[]{:S(2)}, u32[]{:S(2)}) collective-permute-start(bf16[4,64,128]{2,1,0:T(8,128)(2,1)S(1)} %get-tuple-element.49), channel_id=1, source_target_pairs={{0,3},{1,2},{2,1},{3,0},{4,7},{5,6},{6,5},{7,4},{8,11},{9,10},{10,... | collective-permute-start | bytes 196616 | tf_op jit(solution)/shard_map/ppermute | solution.py:419
  24.5 5.9 %collective-permute-start.8 = (bf16[4,64,128]{2,1,0:T(8,128)(2,1)S(1)}, bf16[4,64,128]{2,1,0:T(8,128)(2,1)S(1)}, u32[]{:S(2)}, u32[]{:S(2)}) collective-permute-start(bf16[4,64,128]{2,1,0:T(8,128)(2,1)S(1)} %get-tuple-element.50), channel_id=1, source_target_pairs={{0,2},{1,3},{2,0},{3,1},{4,6},{5,7},{6,4},{7,5},{8,10},{9,11},{10,... | collective-permute-start | bytes 196616 | tf_op jit(solution)/shard_map/ppermute | solution.py:419
  25.9 4.5 %collective-permute-start.9 = (bf16[4,64,128]{2,1,0:T(8,128)(2,1)S(1)}, bf16[4,64,128]{2,1,0:T(8,128)(2,1)S(1)}, u32[]{:S(2)}, u32[]{:S(2)}) collective-permute-start(bf16[4,64,128]{2,1,0:T(8,128)(2,1)S(1)} %get-tuple-element.51), channel_id=1, source_target_pairs={{0,1},{1,0},{2,3},{3,2},{4,5},{5,4},{6,7},{7,6},{8,9},{9,8},{10,11... | collective-permute-start | bytes 196616 | tf_op jit(solution)/shard_map/ppermute | solution.py:419
  26.0 8.1 %collective-permute-start.13 = (bf16[4,64,128]{2,1,0:T(8,128)(2,1)S(1)}, bf16[4,64,128]{2,1,0:T(8,128)(2,1)S(1)}, u32[]{:S(2)}, u32[]{:S(2)}) collective-permute-start(bf16[4,64,128]{2,1,0:T(8,128)(2,1)S(1)} %get-tuple-element.57), channel_id=1, source_target_pairs={{0,12},{1,13},{2,14},{3,15},{4,8},{5,9},{6,10},{7,11},{8,4},{9,5},... | collective-permute-start | bytes 196616 | tf_op jit(solution)/shard_map/ppermute | solution.py:419
  29.6 6.6 %collective-permute-start.14 = (bf16[4,64,128]{2,1,0:T(8,128)(2,1)S(1)}, bf16[4,64,128]{2,1,0:T(8,128)(2,1)S(1)}, u32[]{:S(2)}, u32[]{:S(2)}) collective-permute-start(bf16[4,64,128]{2,1,0:T(8,128)(2,1)S(1)} %get-tuple-element.58), channel_id=1, source_target_pairs={{0,8},{1,9},{2,10},{3,11},{4,12},{5,13},{6,14},{7,15},{8,0},{9,1},... | collective-permute-start | bytes 196616 | tf_op jit(solution)/shard_map/ppermute | solution.py:419
  29.6 6.6 %collective-permute-start.15 = (bf16[4,64,128]{2,1,0:T(8,128)(2,1)S(1)}, bf16[4,64,128]{2,1,0:T(8,128)(2,1)S(1)}, u32[]{:S(2)}, u32[]{:S(2)}) collective-permute-start(bf16[4,64,128]{2,1,0:T(8,128)(2,1)S(1)} %get-tuple-element.59), channel_id=1, source_target_pairs={{0,4},{1,5},{2,6},{3,7},{4,0},{5,1},{6,2},{7,3},{8,12},{9,13},{10,... | collective-permute-start | bytes 196616 | tf_op jit(solution)/shard_map/ppermute | solution.py:419
  30.4 7.6 %collective-permute-start.10 = (bf16[4,64,128]{2,1,0:T(8,128)(2,1)S(1)}, bf16[4,64,128]{2,1,0:T(8,128)(2,1)S(1)}, u32[]{:S(2)}, u32[]{:S(2)}) collective-permute-start(bf16[4,64,128]{2,1,0:T(8,128)(2,1)S(1)} %get-tuple-element.53), channel_id=1, source_target_pairs={{0,12},{1,13},{2,14},{3,15},{4,8},{5,9},{6,10},{7,11},{8,4},{9,5},... | collective-permute-start | bytes 196616 | tf_op jit(solution)/shard_map/ppermute | solution.py:419
  34.1 6.9 %collective-permute-start.11 = (bf16[4,64,128]{2,1,0:T(8,128)(2,1)S(1)}, bf16[4,64,128]{2,1,0:T(8,128)(2,1)S(1)}, u32[]{:S(2)}, u32[]{:S(2)}) collective-permute-start(bf16[4,64,128]{2,1,0:T(8,128)(2,1)S(1)} %get-tuple-element.54), channel_id=1, source_target_pairs={{0,8},{1,9},{2,10},{3,11},{4,12},{5,13},{6,14},{7,15},{8,0},{9,1},... | collective-permute-start | bytes 196616 | tf_op jit(solution)/shard_map/ppermute | solution.py:419
  34.1 6.9 %collective-permute-start.12 = (bf16[4,64,128]{2,1,0:T(8,128)(2,1)S(1)}, bf16[4,64,128]{2,1,0:T(8,128)(2,1)S(1)}, u32[]{:S(2)}, u32[]{:S(2)}) collective-permute-start(bf16[4,64,128]{2,1,0:T(8,128)(2,1)S(1)} %get-tuple-element.55), channel_id=1, source_target_pairs={{0,4},{1,5},{2,6},{3,7},{4,0},{5,1},{6,2},{7,3},{8,12},{9,13},{10,... | collective-permute-start | bytes 196616 | tf_op jit(solution)/shard_map/ppermute | solution.py:419
  36.2 5.6 %collective-permute-start.16 = (bf16[4,64,128]{2,1,0:T(8,128)(2,1)S(1)}, bf16[4,64,128]{2,1,0:T(8,128)(2,1)S(1)}, u32[]{:S(2)}, u32[]{:S(2)}) collective-permute-start(bf16[4,64,128]{2,1,0:T(8,128)(2,1)S(1)} %get-tuple-element.62), channel_id=1, source_target_pairs={{0,1},{1,0},{2,3},{3,2},{4,5},{5,4},{6,7},{7,6},{8,9},{9,8},{10,11... | collective-permute-start | bytes 196616 | tf_op jit(solution)/shard_map/ppermute | solution.py:419
  36.3 5.6 %collective-permute-start.17 = (bf16[4,64,128]{2,1,0:T(8,128)(2,1)S(1)}, bf16[4,64,128]{2,1,0:T(8,128)(2,1)S(1)}, u32[]{:S(2)}, u32[]{:S(2)}) collective-permute-start(bf16[4,64,128]{2,1,0:T(8,128)(2,1)S(1)} %get-tuple-element.63), channel_id=1, source_target_pairs={{0,2},{1,3},{2,0},{3,1},{4,6},{5,7},{6,4},{7,5},{8,10},{9,11},{10,... | collective-permute-start | bytes 196616 | tf_op jit(solution)/shard_map/ppermute | solution.py:419
  38.0 4.2 %collective-permute-start.18 = (bf16[4,64,128]{2,1,0:T(8,128)(2,1)S(1)}, bf16[4,64,128]{2,1,0:T(8,128)(2,1)S(1)}, u32[]{:S(2)}, u32[]{:S(2)}) collective-permute-start(bf16[4,64,128]{2,1,0:T(8,128)(2,1)S(1)} %get-tuple-element.64), channel_id=1, source_target_pairs={{0,3},{1,2},{2,1},{3,0},{4,7},{5,6},{6,5},{7,4},{8,11},{9,10},{10,... | collective-permute-start | bytes 196616 | tf_op jit(solution)/shard_map/ppermute | solution.py:419

commit v11 on v10

--- a/solution.py
+++ b/solution.py
@@ -54,9 +54,7 @@
     return out_re, out_im
 
 
-def transform_kernel(cells_hbm, row_turns, cell_turns, image, cells, high, rest, wide, sums, sem):
-    copy = pltpu.make_async_copy(cells_hbm, cells, sem)
-    copy.start()
+def transform_kernel(cells, row_turns, cell_turns, image, high, rest, wide, sums):
     number = image.shape[1]
     edge, span = cell_turns.shape[1:]
     low = span // edge
@@ -77,7 +75,6 @@
                 held[m, re, span:] = sin_part
                 held[m, im, :span] = -sin_part
                 held[m, im, span:] = cos_part
-    copy.wait()
     step = 16
 
     @pl.loop(0, number // step, unroll=8)
@@ -172,7 +169,7 @@
 
 
 def pack_kernel(me, coefs_hbm, tracks_hbm, *refs):
-    out, for_y, coefs, tracks, sems = refs[:-4], *refs[-4:]
+    out, (coefs, tracks, sems) = refs[:-3], refs[-3:]
     copies = [
         pltpu.make_async_copy(coefs_hbm, coefs, sems.at[0]),
         pltpu.make_async_copy(tracks_hbm, tracks, sems.at[1]),
@@ -197,10 +194,6 @@
         out[r][:rows, :] = coefs[:, :128]
         out[r][rows : 2 * rows, :] = coefs[:, 128:]
         out[r][2 * rows :, :] = pieces.astype(BF16)
-        if r == 0:
-            for_y[:rows, :] = coefs[:, :128]
-            for_y[rows : 2 * rows, :] = coefs[:, 128:]
-            for_y[2 * rows :, :] = own_pair(pieces, me[0] ^ 2).astype(BF16)
 
 
 def own_pair(pieces, device):
@@ -209,20 +202,17 @@
 
 
 def stack_kernel(me, *refs):
-    blocks, near, for_y = refs[:-4], refs[-2], refs[-1]
+    blocks, near, for_y = refs[:-3], refs[-2], refs[-1]
     table = 2 * for_y.shape[1] - near.shape[1]
     for r, block in enumerate(blocks[::-1]):
         near[r] = block[...]
-        if r > 0:
-            for_y[r - 1, :table, :] = block[:table, :]
-            tracks = own_pair(block[table:, :].astype(F32), me[0] ^ 2)
-            for_y[r - 1, table:, :] = tracks.astype(BF16)
-
-
-def relay_kernel(own, others, after, out):
-    out[0] = own[...]
-    for r in range(others.shape[0]):
-        out[r + 1] = others[r]
+        for_y[r, :table, :] = block[:table, :]
+        tracks = own_pair(block[table:, :].astype(F32), me[0] ^ 2)
+        for_y[r, table:, :] = tracks.astype(BF16)
+
+
+def relay_kernel(block, after, out):
+    out[...] = block[...]
 
 
 def unpacked(mine, groups, table, rows_own, capacity):
@@ -326,7 +316,7 @@
             wre[to, :] = i_re * g_re - i_im * g_im
             wim[to, :] = i_re * g_im + i_im * g_re
 
-    unroll = 128
+    unroll = 256
 
     def one(g):
         at = pl.ds(pl.multiple_of(g * 8, 8), 8)
@@ -383,36 +373,29 @@
             in_plane[p][r] = interleaved[start + capacity : start + 2 * capacity, :].astype(BF16)
 
 
-def turn_kernel(*refs):
-    count = refs[0].shape[0]
-    blocks, out = refs[:-count], refs[-count:]
-    for i, block in enumerate(blocks[::-1]):
-        for j in range(count):
+def turn_kernel(*refs, order):
+    blocks, out = refs[: len(order)], refs[len(order) :]
+    for i, block in zip(order, blocks):
+        for j in range(len(out)):
             out[j][i] = block[j]
 
 
-def residual_second(me, observed, *refs):
-    by_z, (out, kept, sem) = refs[:-3][::-1], refs[-3:]
+def residual_kernel(me, observed, *refs, along_z, in_plane, outer):
+    arrived, (out, kept, sems) = refs[: len(along_z) + len(in_plane)], refs[-3:]
     rows = kept.shape[1]
-    for r in range(len(by_z)):
-        for p in range(4):
-            source = me[0] ^ (4 * r + p)
-            kept[source] = observed[source, rows:, :] - by_z[r][p].astype(F32)
-    copy = pltpu.make_async_copy(kept, out.at[:, rows:, :], sem)
-    copy.start()
-    copy.wait()
-
-
-def residual_first(me, observed, second, *refs):
-    by_plane, (out, kept, sem) = refs[:-3], refs[-3:]
-    rows = kept.shape[1]
-    for p in range(4):
-        for r in range(by_plane[p].shape[0]):
-            source = me[0] ^ (4 * r + p)
-            kept[source] = observed[source, :rows, :] - by_plane[p][r].astype(F32)
-    copy = pltpu.make_async_copy(kept, out.at[:, :rows, :], sem)
-    copy.start()
-    copy.wait()
+    pieces = [(r, p, rows, arrived[n].at[p]) for n, r in enumerate(along_z) for p in range(4)]
+    pieces += [
+        (r, p, 0, arrived[len(along_z) + n].at[r]) for n, p in enumerate(in_plane) for r in range(outer)
+    ]
+    copies = []
+    for n, (r, p, start, values) in enumerate(pieces):
+        source = me[0] ^ (4 * r + p)
+        kept[n] = observed[source, start : start + rows, :] - values[...].astype(F32)
+        copy = pltpu.make_async_copy(kept.at[n], out.at[source, pl.ds(start, rows), :], sems.at[n])
+        copy.start()
+        copies.append(copy)
+    for copy in copies:
+        copy.wait()
 
 
 def exchange(value, step, tiles):
@@ -452,11 +435,11 @@
     me = lax.axis_index("tile").astype(jnp.int32).reshape(1)
     block = jax.ShapeDtypeStruct((2 * own_rows + 8 * steps, 128), BF16)
     block_y = jax.ShapeDtypeStruct((2 * own_rows + 4 * steps, 128), BF16)
-    *packed, own_y = pl.pallas_call(
+    packed = pl.pallas_call(
         pack_kernel,
-        out_shape=[block] * outer + [block_y],
+        out_shape=[block] * outer,
         in_specs=[smem, hbm, hbm],
-        out_specs=[vmem] * (outer + 1),
+        out_specs=[vmem] * outer,
         scratch_shapes=[
             pltpu.VMEM((own_rows, terms2), BF16),
             pltpu.VMEM((tiles, 2 * steps, capacity), F32),
@@ -466,7 +449,6 @@
         name="pack",
     )(me, beam_coefs.reshape(own_rows, terms2), own_tracks)
     along = [packed[0]] + [exchange(packed[r], 4 * r, tiles) for r in range(1, outer)]
-    own_over_y = exchange(own_y, 2, tiles)
 
     cells = jnp.transpose(subgrids.reshape(number, 2, 8, 128), (0, 2, 1, 3))
     cells = cells.reshape(number * 16, 128)
@@ -474,15 +456,13 @@
     image = pl.pallas_call(
         transform_kernel,
         out_shape=jax.ShapeDtypeStruct((8, number, 256), BF16),
-        in_specs=[hbm] + [vmem] * 2,
+        in_specs=[vmem] * 3,
         out_specs=vmem,
         scratch_shapes=[
-            pltpu.VMEM((number * 16, 128), BF16),
             pltpu.VMEM((8, 256, 256), BF16),
             pltpu.VMEM((8, 256, 256), BF16),
             pltpu.VMEM((number * 16, 128), F32),
             pltpu.VMEM((8, number, 512), BF16),
-            pltpu.SemaphoreType.DMA,
         ],
         compiler_params=pltpu.CompilerParams(vmem_limit_bytes=14 * MIB),
         name="transform",
@@ -492,13 +472,13 @@
         stack_kernel,
         out_shape=[
             jax.ShapeDtypeStruct((outer,) + block.shape, BF16),
-            jax.ShapeDtypeStruct((outer - 1,) + block_y.shape, BF16),
+            jax.ShapeDtypeStruct((outer,) + block_y.shape, BF16),
         ],
-        in_specs=[smem] + [vmem] * outer + [anywhere] * 2,
+        in_specs=[smem] + [vmem] * outer + [anywhere],
         out_specs=[vmem] * 2,
         compiler_params=pltpu.CompilerParams(vmem_limit_bytes=3 * MIB * (tiles // 16)),
         name="stack",
-    )(me, *along[::-1], own_over_y, image)
+    )(me, *along[::-1], image)
     over_core = exchange(near, 1, tiles)
     over_y = exchange(for_y, 2, tiles)
     route, back, pick, weights, turns = pl.pallas_call(
@@ -528,11 +508,11 @@
     over_y = pl.pallas_call(
         relay_kernel,
         out_shape=jax.ShapeDtypeStruct((outer,) + block_y.shape, BF16),
-        in_specs=[vmem, vmem, anywhere],
+        in_specs=[vmem, anywhere],
         out_specs=vmem,
         compiler_params=pltpu.CompilerParams(vmem_limit_bytes=2 * MIB * (tiles // 16)),
         name="relay",
-    )(own_over_y, over_y, weights)
+    )(over_y, weights)
     over_both = exchange(over_y, 1, tiles)
     coef_early, per_sub_early = pl.pallas_call(
         functools.partial(early_kernel, capacity=capacity),
@@ -581,40 +561,44 @@
         coef_early,
         per_sub_early,
     )
-    def turned(blocks, out_shape):
+    def turned(blocks, order, out_shape):
         return pl.pallas_call(
-            turn_kernel,
+            functools.partial(turn_kernel, order=order),
             out_shape=out_shape,
             in_specs=[vmem] * len(blocks),
             out_specs=[vmem] * len(out_shape),
             compiler_params=pltpu.CompilerParams(vmem_limit_bytes=2 * MIB),
             name="turn",
-        )(*blocks[::-1])
+        )(*[blocks[i] for i in order])
 
     first, second = models[:outer], models[outer:]
     second = [second[0]] + [exchange(second[p], p, tiles) for p in range(1, 4)]
     first = [first[0]] + [exchange(first[r], 4 * r, tiles) for r in range(1, outer)]
-    second = turned(second, [for_z] * outer)
+    second = turned(second, (1, 2, 3, 0), [for_z] * outer)
     second = [second[0]] + [exchange(second[r], 4 * r, tiles) for r in range(1, outer)]
-    first = turned(first, [for_plane] * 4)
+    first = turned(first, tuple(range(outer))[::-1], [for_plane] * 4)
     first = [first[0]] + [exchange(first[p], p, tiles) for p in range(1, 4)]
     ours = observed.reshape(tiles, 2 * capacity, vis)
-    finish = functools.partial(
-        pl.pallas_call,
-        out_shape=jax.ShapeDtypeStruct(ours.shape, F32),
-        out_specs=anywhere,
-        scratch_shapes=[pltpu.VMEM((tiles, capacity, vis), F32), pltpu.SemaphoreType.DMA],
-        compiler_params=pltpu.CompilerParams(vmem_limit_bytes=6 * MIB),
-    )
-    residual = finish(
-        residual_second, in_specs=[smem] + [vmem] * (1 + outer), name="residual_second"
-    )(me, ours, *second[::-1])
-    residual = finish(
-        residual_first,
-        in_specs=[smem, vmem, anywhere] + [vmem] * 4,
-        input_output_aliases={2: 0},
-        name="residual_first",
-    )(me, ours, residual, *first)
+
+    def finish(name, along_z, in_plane, held):
+        count = 4 * len(along_z) + outer * len(in_plane)
+        arrived = [second[r] for r in along_z] + [first[p] for p in in_plane]
+        return pl.pallas_call(
+            functools.partial(residual_kernel, along_z=along_z, in_plane=in_plane, outer=outer),
+            out_shape=jax.ShapeDtypeStruct(ours.shape, F32),
+            in_specs=[smem] + [vmem] * (1 + len(arrived)) + [anywhere] * len(held),
+            out_specs=anywhere,
+            scratch_shapes=[
+                pltpu.VMEM((count, capacity, vis), F32),
+                pltpu.SemaphoreType.DMA((count,)),
+            ],
+            input_output_aliases={2 + len(arrived): 0} if held else {},
+            compiler_params=pltpu.CompilerParams(vmem_limit_bytes=6 * MIB),
+            name=name,
+        )(me, ours, *arrived, *held)
+
+    residual = finish("residual_early", (0, outer - 1), (0,), ())
+    residual = finish("residual_last", tuple(range(1, outer - 1))[::-1], (1, 2, 3), (residual,))
     return residual.reshape(observed.shape)
 
 

time: 43.3 us -> 43.1 us (level)
  waiting for transfers between devices: 8.22 us -> 7.08 us
  Pallas kernels: 12.9 us -> 13.5 us
    ppermute x19 -> x18, waiting for transfers between devices: 8.22 us -> 7.08 us  [exchange(): return lax.ppermute(value, 'tile', [(i, i ^ step) for i in range(tiles)])]
    pallas_call x1, Pallas kernels: 4.9 us -> 5.42 us  [per_device(): pl.pallas_call(predict_kernel, out_shape=[for_z] * outer + [for_plane] *...]
    ppermute x19 -> x18, starting transfers between devices: 19.8 us -> 20.1 us  [exchange(): return lax.ppermute(value, 'tile', [(i, i ^ step) for i in range(tiles)])]
  transfers between devices with their start and end apart: 19 -> 18, of which waited for: 6 -> 6; matrix products, arithmetic and copies ran while one was open for 0% -> 0% of each run, Pallas kernels for 13% -> 13%
where the time goes in v11:
time: 43.1 us; the launch traced here: 42.7 us
  starting transfers between devices  20.1 us (47%)
  Pallas kernels  13.5 us (31%)
  waiting for transfers between devices  7.08 us (16%)
  local copies, waits for them, and re-layouts  1.92 us (4%)
    ppermute x18, starting transfers between devices, exchange(): return lax.ppermute(value, 'tile', [(i, i ^ step) for i in range(tiles)])  20.1 us
    ppermute x18, waiting for transfers between devices, exchange(): return lax.ppermute(value, 'tile', [(i, i ^ step) for i in range(tiles)])  7.08 us
    pallas_call x1, Pallas kernels, per_device(): pl.pallas_call(predict_kernel, out_shape=[for_z] * outer + [for_plane] *...  5.42 us
    pallas_call x1, Pallas kernels, per_device(): pl.pallas_call(transform_kernel, out_shape=jax.ShapeDtypeStruct((8, numbe...  2.36 us
    unnamed x22, local copies, waits for them, and re-layouts  1.92 us
    pallas_call x2, Pallas kernels, finish(): pl.pallas_call(functools.partial(residual_kernel, along_z=along_z, in_pla...  1.84 us
    pallas_call x1, Pallas kernels, per_device(): pl.pallas_call(pack_kernel, out_shape=[block] * outer, in_specs=[smem, hb...  1.62 us
    pallas_call x1, Pallas kernels, per_device(): pl.pallas_call(functools.partial(prepare_kernel, slot_count=slot_count),...  1.59 us
  transfers between devices with their start and end apart: 18, of which 6 were waited for; matrix products, arithmetic and copies ran while one was open for 0% of the time, Pallas kernels for 13%

profile of v11, /device:TPU:0, one launch (start us, length us, event | category | flops | bytes accessed | tf_op | source)
XLA Modules:
  0.0 42.7 jit_solution(8700286646337092227)
XLA Ops:
  0.0 0.0 copy-start.4
  0.0 0.0 copy-start.5
  0.0 1.6 %pack.1 = (bf16[160,128]{1,0:T(8,128)(2,1)}, bf16[160,128]{1,0:T(8,128)(2,1)}, bf16[160,128]{1,0:T(8,128)(2,1)}, bf16[160,128]{1,0:T(8,128)(2,1)}) custom-call(s32[1]{0:T(128)} %bitcast.me, bf16[64,256]{1,0:T(8,128)(2,1)} %bitcast.26, f32[16,8,64]{2,1,0:T(8,128)} %bitcast.25), custom_call_target="tpu_custom_call" | custom-call | tf_op jit(solution)/shard_map/pack/pallas_call | solution.py:438
  1.6 5.1 %collective-permute-start = (bf16[160,128]{1,0:T(8,128)(2,1)}, bf16[160,128]{1,0:T(8,128)(2,1)S(1)}, u32[]{:S(2)}, u32[]{:S(2)}) collective-permute-start(bf16[160,128]{1,0:T(8,128)(2,1)} %get-tuple-element.34), channel_id=1, source_target_pairs={{0,12},{1,13},{2,14},{3,15},{4,8},{5,9},{6,10},{7,11},{8,4},{9,5},... | collective-permute-start | bytes 122888 | tf_op jit(solution)/shard_map/ppermute | solution.py:402
  6.7 0.0 collective-permute-start.1
  6.8 0.6 %collective-permute-start.2 = (bf16[160,128]{1,0:T(8,128)(2,1)}, bf16[160,128]{1,0:T(8,128)(2,1)S(1)}, u32[]{:S(2)}, u32[]{:S(2)}) collective-permute-start(bf16[160,128]{1,0:T(8,128)(2,1)} %get-tuple-element.36), channel_id=1, source_target_pairs={{0,4},{1,5},{2,6},{3,7},{4,0},{5,1},{6,2},{7,3},{8,12},{9,13},{10,... | collective-permute-start | bytes 122888 | tf_op jit(solution)/shard_map/ppermute | solution.py:402
  7.4 0.0 copy-done.4
  7.4 0.0 copy-done.5
  7.4 0.0 copy-start.1
  7.4 1.2 %copy-done.1 = bf16[256,2,1024]{2,1,0:T(2,128)(2,1)S(1)} copy-done((bf16[256,2,1024]{2,1,0:T(2,128)(2,1)S(1)}, bf16[256,2,1024]{2,1,0:T(2,128)(2,1)}, u32[]{:S(2)}) %copy-start.1) | copy-done | bytes 1048600
  8.6 0.0 copy-start.3
  8.6 2.4 %transform.1.refs_4_.image = bf16[8,256,256]{2,1,0:T(8,128)(2,1)S(1)} custom-call(bf16[4096,128]{1,0:T(8,128)(2,1)S(1)} %bitcast.20, f32[2,32,128]{2,1,0:T(8,128)S(1)} %copy-done.5, f32[2,32,128]{2,1,0:T(8,128)S(1)} %copy-done.4), custom_call_target="tpu_custom_call" | custom-call | tf_op jit(solution)/shard_map/transform/pallas_call | solution.py:456
  11.0 0.0 collective-permute-done.refs_0_
  11.0 0.9 %collective-permute-done.1.refs_1_ = bf16[160,128]{1,0:T(8,128)(2,1)S(1)} collective-permute-done((bf16[160,128]{1,0:T(8,128)(2,1)}, bf16[160,128]{1,0:T(8,128)(2,1)S(1)}, u32[]{:S(2)}, u32[]{:S(2)}) %collective-permute-start.1) | collective-permute-done | bytes 40992 | tf_op jit(solution)/shard_map/ppermute | solution.py:402
  11.9 0.0 collective-permute-done.2.refs_2_
  11.9 0.0 copy-done.3
  11.9 0.0 copy-start.2
  11.9 0.0 copy-start.9
  11.9 0.0 copy-start.10
  11.9 0.0 copy-start.6
  12.0 1.6 %collective-permute-start.3 = (bf16[4,144,128]{2,1,0:T(8,128)(2,1)S(1)}, bf16[4,144,128]{2,1,0:T(8,128)(2,1)S(1)}, u32[]{:S(2)}, u32[]{:S(2)}) collective-permute-start(bf16[4,144,128]{2,1,0:T(8,128)(2,1)S(1)} %get-tuple-element.38), channel_id=1, source_target_pairs={{0,2},{1,3},{2,0},{3,1},{4,6},{5,7},{6,4},{7,5},{8,10},{9,11},{10,... | collective-permute-start | bytes 442376 | tf_op jit(solution)/shard_map/ppermute | solution.py:402
  13.5 0.0 collective-permute-start.5
  13.5 0.0 copy-start.7
  13.5 0.0 copy-start.8
  13.5 0.0 copy-done.2
  13.6 0.0 copy-done.9
  13.6 0.0 copy-done.10
  13.6 0.0 copy-done.6
  13.6 0.6 %copy-done.7 = s32[256,2]{0,1:T(2,128)S(1)} copy-done((s32[256,2]{0,1:T(2,128)S(1)}, s32[256,2]{0,1:T(2,128)}, u32[]{:S(2)}) %copy-start.7) | copy-done | bytes 2072
  14.2 0.0 copy-done.8
  14.2 1.6 %prepare.1 = (bf16[256,1024]{1,0:T(8,128)(2,1)S(1)}, bf16[1024,256]{1,0:T(8,128)(2,1)S(1)}, bf16[512,1024]{1,0:T(8,128)(2,1)S(1)}, bf16[8,256,256]{2,1,0:T(8,128)(2,1)S(1)}, f32[1,128]{1,0:T(1,128)S(1)}) custom-call(s32[1]{0:T(128)} %bitcast.me, s32[1,16]{1,0:T(1,128)S(1)} %copy-done.9, s32[16,64]{1,0:T(8,128)S(1)} %bitcast.21, s32[2,256]{1,0:T(2,128)S(1)} %bitcast.22, ...), custom_call_target="tpu_custom_call" | custom-call | tf_op jit(solution)/shard_map/prepare/pallas_call | solution.py:484
  15.8 1.3 %collective-permute-done.3.block = bf16[4,144,128]{2,1,0:T(8,128)(2,1)S(1)} collective-permute-done((bf16[4,144,128]{2,1,0:T(8,128)(2,1)S(1)}, bf16[4,144,128]{2,1,0:T(8,128)(2,1)S(1)}, u32[]{:S(2)}, u32[]{:S(2)}) %collective-permute-start.3) | collective-permute-done | bytes 147488 | tf_op jit(solution)/shard_map/ppermute | solution.py:402
  17.2 0.1 collective-permute-start.4
  17.3 0.0 collective-permute-done.5.over_core
  17.3 0.5 %early.1 = (bf16[512,256]{1,0:T(8,128)(2,1)S(1)}, f32[256,16]{1,0:T(8,128)S(1)}) custom-call(s32[1]{0:T(128)} %bitcast.me, bf16[4,160,128]{2,1,0:T(8,128)(2,1)S(1)} %get-tuple-element.39.after.near, bf16[4,160,128]{2,1,0:T(8,128)(2,1)S(1)} %collective-permute-done.5.over_core, bf16[4,144,128]{2,1,0:T(8,128)(2,1)S(1)} %relay.1.over_y, ...), custom_call_target="tpu_custom_call" | custom-call | tf_op jit(solution)/shard_map/early/pallas_call | solution.py:517
  17.8 0.8 %collective-permute-done.4.over_both = bf16[4,144,128]{2,1,0:T(8,128)(2,1)S(1)} collective-permute-done((bf16[4,144,128]{2,1,0:T(8,128)(2,1)S(1)}, bf16[4,144,128]{2,1,0:T(8,128)(2,1)S(1)}, u32[]{:S(2)}, u32[]{:S(2)}) %collective-permute-start.4) | collective-permute-done | bytes 147488 | tf_op jit(solution)/shard_map/ppermute | solution.py:402
  18.6 5.4 %predict.1 = (bf16[4,64,128]{2,1,0:T(8,128)(2,1)S(1)}, bf16[4,64,128]{2,1,0:T(8,128)(2,1)S(1)}, bf16[4,64,128]{2,1,0:T(8,128)(2,1)S(1)}, bf16[4,64,128]{2,1,0:T(...) custom-call(s32[1]{0:T(128)} %bitcast.me, ...), custom_call_target="tpu_custom_call" | custom-call | tf_op jit(solution)/shard_map/predict/pallas_call | solution.py:532
  24.0 0.2 collective-permute-start.6
  24.3 1.5 %collective-permute-start.7 = (bf16[4,64,128]{2,1,0:T(8,128)(2,1)S(1)}, bf16[4,64,128]{2,1,0:T(8,128)(2,1)S(1)}, u32[]{:S(2)}, u32[]{:S(2)}) collective-permute-start(bf16[4,64,128]{2,1,0:T(8,128)(2,1)S(1)} %get-tuple-element.48), channel_id=1, source_target_pairs={{0,2},{1,3},{2,0},{3,1},{4,6},{5,7},{6,4},{7,5},{8,10},{9,11},{10,... | collective-permute-start | bytes 196616 | tf_op jit(solution)/shard_map/ppermute | solution.py:402
  25.8 0.2 collective-permute-start.8
  26.0 2.9 %collective-permute-start.11 = (bf16[4,64,128]{2,1,0:T(8,128)(2,1)S(1)}, bf16[4,64,128]{2,1,0:T(8,128)(2,1)S(1)}, u32[]{:S(2)}, u32[]{:S(2)}) collective-permute-start(bf16[4,64,128]{2,1,0:T(8,128)(2,1)S(1)} %get-tuple-element.53), channel_id=1, source_target_pairs={{0,12},{1,13},{2,14},{3,15},{4,8},{5,9},{6,10},{7,11},{8,4},{9,5},... | collective-permute-start | bytes 196616 | tf_op jit(solution)/shard_map/ppermute | solution.py:402
  28.9 0.0 collective-permute-start.12
  28.9 0.0 collective-permute-done.6.refs_0_
  28.9 1.5 %collective-permute-start.13 = (bf16[4,64,128]{2,1,0:T(8,128)(2,1)S(1)}, bf16[4,64,128]{2,1,0:T(8,128)(2,1)S(1)}, u32[]{:S(2)}, u32[]{:S(2)}) collective-permute-start(bf16[4,64,128]{2,1,0:T(8,128)(2,1)S(1)} %get-tuple-element.55), channel_id=1, source_target_pairs={{0,4},{1,5},{2,6},{3,7},{4,0},{5,1},{6,2},{7,3},{8,12},{9,13},{10,... | collective-permute-start | bytes 196616 | tf_op jit(solution)/shard_map/ppermute | solution.py:402
  30.4 0.0 collective-permute-done.7.refs_1_
  30.4 0.0 collective-permute-done.8.refs_2_
  30.4 3.0 %collective-permute-start.17 = (bf16[4,64,128]{2,1,0:T(8,128)(2,1)S(1)}, bf16[4,64,128]{2,1,0:T(8,128)(2,1)S(1)}, u32[]{:S(2)}, u32[]{:S(2)}) collective-permute-start(bf16[4,64,128]{2,1,0:T(8,128)(2,1)S(1)} %get-tuple-element.61), channel_id=1, source_target_pairs={{0,12},{1,13},{2,14},{3,15},{4,8},{5,9},{6,10},{7,11},{8,4},{9,5},... | collective-permute-start | bytes 196616 | tf_op jit(solution)/shard_map/ppermute | solution.py:402
  33.4 0.0 collective-permute-start.9
  33.4 0.0 collective-permute-done.11.refs_0_
  33.4 1.5 %collective-permute-start.10 = (bf16[4,64,128]{2,1,0:T(8,128)(2,1)S(1)}, bf16[4,64,128]{2,1,0:T(8,128)(2,1)S(1)}, u32[]{:S(2)}, u32[]{:S(2)}) collective-permute-start(bf16[4,64,128]{2,1,0:T(8,128)(2,1)S(1)} %get-tuple-element.52), channel_id=1, source_target_pairs={{0,4},{1,5},{2,6},{3,7},{4,0},{5,1},{6,2},{7,3},{8,12},{9,13},{10,... | collective-permute-start | bytes 196616 | tf_op jit(solution)/shard_map/ppermute | solution.py:402
  34.9 1.1 %collective-permute-done.12.refs_1_ = bf16[4,64,128]{2,1,0:T(8,128)(2,1)S(1)} collective-permute-done((bf16[4,64,128]{2,1,0:T(8,128)(2,1)S(1)}, bf16[4,64,128]{2,1,0:T(8,128)(2,1)S(1)}, u32[]{:S(2)}, u32[]{:S(2)}) %collective-permute-start.12) | collective-permute-done | bytes 65568 | tf_op jit(solution)/shard_map/ppermute | solution.py:402
  35.9 0.0 collective-permute-done.13.refs_2_
  36.0 0.1 collective-permute-start.14
  36.0 1.6 %collective-permute-start.15 = (bf16[4,64,128]{2,1,0:T(8,128)(2,1)S(1)}, bf16[4,64,128]{2,1,0:T(8,128)(2,1)S(1)}, u32[]{:S(2)}, u32[]{:S(2)}) collective-permute-start(bf16[4,64,128]{2,1,0:T(8,128)(2,1)S(1)} %get-tuple-element.58), channel_id=1, source_target_pairs={{0,2},{1,3},{2,0},{3,1},{4,6},{5,7},{6,4},{7,5},{8,10},{9,11},{10,... | collective-permute-start | bytes 196616 | tf_op jit(solution)/shard_map/ppermute | solution.py:402
  37.7 0.0 collective-permute-done.17.refs_1_
  37.7 0.2 collective-permute-start.16
  37.9 0.0 copy-done
  37.9 0.8 %residual_early.1.refs_5_ = f32[16,128,128]{2,1,0:T(8,128)} custom-call(s32[1]{0:T(128)} %bitcast.me, f32[16,128,128]{2,1,0:T(8,128)S(1)} %bitcast.18, bf16[4,64,128]{2,1,0:T(8,128)(2,1)S(1)} %get-tuple-element.60.refs_0_, bf16[4,64,128]{2,1,0:T(8,128)(2,1)S(1)} %collective-permute-done.17.refs_1_, bf16[4,64,128]{2,1,0:T(8,128)(2,1)S(1)} %get-tuple-element.62.refs_2_), custom_call_target="tpu_custom_call" | custom-call | tf_op jit(solution)/shard_map/residual_early/pallas_call | solution.py:586
  38.8 1.9 %collective-permute-done.9.refs_0_ = bf16[4,64,128]{2,1,0:T(8,128)(2,1)S(1)} collective-permute-done((bf16[4,64,128]{2,1,0:T(8,128)(2,1)S(1)}, bf16[4,64,128]{2,1,0:T(8,128)(2,1)S(1)}, u32[]{:S(2)}, u32[]{:S(2)}) %collective-permute-start.9) | collective-permute-done | bytes 65568 | tf_op jit(solution)/shard_map/ppermute | solution.py:402
  40.6 0.0 collective-permute-done.10.refs_1_
  40.6 0.0 collective-permute-done.14.refs_2_
  40.6 0.0 collective-permute-done.15.refs_3_
  40.6 1.1 %collective-permute-done.16.refs_4_ = bf16[4,64,128]{2,1,0:T(8,128)(2,1)S(1)} collective-permute-done((bf16[4,64,128]{2,1,0:T(8,128)(2,1)S(1)}, bf16[4,64,128]{2,1,0:T(8,128)(2,1)S(1)}, u32[]{:S(2)}, u32[]{:S(2)}) %collective-permute-start.16) | collective-permute-done | bytes 65568 | tf_op jit(solution)/shard_map/ppermute | solution.py:402
  41.7 1.0 %residual_last.1 = f32[16,128,128]{2,1,0:T(8,128)} custom-call(s32[1]{0:T(128)} %bitcast.me, f32[16,128,128]{2,1,0:T(8,128)S(1)} %bitcast.19, bf16[4,64,128]{2,1,0:T(8,128)(2,1)S(1)} %collective-permute-done.9.refs_0_, bf16[4,64,128]{2,1,0:T(8,128)(2,1)S(1)} %collective-permute-done.10.refs_1_, ...), custom_call_target="tpu_custom_call", output_to_operand_aliasing={{}: (7, {})} | custom-call | tf_op jit(solution)/shard_map/residual_last/pallas_call | solution.py:586
  (5 shorter events, 0.1 us)
Async XLA Ops:
  0.0 7.4 %copy-start.4 = (f32[2,32,128]{2,1,0:T(8,128)S(1)}, f32[2,32,128]{2,1,0:T(8,128)}, u32[]{:S(2)}) copy-start(f32[2,32,128]{2,1,0:T(8,128)} %constant.9.clone.cell_turns) | copy-start | bytes 98308
  0.0 7.4 %copy-start.5 = (f32[2,32,128]{2,1,0:T(8,128)S(1)}, f32[2,32,128]{2,1,0:T(8,128)}, u32[]{:S(2)}) copy-start(f32[2,32,128]{2,1,0:T(8,128)} %constant.8.clone.row_turns) | copy-start | bytes 98308
  1.6 9.4 %collective-permute-start = (bf16[160,128]{1,0:T(8,128)(2,1)}, bf16[160,128]{1,0:T(8,128)(2,1)S(1)}, u32[]{:S(2)}, u32[]{:S(2)}) collective-permute-start(bf16[160,128]{1,0:T(8,128)(2,1)} %get-tuple-element.34), channel_id=1, source_target_pairs={{0,12},{1,13},{2,14},{3,15},{4,8},{5,9},{6,10},{7,11},{8,4},{9,5},... | collective-permute-start | bytes 122888 | tf_op jit(solution)/shard_map/ppermute | solution.py:402
  6.7 5.1 %collective-permute-start.1 = (bf16[160,128]{1,0:T(8,128)(2,1)}, bf16[160,128]{1,0:T(8,128)(2,1)S(1)}, u32[]{:S(2)}, u32[]{:S(2)}) collective-permute-start(bf16[160,128]{1,0:T(8,128)(2,1)} %get-tuple-element.35), channel_id=1, source_target_pairs={{0,8},{1,9},{2,10},{3,11},{4,12},{5,13},{6,14},{7,15},{8,0},{9,1},... | collective-permute-start | bytes 122888 | tf_op jit(solution)/shard_map/ppermute | solution.py:402
  6.8 5.1 %collective-permute-start.2 = (bf16[160,128]{1,0:T(8,128)(2,1)}, bf16[160,128]{1,0:T(8,128)(2,1)S(1)}, u32[]{:S(2)}, u32[]{:S(2)}) collective-permute-start(bf16[160,128]{1,0:T(8,128)(2,1)} %get-tuple-element.36), channel_id=1, source_target_pairs={{0,4},{1,5},{2,6},{3,7},{4,0},{5,1},{6,2},{7,3},{8,12},{9,13},{10,... | collective-permute-start | bytes 122888 | tf_op jit(solution)/shard_map/ppermute | solution.py:402
  7.4 1.2 %copy-start.1 = (bf16[256,2,1024]{2,1,0:T(2,128)(2,1)S(1)}, bf16[256,2,1024]{2,1,0:T(2,128)(2,1)}, u32[]{:S(2)}) copy-start(bf16[256,2,1024]{2,1,0:T(2,128)(2,1)} %param.12) | copy-start | bytes 3145732
  8.6 3.2 %copy-start.3 = (bf16[160,128]{1,0:T(8,128)(2,1)S(1)}, bf16[160,128]{1,0:T(8,128)(2,1)}, u32[]{:S(2)}) copy-start(bf16[160,128]{1,0:T(8,128)(2,1)} %get-tuple-element.37.refs_3_) | copy-start | bytes 122884
  11.9 1.7 %copy-start.2 = (bf16[2,128,1024]{2,1,0:T(8,128)(2,1)S(1)}, bf16[2,128,1024]{2,1,0:T(8,128)(2,1)}, u32[]{:S(2)}) copy-start(bf16[2,128,1024]{2,1,0:T(8,128)(2,1)} %basis.1) | copy-start | bytes 1572868
  11.9 1.7 %copy-start.9 = (s32[1,16]{1,0:T(1,128)S(1)}, s32[1,16]{1,0:T(1,128)}, u32[]{:S(2)}) copy-start(s32[1,16]{1,0:T(1,128)} %counts.1) | copy-start | bytes 196
  11.9 1.7 %copy-start.10 = (f32[32]{0:T(128)S(1)}, f32[32]{0:T(128)}, u32[]{:S(2)}) copy-start(f32[32]{0:T(128)} %param.19) | copy-start | bytes 388
  11.9 1.6 %copy-start.6 = (s32[1,16,64]{2,1,0:T(8,128)S(1)}, s32[1,16,64]{2,1,0:T(8,128)}, u32[]{:S(2)}) copy-start(s32[1,16,64]{2,1,0:T(8,128)} %param.15) | copy-start | bytes 12292
  12.0 5.2 %collective-permute-start.3 = (bf16[4,144,128]{2,1,0:T(8,128)(2,1)S(1)}, bf16[4,144,128]{2,1,0:T(8,128)(2,1)S(1)}, u32[]{:S(2)}, u32[]{:S(2)}) collective-permute-start(bf16[4,144,128]{2,1,0:T(8,128)(2,1)S(1)} %get-tuple-element.38), channel_id=1, source_target_pairs={{0,2},{1,3},{2,0},{3,1},{4,6},{5,7},{6,4},{7,5},{8,10},{9,11},{10,... | collective-permute-start | bytes 442376 | tf_op jit(solution)/shard_map/ppermute | solution.py:402
  13.5 3.7 %collective-permute-start.5 = (bf16[4,160,128]{2,1,0:T(8,128)(2,1)S(1)}, bf16[4,160,128]{2,1,0:T(8,128)(2,1)S(1)}, u32[]{:S(2)}, u32[]{:S(2)}) collective-permute-start(bf16[4,160,128]{2,1,0:T(8,128)(2,1)S(1)} %get-tuple-element.39.after.near), channel_id=1, source_target_pairs={{0,1},{1,0},{2,3},{3,2},{4,5},{5,4},{6,7},{7,6},{8,9},{9,8},{10,11... | collective-permute-start | bytes 491528 | tf_op jit(solution)/shard_map/ppermute | solution.py:402
  13.5 0.7 %copy-start.7 = (s32[256,2]{0,1:T(2,128)S(1)}, s32[256,2]{0,1:T(2,128)}, u32[]{:S(2)}) copy-start(s32[256,2]{0,1:T(2,128)} %param.13) | copy-start | bytes 6148
  13.5 0.7 %copy-start.8 = (s32[256]{0:T(256)S(1)}, s32[256]{0:T(256)}, u32[]{:S(2)}) copy-start(s32[256]{0:T(256)} %param.14) | copy-start | bytes 3076
  17.2 1.4 %collective-permute-start.4 = (bf16[4,144,128]{2,1,0:T(8,128)(2,1)S(1)}, bf16[4,144,128]{2,1,0:T(8,128)(2,1)S(1)}, u32[]{:S(2)}, u32[]{:S(2)}) collective-permute-start(bf16[4,144,128]{2,1,0:T(8,128)(2,1)S(1)} %relay.1.over_y), channel_id=1, source_target_pairs={{0,1},{1,0},{2,3},{3,2},{4,5},{5,4},{6,7},{7,6},{8,9},{9,8},{10,11... | collective-permute-start | bytes 442376 | tf_op jit(solution)/shard_map/ppermute | solution.py:402
  18.6 19.3 %copy-start = (f32[1,16,64,2,128]{4,3,2,1,0:T(2,128)S(1)}, f32[1,16,64,2,128]{4,3,2,1,0:T(2,128)}, u32[]{:S(2)}) copy-start(f32[1,16,64,2,128]{4,3,2,1,0:T(2,128)} %param.21) | copy-start | bytes 3145732
  24.0 4.9 %collective-permute-start.6 = (bf16[4,64,128]{2,1,0:T(8,128)(2,1)S(1)}, bf16[4,64,128]{2,1,0:T(8,128)(2,1)S(1)}, u32[]{:S(2)}, u32[]{:S(2)}) collective-permute-start(bf16[4,64,128]{2,1,0:T(8,128)(2,1)S(1)} %get-tuple-element.47), channel_id=1, source_target_pairs={{0,1},{1,0},{2,3},{3,2},{4,5},{5,4},{6,7},{7,6},{8,9},{9,8},{10,11... | collective-permute-start | bytes 196616 | tf_op jit(solution)/shard_map/ppermute | solution.py:402
  24.3 6.1 %collective-permute-start.7 = (bf16[4,64,128]{2,1,0:T(8,128)(2,1)S(1)}, bf16[4,64,128]{2,1,0:T(8,128)(2,1)S(1)}, u32[]{:S(2)}, u32[]{:S(2)}) collective-permute-start(bf16[4,64,128]{2,1,0:T(8,128)(2,1)S(1)} %get-tuple-element.48), channel_id=1, source_target_pairs={{0,2},{1,3},{2,0},{3,1},{4,6},{5,7},{6,4},{7,5},{8,10},{9,11},{10,... | collective-permute-start | bytes 196616 | tf_op jit(solution)/shard_map/ppermute | solution.py:402
  25.8 4.6 %collective-permute-start.8 = (bf16[4,64,128]{2,1,0:T(8,128)(2,1)S(1)}, bf16[4,64,128]{2,1,0:T(8,128)(2,1)S(1)}, u32[]{:S(2)}, u32[]{:S(2)}) collective-permute-start(bf16[4,64,128]{2,1,0:T(8,128)(2,1)S(1)} %get-tuple-element.49), channel_id=1, source_target_pairs={{0,3},{1,2},{2,1},{3,0},{4,7},{5,6},{6,5},{7,4},{8,11},{9,10},{10,... | collective-permute-start | bytes 196616 | tf_op jit(solution)/shard_map/ppermute | solution.py:402
  26.0 7.4 %collective-permute-start.11 = (bf16[4,64,128]{2,1,0:T(8,128)(2,1)S(1)}, bf16[4,64,128]{2,1,0:T(8,128)(2,1)S(1)}, u32[]{:S(2)}, u32[]{:S(2)}) collective-permute-start(bf16[4,64,128]{2,1,0:T(8,128)(2,1)S(1)} %get-tuple-element.53), channel_id=1, source_target_pairs={{0,12},{1,13},{2,14},{3,15},{4,8},{5,9},{6,10},{7,11},{8,4},{9,5},... | collective-permute-start | bytes 196616 | tf_op jit(solution)/shard_map/ppermute | solution.py:402
  28.9 7.1 %collective-permute-start.12 = (bf16[4,64,128]{2,1,0:T(8,128)(2,1)S(1)}, bf16[4,64,128]{2,1,0:T(8,128)(2,1)S(1)}, u32[]{:S(2)}, u32[]{:S(2)}) collective-permute-start(bf16[4,64,128]{2,1,0:T(8,128)(2,1)S(1)} %get-tuple-element.54), channel_id=1, source_target_pairs={{0,8},{1,9},{2,10},{3,11},{4,12},{5,13},{6,14},{7,15},{8,0},{9,1},... | collective-permute-start | bytes 196616 | tf_op jit(solution)/shard_map/ppermute | solution.py:402
  28.9 7.0 %collective-permute-start.13 = (bf16[4,64,128]{2,1,0:T(8,128)(2,1)S(1)}, bf16[4,64,128]{2,1,0:T(8,128)(2,1)S(1)}, u32[]{:S(2)}, u32[]{:S(2)}) collective-permute-start(bf16[4,64,128]{2,1,0:T(8,128)(2,1)S(1)} %get-tuple-element.55), channel_id=1, source_target_pairs={{0,4},{1,5},{2,6},{3,7},{4,0},{5,1},{6,2},{7,3},{8,12},{9,13},{10,... | collective-permute-start | bytes 196616 | tf_op jit(solution)/shard_map/ppermute | solution.py:402
  30.4 7.3 %collective-permute-start.17 = (bf16[4,64,128]{2,1,0:T(8,128)(2,1)S(1)}, bf16[4,64,128]{2,1,0:T(8,128)(2,1)S(1)}, u32[]{:S(2)}, u32[]{:S(2)}) collective-permute-start(bf16[4,64,128]{2,1,0:T(8,128)(2,1)S(1)} %get-tuple-element.61), channel_id=1, source_target_pairs={{0,12},{1,13},{2,14},{3,15},{4,8},{5,9},{6,10},{7,11},{8,4},{9,5},... | collective-permute-start | bytes 196616 | tf_op jit(solution)/shard_map/ppermute | solution.py:402
  33.4 7.3 %collective-permute-start.9 = (bf16[4,64,128]{2,1,0:T(8,128)(2,1)S(1)}, bf16[4,64,128]{2,1,0:T(8,128)(2,1)S(1)}, u32[]{:S(2)}, u32[]{:S(2)}) collective-permute-start(bf16[4,64,128]{2,1,0:T(8,128)(2,1)S(1)} %get-tuple-element.51), channel_id=1, source_target_pairs={{0,8},{1,9},{2,10},{3,11},{4,12},{5,13},{6,14},{7,15},{8,0},{9,1},... | collective-permute-start | bytes 196616 | tf_op jit(solution)/shard_map/ppermute | solution.py:402
  33.4 7.3 %collective-permute-start.10 = (bf16[4,64,128]{2,1,0:T(8,128)(2,1)S(1)}, bf16[4,64,128]{2,1,0:T(8,128)(2,1)S(1)}, u32[]{:S(2)}, u32[]{:S(2)}) collective-permute-start(bf16[4,64,128]{2,1,0:T(8,128)(2,1)S(1)} %get-tuple-element.52), channel_id=1, source_target_pairs={{0,4},{1,5},{2,6},{3,7},{4,0},{5,1},{6,2},{7,3},{8,12},{9,13},{10,... | collective-permute-start | bytes 196616 | tf_op jit(solution)/shard_map/ppermute | solution.py:402
  36.0 4.7 %collective-permute-start.14 = (bf16[4,64,128]{2,1,0:T(8,128)(2,1)S(1)}, bf16[4,64,128]{2,1,0:T(8,128)(2,1)S(1)}, u32[]{:S(2)}, u32[]{:S(2)}) collective-permute-start(bf16[4,64,128]{2,1,0:T(8,128)(2,1)S(1)} %get-tuple-element.57), channel_id=1, source_target_pairs={{0,1},{1,0},{2,3},{3,2},{4,5},{5,4},{6,7},{7,6},{8,9},{9,8},{10,11... | collective-permute-start | bytes 196616 | tf_op jit(solution)/shard_map/ppermute | solution.py:402
  36.0 4.6 %collective-permute-start.15 = (bf16[4,64,128]{2,1,0:T(8,128)(2,1)S(1)}, bf16[4,64,128]{2,1,0:T(8,128)(2,1)S(1)}, u32[]{:S(2)}, u32[]{:S(2)}) collective-permute-start(bf16[4,64,128]{2,1,0:T(8,128)(2,1)S(1)} %get-tuple-element.58), channel_id=1, source_target_pairs={{0,2},{1,3},{2,0},{3,1},{4,6},{5,7},{6,4},{7,5},{8,10},{9,11},{10,... | collective-permute-start | bytes 196616 | tf_op jit(solution)/shard_map/ppermute | solution.py:402
  37.7 4.0 %collective-permute-start.16 = (bf16[4,64,128]{2,1,0:T(8,128)(2,1)S(1)}, bf16[4,64,128]{2,1,0:T(8,128)(2,1)S(1)}, u32[]{:S(2)}, u32[]{:S(2)}) collective-permute-start(bf16[4,64,128]{2,1,0:T(8,128)(2,1)S(1)} %get-tuple-element.59), channel_id=1, source_target_pairs={{0,3},{1,2},{2,1},{3,0},{4,7},{5,6},{6,5},{7,4},{8,11},{9,10},{10,... | collective-permute-start | bytes 196616 | tf_op jit(solution)/shard_map/ppermute | solution.py:402

commit v12 on v11

--- a/solution.py
+++ b/solution.py
@@ -316,7 +316,7 @@
             wre[to, :] = i_re * g_re - i_im * g_im
             wim[to, :] = i_re * g_im + i_im * g_re
 
-    unroll = 256
+    unroll = 128
 
     def one(g):
         at = pl.ds(pl.multiple_of(g * 8, 8), 8)
@@ -598,7 +598,7 @@
         )(me, ours, *arrived, *held)
 
     residual = finish("residual_early", (0, outer - 1), (0,), ())
-    residual = finish("residual_last", tuple(range(1, outer - 1))[::-1], (1, 2, 3), (residual,))
+    residual = finish("residual_last", tuple(range(1, outer - 1))[::-1], (3, 2, 1), (residual,))
     return residual.reshape(observed.shape)
 
 

time: 43.1 us -> 42.6 us (0.988)
  Pallas kernels: 13.5 us -> 12.9 us
    pallas_call x1, Pallas kernels: 5.42 us -> 4.91 us  [per_device(): pl.pallas_call(predict_kernel, out_shape=[for_z] * outer + [for_plane] *...]
where the time goes in v12:
time: 42.6 us; the launch traced here: 42.4 us
  starting transfers between devices  20.1 us (47%)
  Pallas kernels  12.9 us (30%)
  waiting for transfers between devices  7.27 us (17%)
  local copies, waits for them, and re-layouts  1.92 us (5%)
    ppermute x18, starting transfers between devices, exchange(): return lax.ppermute(value, 'tile', [(i, i ^ step) for i in range(tiles)])  20.1 us
    ppermute x18, waiting for transfers between devices, exchange(): return lax.ppermute(value, 'tile', [(i, i ^ step) for i in range(tiles)])  7.27 us
    pallas_call x1, Pallas kernels, per_device(): pl.pallas_call(predict_kernel, out_shape=[for_z] * outer + [for_plane] *...  4.91 us
    pallas_call x1, Pallas kernels, per_device(): pl.pallas_call(transform_kernel, out_shape=jax.ShapeDtypeStruct((8, numbe...  2.36 us
    unnamed x22, local copies, waits for them, and re-layouts  1.92 us
    pallas_call x2, Pallas kernels, finish(): pl.pallas_call(functools.partial(residual_kernel, along_z=along_z, in_pla...  1.84 us
    pallas_call x1, Pallas kernels, per_device(): pl.pallas_call(pack_kernel, out_shape=[block] * outer, in_specs=[smem, hb...  1.62 us
    pallas_call x1, Pallas kernels, per_device(): pl.pallas_call(functools.partial(prepare_kernel, slot_count=slot_count),...  1.59 us
  transfers between devices with their start and end apart: 18, of which 6 were waited for; matrix products, arithmetic and copies ran while one was open for 0% of the time, Pallas kernels for 13%

profile of v12, /device:TPU:0, one launch (start us, length us, event | category | flops | bytes accessed | tf_op | source)
XLA Modules:
  0.0 42.4 jit_solution(11740593019823400726)
XLA Ops:
  0.0 0.0 copy-start.4
  0.0 0.0 copy-start.5
  0.0 1.6 %pack.1 = (bf16[160,128]{1,0:T(8,128)(2,1)}, bf16[160,128]{1,0:T(8,128)(2,1)}, bf16[160,128]{1,0:T(8,128)(2,1)}, bf16[160,128]{1,0:T(8,128)(2,1)}) custom-call(s32[1]{0:T(128)} %bitcast.me, bf16[64,256]{1,0:T(8,128)(2,1)} %bitcast.26, f32[16,8,64]{2,1,0:T(8,128)} %bitcast.25), custom_call_target="tpu_custom_call" | custom-call | tf_op jit(solution)/shard_map/pack/pallas_call | solution.py:438
  1.6 5.1 %collective-permute-start = (bf16[160,128]{1,0:T(8,128)(2,1)}, bf16[160,128]{1,0:T(8,128)(2,1)S(1)}, u32[]{:S(2)}, u32[]{:S(2)}) collective-permute-start(bf16[160,128]{1,0:T(8,128)(2,1)} %get-tuple-element.34), channel_id=1, source_target_pairs={{0,12},{1,13},{2,14},{3,15},{4,8},{5,9},{6,10},{7,11},{8,4},{9,5},... | collective-permute-start | bytes 122888 | tf_op jit(solution)/shard_map/ppermute | solution.py:402
  6.7 0.0 collective-permute-start.1
  6.8 0.6 %collective-permute-start.2 = (bf16[160,128]{1,0:T(8,128)(2,1)}, bf16[160,128]{1,0:T(8,128)(2,1)S(1)}, u32[]{:S(2)}, u32[]{:S(2)}) collective-permute-start(bf16[160,128]{1,0:T(8,128)(2,1)} %get-tuple-element.36), channel_id=1, source_target_pairs={{0,4},{1,5},{2,6},{3,7},{4,0},{5,1},{6,2},{7,3},{8,12},{9,13},{10,... | collective-permute-start | bytes 122888 | tf_op jit(solution)/shard_map/ppermute | solution.py:402
  7.4 0.0 copy-done.4
  7.4 0.0 copy-done.5
  7.4 0.0 copy-start.1
  7.4 1.2 %copy-done.1 = bf16[256,2,1024]{2,1,0:T(2,128)(2,1)S(1)} copy-done((bf16[256,2,1024]{2,1,0:T(2,128)(2,1)S(1)}, bf16[256,2,1024]{2,1,0:T(2,128)(2,1)}, u32[]{:S(2)}) %copy-start.1) | copy-done | bytes 1048600
  8.6 0.0 copy-start.3
  8.6 2.4 %transform.1.refs_4_.image = bf16[8,256,256]{2,1,0:T(8,128)(2,1)S(1)} custom-call(bf16[4096,128]{1,0:T(8,128)(2,1)S(1)} %bitcast.20, f32[2,32,128]{2,1,0:T(8,128)S(1)} %copy-done.5, f32[2,32,128]{2,1,0:T(8,128)S(1)} %copy-done.4), custom_call_target="tpu_custom_call" | custom-call | tf_op jit(solution)/shard_map/transform/pallas_call | solution.py:456
  11.0 0.0 collective-permute-done.refs_0_
  11.0 0.9 %collective-permute-done.1.refs_1_ = bf16[160,128]{1,0:T(8,128)(2,1)S(1)} collective-permute-done((bf16[160,128]{1,0:T(8,128)(2,1)}, bf16[160,128]{1,0:T(8,128)(2,1)S(1)}, u32[]{:S(2)}, u32[]{:S(2)}) %collective-permute-start.1) | collective-permute-done | bytes 40992 | tf_op jit(solution)/shard_map/ppermute | solution.py:402
  11.9 0.0 collective-permute-done.2.refs_2_
  11.9 0.0 copy-done.3
  11.9 0.0 copy-start.2
  11.9 0.0 copy-start.9
  11.9 0.0 copy-start.10
  11.9 0.0 copy-start.6
  12.0 1.6 %collective-permute-start.3 = (bf16[4,144,128]{2,1,0:T(8,128)(2,1)S(1)}, bf16[4,144,128]{2,1,0:T(8,128)(2,1)S(1)}, u32[]{:S(2)}, u32[]{:S(2)}) collective-permute-start(bf16[4,144,128]{2,1,0:T(8,128)(2,1)S(1)} %get-tuple-element.38), channel_id=1, source_target_pairs={{0,2},{1,3},{2,0},{3,1},{4,6},{5,7},{6,4},{7,5},{8,10},{9,11},{10,... | collective-permute-start | bytes 442376 | tf_op jit(solution)/shard_map/ppermute | solution.py:402
  13.5 0.0 collective-permute-start.5
  13.5 0.0 copy-start.7
  13.5 0.0 copy-start.8
  13.5 0.0 copy-done.2
  13.6 0.0 copy-done.9
  13.6 0.0 copy-done.10
  13.6 0.0 copy-done.6
  13.6 0.6 %copy-done.7 = s32[256,2]{0,1:T(2,128)S(1)} copy-done((s32[256,2]{0,1:T(2,128)S(1)}, s32[256,2]{0,1:T(2,128)}, u32[]{:S(2)}) %copy-start.7) | copy-done | bytes 2072
  14.2 0.0 copy-done.8
  14.2 1.6 %prepare.1 = (bf16[256,1024]{1,0:T(8,128)(2,1)S(1)}, bf16[1024,256]{1,0:T(8,128)(2,1)S(1)}, bf16[512,1024]{1,0:T(8,128)(2,1)S(1)}, bf16[8,256,256]{2,1,0:T(8,128)(2,1)S(1)}, f32[1,128]{1,0:T(1,128)S(1)}) custom-call(s32[1]{0:T(128)} %bitcast.me, s32[1,16]{1,0:T(1,128)S(1)} %copy-done.9, s32[16,64]{1,0:T(8,128)S(1)} %bitcast.21, s32[2,256]{1,0:T(2,128)S(1)} %bitcast.22, ...), custom_call_target="tpu_custom_call" | custom-call | tf_op jit(solution)/shard_map/prepare/pallas_call | solution.py:484
  15.8 1.3 %collective-permute-done.3.block = bf16[4,144,128]{2,1,0:T(8,128)(2,1)S(1)} collective-permute-done((bf16[4,144,128]{2,1,0:T(8,128)(2,1)S(1)}, bf16[4,144,128]{2,1,0:T(8,128)(2,1)S(1)}, u32[]{:S(2)}, u32[]{:S(2)}) %collective-permute-start.3) | collective-permute-done | bytes 147488 | tf_op jit(solution)/shard_map/ppermute | solution.py:402
  17.2 0.1 collective-permute-start.4
  17.3 0.0 collective-permute-done.5.over_core
  17.3 0.5 %early.1 = (bf16[512,256]{1,0:T(8,128)(2,1)S(1)}, f32[256,16]{1,0:T(8,128)S(1)}) custom-call(s32[1]{0:T(128)} %bitcast.me, bf16[4,160,128]{2,1,0:T(8,128)(2,1)S(1)} %get-tuple-element.39.after.near, bf16[4,160,128]{2,1,0:T(8,128)(2,1)S(1)} %collective-permute-done.5.over_core, bf16[4,144,128]{2,1,0:T(8,128)(2,1)S(1)} %relay.1.over_y, ...), custom_call_target="tpu_custom_call" | custom-call | tf_op jit(solution)/shard_map/early/pallas_call | solution.py:517
  17.8 0.8 %collective-permute-done.4.over_both = bf16[4,144,128]{2,1,0:T(8,128)(2,1)S(1)} collective-permute-done((bf16[4,144,128]{2,1,0:T(8,128)(2,1)S(1)}, bf16[4,144,128]{2,1,0:T(8,128)(2,1)S(1)}, u32[]{:S(2)}, u32[]{:S(2)}) %collective-permute-start.4) | collective-permute-done | bytes 147488 | tf_op jit(solution)/shard_map/ppermute | solution.py:402
  18.6 4.9 %predict.1 = (bf16[4,64,128]{2,1,0:T(8,128)(2,1)S(1)}, bf16[4,64,128]{2,1,0:T(8,128)(2,1)S(1)}, bf16[4,64,128]{2,1,0:T(8,128)(2,1)S(1)}, bf16[4,64,128]{2,1,0:T(...) custom-call(s32[1]{0:T(128)} %bitcast.me, ...), custom_call_target="tpu_custom_call" | custom-call | tf_op jit(solution)/shard_map/predict/pallas_call | solution.py:532
  23.5 0.2 collective-permute-start.6
  23.7 1.5 %collective-permute-start.7 = (bf16[4,64,128]{2,1,0:T(8,128)(2,1)S(1)}, bf16[4,64,128]{2,1,0:T(8,128)(2,1)S(1)}, u32[]{:S(2)}, u32[]{:S(2)}) collective-permute-start(bf16[4,64,128]{2,1,0:T(8,128)(2,1)S(1)} %get-tuple-element.48), channel_id=1, source_target_pairs={{0,2},{1,3},{2,0},{3,1},{4,6},{5,7},{6,4},{7,5},{8,10},{9,11},{10,... | collective-permute-start | bytes 196616 | tf_op jit(solution)/shard_map/ppermute | solution.py:402
  25.3 0.2 collective-permute-start.8
  25.5 2.9 %collective-permute-start.11 = (bf16[4,64,128]{2,1,0:T(8,128)(2,1)S(1)}, bf16[4,64,128]{2,1,0:T(8,128)(2,1)S(1)}, u32[]{:S(2)}, u32[]{:S(2)}) collective-permute-start(bf16[4,64,128]{2,1,0:T(8,128)(2,1)S(1)} %get-tuple-element.53), channel_id=1, source_target_pairs={{0,12},{1,13},{2,14},{3,15},{4,8},{5,9},{6,10},{7,11},{8,4},{9,5},... | collective-permute-start | bytes 196616 | tf_op jit(solution)/shard_map/ppermute | solution.py:402
  28.4 0.0 collective-permute-start.12
  28.4 0.0 collective-permute-done.6.refs_0_
  28.4 1.5 %collective-permute-start.13 = (bf16[4,64,128]{2,1,0:T(8,128)(2,1)S(1)}, bf16[4,64,128]{2,1,0:T(8,128)(2,1)S(1)}, u32[]{:S(2)}, u32[]{:S(2)}) collective-permute-start(bf16[4,64,128]{2,1,0:T(8,128)(2,1)S(1)} %get-tuple-element.55), channel_id=1, source_target_pairs={{0,4},{1,5},{2,6},{3,7},{4,0},{5,1},{6,2},{7,3},{8,12},{9,13},{10,... | collective-permute-start | bytes 196616 | tf_op jit(solution)/shard_map/ppermute | solution.py:402
  29.9 0.0 collective-permute-done.7.refs_1_
  29.9 0.0 collective-permute-done.8.refs_2_
  29.9 3.0 %collective-permute-start.17 = (bf16[4,64,128]{2,1,0:T(8,128)(2,1)S(1)}, bf16[4,64,128]{2,1,0:T(8,128)(2,1)S(1)}, u32[]{:S(2)}, u32[]{:S(2)}) collective-permute-start(bf16[4,64,128]{2,1,0:T(8,128)(2,1)S(1)} %get-tuple-element.61), channel_id=1, source_target_pairs={{0,12},{1,13},{2,14},{3,15},{4,8},{5,9},{6,10},{7,11},{8,4},{9,5},... | collective-permute-start | bytes 196616 | tf_op jit(solution)/shard_map/ppermute | solution.py:402
  32.9 0.0 collective-permute-start.9
  32.9 0.0 collective-permute-done.11.refs_0_
  32.9 1.5 %collective-permute-start.10 = (bf16[4,64,128]{2,1,0:T(8,128)(2,1)S(1)}, bf16[4,64,128]{2,1,0:T(8,128)(2,1)S(1)}, u32[]{:S(2)}, u32[]{:S(2)}) collective-permute-start(bf16[4,64,128]{2,1,0:T(8,128)(2,1)S(1)} %get-tuple-element.52), channel_id=1, source_target_pairs={{0,4},{1,5},{2,6},{3,7},{4,0},{5,1},{6,2},{7,3},{8,12},{9,13},{10,... | collective-permute-start | bytes 196616 | tf_op jit(solution)/shard_map/ppermute | solution.py:402
  34.3 1.2 %collective-permute-done.12.refs_1_ = bf16[4,64,128]{2,1,0:T(8,128)(2,1)S(1)} collective-permute-done((bf16[4,64,128]{2,1,0:T(8,128)(2,1)S(1)}, bf16[4,64,128]{2,1,0:T(8,128)(2,1)S(1)}, u32[]{:S(2)}, u32[]{:S(2)}) %collective-permute-start.12) | collective-permute-done | bytes 65568 | tf_op jit(solution)/shard_map/ppermute | solution.py:402
  35.5 0.0 collective-permute-done.13.refs_2_
  35.5 1.0 %collective-permute-start.14 = (bf16[4,64,128]{2,1,0:T(8,128)(2,1)S(1)}, bf16[4,64,128]{2,1,0:T(8,128)(2,1)S(1)}, u32[]{:S(2)}, u32[]{:S(2)}) collective-permute-start(bf16[4,64,128]{2,1,0:T(8,128)(2,1)S(1)} %get-tuple-element.57), channel_id=1, source_target_pairs={{0,3},{1,2},{2,1},{3,0},{4,7},{5,6},{6,5},{7,4},{8,11},{9,10},{10,... | collective-permute-start | bytes 196616 | tf_op jit(solution)/shard_map/ppermute | solution.py:402
  36.5 0.7 %collective-permute-start.15 = (bf16[4,64,128]{2,1,0:T(8,128)(2,1)S(1)}, bf16[4,64,128]{2,1,0:T(8,128)(2,1)S(1)}, u32[]{:S(2)}, u32[]{:S(2)}) collective-permute-start(bf16[4,64,128]{2,1,0:T(8,128)(2,1)S(1)} %get-tuple-element.58), channel_id=1, source_target_pairs={{0,2},{1,3},{2,0},{3,1},{4,6},{5,7},{6,4},{7,5},{8,10},{9,11},{10,... | collective-permute-start | bytes 196616 | tf_op jit(solution)/shard_map/ppermute | solution.py:402
  37.2 0.0 collective-permute-done.17.refs_1_
  37.2 0.3 collective-permute-start.16
  37.5 0.0 copy-done
  37.5 0.8 %residual_early.1.refs_5_ = f32[16,128,128]{2,1,0:T(8,128)} custom-call(s32[1]{0:T(128)} %bitcast.me, f32[16,128,128]{2,1,0:T(8,128)S(1)} %bitcast.18, bf16[4,64,128]{2,1,0:T(8,128)(2,1)S(1)} %get-tuple-element.60.refs_0_, bf16[4,64,128]{2,1,0:T(8,128)(2,1)S(1)} %collective-permute-done.17.refs_1_, bf16[4,64,128]{2,1,0:T(8,128)(2,1)S(1)} %get-tuple-element.62.refs_2_), custom_call_target="tpu_custom_call" | custom-call | tf_op jit(solution)/shard_map/residual_early/pallas_call | solution.py:586
  38.3 1.8 %collective-permute-done.9.refs_0_ = bf16[4,64,128]{2,1,0:T(8,128)(2,1)S(1)} collective-permute-done((bf16[4,64,128]{2,1,0:T(8,128)(2,1)S(1)}, bf16[4,64,128]{2,1,0:T(8,128)(2,1)S(1)}, u32[]{:S(2)}, u32[]{:S(2)}) %collective-permute-start.9) | collective-permute-done | bytes 65568 | tf_op jit(solution)/shard_map/ppermute | solution.py:402
  40.1 0.0 collective-permute-done.10.refs_1_
  40.1 0.0 collective-permute-done.14.refs_2_
  40.1 1.3 %collective-permute-done.15.refs_3_ = bf16[4,64,128]{2,1,0:T(8,128)(2,1)S(1)} collective-permute-done((bf16[4,64,128]{2,1,0:T(8,128)(2,1)S(1)}, bf16[4,64,128]{2,1,0:T(8,128)(2,1)S(1)}, u32[]{:S(2)}, u32[]{:S(2)}) %collective-permute-start.15) | collective-permute-done | bytes 65568 | tf_op jit(solution)/shard_map/ppermute | solution.py:402
  41.4 0.0 collective-permute-done.16.refs_4_
  41.4 1.0 %residual_last.1 = f32[16,128,128]{2,1,0:T(8,128)} custom-call(s32[1]{0:T(128)} %bitcast.me, f32[16,128,128]{2,1,0:T(8,128)S(1)} %bitcast.19, bf16[4,64,128]{2,1,0:T(8,128)(2,1)S(1)} %collective-permute-done.9.refs_0_, bf16[4,64,128]{2,1,0:T(8,128)(2,1)S(1)} %collective-permute-done.10.refs_1_, ...), custom_call_target="tpu_custom_call", output_to_operand_aliasing={{}: (7, {})} | custom-call | tf_op jit(solution)/shard_map/residual_last/pallas_call | solution.py:586
  (5 shorter events, 0.1 us)
Async XLA Ops:
  0.0 7.4 %copy-start.4 = (f32[2,32,128]{2,1,0:T(8,128)S(1)}, f32[2,32,128]{2,1,0:T(8,128)}, u32[]{:S(2)}) copy-start(f32[2,32,128]{2,1,0:T(8,128)} %constant.9.clone.cell_turns) | copy-start | bytes 98308
  0.0 7.4 %copy-start.5 = (f32[2,32,128]{2,1,0:T(8,128)S(1)}, f32[2,32,128]{2,1,0:T(8,128)}, u32[]{:S(2)}) copy-start(f32[2,32,128]{2,1,0:T(8,128)} %constant.8.clone.row_turns) | copy-start | bytes 98308
  1.6 9.4 %collective-permute-start = (bf16[160,128]{1,0:T(8,128)(2,1)}, bf16[160,128]{1,0:T(8,128)(2,1)S(1)}, u32[]{:S(2)}, u32[]{:S(2)}) collective-permute-start(bf16[160,128]{1,0:T(8,128)(2,1)} %get-tuple-element.34), channel_id=1, source_target_pairs={{0,12},{1,13},{2,14},{3,15},{4,8},{5,9},{6,10},{7,11},{8,4},{9,5},... | collective-permute-start | bytes 122888 | tf_op jit(solution)/shard_map/ppermute | solution.py:402
  6.7 5.1 %collective-permute-start.1 = (bf16[160,128]{1,0:T(8,128)(2,1)}, bf16[160,128]{1,0:T(8,128)(2,1)S(1)}, u32[]{:S(2)}, u32[]{:S(2)}) collective-permute-start(bf16[160,128]{1,0:T(8,128)(2,1)} %get-tuple-element.35), channel_id=1, source_target_pairs={{0,8},{1,9},{2,10},{3,11},{4,12},{5,13},{6,14},{7,15},{8,0},{9,1},... | collective-permute-start | bytes 122888 | tf_op jit(solution)/shard_map/ppermute | solution.py:402
  6.8 5.1 %collective-permute-start.2 = (bf16[160,128]{1,0:T(8,128)(2,1)}, bf16[160,128]{1,0:T(8,128)(2,1)S(1)}, u32[]{:S(2)}, u32[]{:S(2)}) collective-permute-start(bf16[160,128]{1,0:T(8,128)(2,1)} %get-tuple-element.36), channel_id=1, source_target_pairs={{0,4},{1,5},{2,6},{3,7},{4,0},{5,1},{6,2},{7,3},{8,12},{9,13},{10,... | collective-permute-start | bytes 122888 | tf_op jit(solution)/shard_map/ppermute | solution.py:402
  7.4 1.2 %copy-start.1 = (bf16[256,2,1024]{2,1,0:T(2,128)(2,1)S(1)}, bf16[256,2,1024]{2,1,0:T(2,128)(2,1)}, u32[]{:S(2)}) copy-start(bf16[256,2,1024]{2,1,0:T(2,128)(2,1)} %param.12) | copy-start | bytes 3145732
  8.6 3.2 %copy-start.3 = (bf16[160,128]{1,0:T(8,128)(2,1)S(1)}, bf16[160,128]{1,0:T(8,128)(2,1)}, u32[]{:S(2)}) copy-start(bf16[160,128]{1,0:T(8,128)(2,1)} %get-tuple-element.37.refs_3_) | copy-start | bytes 122884
  11.9 1.7 %copy-start.2 = (bf16[2,128,1024]{2,1,0:T(8,128)(2,1)S(1)}, bf16[2,128,1024]{2,1,0:T(8,128)(2,1)}, u32[]{:S(2)}) copy-start(bf16[2,128,1024]{2,1,0:T(8,128)(2,1)} %basis.1) | copy-start | bytes 1572868
  11.9 1.7 %copy-start.9 = (s32[1,16]{1,0:T(1,128)S(1)}, s32[1,16]{1,0:T(1,128)}, u32[]{:S(2)}) copy-start(s32[1,16]{1,0:T(1,128)} %counts.1) | copy-start | bytes 196
  11.9 1.7 %copy-start.10 = (f32[32]{0:T(128)S(1)}, f32[32]{0:T(128)}, u32[]{:S(2)}) copy-start(f32[32]{0:T(128)} %param.19) | copy-start | bytes 388
  11.9 1.6 %copy-start.6 = (s32[1,16,64]{2,1,0:T(8,128)S(1)}, s32[1,16,64]{2,1,0:T(8,128)}, u32[]{:S(2)}) copy-start(s32[1,16,64]{2,1,0:T(8,128)} %param.15) | copy-start | bytes 12292
  12.0 5.2 %collective-permute-start.3 = (bf16[4,144,128]{2,1,0:T(8,128)(2,1)S(1)}, bf16[4,144,128]{2,1,0:T(8,128)(2,1)S(1)}, u32[]{:S(2)}, u32[]{:S(2)}) collective-permute-start(bf16[4,144,128]{2,1,0:T(8,128)(2,1)S(1)} %get-tuple-element.38), channel_id=1, source_target_pairs={{0,2},{1,3},{2,0},{3,1},{4,6},{5,7},{6,4},{7,5},{8,10},{9,11},{10,... | collective-permute-start | bytes 442376 | tf_op jit(solution)/shard_map/ppermute | solution.py:402
  13.5 3.7 %collective-permute-start.5 = (bf16[4,160,128]{2,1,0:T(8,128)(2,1)S(1)}, bf16[4,160,128]{2,1,0:T(8,128)(2,1)S(1)}, u32[]{:S(2)}, u32[]{:S(2)}) collective-permute-start(bf16[4,160,128]{2,1,0:T(8,128)(2,1)S(1)} %get-tuple-element.39.after.near), channel_id=1, source_target_pairs={{0,1},{1,0},{2,3},{3,2},{4,5},{5,4},{6,7},{7,6},{8,9},{9,8},{10,11... | collective-permute-start | bytes 491528 | tf_op jit(solution)/shard_map/ppermute | solution.py:402
  13.5 0.7 %copy-start.7 = (s32[256,2]{0,1:T(2,128)S(1)}, s32[256,2]{0,1:T(2,128)}, u32[]{:S(2)}) copy-start(s32[256,2]{0,1:T(2,128)} %param.13) | copy-start | bytes 6148
  13.5 0.7 %copy-start.8 = (s32[256]{0:T(256)S(1)}, s32[256]{0:T(256)}, u32[]{:S(2)}) copy-start(s32[256]{0:T(256)} %param.14) | copy-start | bytes 3076
  17.2 1.4 %collective-permute-start.4 = (bf16[4,144,128]{2,1,0:T(8,128)(2,1)S(1)}, bf16[4,144,128]{2,1,0:T(8,128)(2,1)S(1)}, u32[]{:S(2)}, u32[]{:S(2)}) collective-permute-start(bf16[4,144,128]{2,1,0:T(8,128)(2,1)S(1)} %relay.1.over_y), channel_id=1, source_target_pairs={{0,1},{1,0},{2,3},{3,2},{4,5},{5,4},{6,7},{7,6},{8,9},{9,8},{10,11... | collective-permute-start | bytes 442376 | tf_op jit(solution)/shard_map/ppermute | solution.py:402
  18.6 18.9 %copy-start = (f32[1,16,64,2,128]{4,3,2,1,0:T(2,128)S(1)}, f32[1,16,64,2,128]{4,3,2,1,0:T(2,128)}, u32[]{:S(2)}) copy-start(f32[1,16,64,2,128]{4,3,2,1,0:T(2,128)} %param.21) | copy-start | bytes 3145732
  23.5 4.8 %collective-permute-start.6 = (bf16[4,64,128]{2,1,0:T(8,128)(2,1)S(1)}, bf16[4,64,128]{2,1,0:T(8,128)(2,1)S(1)}, u32[]{:S(2)}, u32[]{:S(2)}) collective-permute-start(bf16[4,64,128]{2,1,0:T(8,128)(2,1)S(1)} %get-tuple-element.47), channel_id=1, source_target_pairs={{0,1},{1,0},{2,3},{3,2},{4,5},{5,4},{6,7},{7,6},{8,9},{9,8},{10,11... | collective-permute-start | bytes 196616 | tf_op jit(solution)/shard_map/ppermute | solution.py:402
  23.7 6.1 %collective-permute-start.7 = (bf16[4,64,128]{2,1,0:T(8,128)(2,1)S(1)}, bf16[4,64,128]{2,1,0:T(8,128)(2,1)S(1)}, u32[]{:S(2)}, u32[]{:S(2)}) collective-permute-start(bf16[4,64,128]{2,1,0:T(8,128)(2,1)S(1)} %get-tuple-element.48), channel_id=1, source_target_pairs={{0,2},{1,3},{2,0},{3,1},{4,6},{5,7},{6,4},{7,5},{8,10},{9,11},{10,... | collective-permute-start | bytes 196616 | tf_op jit(solution)/shard_map/ppermute | solution.py:402
  25.3 4.6 %collective-permute-start.8 = (bf16[4,64,128]{2,1,0:T(8,128)(2,1)S(1)}, bf16[4,64,128]{2,1,0:T(8,128)(2,1)S(1)}, u32[]{:S(2)}, u32[]{:S(2)}) collective-permute-start(bf16[4,64,128]{2,1,0:T(8,128)(2,1)S(1)} %get-tuple-element.49), channel_id=1, source_target_pairs={{0,3},{1,2},{2,1},{3,0},{4,7},{5,6},{6,5},{7,4},{8,11},{9,10},{10,... | collective-permute-start | bytes 196616 | tf_op jit(solution)/shard_map/ppermute | solution.py:402
  25.5 7.4 %collective-permute-start.11 = (bf16[4,64,128]{2,1,0:T(8,128)(2,1)S(1)}, bf16[4,64,128]{2,1,0:T(8,128)(2,1)S(1)}, u32[]{:S(2)}, u32[]{:S(2)}) collective-permute-start(bf16[4,64,128]{2,1,0:T(8,128)(2,1)S(1)} %get-tuple-element.53), channel_id=1, source_target_pairs={{0,12},{1,13},{2,14},{3,15},{4,8},{5,9},{6,10},{7,11},{8,4},{9,5},... | collective-permute-start | bytes 196616 | tf_op jit(solution)/shard_map/ppermute | solution.py:402
  28.4 7.1 %collective-permute-start.12 = (bf16[4,64,128]{2,1,0:T(8,128)(2,1)S(1)}, bf16[4,64,128]{2,1,0:T(8,128)(2,1)S(1)}, u32[]{:S(2)}, u32[]{:S(2)}) collective-permute-start(bf16[4,64,128]{2,1,0:T(8,128)(2,1)S(1)} %get-tuple-element.54), channel_id=1, source_target_pairs={{0,8},{1,9},{2,10},{3,11},{4,12},{5,13},{6,14},{7,15},{8,0},{9,1},... | collective-permute-start | bytes 196616 | tf_op jit(solution)/shard_map/ppermute | solution.py:402
  28.4 7.1 %collective-permute-start.13 = (bf16[4,64,128]{2,1,0:T(8,128)(2,1)S(1)}, bf16[4,64,128]{2,1,0:T(8,128)(2,1)S(1)}, u32[]{:S(2)}, u32[]{:S(2)}) collective-permute-start(bf16[4,64,128]{2,1,0:T(8,128)(2,1)S(1)} %get-tuple-element.55), channel_id=1, source_target_pairs={{0,4},{1,5},{2,6},{3,7},{4,0},{5,1},{6,2},{7,3},{8,12},{9,13},{10,... | collective-permute-start | bytes 196616 | tf_op jit(solution)/shard_map/ppermute | solution.py:402
  29.9 7.3 %collective-permute-start.17 = (bf16[4,64,128]{2,1,0:T(8,128)(2,1)S(1)}, bf16[4,64,128]{2,1,0:T(8,128)(2,1)S(1)}, u32[]{:S(2)}, u32[]{:S(2)}) collective-permute-start(bf16[4,64,128]{2,1,0:T(8,128)(2,1)S(1)} %get-tuple-element.61), channel_id=1, source_target_pairs={{0,12},{1,13},{2,14},{3,15},{4,8},{5,9},{6,10},{7,11},{8,4},{9,5},... | collective-permute-start | bytes 196616 | tf_op jit(solution)/shard_map/ppermute | solution.py:402
  32.9 7.3 %collective-permute-start.9 = (bf16[4,64,128]{2,1,0:T(8,128)(2,1)S(1)}, bf16[4,64,128]{2,1,0:T(8,128)(2,1)S(1)}, u32[]{:S(2)}, u32[]{:S(2)}) collective-permute-start(bf16[4,64,128]{2,1,0:T(8,128)(2,1)S(1)} %get-tuple-element.51), channel_id=1, source_target_pairs={{0,8},{1,9},{2,10},{3,11},{4,12},{5,13},{6,14},{7,15},{8,0},{9,1},... | collective-permute-start | bytes 196616 | tf_op jit(solution)/shard_map/ppermute | solution.py:402
  32.9 7.3 %collective-permute-start.10 = (bf16[4,64,128]{2,1,0:T(8,128)(2,1)S(1)}, bf16[4,64,128]{2,1,0:T(8,128)(2,1)S(1)}, u32[]{:S(2)}, u32[]{:S(2)}) collective-permute-start(bf16[4,64,128]{2,1,0:T(8,128)(2,1)S(1)} %get-tuple-element.52), channel_id=1, source_target_pairs={{0,4},{1,5},{2,6},{3,7},{4,0},{5,1},{6,2},{7,3},{8,12},{9,13},{10,... | collective-permute-start | bytes 196616 | tf_op jit(solution)/shard_map/ppermute | solution.py:402
  35.5 4.6 %collective-permute-start.14 = (bf16[4,64,128]{2,1,0:T(8,128)(2,1)S(1)}, bf16[4,64,128]{2,1,0:T(8,128)(2,1)S(1)}, u32[]{:S(2)}, u32[]{:S(2)}) collective-permute-start(bf16[4,64,128]{2,1,0:T(8,128)(2,1)S(1)} %get-tuple-element.57), channel_id=1, source_target_pairs={{0,3},{1,2},{2,1},{3,0},{4,7},{5,6},{6,5},{7,4},{8,11},{9,10},{10,... | collective-permute-start | bytes 196616 | tf_op jit(solution)/shard_map/ppermute | solution.py:402
  36.5 4.9 %collective-permute-start.15 = (bf16[4,64,128]{2,1,0:T(8,128)(2,1)S(1)}, bf16[4,64,128]{2,1,0:T(8,128)(2,1)S(1)}, u32[]{:S(2)}, u32[]{:S(2)}) collective-permute-start(bf16[4,64,128]{2,1,0:T(8,128)(2,1)S(1)} %get-tuple-element.58), channel_id=1, source_target_pairs={{0,2},{1,3},{2,0},{3,1},{4,6},{5,7},{6,4},{7,5},{8,10},{9,11},{10,... | collective-permute-start | bytes 196616 | tf_op jit(solution)/shard_map/ppermute | solution.py:402
  37.2 4.2 %collective-permute-start.16 = (bf16[4,64,128]{2,1,0:T(8,128)(2,1)S(1)}, bf16[4,64,128]{2,1,0:T(8,128)(2,1)S(1)}, u32[]{:S(2)}, u32[]{:S(2)}) collective-permute-start(bf16[4,64,128]{2,1,0:T(8,128)(2,1)S(1)} %get-tuple-element.59), channel_id=1, source_target_pairs={{0,1},{1,0},{2,3},{3,2},{4,5},{5,4},{6,7},{7,6},{8,9},{9,8},{10,11... | collective-permute-start | bytes 196616 | tf_op jit(solution)/shard_map/ppermute | solution.py:402

commit v13 on v12

--- a/solution.py
+++ b/solution.py
@@ -366,11 +366,12 @@
     interleaved[pl.ds(0, slots, stride=2), :] = sent[:, :128]
     interleaved[pl.ds(1, slots, stride=2), :] = sent[:, 128:]
     along_z, in_plane = refs[:outer], refs[outer : outer + 4]
+    rows = along_z[0].shape[1]
     for r in range(outer):
         for p in range(4):
             start = (p * outer + r) * (2 * capacity)
-            along_z[r][p] = interleaved[start : start + capacity, :].astype(BF16)
-            in_plane[p][r] = interleaved[start + capacity : start + 2 * capacity, :].astype(BF16)
+            along_z[r][p] = interleaved[start : start + rows, :].astype(BF16)
+            in_plane[p][r] = interleaved[start + rows : start + 2 * capacity, :].astype(BF16)
 
 
 def turn_kernel(*refs, order):
@@ -382,7 +383,7 @@
 
 def residual_kernel(me, observed, *refs, along_z, in_plane, outer):
     arrived, (out, kept, sems) = refs[: len(along_z) + len(in_plane)], refs[-3:]
-    rows = kept.shape[1]
+    rows = arrived[-1].shape[1]
     pieces = [(r, p, rows, arrived[n].at[p]) for n, r in enumerate(along_z) for p in range(4)]
     pieces += [
         (r, p, 0, arrived[len(along_z) + n].at[r]) for n, p in enumerate(in_plane) for r in range(outer)
@@ -390,8 +391,11 @@
     copies = []
     for n, (r, p, start, values) in enumerate(pieces):
         source = me[0] ^ (4 * r + p)
-        kept[n] = observed[source, start : start + rows, :] - values[...].astype(F32)
-        copy = pltpu.make_async_copy(kept.at[n], out.at[source, pl.ds(start, rows), :], sems.at[n])
+        count = values.shape[0]
+        kept[n, :count, :] = observed[source, start : start + count, :] - values[...].astype(F32)
+        copy = pltpu.make_async_copy(
+            kept.at[n, pl.ds(0, count), :], out.at[source, pl.ds(start, count), :], sems.at[n]
+        )
         copy.start()
         copies.append(copy)
     for copy in copies:
@@ -527,8 +531,10 @@
         name="early",
     )(me, near, over_core, over_y, route, pick)
 
-    for_z = jax.ShapeDtypeStruct((4, capacity, vis), BF16)
-    for_plane = jax.ShapeDtypeStruct((outer, capacity, vis), BF16)
+    rows_first = max(16, 2 * capacity * 3 // 8 // 16 * 16)
+    rows_second = 2 * capacity - rows_first
+    for_z = jax.ShapeDtypeStruct((4, rows_first, vis), BF16)
+    for_plane = jax.ShapeDtypeStruct((outer, rows_second, vis), BF16)
     models = pl.pallas_call(
         predict_kernel,
         out_shape=[for_z] * outer + [for_plane] * 4,
@@ -574,9 +580,15 @@
     first, second = models[:outer], models[outer:]
     second = [second[0]] + [exchange(second[p], p, tiles) for p in range(1, 4)]
     first = [first[0]] + [exchange(first[r], 4 * r, tiles) for r in range(1, outer)]
-    second = turned(second, (1, 2, 3, 0), [for_z] * outer)
+    second = turned(
+        second, (1, 2, 3, 0), [jax.ShapeDtypeStruct((4, rows_second, vis), BF16)] * outer
+    )
     second = [second[0]] + [exchange(second[r], 4 * r, tiles) for r in range(1, outer)]
-    first = turned(first, tuple(range(outer))[::-1], [for_plane] * 4)
+    first = turned(
+        first,
+        tuple(range(outer))[::-1],
+        [jax.ShapeDtypeStruct((outer, rows_first, vis), BF16)] * 4,
+    )
     first = [first[0]] + [exchange(first[p], p, tiles) for p in range(1, 4)]
     ours = observed.reshape(tiles, 2 * capacity, vis)
 
@@ -589,7 +601,7 @@
             in_specs=[smem] + [vmem] * (1 + len(arrived)) + [anywhere] * len(held),
             out_specs=anywhere,
             scratch_shapes=[
-                pltpu.VMEM((count, capacity, vis), F32),
+                pltpu.VMEM((count, max(rows_first, rows_second), vis), F32),
                 pltpu.SemaphoreType.DMA((count,)),
             ],
             input_output_aliases={2 + len(arrived): 0} if held else {},

time: 42.6 us -> 49.3 us (1.16)
  waiting for transfers between devices: 7.27 us -> 13.6 us
    ppermute x18, waiting for transfers between devices: 7.27 us -> 13.6 us  [exchange(): return lax.ppermute(value, 'tile', [(i, i ^ step) for i in range(tiles)])]
  transfers between devices with their start and end apart: 18 -> 18, of which waited for: 6 -> 9; matrix products, arithmetic and copies ran while one was open for 0% -> 0% of each run, Pallas kernels for 13% -> 11%
where the time goes in v13:
time: 49.3 us; the launch traced here: 49.1 us
  starting transfers between devices  20.5 us (42%)
  waiting for transfers between devices  13.6 us (28%)
  Pallas kernels  12.9 us (26%)
  local copies, waits for them, and re-layouts  1.92 us (4%)
    ppermute x18, starting transfers between devices, exchange(): return lax.ppermute(value, 'tile', [(i, i ^ step) for i in range(tiles)])  20.5 us
    ppermute x18, waiting for transfers between devices, exchange(): return lax.ppermute(value, 'tile', [(i, i ^ step) for i in range(tiles)])  13.6 us
    pallas_call x1, Pallas kernels, per_device(): pl.pallas_call(predict_kernel, out_shape=[for_z] * outer + [for_plane] *...  4.92 us
    pallas_call x1, Pallas kernels, per_device(): pl.pallas_call(transform_kernel, out_shape=jax.ShapeDtypeStruct((8, numbe...  2.36 us
    unnamed x22, local copies, waits for them, and re-layouts  1.92 us
    pallas_call x2, Pallas kernels, finish(): pl.pallas_call(functools.partial(residual_kernel, along_z=along_z, in_pla...  1.84 us
    pallas_call x1, Pallas kernels, per_device(): pl.pallas_call(pack_kernel, out_shape=[block] * outer, in_specs=[smem, hb...  1.62 us
    pallas_call x1, Pallas kernels, per_device(): pl.pallas_call(functools.partial(prepare_kernel, slot_count=slot_count),...  1.59 us
  transfers between devices with their start and end apart: 18, of which 9 were waited for; matrix products, arithmetic and copies ran while one was open for 0% of the time, Pallas kernels for 11%

profile of v13, /device:TPU:0, one launch (start us, length us, event | category | flops | bytes accessed | tf_op | source)
XLA Modules:
  0.0 49.1 jit_solution(1304306624250538721)
XLA Ops:
  0.0 0.0 copy-start.4
  0.0 0.0 copy-start.5
  0.0 1.6 %pack.1 = (bf16[160,128]{1,0:T(8,128)(2,1)}, bf16[160,128]{1,0:T(8,128)(2,1)}, bf16[160,128]{1,0:T(8,128)(2,1)}, bf16[160,128]{1,0:T(8,128)(2,1)}) custom-call(s32[1]{0:T(128)} %bitcast.me, bf16[64,256]{1,0:T(8,128)(2,1)} %bitcast.26, f32[16,8,64]{2,1,0:T(8,128)} %bitcast.25), custom_call_target="tpu_custom_call" | custom-call | tf_op jit(solution)/shard_map/pack/pallas_call | solution.py:442
  1.6 5.1 %collective-permute-start = (bf16[160,128]{1,0:T(8,128)(2,1)}, bf16[160,128]{1,0:T(8,128)(2,1)S(1)}, u32[]{:S(2)}, u32[]{:S(2)}) collective-permute-start(bf16[160,128]{1,0:T(8,128)(2,1)} %get-tuple-element.34), channel_id=1, source_target_pairs={{0,12},{1,13},{2,14},{3,15},{4,8},{5,9},{6,10},{7,11},{8,4},{9,5},... | collective-permute-start | bytes 122888 | tf_op jit(solution)/shard_map/ppermute | solution.py:406
  6.7 0.0 collective-permute-start.1
  6.8 0.6 %collective-permute-start.2 = (bf16[160,128]{1,0:T(8,128)(2,1)}, bf16[160,128]{1,0:T(8,128)(2,1)S(1)}, u32[]{:S(2)}, u32[]{:S(2)}) collective-permute-start(bf16[160,128]{1,0:T(8,128)(2,1)} %get-tuple-element.36), channel_id=1, source_target_pairs={{0,4},{1,5},{2,6},{3,7},{4,0},{5,1},{6,2},{7,3},{8,12},{9,13},{10,... | collective-permute-start | bytes 122888 | tf_op jit(solution)/shard_map/ppermute | solution.py:406
  7.4 0.0 copy-done.4
  7.4 0.0 copy-done.5
  7.4 0.0 copy-start.1
  7.4 1.2 %copy-done.1 = bf16[256,2,1024]{2,1,0:T(2,128)(2,1)S(1)} copy-done((bf16[256,2,1024]{2,1,0:T(2,128)(2,1)S(1)}, bf16[256,2,1024]{2,1,0:T(2,128)(2,1)}, u32[]{:S(2)}) %copy-start.1) | copy-done | bytes 1048600
  8.6 0.0 copy-start.3
  8.6 2.4 %transform.1.refs_4_.image = bf16[8,256,256]{2,1,0:T(8,128)(2,1)S(1)} custom-call(bf16[4096,128]{1,0:T(8,128)(2,1)S(1)} %bitcast.20, f32[2,32,128]{2,1,0:T(8,128)S(1)} %copy-done.5, f32[2,32,128]{2,1,0:T(8,128)S(1)} %copy-done.4), custom_call_target="tpu_custom_call" | custom-call | tf_op jit(solution)/shard_map/transform/pallas_call | solution.py:460
  11.0 0.0 collective-permute-done.refs_0_
  11.0 0.9 %collective-permute-done.1.refs_1_ = bf16[160,128]{1,0:T(8,128)(2,1)S(1)} collective-permute-done((bf16[160,128]{1,0:T(8,128)(2,1)}, bf16[160,128]{1,0:T(8,128)(2,1)S(1)}, u32[]{:S(2)}, u32[]{:S(2)}) %collective-permute-start.1) | collective-permute-done | bytes 40992 | tf_op jit(solution)/shard_map/ppermute | solution.py:406
  11.9 0.0 collective-permute-done.2.refs_2_
  11.9 0.0 copy-done.3
  11.9 0.0 copy-start.2
  11.9 0.0 copy-start.9
  11.9 0.0 copy-start.10
  11.9 0.0 copy-start.6
  12.0 1.6 %collective-permute-start.3 = (bf16[4,144,128]{2,1,0:T(8,128)(2,1)S(1)}, bf16[4,144,128]{2,1,0:T(8,128)(2,1)S(1)}, u32[]{:S(2)}, u32[]{:S(2)}) collective-permute-start(bf16[4,144,128]{2,1,0:T(8,128)(2,1)S(1)} %get-tuple-element.38), channel_id=1, source_target_pairs={{0,2},{1,3},{2,0},{3,1},{4,6},{5,7},{6,4},{7,5},{8,10},{9,11},{10,... | collective-permute-start | bytes 442376 | tf_op jit(solution)/shard_map/ppermute | solution.py:406
  13.5 0.0 collective-permute-start.5
  13.5 0.0 copy-start.7
  13.5 0.0 copy-start.8
  13.5 0.0 copy-done.2
  13.6 0.0 copy-done.9
  13.6 0.0 copy-done.10
  13.6 0.0 copy-done.6
  13.6 0.6 %copy-done.7 = s32[256,2]{0,1:T(2,128)S(1)} copy-done((s32[256,2]{0,1:T(2,128)S(1)}, s32[256,2]{0,1:T(2,128)}, u32[]{:S(2)}) %copy-start.7) | copy-done | bytes 2072
  14.2 0.0 copy-done.8
  14.2 1.6 %prepare.1 = (bf16[256,1024]{1,0:T(8,128)(2,1)S(1)}, bf16[1024,256]{1,0:T(8,128)(2,1)S(1)}, bf16[512,1024]{1,0:T(8,128)(2,1)S(1)}, bf16[8,256,256]{2,1,0:T(8,128)(2,1)S(1)}, f32[1,128]{1,0:T(1,128)S(1)}) custom-call(s32[1]{0:T(128)} %bitcast.me, s32[1,16]{1,0:T(1,128)S(1)} %copy-done.9, s32[16,64]{1,0:T(8,128)S(1)} %bitcast.21, s32[2,256]{1,0:T(2,128)S(1)} %bitcast.22, ...), custom_call_target="tpu_custom_call" | custom-call | tf_op jit(solution)/shard_map/prepare/pallas_call | solution.py:488
  15.8 1.3 %collective-permute-done.3.block = bf16[4,144,128]{2,1,0:T(8,128)(2,1)S(1)} collective-permute-done((bf16[4,144,128]{2,1,0:T(8,128)(2,1)S(1)}, bf16[4,144,128]{2,1,0:T(8,128)(2,1)S(1)}, u32[]{:S(2)}, u32[]{:S(2)}) %collective-permute-start.3) | collective-permute-done | bytes 147488 | tf_op jit(solution)/shard_map/ppermute | solution.py:406
  17.2 0.1 collective-permute-start.4
  17.3 0.0 collective-permute-done.5.over_core
  17.3 0.5 %early.1 = (bf16[512,256]{1,0:T(8,128)(2,1)S(1)}, f32[256,16]{1,0:T(8,128)S(1)}) custom-call(s32[1]{0:T(128)} %bitcast.me, bf16[4,160,128]{2,1,0:T(8,128)(2,1)S(1)} %get-tuple-element.39.after.near, bf16[4,160,128]{2,1,0:T(8,128)(2,1)S(1)} %collective-permute-done.5.over_core, bf16[4,144,128]{2,1,0:T(8,128)(2,1)S(1)} %relay.1.over_y, ...), custom_call_target="tpu_custom_call" | custom-call | tf_op jit(solution)/shard_map/early/pallas_call | solution.py:521
  17.8 0.8 %collective-permute-done.4.over_both = bf16[4,144,128]{2,1,0:T(8,128)(2,1)S(1)} collective-permute-done((bf16[4,144,128]{2,1,0:T(8,128)(2,1)S(1)}, bf16[4,144,128]{2,1,0:T(8,128)(2,1)S(1)}, u32[]{:S(2)}, u32[]{:S(2)}) %collective-permute-start.4) | collective-permute-done | bytes 147488 | tf_op jit(solution)/shard_map/ppermute | solution.py:406
  18.6 4.9 %predict.1 = (bf16[4,48,128]{2,1,0:T(8,128)(2,1)S(1)}, bf16[4,48,128]{2,1,0:T(8,128)(2,1)S(1)}, bf16[4,48,128]{2,1,0:T(8,128)(2,1)S(1)}, bf16[4,48,128]{2,1,0:T(...) custom-call(s32[1]{0:T(128)} %bitcast.me, ...), custom_call_target="tpu_custom_call" | custom-call | tf_op jit(solution)/shard_map/predict/pallas_call | solution.py:538
  23.5 0.2 collective-permute-start.6
  23.7 1.5 %collective-permute-start.7 = (bf16[4,80,128]{2,1,0:T(8,128)(2,1)S(1)}, bf16[4,80,128]{2,1,0:T(8,128)(2,1)S(1)}, u32[]{:S(2)}, u32[]{:S(2)}) collective-permute-start(bf16[4,80,128]{2,1,0:T(8,128)(2,1)S(1)} %get-tuple-element.48), channel_id=1, source_target_pairs={{0,2},{1,3},{2,0},{3,1},{4,6},{5,7},{6,4},{7,5},{8,10},{9,11},{10,... | collective-permute-start | bytes 245768 | tf_op jit(solution)/shard_map/ppermute | solution.py:406
  25.3 0.2 collective-permute-start.8
  25.5 0.0 collective-permute-done.6.refs_0_
  25.5 3.2 %collective-permute-done.7.refs_1_ = bf16[4,80,128]{2,1,0:T(8,128)(2,1)S(1)} collective-permute-done((bf16[4,80,128]{2,1,0:T(8,128)(2,1)S(1)}, bf16[4,80,128]{2,1,0:T(8,128)(2,1)S(1)}, u32[]{:S(2)}, u32[]{:S(2)}) %collective-permute-start.7) | collective-permute-done | bytes 81952 | tf_op jit(solution)/shard_map/ppermute | solution.py:406
  28.7 1.3 %collective-permute-done.8.refs_2_ = bf16[4,80,128]{2,1,0:T(8,128)(2,1)S(1)} collective-permute-done((bf16[4,80,128]{2,1,0:T(8,128)(2,1)S(1)}, bf16[4,80,128]{2,1,0:T(8,128)(2,1)S(1)}, u32[]{:S(2)}, u32[]{:S(2)}) %collective-permute-start.8) | collective-permute-done | bytes 81952 | tf_op jit(solution)/shard_map/ppermute | solution.py:406
  30.0 3.0 %collective-permute-start.17 = (bf16[4,80,128]{2,1,0:T(8,128)(2,1)S(1)}, bf16[4,80,128]{2,1,0:T(8,128)(2,1)S(1)}, u32[]{:S(2)}, u32[]{:S(2)}) collective-permute-start(bf16[4,80,128]{2,1,0:T(8,128)(2,1)S(1)} %get-tuple-element.61), channel_id=1, source_target_pairs={{0,12},{1,13},{2,14},{3,15},{4,8},{5,9},{6,10},{7,11},{8,4},{9,5},... | collective-permute-start | bytes 245768 | tf_op jit(solution)/shard_map/ppermute | solution.py:406
  33.0 0.9 %collective-permute-start.11 = (bf16[4,48,128]{2,1,0:T(8,128)(2,1)S(1)}, bf16[4,48,128]{2,1,0:T(8,128)(2,1)S(1)}, u32[]{:S(2)}, u32[]{:S(2)}) collective-permute-start(bf16[4,48,128]{2,1,0:T(8,128)(2,1)S(1)} %get-tuple-element.53), channel_id=1, source_target_pairs={{0,12},{1,13},{2,14},{3,15},{4,8},{5,9},{6,10},{7,11},{8,4},{9,5},... | collective-permute-start | bytes 147464 | tf_op jit(solution)/shard_map/ppermute | solution.py:406
  33.9 0.2 collective-permute-start.12
  34.1 3.3 %collective-permute-start.13 = (bf16[4,48,128]{2,1,0:T(8,128)(2,1)S(1)}, bf16[4,48,128]{2,1,0:T(8,128)(2,1)S(1)}, u32[]{:S(2)}, u32[]{:S(2)}) collective-permute-start(bf16[4,48,128]{2,1,0:T(8,128)(2,1)S(1)} %get-tuple-element.55), channel_id=1, source_target_pairs={{0,4},{1,5},{2,6},{3,7},{4,0},{5,1},{6,2},{7,3},{8,12},{9,13},{10,... | collective-permute-start | bytes 147464 | tf_op jit(solution)/shard_map/ppermute | solution.py:406
  37.4 0.0 collective-permute-start.9
  37.4 2.0 %collective-permute-done.11.refs_0_ = bf16[4,48,128]{2,1,0:T(8,128)(2,1)S(1)} collective-permute-done((bf16[4,48,128]{2,1,0:T(8,128)(2,1)S(1)}, bf16[4,48,128]{2,1,0:T(8,128)(2,1)S(1)}, u32[]{:S(2)}, u32[]{:S(2)}) %collective-permute-start.11) | collective-permute-done | bytes 49184 | tf_op jit(solution)/shard_map/ppermute | solution.py:406
  39.4 1.9 %collective-permute-start.10 = (bf16[4,80,128]{2,1,0:T(8,128)(2,1)S(1)}, bf16[4,80,128]{2,1,0:T(8,128)(2,1)S(1)}, u32[]{:S(2)}, u32[]{:S(2)}) collective-permute-start(bf16[4,80,128]{2,1,0:T(8,128)(2,1)S(1)} %get-tuple-element.52), channel_id=1, source_target_pairs={{0,4},{1,5},{2,6},{3,7},{4,0},{5,1},{6,2},{7,3},{8,12},{9,13},{10,... | collective-permute-start | bytes 245768 | tf_op jit(solution)/shard_map/ppermute | solution.py:406
  41.3 1.6 %collective-permute-done.12.refs_1_ = bf16[4,48,128]{2,1,0:T(8,128)(2,1)S(1)} collective-permute-done((bf16[4,48,128]{2,1,0:T(8,128)(2,1)S(1)}, bf16[4,48,128]{2,1,0:T(8,128)(2,1)S(1)}, u32[]{:S(2)}, u32[]{:S(2)}) %collective-permute-start.12) | collective-permute-done | bytes 49184 | tf_op jit(solution)/shard_map/ppermute | solution.py:406
  42.9 0.0 collective-permute-done.13.refs_2_
  42.9 0.6 %collective-permute-start.14 = (bf16[4,48,128]{2,1,0:T(8,128)(2,1)S(1)}, bf16[4,48,128]{2,1,0:T(8,128)(2,1)S(1)}, u32[]{:S(2)}, u32[]{:S(2)}) collective-permute-start(bf16[4,48,128]{2,1,0:T(8,128)(2,1)S(1)} %get-tuple-element.57), channel_id=1, source_target_pairs={{0,3},{1,2},{2,1},{3,0},{4,7},{5,6},{6,5},{7,4},{8,11},{9,10},{10,... | collective-permute-start | bytes 147464 | tf_op jit(solution)/shard_map/ppermute | solution.py:406
  43.5 0.9 %collective-permute-start.15 = (bf16[4,48,128]{2,1,0:T(8,128)(2,1)S(1)}, bf16[4,48,128]{2,1,0:T(8,128)(2,1)S(1)}, u32[]{:S(2)}, u32[]{:S(2)}) collective-permute-start(bf16[4,48,128]{2,1,0:T(8,128)(2,1)S(1)} %get-tuple-element.58), channel_id=1, source_target_pairs={{0,2},{1,3},{2,0},{3,1},{4,6},{5,7},{6,4},{7,5},{8,10},{9,11},{10,... | collective-permute-start | bytes 147464 | tf_op jit(solution)/shard_map/ppermute | solution.py:406
  44.4 0.0 collective-permute-done.17.refs_1_
  44.4 0.4 collective-permute-start.16
  44.8 0.0 copy-done
  44.8 0.8 %residual_early.1.refs_5_ = f32[16,128,128]{2,1,0:T(8,128)} custom-call(s32[1]{0:T(128)} %bitcast.me, f32[16,128,128]{2,1,0:T(8,128)S(1)} %bitcast.18, bf16[4,80,128]{2,1,0:T(8,128)(2,1)S(1)} %get-tuple-element.60.refs_0_, bf16[4,80,128]{2,1,0:T(8,128)(2,1)S(1)} %collective-permute-done.17.refs_1_, bf16[4,48,128]{2,1,0:T(8,128)(2,1)S(1)} %get-tuple-element.62.refs_2_), custom_call_target="tpu_custom_call" | custom-call | tf_op jit(solution)/shard_map/residual_early/pallas_call | solution.py:598
  45.7 1.3 %collective-permute-done.14.refs_2_ = bf16[4,48,128]{2,1,0:T(8,128)(2,1)S(1)} collective-permute-done((bf16[4,48,128]{2,1,0:T(8,128)(2,1)S(1)}, bf16[4,48,128]{2,1,0:T(8,128)(2,1)S(1)}, u32[]{:S(2)}, u32[]{:S(2)}) %collective-permute-start.14) | collective-permute-done | bytes 49184 | tf_op jit(solution)/shard_map/ppermute | solution.py:406
  46.9 1.2 %collective-permute-done.15.refs_3_ = bf16[4,48,128]{2,1,0:T(8,128)(2,1)S(1)} collective-permute-done((bf16[4,48,128]{2,1,0:T(8,128)(2,1)S(1)}, bf16[4,48,128]{2,1,0:T(8,128)(2,1)S(1)}, u32[]{:S(2)}, u32[]{:S(2)}) %collective-permute-start.15) | collective-permute-done | bytes 49184 | tf_op jit(solution)/shard_map/ppermute | solution.py:406
  48.1 0.0 collective-permute-done.16.refs_4_
  48.1 0.0 collective-permute-done.9.refs_0_
  48.1 0.0 collective-permute-done.10.refs_1_
  48.1 1.0 %residual_last.1 = f32[16,128,128]{2,1,0:T(8,128)} custom-call(s32[1]{0:T(128)} %bitcast.me, f32[16,128,128]{2,1,0:T(8,128)S(1)} %bitcast.19, bf16[4,80,128]{2,1,0:T(8,128)(2,1)S(1)} %collective-permute-done.9.refs_0_, bf16[4,80,128]{2,1,0:T(8,128)(2,1)S(1)} %collective-permute-done.10.refs_1_, ...), custom_call_target="tpu_custom_call", output_to_operand_aliasing={{}: (7, {})} | custom-call | tf_op jit(solution)/shard_map/residual_last/pallas_call | solution.py:598
  (5 shorter events, 0.1 us)
Async XLA Ops:
  0.0 7.4 %copy-start.4 = (f32[2,32,128]{2,1,0:T(8,128)S(1)}, f32[2,32,128]{2,1,0:T(8,128)}, u32[]{:S(2)}) copy-start(f32[2,32,128]{2,1,0:T(8,128)} %constant.9.clone.cell_turns) | copy-start | bytes 98308
  0.0 7.4 %copy-start.5 = (f32[2,32,128]{2,1,0:T(8,128)S(1)}, f32[2,32,128]{2,1,0:T(8,128)}, u32[]{:S(2)}) copy-start(f32[2,32,128]{2,1,0:T(8,128)} %constant.8.clone.row_turns) | copy-start | bytes 98308
  1.6 9.4 %collective-permute-start = (bf16[160,128]{1,0:T(8,128)(2,1)}, bf16[160,128]{1,0:T(8,128)(2,1)S(1)}, u32[]{:S(2)}, u32[]{:S(2)}) collective-permute-start(bf16[160,128]{1,0:T(8,128)(2,1)} %get-tuple-element.34), channel_id=1, source_target_pairs={{0,12},{1,13},{2,14},{3,15},{4,8},{5,9},{6,10},{7,11},{8,4},{9,5},... | collective-permute-start | bytes 122888 | tf_op jit(solution)/shard_map/ppermute | solution.py:406
  6.7 5.1 %collective-permute-start.1 = (bf16[160,128]{1,0:T(8,128)(2,1)}, bf16[160,128]{1,0:T(8,128)(2,1)S(1)}, u32[]{:S(2)}, u32[]{:S(2)}) collective-permute-start(bf16[160,128]{1,0:T(8,128)(2,1)} %get-tuple-element.35), channel_id=1, source_target_pairs={{0,8},{1,9},{2,10},{3,11},{4,12},{5,13},{6,14},{7,15},{8,0},{9,1},... | collective-permute-start | bytes 122888 | tf_op jit(solution)/shard_map/ppermute | solution.py:406
  6.8 5.1 %collective-permute-start.2 = (bf16[160,128]{1,0:T(8,128)(2,1)}, bf16[160,128]{1,0:T(8,128)(2,1)S(1)}, u32[]{:S(2)}, u32[]{:S(2)}) collective-permute-start(bf16[160,128]{1,0:T(8,128)(2,1)} %get-tuple-element.36), channel_id=1, source_target_pairs={{0,4},{1,5},{2,6},{3,7},{4,0},{5,1},{6,2},{7,3},{8,12},{9,13},{10,... | collective-permute-start | bytes 122888 | tf_op jit(solution)/shard_map/ppermute | solution.py:406
  7.4 1.2 %copy-start.1 = (bf16[256,2,1024]{2,1,0:T(2,128)(2,1)S(1)}, bf16[256,2,1024]{2,1,0:T(2,128)(2,1)}, u32[]{:S(2)}) copy-start(bf16[256,2,1024]{2,1,0:T(2,128)(2,1)} %param.12) | copy-start | bytes 3145732
  8.6 3.2 %copy-start.3 = (bf16[160,128]{1,0:T(8,128)(2,1)S(1)}, bf16[160,128]{1,0:T(8,128)(2,1)}, u32[]{:S(2)}) copy-start(bf16[160,128]{1,0:T(8,128)(2,1)} %get-tuple-element.37.refs_3_) | copy-start | bytes 122884
  11.9 1.7 %copy-start.2 = (bf16[2,128,1024]{2,1,0:T(8,128)(2,1)S(1)}, bf16[2,128,1024]{2,1,0:T(8,128)(2,1)}, u32[]{:S(2)}) copy-start(bf16[2,128,1024]{2,1,0:T(8,128)(2,1)} %basis.1) | copy-start | bytes 1572868
  11.9 1.7 %copy-start.9 = (s32[1,16]{1,0:T(1,128)S(1)}, s32[1,16]{1,0:T(1,128)}, u32[]{:S(2)}) copy-start(s32[1,16]{1,0:T(1,128)} %counts.1) | copy-start | bytes 196
  11.9 1.7 %copy-start.10 = (f32[32]{0:T(128)S(1)}, f32[32]{0:T(128)}, u32[]{:S(2)}) copy-start(f32[32]{0:T(128)} %param.19) | copy-start | bytes 388
  11.9 1.6 %copy-start.6 = (s32[1,16,64]{2,1,0:T(8,128)S(1)}, s32[1,16,64]{2,1,0:T(8,128)}, u32[]{:S(2)}) copy-start(s32[1,16,64]{2,1,0:T(8,128)} %param.15) | copy-start | bytes 12292
  12.0 5.2 %collective-permute-start.3 = (bf16[4,144,128]{2,1,0:T(8,128)(2,1)S(1)}, bf16[4,144,128]{2,1,0:T(8,128)(2,1)S(1)}, u32[]{:S(2)}, u32[]{:S(2)}) collective-permute-start(bf16[4,144,128]{2,1,0:T(8,128)(2,1)S(1)} %get-tuple-element.38), channel_id=1, source_target_pairs={{0,2},{1,3},{2,0},{3,1},{4,6},{5,7},{6,4},{7,5},{8,10},{9,11},{10,... | collective-permute-start | bytes 442376 | tf_op jit(solution)/shard_map/ppermute | solution.py:406
  13.5 3.7 %collective-permute-start.5 = (bf16[4,160,128]{2,1,0:T(8,128)(2,1)S(1)}, bf16[4,160,128]{2,1,0:T(8,128)(2,1)S(1)}, u32[]{:S(2)}, u32[]{:S(2)}) collective-permute-start(bf16[4,160,128]{2,1,0:T(8,128)(2,1)S(1)} %get-tuple-element.39.after.near), channel_id=1, source_target_pairs={{0,1},{1,0},{2,3},{3,2},{4,5},{5,4},{6,7},{7,6},{8,9},{9,8},{10,11... | collective-permute-start | bytes 491528 | tf_op jit(solution)/shard_map/ppermute | solution.py:406
  13.5 0.7 %copy-start.7 = (s32[256,2]{0,1:T(2,128)S(1)}, s32[256,2]{0,1:T(2,128)}, u32[]{:S(2)}) copy-start(s32[256,2]{0,1:T(2,128)} %param.13) | copy-start | bytes 6148
  13.5 0.7 %copy-start.8 = (s32[256]{0:T(256)S(1)}, s32[256]{0:T(256)}, u32[]{:S(2)}) copy-start(s32[256]{0:T(256)} %param.14) | copy-start | bytes 3076
  17.2 1.4 %collective-permute-start.4 = (bf16[4,144,128]{2,1,0:T(8,128)(2,1)S(1)}, bf16[4,144,128]{2,1,0:T(8,128)(2,1)S(1)}, u32[]{:S(2)}, u32[]{:S(2)}) collective-permute-start(bf16[4,144,128]{2,1,0:T(8,128)(2,1)S(1)} %relay.1.over_y), channel_id=1, source_target_pairs={{0,1},{1,0},{2,3},{3,2},{4,5},{5,4},{6,7},{7,6},{8,9},{9,8},{10,11... | collective-permute-start | bytes 442376 | tf_op jit(solution)/shard_map/ppermute | solution.py:406
  18.6 26.2 %copy-start = (f32[1,16,64,2,128]{4,3,2,1,0:T(2,128)S(1)}, f32[1,16,64,2,128]{4,3,2,1,0:T(2,128)}, u32[]{:S(2)}) copy-start(f32[1,16,64,2,128]{4,3,2,1,0:T(2,128)} %param.21) | copy-start | bytes 3145732
  23.5 1.9 %collective-permute-start.6 = (bf16[4,80,128]{2,1,0:T(8,128)(2,1)S(1)}, bf16[4,80,128]{2,1,0:T(8,128)(2,1)S(1)}, u32[]{:S(2)}, u32[]{:S(2)}) collective-permute-start(bf16[4,80,128]{2,1,0:T(8,128)(2,1)S(1)} %get-tuple-element.47), channel_id=1, source_target_pairs={{0,1},{1,0},{2,3},{3,2},{4,5},{5,4},{6,7},{7,6},{8,9},{9,8},{10,11... | collective-permute-start | bytes 245768 | tf_op jit(solution)/shard_map/ppermute | solution.py:406
  23.7 5.0 %collective-permute-start.7 = (bf16[4,80,128]{2,1,0:T(8,128)(2,1)S(1)}, bf16[4,80,128]{2,1,0:T(8,128)(2,1)S(1)}, u32[]{:S(2)}, u32[]{:S(2)}) collective-permute-start(bf16[4,80,128]{2,1,0:T(8,128)(2,1)S(1)} %get-tuple-element.48), channel_id=1, source_target_pairs={{0,2},{1,3},{2,0},{3,1},{4,6},{5,7},{6,4},{7,5},{8,10},{9,11},{10,... | collective-permute-start | bytes 245768 | tf_op jit(solution)/shard_map/ppermute | solution.py:406
  25.3 4.7 %collective-permute-start.8 = (bf16[4,80,128]{2,1,0:T(8,128)(2,1)S(1)}, bf16[4,80,128]{2,1,0:T(8,128)(2,1)S(1)}, u32[]{:S(2)}, u32[]{:S(2)}) collective-permute-start(bf16[4,80,128]{2,1,0:T(8,128)(2,1)S(1)} %get-tuple-element.49), channel_id=1, source_target_pairs={{0,3},{1,2},{2,1},{3,0},{4,7},{5,6},{6,5},{7,4},{8,11},{9,10},{10,... | collective-permute-start | bytes 245768 | tf_op jit(solution)/shard_map/ppermute | solution.py:406
  30.0 14.4 %collective-permute-start.17 = (bf16[4,80,128]{2,1,0:T(8,128)(2,1)S(1)}, bf16[4,80,128]{2,1,0:T(8,128)(2,1)S(1)}, u32[]{:S(2)}, u32[]{:S(2)}) collective-permute-start(bf16[4,80,128]{2,1,0:T(8,128)(2,1)S(1)} %get-tuple-element.61), channel_id=1, source_target_pairs={{0,12},{1,13},{2,14},{3,15},{4,8},{5,9},{6,10},{7,11},{8,4},{9,5},... | collective-permute-start | bytes 245768 | tf_op jit(solution)/shard_map/ppermute | solution.py:406
  33.0 6.4 %collective-permute-start.11 = (bf16[4,48,128]{2,1,0:T(8,128)(2,1)S(1)}, bf16[4,48,128]{2,1,0:T(8,128)(2,1)S(1)}, u32[]{:S(2)}, u32[]{:S(2)}) collective-permute-start(bf16[4,48,128]{2,1,0:T(8,128)(2,1)S(1)} %get-tuple-element.53), channel_id=1, source_target_pairs={{0,12},{1,13},{2,14},{3,15},{4,8},{5,9},{6,10},{7,11},{8,4},{9,5},... | collective-permute-start | bytes 147464 | tf_op jit(solution)/shard_map/ppermute | solution.py:406
  33.9 9.0 %collective-permute-start.12 = (bf16[4,48,128]{2,1,0:T(8,128)(2,1)S(1)}, bf16[4,48,128]{2,1,0:T(8,128)(2,1)S(1)}, u32[]{:S(2)}, u32[]{:S(2)}) collective-permute-start(bf16[4,48,128]{2,1,0:T(8,128)(2,1)S(1)} %get-tuple-element.54), channel_id=1, source_target_pairs={{0,8},{1,9},{2,10},{3,11},{4,12},{5,13},{6,14},{7,15},{8,0},{9,1},... | collective-permute-start | bytes 147464 | tf_op jit(solution)/shard_map/ppermute | solution.py:406
  34.1 8.7 %collective-permute-start.13 = (bf16[4,48,128]{2,1,0:T(8,128)(2,1)S(1)}, bf16[4,48,128]{2,1,0:T(8,128)(2,1)S(1)}, u32[]{:S(2)}, u32[]{:S(2)}) collective-permute-start(bf16[4,48,128]{2,1,0:T(8,128)(2,1)S(1)} %get-tuple-element.55), channel_id=1, source_target_pairs={{0,4},{1,5},{2,6},{3,7},{4,0},{5,1},{6,2},{7,3},{8,12},{9,13},{10,... | collective-permute-start | bytes 147464 | tf_op jit(solution)/shard_map/ppermute | solution.py:406
  37.4 10.7 %collective-permute-start.9 = (bf16[4,80,128]{2,1,0:T(8,128)(2,1)S(1)}, bf16[4,80,128]{2,1,0:T(8,128)(2,1)S(1)}, u32[]{:S(2)}, u32[]{:S(2)}) collective-permute-start(bf16[4,80,128]{2,1,0:T(8,128)(2,1)S(1)} %get-tuple-element.51), channel_id=1, source_target_pairs={{0,8},{1,9},{2,10},{3,11},{4,12},{5,13},{6,14},{7,15},{8,0},{9,1},... | collective-permute-start | bytes 245768 | tf_op jit(solution)/shard_map/ppermute | solution.py:406
  39.4 8.7 %collective-permute-start.10 = (bf16[4,80,128]{2,1,0:T(8,128)(2,1)S(1)}, bf16[4,80,128]{2,1,0:T(8,128)(2,1)S(1)}, u32[]{:S(2)}, u32[]{:S(2)}) collective-permute-start(bf16[4,80,128]{2,1,0:T(8,128)(2,1)S(1)} %get-tuple-element.52), channel_id=1, source_target_pairs={{0,4},{1,5},{2,6},{3,7},{4,0},{5,1},{6,2},{7,3},{8,12},{9,13},{10,... | collective-permute-start | bytes 245768 | tf_op jit(solution)/shard_map/ppermute | solution.py:406
  42.9 4.1 %collective-permute-start.14 = (bf16[4,48,128]{2,1,0:T(8,128)(2,1)S(1)}, bf16[4,48,128]{2,1,0:T(8,128)(2,1)S(1)}, u32[]{:S(2)}, u32[]{:S(2)}) collective-permute-start(bf16[4,48,128]{2,1,0:T(8,128)(2,1)S(1)} %get-tuple-element.57), channel_id=1, source_target_pairs={{0,3},{1,2},{2,1},{3,0},{4,7},{5,6},{6,5},{7,4},{8,11},{9,10},{10,... | collective-permute-start | bytes 147464 | tf_op jit(solution)/shard_map/ppermute | solution.py:406
  43.5 4.6 %collective-permute-start.15 = (bf16[4,48,128]{2,1,0:T(8,128)(2,1)S(1)}, bf16[4,48,128]{2,1,0:T(8,128)(2,1)S(1)}, u32[]{:S(2)}, u32[]{:S(2)}) collective-permute-start(bf16[4,48,128]{2,1,0:T(8,128)(2,1)S(1)} %get-tuple-element.58), channel_id=1, source_target_pairs={{0,2},{1,3},{2,0},{3,1},{4,6},{5,7},{6,4},{7,5},{8,10},{9,11},{10,... | collective-permute-start | bytes 147464 | tf_op jit(solution)/shard_map/ppermute | solution.py:406
  44.4 3.7 %collective-permute-start.16 = (bf16[4,48,128]{2,1,0:T(8,128)(2,1)S(1)}, bf16[4,48,128]{2,1,0:T(8,128)(2,1)S(1)}, u32[]{:S(2)}, u32[]{:S(2)}) collective-permute-start(bf16[4,48,128]{2,1,0:T(8,128)(2,1)S(1)} %get-tuple-element.59), channel_id=1, source_target_pairs={{0,1},{1,0},{2,3},{3,2},{4,5},{5,4},{6,7},{7,6},{8,9},{9,8},{10,11... | collective-permute-start | bytes 147464 | tf_op jit(solution)/shard_map/ppermute | solution.py:406

commit v14 on v12

--- a/solution.py
+++ b/solution.py
@@ -381,7 +381,8 @@
 
 
 def residual_kernel(me, observed, *refs, along_z, in_plane, outer):
-    arrived, (out, kept, sems) = refs[: len(along_z) + len(in_plane)], refs[-3:]
+    (out, kept, sems), arrived = refs[-3:], refs[:-3]
+    arrived = arrived[len(arrived) - len(along_z) - len(in_plane) :]
     rows = kept.shape[1]
     pieces = [(r, p, rows, arrived[n].at[p]) for n, r in enumerate(along_z) for p in range(4)]
     pieces += [
@@ -586,19 +587,20 @@
         return pl.pallas_call(
             functools.partial(residual_kernel, along_z=along_z, in_plane=in_plane, outer=outer),
             out_shape=jax.ShapeDtypeStruct(ours.shape, F32),
-            in_specs=[smem] + [vmem] * (1 + len(arrived)) + [anywhere] * len(held),
+            in_specs=[smem, vmem] + [anywhere] * len(held) + [vmem] * len(arrived),
             out_specs=anywhere,
             scratch_shapes=[
                 pltpu.VMEM((count, capacity, vis), F32),
                 pltpu.SemaphoreType.DMA((count,)),
             ],
-            input_output_aliases={2 + len(arrived): 0} if held else {},
+            input_output_aliases={2: 0} if held else {},
             compiler_params=pltpu.CompilerParams(vmem_limit_bytes=6 * MIB),
             name=name,
-        )(me, ours, *arrived, *held)
+        )(me, ours, *held, *arrived)
 
     residual = finish("residual_early", (0, outer - 1), (0,), ())
-    residual = finish("residual_last", tuple(range(1, outer - 1))[::-1], (3, 2, 1), (residual,))
+    residual = finish("residual_next", tuple(range(1, outer - 1))[::-1], (3,), (residual,))
+    residual = finish("residual_last", (), (2, 1), (residual,))
     return residual.reshape(observed.shape)
 
 

time: 42.6 us -> 42.3 us (level)
  waiting for transfers between devices: 7.27 us -> 6.36 us
  Pallas kernels: 12.9 us -> 13.5 us
    ppermute x18, waiting for transfers between devices: 7.27 us -> 6.36 us  [exchange(): return lax.ppermute(value, 'tile', [(i, i ^ step) for i in range(tiles)])]
    pallas_call x2 -> x3, Pallas kernels: 1.84 us -> 2.45 us  [finish(): pl.pallas_call(functools.partial(residual_kernel, along_z=along_z, in_pla...]
  transfers between devices with their start and end apart: 18 -> 18, of which waited for: 6 -> 6; matrix products, arithmetic and copies ran while one was open for 0% -> 0% of each run, Pallas kernels for 13% -> 15%
where the time goes in v14:
time: 42.3 us; the launch traced here: 42.1 us
  starting transfers between devices  20.1 us (48%)
  Pallas kernels  13.5 us (32%)
  waiting for transfers between devices  6.36 us (15%)
  local copies, waits for them, and re-layouts  1.92 us (5%)
    ppermute x18, starting transfers between devices, exchange(): return lax.ppermute(value, 'tile', [(i, i ^ step) for i in range(tiles)])  20.1 us
    ppermute x18, waiting for transfers between devices, exchange(): return lax.ppermute(value, 'tile', [(i, i ^ step) for i in range(tiles)])  6.36 us
    pallas_call x1, Pallas kernels, per_device(): pl.pallas_call(predict_kernel, out_shape=[for_z] * outer + [for_plane] *...  4.89 us
    pallas_call x3, Pallas kernels, finish(): pl.pallas_call(functools.partial(residual_kernel, along_z=along_z, in_pla...  2.45 us
    pallas_call x1, Pallas kernels, per_device(): pl.pallas_call(transform_kernel, out_shape=jax.ShapeDtypeStruct((8, numbe...  2.36 us
    unnamed x22, local copies, waits for them, and re-layouts  1.92 us
    pallas_call x1, Pallas kernels, per_device(): pl.pallas_call(pack_kernel, out_shape=[block] * outer, in_specs=[smem, hb...  1.62 us
    pallas_call x1, Pallas kernels, per_device(): pl.pallas_call(functools.partial(prepare_kernel, slot_count=slot_count),...  1.59 us
  transfers between devices with their start and end apart: 18, of which 6 were waited for; matrix products, arithmetic and copies ran while one was open for 0% of the time, Pallas kernels for 15%

profile of v14, /device:TPU:0, one launch (start us, length us, event | category | flops | bytes accessed | tf_op | source)
XLA Modules:
  0.0 42.1 jit_solution(17762953733742891379)
XLA Ops:
  0.0 0.0 copy-start.4
  0.0 0.0 copy-start.5
  0.0 1.6 %pack.1 = (bf16[160,128]{1,0:T(8,128)(2,1)}, bf16[160,128]{1,0:T(8,128)(2,1)}, bf16[160,128]{1,0:T(8,128)(2,1)}, bf16[160,128]{1,0:T(8,128)(2,1)}) custom-call(s32[1]{0:T(128)} %bitcast.me, bf16[64,256]{1,0:T(8,128)(2,1)} %bitcast.27, f32[16,8,64]{2,1,0:T(8,128)} %bitcast.26), custom_call_target="tpu_custom_call" | custom-call | tf_op jit(solution)/shard_map/pack/pallas_call | solution.py:439
  1.6 5.1 %collective-permute-start = (bf16[160,128]{1,0:T(8,128)(2,1)}, bf16[160,128]{1,0:T(8,128)(2,1)S(1)}, u32[]{:S(2)}, u32[]{:S(2)}) collective-permute-start(bf16[160,128]{1,0:T(8,128)(2,1)} %get-tuple-element.34), channel_id=1, source_target_pairs={{0,12},{1,13},{2,14},{3,15},{4,8},{5,9},{6,10},{7,11},{8,4},{9,5},... | collective-permute-start | bytes 122888 | tf_op jit(solution)/shard_map/ppermute | solution.py:403
  6.7 0.0 collective-permute-start.1
  6.8 0.6 %collective-permute-start.2 = (bf16[160,128]{1,0:T(8,128)(2,1)}, bf16[160,128]{1,0:T(8,128)(2,1)S(1)}, u32[]{:S(2)}, u32[]{:S(2)}) collective-permute-start(bf16[160,128]{1,0:T(8,128)(2,1)} %get-tuple-element.36), channel_id=1, source_target_pairs={{0,4},{1,5},{2,6},{3,7},{4,0},{5,1},{6,2},{7,3},{8,12},{9,13},{10,... | collective-permute-start | bytes 122888 | tf_op jit(solution)/shard_map/ppermute | solution.py:403
  7.4 0.0 copy-done.4
  7.4 0.0 copy-done.5
  7.4 0.0 copy-start.1
  7.4 1.2 %copy-done.1 = bf16[256,2,1024]{2,1,0:T(2,128)(2,1)S(1)} copy-done((bf16[256,2,1024]{2,1,0:T(2,128)(2,1)S(1)}, bf16[256,2,1024]{2,1,0:T(2,128)(2,1)}, u32[]{:S(2)}) %copy-start.1) | copy-done | bytes 1048600
  8.6 0.0 copy-start.3
  8.6 2.4 %transform.1.refs_4_.image = bf16[8,256,256]{2,1,0:T(8,128)(2,1)S(1)} custom-call(bf16[4096,128]{1,0:T(8,128)(2,1)S(1)} %bitcast.21, f32[2,32,128]{2,1,0:T(8,128)S(1)} %copy-done.5, f32[2,32,128]{2,1,0:T(8,128)S(1)} %copy-done.4), custom_call_target="tpu_custom_call" | custom-call | tf_op jit(solution)/shard_map/transform/pallas_call | solution.py:457
  11.0 0.0 collective-permute-done.refs_0_
  11.0 0.9 %collective-permute-done.1.refs_1_ = bf16[160,128]{1,0:T(8,128)(2,1)S(1)} collective-permute-done((bf16[160,128]{1,0:T(8,128)(2,1)}, bf16[160,128]{1,0:T(8,128)(2,1)S(1)}, u32[]{:S(2)}, u32[]{:S(2)}) %collective-permute-start.1) | collective-permute-done | bytes 40992 | tf_op jit(solution)/shard_map/ppermute | solution.py:403
  11.9 0.0 collective-permute-done.2.refs_2_
  11.9 0.0 copy-done.3
  11.9 0.0 copy-start.2
  11.9 0.0 copy-start.9
  11.9 0.0 copy-start.10
  11.9 0.0 copy-start.6
  12.0 1.6 %collective-permute-start.3 = (bf16[4,144,128]{2,1,0:T(8,128)(2,1)S(1)}, bf16[4,144,128]{2,1,0:T(8,128)(2,1)S(1)}, u32[]{:S(2)}, u32[]{:S(2)}) collective-permute-start(bf16[4,144,128]{2,1,0:T(8,128)(2,1)S(1)} %get-tuple-element.38), channel_id=1, source_target_pairs={{0,2},{1,3},{2,0},{3,1},{4,6},{5,7},{6,4},{7,5},{8,10},{9,11},{10,... | collective-permute-start | bytes 442376 | tf_op jit(solution)/shard_map/ppermute | solution.py:403
  13.5 0.0 collective-permute-start.5
  13.5 0.0 copy-start.7
  13.5 0.0 copy-done.2
  13.6 0.0 copy-done.9
  13.6 0.0 copy-done.10
  13.6 0.0 copy-done.6
  13.6 0.6 %copy-done.7 = s32[256,2]{0,1:T(2,128)S(1)} copy-done((s32[256,2]{0,1:T(2,128)S(1)}, s32[256,2]{0,1:T(2,128)}, u32[]{:S(2)}) %copy-start.7) | copy-done | bytes 2072
  14.2 0.0 copy-done.8
  14.2 1.6 %prepare.1 = (bf16[256,1024]{1,0:T(8,128)(2,1)S(1)}, bf16[1024,256]{1,0:T(8,128)(2,1)S(1)}, bf16[512,1024]{1,0:T(8,128)(2,1)S(1)}, bf16[8,256,256]{2,1,0:T(8,128)(2,1)S(1)}, f32[1,128]{1,0:T(1,128)S(1)}) custom-call(s32[1]{0:T(128)} %bitcast.me, s32[1,16]{1,0:T(1,128)S(1)} %copy-done.9, s32[16,64]{1,0:T(8,128)S(1)} %bitcast.22, s32[2,256]{1,0:T(2,128)S(1)} %bitcast.23, ...), custom_call_target="tpu_custom_call" | custom-call | tf_op jit(solution)/shard_map/prepare/pallas_call | solution.py:485
  15.8 1.3 %collective-permute-done.3.block = bf16[4,144,128]{2,1,0:T(8,128)(2,1)S(1)} collective-permute-done((bf16[4,144,128]{2,1,0:T(8,128)(2,1)S(1)}, bf16[4,144,128]{2,1,0:T(8,128)(2,1)S(1)}, u32[]{:S(2)}, u32[]{:S(2)}) %collective-permute-start.3) | collective-permute-done | bytes 147488 | tf_op jit(solution)/shard_map/ppermute | solution.py:403
  17.2 0.1 collective-permute-start.4
  17.3 0.0 collective-permute-done.5.over_core
  17.3 0.5 %early.1 = (bf16[512,256]{1,0:T(8,128)(2,1)S(1)}, f32[256,16]{1,0:T(8,128)S(1)}) custom-call(s32[1]{0:T(128)} %bitcast.me, bf16[4,160,128]{2,1,0:T(8,128)(2,1)S(1)} %get-tuple-element.39.after.near, bf16[4,160,128]{2,1,0:T(8,128)(2,1)S(1)} %collective-permute-done.5.over_core, bf16[4,144,128]{2,1,0:T(8,128)(2,1)S(1)} %relay.1.over_y, ...), custom_call_target="tpu_custom_call" | custom-call | tf_op jit(solution)/shard_map/early/pallas_call | solution.py:518
  17.8 0.8 %collective-permute-done.4.over_both = bf16[4,144,128]{2,1,0:T(8,128)(2,1)S(1)} collective-permute-done((bf16[4,144,128]{2,1,0:T(8,128)(2,1)S(1)}, bf16[4,144,128]{2,1,0:T(8,128)(2,1)S(1)}, u32[]{:S(2)}, u32[]{:S(2)}) %collective-permute-start.4) | collective-permute-done | bytes 147488 | tf_op jit(solution)/shard_map/ppermute | solution.py:403
  18.6 4.9 %predict.1 = (bf16[4,64,128]{2,1,0:T(8,128)(2,1)S(1)}, bf16[4,64,128]{2,1,0:T(8,128)(2,1)S(1)}, bf16[4,64,128]{2,1,0:T(8,128)(2,1)S(1)}, bf16[4,64,128]{2,1,0:T(...) custom-call(s32[1]{0:T(128)} %bitcast.me, ...), custom_call_target="tpu_custom_call" | custom-call | tf_op jit(solution)/shard_map/predict/pallas_call | solution.py:533
  23.5 0.2 collective-permute-start.6
  23.7 1.5 %collective-permute-start.7 = (bf16[4,64,128]{2,1,0:T(8,128)(2,1)S(1)}, bf16[4,64,128]{2,1,0:T(8,128)(2,1)S(1)}, u32[]{:S(2)}, u32[]{:S(2)}) collective-permute-start(bf16[4,64,128]{2,1,0:T(8,128)(2,1)S(1)} %get-tuple-element.48), channel_id=1, source_target_pairs={{0,2},{1,3},{2,0},{3,1},{4,6},{5,7},{6,4},{7,5},{8,10},{9,11},{10,... | collective-permute-start | bytes 196616 | tf_op jit(solution)/shard_map/ppermute | solution.py:403
  25.3 0.2 collective-permute-start.8
  25.4 2.9 %collective-permute-start.10 = (bf16[4,64,128]{2,1,0:T(8,128)(2,1)S(1)}, bf16[4,64,128]{2,1,0:T(8,128)(2,1)S(1)}, u32[]{:S(2)}, u32[]{:S(2)}) collective-permute-start(bf16[4,64,128]{2,1,0:T(8,128)(2,1)S(1)} %get-tuple-element.53), channel_id=1, source_target_pairs={{0,12},{1,13},{2,14},{3,15},{4,8},{5,9},{6,10},{7,11},{8,4},{9,5},... | collective-permute-start | bytes 196616 | tf_op jit(solution)/shard_map/ppermute | solution.py:403
  28.4 0.0 collective-permute-start.11
  28.4 0.0 collective-permute-done.6.refs_0_
  28.4 1.5 %collective-permute-start.12 = (bf16[4,64,128]{2,1,0:T(8,128)(2,1)S(1)}, bf16[4,64,128]{2,1,0:T(8,128)(2,1)S(1)}, u32[]{:S(2)}, u32[]{:S(2)}) collective-permute-start(bf16[4,64,128]{2,1,0:T(8,128)(2,1)S(1)} %get-tuple-element.55), channel_id=1, source_target_pairs={{0,4},{1,5},{2,6},{3,7},{4,0},{5,1},{6,2},{7,3},{8,12},{9,13},{10,... | collective-permute-start | bytes 196616 | tf_op jit(solution)/shard_map/ppermute | solution.py:403
  29.8 0.0 collective-permute-done.7.refs_1_
  29.8 0.0 collective-permute-done.8.refs_2_
  29.9 3.0 %collective-permute-start.9 = (bf16[4,64,128]{2,1,0:T(8,128)(2,1)S(1)}, bf16[4,64,128]{2,1,0:T(8,128)(2,1)S(1)}, u32[]{:S(2)}, u32[]{:S(2)}) collective-permute-start(bf16[4,64,128]{2,1,0:T(8,128)(2,1)S(1)} %get-tuple-element.52), channel_id=1, source_target_pairs={{0,12},{1,13},{2,14},{3,15},{4,8},{5,9},{6,10},{7,11},{8,4},{9,5},... | collective-permute-start | bytes 196616 | tf_op jit(solution)/shard_map/ppermute | solution.py:403
  32.8 0.0 collective-permute-start.13
  32.9 0.0 collective-permute-done.10.refs_0_
  32.9 1.5 %collective-permute-start.14 = (bf16[4,64,128]{2,1,0:T(8,128)(2,1)S(1)}, bf16[4,64,128]{2,1,0:T(8,128)(2,1)S(1)}, u32[]{:S(2)}, u32[]{:S(2)}) collective-permute-start(bf16[4,64,128]{2,1,0:T(8,128)(2,1)S(1)} %get-tuple-element.59), channel_id=1, source_target_pairs={{0,4},{1,5},{2,6},{3,7},{4,0},{5,1},{6,2},{7,3},{8,12},{9,13},{10,... | collective-permute-start | bytes 196616 | tf_op jit(solution)/shard_map/ppermute | solution.py:403
  34.3 1.1 %collective-permute-done.11.refs_1_ = bf16[4,64,128]{2,1,0:T(8,128)(2,1)S(1)} collective-permute-done((bf16[4,64,128]{2,1,0:T(8,128)(2,1)S(1)}, bf16[4,64,128]{2,1,0:T(8,128)(2,1)S(1)}, u32[]{:S(2)}, u32[]{:S(2)}) %collective-permute-start.11) | collective-permute-done | bytes 65568 | tf_op jit(solution)/shard_map/ppermute | solution.py:403
  35.4 0.0 collective-permute-done.12.refs_2_
  35.5 1.0 %collective-permute-start.15 = (bf16[4,64,128]{2,1,0:T(8,128)(2,1)S(1)}, bf16[4,64,128]{2,1,0:T(8,128)(2,1)S(1)}, u32[]{:S(2)}, u32[]{:S(2)}) collective-permute-start(bf16[4,64,128]{2,1,0:T(8,128)(2,1)S(1)} %get-tuple-element.60), channel_id=1, source_target_pairs={{0,3},{1,2},{2,1},{3,0},{4,7},{5,6},{6,5},{7,4},{8,11},{9,10},{10,... | collective-permute-start | bytes 196616 | tf_op jit(solution)/shard_map/ppermute | solution.py:403
  36.5 0.7 %collective-permute-start.16 = (bf16[4,64,128]{2,1,0:T(8,128)(2,1)S(1)}, bf16[4,64,128]{2,1,0:T(8,128)(2,1)S(1)}, u32[]{:S(2)}, u32[]{:S(2)}) collective-permute-start(bf16[4,64,128]{2,1,0:T(8,128)(2,1)S(1)} %get-tuple-element.61), channel_id=1, source_target_pairs={{0,2},{1,3},{2,0},{3,1},{4,6},{5,7},{6,4},{7,5},{8,10},{9,11},{10,... | collective-permute-start | bytes 196616 | tf_op jit(solution)/shard_map/ppermute | solution.py:403
  37.2 0.0 collective-permute-done.9.refs_1_
  37.2 0.2 collective-permute-start.17
  37.4 0.0 copy-done
  37.4 0.8 %residual_early.1.refs_0_ = f32[16,128,128]{2,1,0:T(8,128)} custom-call(s32[1]{0:T(128)} %bitcast.me, f32[16,128,128]{2,1,0:T(8,128)S(1)} %bitcast.18, bf16[4,64,128]{2,1,0:T(8,128)(2,1)S(1)} %get-tuple-element.51.refs_0_, bf16[4,64,128]{2,1,0:T(8,128)(2,1)S(1)} %collective-permute-done.9.refs_1_, bf16[4,64,128]{2,1,0:T(8,128)(2,1)S(1)} %get-tuple-element.57.refs_2_), custom_call_target="tpu_custom_call" | custom-call | tf_op jit(solution)/shard_map/residual_early/pallas_call | solution.py:587
  38.3 1.9 %collective-permute-done.13.refs_1_ = bf16[4,64,128]{2,1,0:T(8,128)(2,1)S(1)} collective-permute-done((bf16[4,64,128]{2,1,0:T(8,128)(2,1)S(1)}, bf16[4,64,128]{2,1,0:T(8,128)(2,1)S(1)}, u32[]{:S(2)}, u32[]{:S(2)}) %collective-permute-start.13) | collective-permute-done | bytes 65568 | tf_op jit(solution)/shard_map/ppermute | solution.py:403
  40.1 0.0 collective-permute-done.14.refs_2_
  40.1 0.0 collective-permute-done.15.refs_3_
  40.1 0.8 %residual_next.1.refs_0_ = f32[16,128,128]{2,1,0:T(8,128)} custom-call(s32[1]{0:T(128)} %bitcast.me, f32[16,128,128]{2,1,0:T(8,128)S(1)} %bitcast.19, f32[16,128,128]{2,1,0:T(8,128)} %residual_early.1.refs_0_, bf16[4,64,128]{2,1,0:T(8,128)(2,1)S(1)} %collective-permute-done.13.refs_1_, ...), custom_call_target="tpu_custom_call", output_to_operand_aliasing={{}: (2, {})} | custom-call | tf_op jit(solution)/shard_map/residual_next/pallas_call | solution.py:587
  41.0 0.4 collective-permute-done.16.refs_1_
  41.3 0.0 collective-permute-done.17.refs_2_
  41.3 0.8 %residual_last.1 = f32[16,128,128]{2,1,0:T(8,128)} custom-call(s32[1]{0:T(128)} %bitcast.me, f32[16,128,128]{2,1,0:T(8,128)S(1)} %bitcast.20, f32[16,128,128]{2,1,0:T(8,128)} %residual_next.1.refs_0_, bf16[4,64,128]{2,1,0:T(8,128)(2,1)S(1)} %collective-permute-done.16.refs_1_, ...), custom_call_target="tpu_custom_call", output_to_operand_aliasing={{}: (2, {})} | custom-call | tf_op jit(solution)/shard_map/residual_last/pallas_call | solution.py:587
  (6 shorter events, 0.1 us)
Async XLA Ops:
  0.0 7.4 %copy-start.4 = (f32[2,32,128]{2,1,0:T(8,128)S(1)}, f32[2,32,128]{2,1,0:T(8,128)}, u32[]{:S(2)}) copy-start(f32[2,32,128]{2,1,0:T(8,128)} %constant.9.clone.cell_turns) | copy-start | bytes 98308
  0.0 7.4 %copy-start.5 = (f32[2,32,128]{2,1,0:T(8,128)S(1)}, f32[2,32,128]{2,1,0:T(8,128)}, u32[]{:S(2)}) copy-start(f32[2,32,128]{2,1,0:T(8,128)} %constant.8.clone.row_turns) | copy-start | bytes 98308
  1.6 9.4 %collective-permute-start = (bf16[160,128]{1,0:T(8,128)(2,1)}, bf16[160,128]{1,0:T(8,128)(2,1)S(1)}, u32[]{:S(2)}, u32[]{:S(2)}) collective-permute-start(bf16[160,128]{1,0:T(8,128)(2,1)} %get-tuple-element.34), channel_id=1, source_target_pairs={{0,12},{1,13},{2,14},{3,15},{4,8},{5,9},{6,10},{7,11},{8,4},{9,5},... | collective-permute-start | bytes 122888 | tf_op jit(solution)/shard_map/ppermute | solution.py:403
  6.7 5.1 %collective-permute-start.1 = (bf16[160,128]{1,0:T(8,128)(2,1)}, bf16[160,128]{1,0:T(8,128)(2,1)S(1)}, u32[]{:S(2)}, u32[]{:S(2)}) collective-permute-start(bf16[160,128]{1,0:T(8,128)(2,1)} %get-tuple-element.35), channel_id=1, source_target_pairs={{0,8},{1,9},{2,10},{3,11},{4,12},{5,13},{6,14},{7,15},{8,0},{9,1},... | collective-permute-start | bytes 122888 | tf_op jit(solution)/shard_map/ppermute | solution.py:403
  6.8 5.1 %collective-permute-start.2 = (bf16[160,128]{1,0:T(8,128)(2,1)}, bf16[160,128]{1,0:T(8,128)(2,1)S(1)}, u32[]{:S(2)}, u32[]{:S(2)}) collective-permute-start(bf16[160,128]{1,0:T(8,128)(2,1)} %get-tuple-element.36), channel_id=1, source_target_pairs={{0,4},{1,5},{2,6},{3,7},{4,0},{5,1},{6,2},{7,3},{8,12},{9,13},{10,... | collective-permute-start | bytes 122888 | tf_op jit(solution)/shard_map/ppermute | solution.py:403
  7.4 1.2 %copy-start.1 = (bf16[256,2,1024]{2,1,0:T(2,128)(2,1)S(1)}, bf16[256,2,1024]{2,1,0:T(2,128)(2,1)}, u32[]{:S(2)}) copy-start(bf16[256,2,1024]{2,1,0:T(2,128)(2,1)} %param.12) | copy-start | bytes 3145732
  8.6 3.2 %copy-start.3 = (bf16[160,128]{1,0:T(8,128)(2,1)S(1)}, bf16[160,128]{1,0:T(8,128)(2,1)}, u32[]{:S(2)}) copy-start(bf16[160,128]{1,0:T(8,128)(2,1)} %get-tuple-element.37.refs_3_) | copy-start | bytes 122884
  11.9 1.7 %copy-start.2 = (bf16[2,128,1024]{2,1,0:T(8,128)(2,1)S(1)}, bf16[2,128,1024]{2,1,0:T(8,128)(2,1)}, u32[]{:S(2)}) copy-start(bf16[2,128,1024]{2,1,0:T(8,128)(2,1)} %basis.1) | copy-start | bytes 1572868
  11.9 1.7 %copy-start.9 = (s32[1,16]{1,0:T(1,128)S(1)}, s32[1,16]{1,0:T(1,128)}, u32[]{:S(2)}) copy-start(s32[1,16]{1,0:T(1,128)} %counts.1) | copy-start | bytes 196
  11.9 1.7 %copy-start.10 = (f32[32]{0:T(128)S(1)}, f32[32]{0:T(128)}, u32[]{:S(2)}) copy-start(f32[32]{0:T(128)} %param.19) | copy-start | bytes 388
  11.9 1.6 %copy-start.6 = (s32[1,16,64]{2,1,0:T(8,128)S(1)}, s32[1,16,64]{2,1,0:T(8,128)}, u32[]{:S(2)}) copy-start(s32[1,16,64]{2,1,0:T(8,128)} %param.15) | copy-start | bytes 12292
  12.0 5.2 %collective-permute-start.3 = (bf16[4,144,128]{2,1,0:T(8,128)(2,1)S(1)}, bf16[4,144,128]{2,1,0:T(8,128)(2,1)S(1)}, u32[]{:S(2)}, u32[]{:S(2)}) collective-permute-start(bf16[4,144,128]{2,1,0:T(8,128)(2,1)S(1)} %get-tuple-element.38), channel_id=1, source_target_pairs={{0,2},{1,3},{2,0},{3,1},{4,6},{5,7},{6,4},{7,5},{8,10},{9,11},{10,... | collective-permute-start | bytes 442376 | tf_op jit(solution)/shard_map/ppermute | solution.py:403
  13.5 3.7 %collective-permute-start.5 = (bf16[4,160,128]{2,1,0:T(8,128)(2,1)S(1)}, bf16[4,160,128]{2,1,0:T(8,128)(2,1)S(1)}, u32[]{:S(2)}, u32[]{:S(2)}) collective-permute-start(bf16[4,160,128]{2,1,0:T(8,128)(2,1)S(1)} %get-tuple-element.39.after.near), channel_id=1, source_target_pairs={{0,1},{1,0},{2,3},{3,2},{4,5},{5,4},{6,7},{7,6},{8,9},{9,8},{10,11... | collective-permute-start | bytes 491528 | tf_op jit(solution)/shard_map/ppermute | solution.py:403
  13.5 0.7 %copy-start.7 = (s32[256,2]{0,1:T(2,128)S(1)}, s32[256,2]{0,1:T(2,128)}, u32[]{:S(2)}) copy-start(s32[256,2]{0,1:T(2,128)} %param.13) | copy-start | bytes 6148
  13.5 0.7 %copy-start.8 = (s32[256]{0:T(256)S(1)}, s32[256]{0:T(256)}, u32[]{:S(2)}) copy-start(s32[256]{0:T(256)} %param.14) | copy-start | bytes 3076
  17.2 1.4 %collective-permute-start.4 = (bf16[4,144,128]{2,1,0:T(8,128)(2,1)S(1)}, bf16[4,144,128]{2,1,0:T(8,128)(2,1)S(1)}, u32[]{:S(2)}, u32[]{:S(2)}) collective-permute-start(bf16[4,144,128]{2,1,0:T(8,128)(2,1)S(1)} %relay.1.over_y), channel_id=1, source_target_pairs={{0,1},{1,0},{2,3},{3,2},{4,5},{5,4},{6,7},{7,6},{8,9},{9,8},{10,11... | collective-permute-start | bytes 442376 | tf_op jit(solution)/shard_map/ppermute | solution.py:403
  18.6 18.8 %copy-start = (f32[1,16,64,2,128]{4,3,2,1,0:T(2,128)S(1)}, f32[1,16,64,2,128]{4,3,2,1,0:T(2,128)}, u32[]{:S(2)}) copy-start(f32[1,16,64,2,128]{4,3,2,1,0:T(2,128)} %param.21) | copy-start | bytes 3145732
  23.5 4.8 %collective-permute-start.6 = (bf16[4,64,128]{2,1,0:T(8,128)(2,1)S(1)}, bf16[4,64,128]{2,1,0:T(8,128)(2,1)S(1)}, u32[]{:S(2)}, u32[]{:S(2)}) collective-permute-start(bf16[4,64,128]{2,1,0:T(8,128)(2,1)S(1)} %get-tuple-element.47), channel_id=1, source_target_pairs={{0,1},{1,0},{2,3},{3,2},{4,5},{5,4},{6,7},{7,6},{8,9},{9,8},{10,11... | collective-permute-start | bytes 196616 | tf_op jit(solution)/shard_map/ppermute | solution.py:403
  23.7 6.1 %collective-permute-start.7 = (bf16[4,64,128]{2,1,0:T(8,128)(2,1)S(1)}, bf16[4,64,128]{2,1,0:T(8,128)(2,1)S(1)}, u32[]{:S(2)}, u32[]{:S(2)}) collective-permute-start(bf16[4,64,128]{2,1,0:T(8,128)(2,1)S(1)} %get-tuple-element.48), channel_id=1, source_target_pairs={{0,2},{1,3},{2,0},{3,1},{4,6},{5,7},{6,4},{7,5},{8,10},{9,11},{10,... | collective-permute-start | bytes 196616 | tf_op jit(solution)/shard_map/ppermute | solution.py:403
  25.3 4.6 %collective-permute-start.8 = (bf16[4,64,128]{2,1,0:T(8,128)(2,1)S(1)}, bf16[4,64,128]{2,1,0:T(8,128)(2,1)S(1)}, u32[]{:S(2)}, u32[]{:S(2)}) collective-permute-start(bf16[4,64,128]{2,1,0:T(8,128)(2,1)S(1)} %get-tuple-element.49), channel_id=1, source_target_pairs={{0,3},{1,2},{2,1},{3,0},{4,7},{5,6},{6,5},{7,4},{8,11},{9,10},{10,... | collective-permute-start | bytes 196616 | tf_op jit(solution)/shard_map/ppermute | solution.py:403
  25.4 7.4 %collective-permute-start.10 = (bf16[4,64,128]{2,1,0:T(8,128)(2,1)S(1)}, bf16[4,64,128]{2,1,0:T(8,128)(2,1)S(1)}, u32[]{:S(2)}, u32[]{:S(2)}) collective-permute-start(bf16[4,64,128]{2,1,0:T(8,128)(2,1)S(1)} %get-tuple-element.53), channel_id=1, source_target_pairs={{0,12},{1,13},{2,14},{3,15},{4,8},{5,9},{6,10},{7,11},{8,4},{9,5},... | collective-permute-start | bytes 196616 | tf_op jit(solution)/shard_map/ppermute | solution.py:403
  28.4 7.1 %collective-permute-start.11 = (bf16[4,64,128]{2,1,0:T(8,128)(2,1)S(1)}, bf16[4,64,128]{2,1,0:T(8,128)(2,1)S(1)}, u32[]{:S(2)}, u32[]{:S(2)}) collective-permute-start(bf16[4,64,128]{2,1,0:T(8,128)(2,1)S(1)} %get-tuple-element.54), channel_id=1, source_target_pairs={{0,8},{1,9},{2,10},{3,11},{4,12},{5,13},{6,14},{7,15},{8,0},{9,1},... | collective-permute-start | bytes 196616 | tf_op jit(solution)/shard_map/ppermute | solution.py:403
  28.4 7.1 %collective-permute-start.12 = (bf16[4,64,128]{2,1,0:T(8,128)(2,1)S(1)}, bf16[4,64,128]{2,1,0:T(8,128)(2,1)S(1)}, u32[]{:S(2)}, u32[]{:S(2)}) collective-permute-start(bf16[4,64,128]{2,1,0:T(8,128)(2,1)S(1)} %get-tuple-element.55), channel_id=1, source_target_pairs={{0,4},{1,5},{2,6},{3,7},{4,0},{5,1},{6,2},{7,3},{8,12},{9,13},{10,... | collective-permute-start | bytes 196616 | tf_op jit(solution)/shard_map/ppermute | solution.py:403
  29.9 7.3 %collective-permute-start.9 = (bf16[4,64,128]{2,1,0:T(8,128)(2,1)S(1)}, bf16[4,64,128]{2,1,0:T(8,128)(2,1)S(1)}, u32[]{:S(2)}, u32[]{:S(2)}) collective-permute-start(bf16[4,64,128]{2,1,0:T(8,128)(2,1)S(1)} %get-tuple-element.52), channel_id=1, source_target_pairs={{0,12},{1,13},{2,14},{3,15},{4,8},{5,9},{6,10},{7,11},{8,4},{9,5},... | collective-permute-start | bytes 196616 | tf_op jit(solution)/shard_map/ppermute | solution.py:403
  32.8 7.3 %collective-permute-start.13 = (bf16[4,64,128]{2,1,0:T(8,128)(2,1)S(1)}, bf16[4,64,128]{2,1,0:T(8,128)(2,1)S(1)}, u32[]{:S(2)}, u32[]{:S(2)}) collective-permute-start(bf16[4,64,128]{2,1,0:T(8,128)(2,1)S(1)} %get-tuple-element.58), channel_id=1, source_target_pairs={{0,8},{1,9},{2,10},{3,11},{4,12},{5,13},{6,14},{7,15},{8,0},{9,1},... | collective-permute-start | bytes 196616 | tf_op jit(solution)/shard_map/ppermute | solution.py:403
  32.9 7.3 %collective-permute-start.14 = (bf16[4,64,128]{2,1,0:T(8,128)(2,1)S(1)}, bf16[4,64,128]{2,1,0:T(8,128)(2,1)S(1)}, u32[]{:S(2)}, u32[]{:S(2)}) collective-permute-start(bf16[4,64,128]{2,1,0:T(8,128)(2,1)S(1)} %get-tuple-element.59), channel_id=1, source_target_pairs={{0,4},{1,5},{2,6},{3,7},{4,0},{5,1},{6,2},{7,3},{8,12},{9,13},{10,... | collective-permute-start | bytes 196616 | tf_op jit(solution)/shard_map/ppermute | solution.py:403
  35.5 4.7 %collective-permute-start.15 = (bf16[4,64,128]{2,1,0:T(8,128)(2,1)S(1)}, bf16[4,64,128]{2,1,0:T(8,128)(2,1)S(1)}, u32[]{:S(2)}, u32[]{:S(2)}) collective-permute-start(bf16[4,64,128]{2,1,0:T(8,128)(2,1)S(1)} %get-tuple-element.60), channel_id=1, source_target_pairs={{0,3},{1,2},{2,1},{3,0},{4,7},{5,6},{6,5},{7,4},{8,11},{9,10},{10,... | collective-permute-start | bytes 196616 | tf_op jit(solution)/shard_map/ppermute | solution.py:403
  36.5 4.8 %collective-permute-start.16 = (bf16[4,64,128]{2,1,0:T(8,128)(2,1)S(1)}, bf16[4,64,128]{2,1,0:T(8,128)(2,1)S(1)}, u32[]{:S(2)}, u32[]{:S(2)}) collective-permute-start(bf16[4,64,128]{2,1,0:T(8,128)(2,1)S(1)} %get-tuple-element.61), channel_id=1, source_target_pairs={{0,2},{1,3},{2,0},{3,1},{4,6},{5,7},{6,4},{7,5},{8,10},{9,11},{10,... | collective-permute-start | bytes 196616 | tf_op jit(solution)/shard_map/ppermute | solution.py:403
  37.2 4.2 %collective-permute-start.17 = (bf16[4,64,128]{2,1,0:T(8,128)(2,1)S(1)}, bf16[4,64,128]{2,1,0:T(8,128)(2,1)S(1)}, u32[]{:S(2)}, u32[]{:S(2)}) collective-permute-start(bf16[4,64,128]{2,1,0:T(8,128)(2,1)S(1)} %get-tuple-element.62), channel_id=1, source_target_pairs={{0,1},{1,0},{2,3},{3,2},{4,5},{5,4},{6,7},{7,6},{8,9},{9,8},{10,11... | collective-permute-start | bytes 196616 | tf_op jit(solution)/shard_map/ppermute | solution.py:403

commit v15 on v14

--- a/solution.py
+++ b/solution.py
@@ -253,7 +253,7 @@
     per_sub_early,
     *refs,
 ):
-    table, coef, wre, wim, pure, puim, zrow, hre, him, zv, interleaved = refs[-11:]
+    table, coef, wre, wim, pure, puim, zrow, hre, him, zv = refs[-10:]
     number = image.shape[1]
     slots = back.shape[0]
     outer = over_both.shape[0]
@@ -363,14 +363,15 @@
     m_re, m_im = a_re * cr + a_im * ci, a_im * cr - a_re * ci
     models = jnp.concatenate([m_re, m_im], axis=1).astype(BF16)
     sent = dot(back[...], models)
-    interleaved[pl.ds(0, slots, stride=2), :] = sent[:, :128]
-    interleaved[pl.ds(1, slots, stride=2), :] = sent[:, 128:]
     along_z, in_plane = refs[:outer], refs[outer : outer + 4]
+    half = capacity // 2
     for r in range(outer):
         for p in range(4):
-            start = (p * outer + r) * (2 * capacity)
-            along_z[r][p] = interleaved[start : start + capacity, :].astype(BF16)
-            in_plane[p][r] = interleaved[start + capacity : start + 2 * capacity, :].astype(BF16)
+            for start, out in ((0, along_z[r].at[p]), (half, in_plane[p].at[r])):
+                at = (p * outer + r) * capacity + start
+                block = sent[at : at + half, :]
+                block = jnp.concatenate([block[:, :vis], block[:, vis:]], axis=0)
+                out[...] = block.astype(BF16)
 
 
 def turn_kernel(*refs, order):
@@ -391,7 +392,12 @@
     copies = []
     for n, (r, p, start, values) in enumerate(pieces):
         source = me[0] ^ (4 * r + p)
-        kept[n] = observed[source, start : start + rows, :] - values[...].astype(F32)
+        models = values[...].astype(F32)
+        for part in range(2):
+            own = observed[source, pl.ds(start + part, rows // 2, stride=2), :]
+            kept[n, pl.ds(part, rows // 2, stride=2), :] = (
+                own - models[part * (rows // 2) : (part + 1) * (rows // 2), :]
+            )
         copy = pltpu.make_async_copy(kept.at[n], out.at[source, pl.ds(start, rows), :], sems.at[n])
         copy.start()
         copies.append(copy)
@@ -546,7 +552,6 @@
             pltpu.VMEM((number * 8, vis), F32),
             pltpu.VMEM((number * 8, vis), F32),
             pltpu.VMEM((2, number, vis), F32),
-            pltpu.VMEM((2 * slots, vis), F32),
         ],
         compiler_params=pltpu.CompilerParams(vmem_limit_bytes=20 * MIB * (1 + tiles // 64)),
         name="predict",

time: 42.3 us -> 42.3 us (level)
  no operation moved by 1% of the time
where the time goes in v15:
time: 42.3 us; the launch traced here: 42 us
  starting transfers between devices  20.1 us (48%)
  Pallas kernels  13.5 us (32%)
  waiting for transfers between devices  6.37 us (15%)
  local copies, waits for them, and re-layouts  1.92 us (5%)
    ppermute x18, starting transfers between devices, exchange(): return lax.ppermute(value, 'tile', [(i, i ^ step) for i in range(tiles)])  20.1 us
    ppermute x18, waiting for transfers between devices, exchange(): return lax.ppermute(value, 'tile', [(i, i ^ step) for i in range(tiles)])  6.37 us
    pallas_call x1, Pallas kernels, per_device(): pl.pallas_call(predict_kernel, out_shape=[for_z] * outer + [for_plane] *...  4.84 us
    pallas_call x3, Pallas kernels, finish(): pl.pallas_call(functools.partial(residual_kernel, along_z=along_z, in_pla...  2.45 us
    pallas_call x1, Pallas kernels, per_device(): pl.pallas_call(transform_kernel, out_shape=jax.ShapeDtypeStruct((8, numbe...  2.36 us
    unnamed x22, local copies, waits for them, and re-layouts  1.92 us
    pallas_call x1, Pallas kernels, per_device(): pl.pallas_call(pack_kernel, out_shape=[block] * outer, in_specs=[smem, hb...  1.62 us
    pallas_call x1, Pallas kernels, per_device(): pl.pallas_call(functools.partial(prepare_kernel, slot_count=slot_count),...  1.59 us
  transfers between devices with their start and end apart: 18, of which 6 were waited for; matrix products, arithmetic and copies ran while one was open for 0% of the time, Pallas kernels for 15%

profile of v15, /device:TPU:0, one launch (start us, length us, event | category | flops | bytes accessed | tf_op | source)
XLA Modules:
  0.0 42.0 jit_solution(1804855508582187957)
XLA Ops:
  0.0 0.0 copy-start.4
  0.0 0.0 copy-start.5
  0.0 1.6 %pack.1 = (bf16[160,128]{1,0:T(8,128)(2,1)}, bf16[160,128]{1,0:T(8,128)(2,1)}, bf16[160,128]{1,0:T(8,128)(2,1)}, bf16[160,128]{1,0:T(8,128)(2,1)}) custom-call(s32[1]{0:T(128)} %bitcast.me, bf16[64,256]{1,0:T(8,128)(2,1)} %bitcast.27, f32[16,8,64]{2,1,0:T(8,128)} %bitcast.26), custom_call_target="tpu_custom_call" | custom-call | tf_op jit(solution)/shard_map/pack/pallas_call | solution.py:445
  1.6 5.1 %collective-permute-start = (bf16[160,128]{1,0:T(8,128)(2,1)}, bf16[160,128]{1,0:T(8,128)(2,1)S(1)}, u32[]{:S(2)}, u32[]{:S(2)}) collective-permute-start(bf16[160,128]{1,0:T(8,128)(2,1)} %get-tuple-element.34), channel_id=1, source_target_pairs={{0,12},{1,13},{2,14},{3,15},{4,8},{5,9},{6,10},{7,11},{8,4},{9,5},... | collective-permute-start | bytes 122888 | tf_op jit(solution)/shard_map/ppermute | solution.py:409
  6.7 0.0 collective-permute-start.1
  6.8 0.6 %collective-permute-start.2 = (bf16[160,128]{1,0:T(8,128)(2,1)}, bf16[160,128]{1,0:T(8,128)(2,1)S(1)}, u32[]{:S(2)}, u32[]{:S(2)}) collective-permute-start(bf16[160,128]{1,0:T(8,128)(2,1)} %get-tuple-element.36), channel_id=1, source_target_pairs={{0,4},{1,5},{2,6},{3,7},{4,0},{5,1},{6,2},{7,3},{8,12},{9,13},{10,... | collective-permute-start | bytes 122888 | tf_op jit(solution)/shard_map/ppermute | solution.py:409
  7.4 0.0 copy-done.4
  7.4 0.0 copy-done.5
  7.4 0.0 copy-start.1
  7.4 1.2 %copy-done.1 = bf16[256,2,1024]{2,1,0:T(2,128)(2,1)S(1)} copy-done((bf16[256,2,1024]{2,1,0:T(2,128)(2,1)S(1)}, bf16[256,2,1024]{2,1,0:T(2,128)(2,1)}, u32[]{:S(2)}) %copy-start.1) | copy-done | bytes 1048600
  8.6 0.0 copy-start.3
  8.6 2.4 %transform.1.refs_4_.image = bf16[8,256,256]{2,1,0:T(8,128)(2,1)S(1)} custom-call(bf16[4096,128]{1,0:T(8,128)(2,1)S(1)} %bitcast.21, f32[2,32,128]{2,1,0:T(8,128)S(1)} %copy-done.5, f32[2,32,128]{2,1,0:T(8,128)S(1)} %copy-done.4), custom_call_target="tpu_custom_call" | custom-call | tf_op jit(solution)/shard_map/transform/pallas_call | solution.py:463
  11.0 0.0 collective-permute-done.refs_0_
  11.0 0.9 %collective-permute-done.1.refs_1_ = bf16[160,128]{1,0:T(8,128)(2,1)S(1)} collective-permute-done((bf16[160,128]{1,0:T(8,128)(2,1)}, bf16[160,128]{1,0:T(8,128)(2,1)S(1)}, u32[]{:S(2)}, u32[]{:S(2)}) %collective-permute-start.1) | collective-permute-done | bytes 40992 | tf_op jit(solution)/shard_map/ppermute | solution.py:409
  11.9 0.0 collective-permute-done.2.refs_2_
  11.9 0.0 copy-done.3
  11.9 0.0 copy-start.2
  11.9 0.0 copy-start.9
  11.9 0.0 copy-start.10
  11.9 0.0 copy-start.6
  12.0 1.6 %collective-permute-start.3 = (bf16[4,144,128]{2,1,0:T(8,128)(2,1)S(1)}, bf16[4,144,128]{2,1,0:T(8,128)(2,1)S(1)}, u32[]{:S(2)}, u32[]{:S(2)}) collective-permute-start(bf16[4,144,128]{2,1,0:T(8,128)(2,1)S(1)} %get-tuple-element.38), channel_id=1, source_target_pairs={{0,2},{1,3},{2,0},{3,1},{4,6},{5,7},{6,4},{7,5},{8,10},{9,11},{10,... | collective-permute-start | bytes 442376 | tf_op jit(solution)/shard_map/ppermute | solution.py:409
  13.5 0.0 collective-permute-start.5
  13.5 0.0 copy-start.7
  13.5 0.0 copy-done.2
  13.6 0.0 copy-done.9
  13.6 0.0 copy-done.10
  13.6 0.0 copy-done.6
  13.6 0.6 %copy-done.7 = s32[256,2]{0,1:T(2,128)S(1)} copy-done((s32[256,2]{0,1:T(2,128)S(1)}, s32[256,2]{0,1:T(2,128)}, u32[]{:S(2)}) %copy-start.7) | copy-done | bytes 2072
  14.2 0.0 copy-done.8
  14.2 1.6 %prepare.1 = (bf16[256,1024]{1,0:T(8,128)(2,1)S(1)}, bf16[1024,256]{1,0:T(8,128)(2,1)S(1)}, bf16[512,1024]{1,0:T(8,128)(2,1)S(1)}, bf16[8,256,256]{2,1,0:T(8,128)(2,1)S(1)}, f32[1,128]{1,0:T(1,128)S(1)}) custom-call(s32[1]{0:T(128)} %bitcast.me, s32[1,16]{1,0:T(1,128)S(1)} %copy-done.9, s32[16,64]{1,0:T(8,128)S(1)} %bitcast.22, s32[2,256]{1,0:T(2,128)S(1)} %bitcast.23, ...), custom_call_target="tpu_custom_call" | custom-call | tf_op jit(solution)/shard_map/prepare/pallas_call | solution.py:491
  15.8 1.3 %collective-permute-done.3.block = bf16[4,144,128]{2,1,0:T(8,128)(2,1)S(1)} collective-permute-done((bf16[4,144,128]{2,1,0:T(8,128)(2,1)S(1)}, bf16[4,144,128]{2,1,0:T(8,128)(2,1)S(1)}, u32[]{:S(2)}, u32[]{:S(2)}) %collective-permute-start.3) | collective-permute-done | bytes 147488 | tf_op jit(solution)/shard_map/ppermute | solution.py:409
  17.2 0.1 collective-permute-start.4
  17.3 0.0 collective-permute-done.5.over_core
  17.3 0.5 %early.1 = (bf16[512,256]{1,0:T(8,128)(2,1)S(1)}, f32[256,16]{1,0:T(8,128)S(1)}) custom-call(s32[1]{0:T(128)} %bitcast.me, bf16[4,160,128]{2,1,0:T(8,128)(2,1)S(1)} %get-tuple-element.39.after.near, bf16[4,160,128]{2,1,0:T(8,128)(2,1)S(1)} %collective-permute-done.5.over_core, bf16[4,144,128]{2,1,0:T(8,128)(2,1)S(1)} %relay.1.over_y, ...), custom_call_target="tpu_custom_call" | custom-call | tf_op jit(solution)/shard_map/early/pallas_call | solution.py:524
  17.8 0.8 %collective-permute-done.4.over_both = bf16[4,144,128]{2,1,0:T(8,128)(2,1)S(1)} collective-permute-done((bf16[4,144,128]{2,1,0:T(8,128)(2,1)S(1)}, bf16[4,144,128]{2,1,0:T(8,128)(2,1)S(1)}, u32[]{:S(2)}, u32[]{:S(2)}) %collective-permute-start.4) | collective-permute-done | bytes 147488 | tf_op jit(solution)/shard_map/ppermute | solution.py:409
  18.6 4.8 %predict.1 = (bf16[4,64,128]{2,1,0:T(8,128)(2,1)S(1)}, bf16[4,64,128]{2,1,0:T(8,128)(2,1)S(1)}, bf16[4,64,128]{2,1,0:T(8,128)(2,1)S(1)}, bf16[4,64,128]{2,1,0:T(...) custom-call(s32[1]{0:T(128)} %bitcast.me, ...), custom_call_target="tpu_custom_call" | custom-call | tf_op jit(solution)/shard_map/predict/pallas_call | solution.py:539
  23.5 0.2 collective-permute-start.6
  23.7 1.5 %collective-permute-start.7 = (bf16[4,64,128]{2,1,0:T(8,128)(2,1)S(1)}, bf16[4,64,128]{2,1,0:T(8,128)(2,1)S(1)}, u32[]{:S(2)}, u32[]{:S(2)}) collective-permute-start(bf16[4,64,128]{2,1,0:T(8,128)(2,1)S(1)} %get-tuple-element.48), channel_id=1, source_target_pairs={{0,2},{1,3},{2,0},{3,1},{4,6},{5,7},{6,4},{7,5},{8,10},{9,11},{10,... | collective-permute-start | bytes 196616 | tf_op jit(solution)/shard_map/ppermute | solution.py:409
  25.2 0.2 collective-permute-start.8
  25.4 2.9 %collective-permute-start.10 = (bf16[4,64,128]{2,1,0:T(8,128)(2,1)S(1)}, bf16[4,64,128]{2,1,0:T(8,128)(2,1)S(1)}, u32[]{:S(2)}, u32[]{:S(2)}) collective-permute-start(bf16[4,64,128]{2,1,0:T(8,128)(2,1)S(1)} %get-tuple-element.53), channel_id=1, source_target_pairs={{0,12},{1,13},{2,14},{3,15},{4,8},{5,9},{6,10},{7,11},{8,4},{9,5},... | collective-permute-start | bytes 196616 | tf_op jit(solution)/shard_map/ppermute | solution.py:409
  28.3 0.0 collective-permute-start.11
  28.3 0.0 collective-permute-done.6.refs_0_
  28.3 1.5 %collective-permute-start.12 = (bf16[4,64,128]{2,1,0:T(8,128)(2,1)S(1)}, bf16[4,64,128]{2,1,0:T(8,128)(2,1)S(1)}, u32[]{:S(2)}, u32[]{:S(2)}) collective-permute-start(bf16[4,64,128]{2,1,0:T(8,128)(2,1)S(1)} %get-tuple-element.55), channel_id=1, source_target_pairs={{0,4},{1,5},{2,6},{3,7},{4,0},{5,1},{6,2},{7,3},{8,12},{9,13},{10,... | collective-permute-start | bytes 196616 | tf_op jit(solution)/shard_map/ppermute | solution.py:409
  29.8 0.0 collective-permute-done.7.refs_1_
  29.8 0.0 collective-permute-done.8.refs_2_
  29.8 3.0 %collective-permute-start.9 = (bf16[4,64,128]{2,1,0:T(8,128)(2,1)S(1)}, bf16[4,64,128]{2,1,0:T(8,128)(2,1)S(1)}, u32[]{:S(2)}, u32[]{:S(2)}) collective-permute-start(bf16[4,64,128]{2,1,0:T(8,128)(2,1)S(1)} %get-tuple-element.52), channel_id=1, source_target_pairs={{0,12},{1,13},{2,14},{3,15},{4,8},{5,9},{6,10},{7,11},{8,4},{9,5},... | collective-permute-start | bytes 196616 | tf_op jit(solution)/shard_map/ppermute | solution.py:409
  32.8 0.0 collective-permute-start.13
  32.8 0.0 collective-permute-done.10.refs_0_
  32.8 1.5 %collective-permute-start.14 = (bf16[4,64,128]{2,1,0:T(8,128)(2,1)S(1)}, bf16[4,64,128]{2,1,0:T(8,128)(2,1)S(1)}, u32[]{:S(2)}, u32[]{:S(2)}) collective-permute-start(bf16[4,64,128]{2,1,0:T(8,128)(2,1)S(1)} %get-tuple-element.59), channel_id=1, source_target_pairs={{0,4},{1,5},{2,6},{3,7},{4,0},{5,1},{6,2},{7,3},{8,12},{9,13},{10,... | collective-permute-start | bytes 196616 | tf_op jit(solution)/shard_map/ppermute | solution.py:409
  34.3 1.1 %collective-permute-done.11.refs_1_ = bf16[4,64,128]{2,1,0:T(8,128)(2,1)S(1)} collective-permute-done((bf16[4,64,128]{2,1,0:T(8,128)(2,1)S(1)}, bf16[4,64,128]{2,1,0:T(8,128)(2,1)S(1)}, u32[]{:S(2)}, u32[]{:S(2)}) %collective-permute-start.11) | collective-permute-done | bytes 65568 | tf_op jit(solution)/shard_map/ppermute | solution.py:409
  35.4 0.0 collective-permute-done.12.refs_2_
  35.4 1.0 %collective-permute-start.15 = (bf16[4,64,128]{2,1,0:T(8,128)(2,1)S(1)}, bf16[4,64,128]{2,1,0:T(8,128)(2,1)S(1)}, u32[]{:S(2)}, u32[]{:S(2)}) collective-permute-start(bf16[4,64,128]{2,1,0:T(8,128)(2,1)S(1)} %get-tuple-element.60), channel_id=1, source_target_pairs={{0,3},{1,2},{2,1},{3,0},{4,7},{5,6},{6,5},{7,4},{8,11},{9,10},{10,... | collective-permute-start | bytes 196616 | tf_op jit(solution)/shard_map/ppermute | solution.py:409
  36.5 0.7 %collective-permute-start.16 = (bf16[4,64,128]{2,1,0:T(8,128)(2,1)S(1)}, bf16[4,64,128]{2,1,0:T(8,128)(2,1)S(1)}, u32[]{:S(2)}, u32[]{:S(2)}) collective-permute-start(bf16[4,64,128]{2,1,0:T(8,128)(2,1)S(1)} %get-tuple-element.61), channel_id=1, source_target_pairs={{0,2},{1,3},{2,0},{3,1},{4,6},{5,7},{6,4},{7,5},{8,10},{9,11},{10,... | collective-permute-start | bytes 196616 | tf_op jit(solution)/shard_map/ppermute | solution.py:409
  37.1 0.0 collective-permute-done.9.refs_1_
  37.1 0.2 collective-permute-start.17
  37.3 0.0 copy-done
  37.4 0.8 %residual_early.1.refs_0_ = f32[16,128,128]{2,1,0:T(8,128)} custom-call(s32[1]{0:T(128)} %bitcast.me, f32[16,128,128]{2,1,0:T(8,128)S(1)} %bitcast.18, bf16[4,64,128]{2,1,0:T(8,128)(2,1)S(1)} %get-tuple-element.51.refs_0_, bf16[4,64,128]{2,1,0:T(8,128)(2,1)S(1)} %collective-permute-done.9.refs_1_, bf16[4,64,128]{2,1,0:T(8,128)(2,1)S(1)} %get-tuple-element.57.refs_2_), custom_call_target="tpu_custom_call" | custom-call | tf_op jit(solution)/shard_map/residual_early/pallas_call | solution.py:592
  38.2 1.9 %collective-permute-done.13.refs_1_ = bf16[4,64,128]{2,1,0:T(8,128)(2,1)S(1)} collective-permute-done((bf16[4,64,128]{2,1,0:T(8,128)(2,1)S(1)}, bf16[4,64,128]{2,1,0:T(8,128)(2,1)S(1)}, u32[]{:S(2)}, u32[]{:S(2)}) %collective-permute-start.13) | collective-permute-done | bytes 65568 | tf_op jit(solution)/shard_map/ppermute | solution.py:409
  40.1 0.0 collective-permute-done.14.refs_2_
  40.1 0.0 collective-permute-done.15.refs_3_
  40.1 0.8 %residual_next.1.refs_0_ = f32[16,128,128]{2,1,0:T(8,128)} custom-call(s32[1]{0:T(128)} %bitcast.me, f32[16,128,128]{2,1,0:T(8,128)S(1)} %bitcast.19, f32[16,128,128]{2,1,0:T(8,128)} %residual_early.1.refs_0_, bf16[4,64,128]{2,1,0:T(8,128)(2,1)S(1)} %collective-permute-done.13.refs_1_, ...), custom_call_target="tpu_custom_call", output_to_operand_aliasing={{}: (2, {})} | custom-call | tf_op jit(solution)/shard_map/residual_next/pallas_call | solution.py:592
  40.9 0.4 collective-permute-done.16.refs_1_
  41.3 0.0 collective-permute-done.17.refs_2_
  41.3 0.8 %residual_last.1 = f32[16,128,128]{2,1,0:T(8,128)} custom-call(s32[1]{0:T(128)} %bitcast.me, f32[16,128,128]{2,1,0:T(8,128)S(1)} %bitcast.20, f32[16,128,128]{2,1,0:T(8,128)} %residual_next.1.refs_0_, bf16[4,64,128]{2,1,0:T(8,128)(2,1)S(1)} %collective-permute-done.16.refs_1_, ...), custom_call_target="tpu_custom_call", output_to_operand_aliasing={{}: (2, {})} | custom-call | tf_op jit(solution)/shard_map/residual_last/pallas_call | solution.py:592
  (6 shorter events, 0.1 us)
Async XLA Ops:
  0.0 7.4 %copy-start.4 = (f32[2,32,128]{2,1,0:T(8,128)S(1)}, f32[2,32,128]{2,1,0:T(8,128)}, u32[]{:S(2)}) copy-start(f32[2,32,128]{2,1,0:T(8,128)} %constant.9.clone.cell_turns) | copy-start | bytes 98308
  0.0 7.4 %copy-start.5 = (f32[2,32,128]{2,1,0:T(8,128)S(1)}, f32[2,32,128]{2,1,0:T(8,128)}, u32[]{:S(2)}) copy-start(f32[2,32,128]{2,1,0:T(8,128)} %constant.8.clone.row_turns) | copy-start | bytes 98308
  1.6 9.4 %collective-permute-start = (bf16[160,128]{1,0:T(8,128)(2,1)}, bf16[160,128]{1,0:T(8,128)(2,1)S(1)}, u32[]{:S(2)}, u32[]{:S(2)}) collective-permute-start(bf16[160,128]{1,0:T(8,128)(2,1)} %get-tuple-element.34), channel_id=1, source_target_pairs={{0,12},{1,13},{2,14},{3,15},{4,8},{5,9},{6,10},{7,11},{8,4},{9,5},... | collective-permute-start | bytes 122888 | tf_op jit(solution)/shard_map/ppermute | solution.py:409
  6.7 5.1 %collective-permute-start.1 = (bf16[160,128]{1,0:T(8,128)(2,1)}, bf16[160,128]{1,0:T(8,128)(2,1)S(1)}, u32[]{:S(2)}, u32[]{:S(2)}) collective-permute-start(bf16[160,128]{1,0:T(8,128)(2,1)} %get-tuple-element.35), channel_id=1, source_target_pairs={{0,8},{1,9},{2,10},{3,11},{4,12},{5,13},{6,14},{7,15},{8,0},{9,1},... | collective-permute-start | bytes 122888 | tf_op jit(solution)/shard_map/ppermute | solution.py:409
  6.8 5.1 %collective-permute-start.2 = (bf16[160,128]{1,0:T(8,128)(2,1)}, bf16[160,128]{1,0:T(8,128)(2,1)S(1)}, u32[]{:S(2)}, u32[]{:S(2)}) collective-permute-start(bf16[160,128]{1,0:T(8,128)(2,1)} %get-tuple-element.36), channel_id=1, source_target_pairs={{0,4},{1,5},{2,6},{3,7},{4,0},{5,1},{6,2},{7,3},{8,12},{9,13},{10,... | collective-permute-start | bytes 122888 | tf_op jit(solution)/shard_map/ppermute | solution.py:409
  7.4 1.2 %copy-start.1 = (bf16[256,2,1024]{2,1,0:T(2,128)(2,1)S(1)}, bf16[256,2,1024]{2,1,0:T(2,128)(2,1)}, u32[]{:S(2)}) copy-start(bf16[256,2,1024]{2,1,0:T(2,128)(2,1)} %param.12) | copy-start | bytes 3145732
  8.6 3.2 %copy-start.3 = (bf16[160,128]{1,0:T(8,128)(2,1)S(1)}, bf16[160,128]{1,0:T(8,128)(2,1)}, u32[]{:S(2)}) copy-start(bf16[160,128]{1,0:T(8,128)(2,1)} %get-tuple-element.37.refs_3_) | copy-start | bytes 122884
  11.9 1.7 %copy-start.2 = (bf16[2,128,1024]{2,1,0:T(8,128)(2,1)S(1)}, bf16[2,128,1024]{2,1,0:T(8,128)(2,1)}, u32[]{:S(2)}) copy-start(bf16[2,128,1024]{2,1,0:T(8,128)(2,1)} %basis.1) | copy-start | bytes 1572868
  11.9 1.7 %copy-start.9 = (s32[1,16]{1,0:T(1,128)S(1)}, s32[1,16]{1,0:T(1,128)}, u32[]{:S(2)}) copy-start(s32[1,16]{1,0:T(1,128)} %counts.1) | copy-start | bytes 196
  11.9 1.7 %copy-start.10 = (f32[32]{0:T(128)S(1)}, f32[32]{0:T(128)}, u32[]{:S(2)}) copy-start(f32[32]{0:T(128)} %param.19) | copy-start | bytes 388
  11.9 1.6 %copy-start.6 = (s32[1,16,64]{2,1,0:T(8,128)S(1)}, s32[1,16,64]{2,1,0:T(8,128)}, u32[]{:S(2)}) copy-start(s32[1,16,64]{2,1,0:T(8,128)} %param.15) | copy-start | bytes 12292
  12.0 5.2 %collective-permute-start.3 = (bf16[4,144,128]{2,1,0:T(8,128)(2,1)S(1)}, bf16[4,144,128]{2,1,0:T(8,128)(2,1)S(1)}, u32[]{:S(2)}, u32[]{:S(2)}) collective-permute-start(bf16[4,144,128]{2,1,0:T(8,128)(2,1)S(1)} %get-tuple-element.38), channel_id=1, source_target_pairs={{0,2},{1,3},{2,0},{3,1},{4,6},{5,7},{6,4},{7,5},{8,10},{9,11},{10,... | collective-permute-start | bytes 442376 | tf_op jit(solution)/shard_map/ppermute | solution.py:409
  13.5 3.7 %collective-permute-start.5 = (bf16[4,160,128]{2,1,0:T(8,128)(2,1)S(1)}, bf16[4,160,128]{2,1,0:T(8,128)(2,1)S(1)}, u32[]{:S(2)}, u32[]{:S(2)}) collective-permute-start(bf16[4,160,128]{2,1,0:T(8,128)(2,1)S(1)} %get-tuple-element.39.after.near), channel_id=1, source_target_pairs={{0,1},{1,0},{2,3},{3,2},{4,5},{5,4},{6,7},{7,6},{8,9},{9,8},{10,11... | collective-permute-start | bytes 491528 | tf_op jit(solution)/shard_map/ppermute | solution.py:409
  13.5 0.7 %copy-start.7 = (s32[256,2]{0,1:T(2,128)S(1)}, s32[256,2]{0,1:T(2,128)}, u32[]{:S(2)}) copy-start(s32[256,2]{0,1:T(2,128)} %param.13) | copy-start | bytes 6148
  13.5 0.7 %copy-start.8 = (s32[256]{0:T(256)S(1)}, s32[256]{0:T(256)}, u32[]{:S(2)}) copy-start(s32[256]{0:T(256)} %param.14) | copy-start | bytes 3076
  17.2 1.4 %collective-permute-start.4 = (bf16[4,144,128]{2,1,0:T(8,128)(2,1)S(1)}, bf16[4,144,128]{2,1,0:T(8,128)(2,1)S(1)}, u32[]{:S(2)}, u32[]{:S(2)}) collective-permute-start(bf16[4,144,128]{2,1,0:T(8,128)(2,1)S(1)} %relay.1.over_y), channel_id=1, source_target_pairs={{0,1},{1,0},{2,3},{3,2},{4,5},{5,4},{6,7},{7,6},{8,9},{9,8},{10,11... | collective-permute-start | bytes 442376 | tf_op jit(solution)/shard_map/ppermute | solution.py:409
  18.6 18.7 %copy-start = (f32[1,16,64,2,128]{4,3,2,1,0:T(2,128)S(1)}, f32[1,16,64,2,128]{4,3,2,1,0:T(2,128)}, u32[]{:S(2)}) copy-start(f32[1,16,64,2,128]{4,3,2,1,0:T(2,128)} %param.21) | copy-start | bytes 3145732
  23.5 4.8 %collective-permute-start.6 = (bf16[4,64,128]{2,1,0:T(8,128)(2,1)S(1)}, bf16[4,64,128]{2,1,0:T(8,128)(2,1)S(1)}, u32[]{:S(2)}, u32[]{:S(2)}) collective-permute-start(bf16[4,64,128]{2,1,0:T(8,128)(2,1)S(1)} %get-tuple-element.47), channel_id=1, source_target_pairs={{0,1},{1,0},{2,3},{3,2},{4,5},{5,4},{6,7},{7,6},{8,9},{9,8},{10,11... | collective-permute-start | bytes 196616 | tf_op jit(solution)/shard_map/ppermute | solution.py:409
  23.7 6.1 %collective-permute-start.7 = (bf16[4,64,128]{2,1,0:T(8,128)(2,1)S(1)}, bf16[4,64,128]{2,1,0:T(8,128)(2,1)S(1)}, u32[]{:S(2)}, u32[]{:S(2)}) collective-permute-start(bf16[4,64,128]{2,1,0:T(8,128)(2,1)S(1)} %get-tuple-element.48), channel_id=1, source_target_pairs={{0,2},{1,3},{2,0},{3,1},{4,6},{5,7},{6,4},{7,5},{8,10},{9,11},{10,... | collective-permute-start | bytes 196616 | tf_op jit(solution)/shard_map/ppermute | solution.py:409
  25.2 4.6 %collective-permute-start.8 = (bf16[4,64,128]{2,1,0:T(8,128)(2,1)S(1)}, bf16[4,64,128]{2,1,0:T(8,128)(2,1)S(1)}, u32[]{:S(2)}, u32[]{:S(2)}) collective-permute-start(bf16[4,64,128]{2,1,0:T(8,128)(2,1)S(1)} %get-tuple-element.49), channel_id=1, source_target_pairs={{0,3},{1,2},{2,1},{3,0},{4,7},{5,6},{6,5},{7,4},{8,11},{9,10},{10,... | collective-permute-start | bytes 196616 | tf_op jit(solution)/shard_map/ppermute | solution.py:409
  25.4 7.4 %collective-permute-start.10 = (bf16[4,64,128]{2,1,0:T(8,128)(2,1)S(1)}, bf16[4,64,128]{2,1,0:T(8,128)(2,1)S(1)}, u32[]{:S(2)}, u32[]{:S(2)}) collective-permute-start(bf16[4,64,128]{2,1,0:T(8,128)(2,1)S(1)} %get-tuple-element.53), channel_id=1, source_target_pairs={{0,12},{1,13},{2,14},{3,15},{4,8},{5,9},{6,10},{7,11},{8,4},{9,5},... | collective-permute-start | bytes 196616 | tf_op jit(solution)/shard_map/ppermute | solution.py:409
  28.3 7.1 %collective-permute-start.11 = (bf16[4,64,128]{2,1,0:T(8,128)(2,1)S(1)}, bf16[4,64,128]{2,1,0:T(8,128)(2,1)S(1)}, u32[]{:S(2)}, u32[]{:S(2)}) collective-permute-start(bf16[4,64,128]{2,1,0:T(8,128)(2,1)S(1)} %get-tuple-element.54), channel_id=1, source_target_pairs={{0,8},{1,9},{2,10},{3,11},{4,12},{5,13},{6,14},{7,15},{8,0},{9,1},... | collective-permute-start | bytes 196616 | tf_op jit(solution)/shard_map/ppermute | solution.py:409
  28.3 7.1 %collective-permute-start.12 = (bf16[4,64,128]{2,1,0:T(8,128)(2,1)S(1)}, bf16[4,64,128]{2,1,0:T(8,128)(2,1)S(1)}, u32[]{:S(2)}, u32[]{:S(2)}) collective-permute-start(bf16[4,64,128]{2,1,0:T(8,128)(2,1)S(1)} %get-tuple-element.55), channel_id=1, source_target_pairs={{0,4},{1,5},{2,6},{3,7},{4,0},{5,1},{6,2},{7,3},{8,12},{9,13},{10,... | collective-permute-start | bytes 196616 | tf_op jit(solution)/shard_map/ppermute | solution.py:409
  29.8 7.3 %collective-permute-start.9 = (bf16[4,64,128]{2,1,0:T(8,128)(2,1)S(1)}, bf16[4,64,128]{2,1,0:T(8,128)(2,1)S(1)}, u32[]{:S(2)}, u32[]{:S(2)}) collective-permute-start(bf16[4,64,128]{2,1,0:T(8,128)(2,1)S(1)} %get-tuple-element.52), channel_id=1, source_target_pairs={{0,12},{1,13},{2,14},{3,15},{4,8},{5,9},{6,10},{7,11},{8,4},{9,5},... | collective-permute-start | bytes 196616 | tf_op jit(solution)/shard_map/ppermute | solution.py:409
  32.8 7.3 %collective-permute-start.13 = (bf16[4,64,128]{2,1,0:T(8,128)(2,1)S(1)}, bf16[4,64,128]{2,1,0:T(8,128)(2,1)S(1)}, u32[]{:S(2)}, u32[]{:S(2)}) collective-permute-start(bf16[4,64,128]{2,1,0:T(8,128)(2,1)S(1)} %get-tuple-element.58), channel_id=1, source_target_pairs={{0,8},{1,9},{2,10},{3,11},{4,12},{5,13},{6,14},{7,15},{8,0},{9,1},... | collective-permute-start | bytes 196616 | tf_op jit(solution)/shard_map/ppermute | solution.py:409
  32.8 7.3 %collective-permute-start.14 = (bf16[4,64,128]{2,1,0:T(8,128)(2,1)S(1)}, bf16[4,64,128]{2,1,0:T(8,128)(2,1)S(1)}, u32[]{:S(2)}, u32[]{:S(2)}) collective-permute-start(bf16[4,64,128]{2,1,0:T(8,128)(2,1)S(1)} %get-tuple-element.59), channel_id=1, source_target_pairs={{0,4},{1,5},{2,6},{3,7},{4,0},{5,1},{6,2},{7,3},{8,12},{9,13},{10,... | collective-permute-start | bytes 196616 | tf_op jit(solution)/shard_map/ppermute | solution.py:409
  35.4 4.7 %collective-permute-start.15 = (bf16[4,64,128]{2,1,0:T(8,128)(2,1)S(1)}, bf16[4,64,128]{2,1,0:T(8,128)(2,1)S(1)}, u32[]{:S(2)}, u32[]{:S(2)}) collective-permute-start(bf16[4,64,128]{2,1,0:T(8,128)(2,1)S(1)} %get-tuple-element.60), channel_id=1, source_target_pairs={{0,3},{1,2},{2,1},{3,0},{4,7},{5,6},{6,5},{7,4},{8,11},{9,10},{10,... | collective-permute-start | bytes 196616 | tf_op jit(solution)/shard_map/ppermute | solution.py:409
  36.5 4.8 %collective-permute-start.16 = (bf16[4,64,128]{2,1,0:T(8,128)(2,1)S(1)}, bf16[4,64,128]{2,1,0:T(8,128)(2,1)S(1)}, u32[]{:S(2)}, u32[]{:S(2)}) collective-permute-start(bf16[4,64,128]{2,1,0:T(8,128)(2,1)S(1)} %get-tuple-element.61), channel_id=1, source_target_pairs={{0,2},{1,3},{2,0},{3,1},{4,6},{5,7},{6,4},{7,5},{8,10},{9,11},{10,... | collective-permute-start | bytes 196616 | tf_op jit(solution)/shard_map/ppermute | solution.py:409
  37.1 4.2 %collective-permute-start.17 = (bf16[4,64,128]{2,1,0:T(8,128)(2,1)S(1)}, bf16[4,64,128]{2,1,0:T(8,128)(2,1)S(1)}, u32[]{:S(2)}, u32[]{:S(2)}) collective-permute-start(bf16[4,64,128]{2,1,0:T(8,128)(2,1)S(1)} %get-tuple-element.62), channel_id=1, source_target_pairs={{0,1},{1,0},{2,3},{3,2},{4,5},{5,4},{6,7},{7,6},{8,9},{9,8},{10,11... | collective-permute-start | bytes 196616 | tf_op jit(solution)/shard_map/ppermute | solution.py:409
